TPU v7x, 128 devices: a whole 4x4x4 slice. The times are simulated.
128 devices in a mesh: side: 2 (over z_hi), dev: 64 (over z_lo, x, y, core).
Axes of the slice: x: 4, y: 4, z: 4 (z_hi: 2, z_lo: 2; z = z_hi * 2 + z_lo), core: 2. Of those that a mesh axis runs over, the one named last changes fastest.
Arguments:
- query_latent: bfloat16 [384, 128, 576], P('dev'), may hold values from -192 to 192
- latent_cache: bfloat16 [384, 1024, 576], P('dev', 'side'), may hold values from -6 to 6
- lengths: int32 [384], P('dev'), may hold values from 128 to 1024, as said below
- stream: bfloat16 [384, 7168], P(('side', 'dev')), may hold values from -6 to 6
- norm_gain: float32 [7168], replicated, may hold values from 0.25 to 1.75
- value_up: bfloat16 [128, 512, 128], P(('side', 'dev')), may hold values from -1.5 to 1.5
- out_proj: bfloat16 [16384, 7168], P(('side', 'dev')), may hold values from -0.046875 to 0.046875
- gate_proj: bfloat16 [7168, 18432], P(None, 'dev'), may hold values from -0.0625 to 0.0625
- up_proj: bfloat16 [7168, 18432], P(None, 'dev'), may hold values from -0.0625 to 0.0625
- down_proj: bfloat16 [18432, 7168], P('dev'), may hold values from -0.046875 to 0.046875
Outputs:
- new_stream: bfloat16 [384, 7168], P(('side', 'dev'))
Inputs may be any that keep to these rules, and one draw needn't show every extreme that they name: `lengths`: each row's number of valid cached positions, at least 128; some row has exactly 1024.
All inputs are finite; a program needn't handle non-finite values.
Results may differ from a plain program's by a relative error of at most 0.02.
Values may be sent and summed in bfloat16 or wider, within the bound.
No kernel may reach another device: no remote copies, remote signals or barrier semaphores. Data moves between devices by JAX's collectives and lax.ppermute only.
A program may use at most 128 MiB of HBM per device.

v0:
```python
import math

import jax
import jax.numpy as jnp
from jax import lax
from jax.sharding import PartitionSpec as P

LAT = 512
QKD = 192


def local(
    query_latent,
    latent_cache,
    lengths,
    stream,
    norm_gain,
    value_up,
    out_proj,
    gate_proj,
    up_proj,
    down_proj,
):
    side_index = lax.axis_index("side")
    half_keys = latent_cache.shape[1]
    positions = side_index * half_keys + lax.iota(jnp.int32, half_keys)
    usable = (positions[None, :] < lengths[:, None])[:, None, :]
    scores = jnp.einsum(
        "rhc,rkc->rhk", query_latent, latent_cache, preferred_element_type=jnp.float32
    ) * (1.0 / math.sqrt(QKD))
    scores = jnp.where(usable, scores, jnp.float32(-1e30))
    row_peak = lax.pmax(jnp.max(scores, axis=2), "side")
    exponent = jnp.where(usable, jnp.exp(scores - row_peak[:, :, None]), jnp.float32(0.0))
    row_total = jnp.sum(exponent, axis=2)
    weighted = jnp.einsum(
        "rhk,rkc->rhc",
        exponent.astype(jnp.bfloat16),
        latent_cache[:, :, :LAT],
        preferred_element_type=jnp.float32,
    )
    weighted, row_total = (
        lax.psum_scatter(
            weighted.astype(jnp.bfloat16), "side", scatter_dimension=1, tiled=True
        ).astype(jnp.float32),
        lax.psum_scatter(
            row_total.astype(jnp.bfloat16), "side", scatter_dimension=1, tiled=True
        ).astype(jnp.float32),
    )
    latent = (weighted / row_total[:, :, None]).astype(jnp.bfloat16)
    received = lax.all_to_all(latent, "dev", split_axis=1, concat_axis=0, tiled=True)
    all_rows = received.shape[0]
    values = jnp.einsum(
        "rhc,hcd->rhd", received, value_up, preferred_element_type=jnp.float32
    ).astype(jnp.bfloat16)
    values = values.reshape(all_rows, -1)
    block = values
    attended = lax.psum_scatter(
        jnp.dot(block, out_proj, preferred_element_type=jnp.float32),
        ("side", "dev"),
        scatter_dimension=0,
        tiled=True,
    )
    residual = stream.astype(jnp.float32) + attended
    mean_square = jnp.mean(residual * residual, axis=1, keepdims=True)
    normalized = (residual * lax.rsqrt(mean_square + 1e-06) * norm_gain).astype(jnp.bfloat16)
    piece = lax.all_gather(normalized, "dev", axis=0, tiled=True)
    gate = jnp.dot(piece, gate_proj, preferred_element_type=jnp.float32)
    upper = jnp.dot(piece, up_proj, preferred_element_type=jnp.float32)
    hidden = (jax.nn.silu(gate) * upper).astype(jnp.bfloat16)
    block = hidden
    feed_out = lax.psum_scatter(
        jnp.dot(block, down_proj, preferred_element_type=jnp.float32),
        "dev",
        scatter_dimension=0,
        tiled=True,
    )
    return (residual + feed_out).astype(jnp.bfloat16)


def solution(mesh):
    placed = (
        P("dev", None, None),
        P("dev", "side", None),
        P("dev"),
        P(("side", "dev"), None),
        P(),
        P(("side", "dev"), None, None),
        P(("side", "dev"), None),
        P(None, "dev"),
        P(None, "dev"),
        P("dev", None),
    )
    return jax.shard_map(
        local, mesh=mesh, in_specs=placed, out_specs=P(("side", "dev"), None), check_vma=False
    )
```

profile of v0, /device:TPU:1, one launch (start us, length us, event | category | flops | bytes accessed | tf_op | source)
XLA Modules:
  0.0 944.5 jit_solution(4021450080297066282)
XLA Ops:
  6.5 0.0 copy-start
  6.5 0.0 reduce-scatter.7.cloned.1.call-start
  6.5 0.9 broadcast_compare_fusion
  7.4 3.2 fusion.26
  10.6 6.7 pmax.7
  17.4 0.5 fusion.5
  17.9 0.7 copy.16
  18.6 0.0 reduce-scatter.7.cloned.1.call-update
  18.6 0.0 reduce-scatter.5.cloned.1.call-start
  18.7 4.0 fusion.2
  22.6 0.0 copy-start.2
  22.6 0.0 reduce-scatter.5.cloned.1.call-update
  22.7 0.0 all-reduce.5.cloned.1.call-start
  22.7 12.5 %reduce-scatter.7.cloned.1.call-done = bf16[64,6]{1,0:T(8,128)(2,1)} async-done(((bf16[128,6]{1,0:T(8,128)(2,1)}), bf16[64,6]{1,0:T(8,128)(2,1)}) %reduce-scatter.7.cloned.1.call-update) | async-done | bytes 784
  35.2 0.8 copy.17
  36.0 22.9 %reduce-scatter.5.cloned.1.call-done = bf16[6,64,512]{2,1,0:T(8,128)(2,1)} async-done(((bf16[6,128,512]{2,1,0:T(8,128)(2,1)}), bf16[6,64,512]{2,1,0:T(8,128)(2,1)}) %reduce-scatter.5.cloned.1.call-update) | async-done | bytes 393232 | tf_op jit(solution)/shard_map/reduce_scatter | solution.py:42
  58.9 1.1 divide_convert_fusion
  60.1 0.2 copy.15
  60.3 19.8 %all_to_all.15 = bf16[6,64,512]{2,0,1:T(8,128)(2,1)S(1)} all-to-all(bf16[6,64,512]{2,0,1:T(8,128)(2,1)S(1)} %copy.15), channel_id=1, replica_groups=mesh['side'=2,'dev'=64] {'dev'}, dimensions={1} | all-to-all | bytes 786432 | tf_op jit(solution)/shard_map/all_to_all | solution.py:50
  80.1 0.1 reshape.48
  80.2 0.0 copy-done
  80.2 0.0 copy-done.2
  80.2 6.0 fusion.9
  86.2 0.0 copy-start.1
  86.2 0.0 copy-start.3
  86.2 0.0 all-reduce.5.cloned.1.call-update
  86.2 0.0 all-gather.3.cloned.1.call-start
  86.3 162.6 %all-reduce.5.cloned.1.call-done = f32[384,7168]{1,0:T(8,128)} async-done(((f32[384,7168]{1,0:T(8,128)}), f32[384,7168]{1,0:T(8,128)}) %all-reduce.5.cloned.1.call-update) | async-done | bytes 11010064
  248.9 0.0 copy-done.1
  248.9 1.2 multiply_reduce_fusion
  250.1 0.0 copy-done.3
  250.1 1.7 fusion.23
  251.9 0.0 all-gather.3.cloned.1.call-update
  251.9 0.0 all-reduce.7.cloned.1.call-start
  252.0 104.3 %all-gather.3.cloned.1.call-done = bf16[64,3,7168]{2,1,0:T(4,128)(2,1)} async-done(((bf16[1,3,7168]{2,1,0:T(4,128)(2,1)}), bf16[64,3,7168]{2,1,0:T(4,128)(2,1)}) %all-gather.3.cloned.1.call-update) | async-done | bytes 2752528 | tf_op jit(solution)/shard_map/all_gather | solution.py:66
  356.2 7.1 reshape.51
  363.3 5.0 fusion.27
  368.3 10.5 %fusion.8 = f32[192,7168]{1,0:T(8,128)} fusion(bf16[288,7168]{1,0:T(8,128)(2,1)} %param.19, bf16[192,7168]{1,0:T(8,128)(2,1)} %reshape.51, bf16[7168,288]{0,1:T(8,128)(2,1)} %param.18, f32[192,288]{1,0:T(8,128)S(1)} %fusion.27), kind=kOutput, calls=%fused_computation.9 | convolution fusion | flops 1585778688 | bytes 16736256 | tf_op jit(solution)/shard_map/dot_general | solution.py:72
  378.9 0.0 copy-start.4
  378.9 0.0 all-reduce.7.cloned.1.call-update
  378.9 0.6 copy-done.4
  379.5 0.6 dynamic-slice.1
  380.7 555.3 %all-reduce.7.cloned.1.call-done = f32[192,7168]{1,0:T(8,128)} async-done(((f32[192,7168]{1,0:T(8,128)}), f32[192,7168]{1,0:T(8,128)}) %all-reduce.7.cloned.1.call-update) | async-done | bytes 5505040
  936.1 1.8 fusion.22
  (3 shorter events, 0.0 us)
Async XLA Ops:
  6.5 73.7 %copy-start = (bf16[128,7168]{1,0:T(8,128)(2,1)S(1)}, bf16[128,7168]{1,0:T(8,128)(2,1)}, u32[]{:S(2)}) copy-start(bf16[128,7168]{1,0:T(8,128)(2,1)} %param.16) | copy-start | bytes 5505028
  6.5 28.7 %reduce-scatter.7.cloned.1.call-start = ((), (), s32[]{:S(2)}) async-start(), calls=%async_computation.5 | async-start | bytes 49152
  18.6 40.3 %reduce-scatter.5.cloned.1.call-start = ((), (), s32[]{:S(2)}) async-start(), calls=%async_computation.3 | async-start | bytes 1179648 | tf_op jit(solution)/shard_map/reduce_scatter | solution.py:42
  22.6 57.6 %copy-start.2 = (bf16[1,512,128]{2,1,0:T(8,128)(2,1)S(1)}, bf16[1,512,128]{2,1,0:T(8,128)(2,1)}, u32[]{:S(2)}) copy-start(bf16[1,512,128]{2,1,0:T(8,128)(2,1)} %param.15) | copy-start | bytes 393220
  22.7 226.3 %all-reduce.5.cloned.1.call-start = ((), (), s32[]{:S(2)}) async-start(), calls=%async_computation.6 | async-start | bytes 22020096
  86.2 162.7 %copy-start.1 = (bf16[3,7168]{1,0:T(4,128)(2,1)S(1)}, bf16[3,7168]{1,0:T(4,128)(2,1)}, u32[]{:S(2)}) copy-start(bf16[3,7168]{1,0:T(4,128)(2,1)} %param.13) | copy-start | bytes 129028
  86.2 163.9 %copy-start.3 = (f32[7168]{0:T(1024)S(1)}, f32[7168]{0:T(1024)}, u32[]{:S(2)}) copy-start(f32[7168]{0:T(1024)} %param.14) | copy-start | bytes 86020
  86.2 270.0 %all-gather.3.cloned.1.call-start = ((), (), s32[]{:S(2)}) async-start(), calls=%async_computation.4 | async-start | bytes 3727360 | tf_op jit(solution)/shard_map/all_gather | solution.py:66
  251.9 684.2 %all-reduce.7.cloned.1.call-start = ((), (), s32[]{:S(2)}) async-start(), calls=%async_computation.7 | async-start | bytes 11010048
  378.9 0.7 copy-start.4
Sparse Core Ops, SparseCore 0:
  18.7 16.4 reduce-scatter.6
  37.6 21.2 reduce-scatter.4
  86.4 162.5 all-reduce.4
  252.0 104.1 all-gather.2
  379.0 557.0 all-reduce.6
where the time goes:
time: 948 us; the launch traced here: 944 us
  waiting for transfers between devices  858 us (91%)
  matrix products  28.7 us (3%)
  blocking collectives  26.5 us (3%)
  between operations  13.9 us (1%)
  local copies, waits for them, and re-layouts  10.2 us (1%)
    unnamed x8, waiting for transfers between devices  731 us
    all_gather x1, waiting for transfers between devices, local(): piece = lax.all_gather(normalized, 'dev', axis=0, tiled=True)  104 us
    reduce_scatter x1, waiting for transfers between devices, local(): lax.psum_scatter(weighted.astype(jnp.bfloat16), 'side', scatter_dimension...  22.9 us
    all_to_all x1, blocking collectives, local(): lax.all_to_all(latent, 'dev', split_axis=1, concat_axis=0, tiled=True)  19.8 us
  transfers between devices with their start and end apart: 5, of which 5 were waited for; matrix products, arithmetic and copies ran while one was open for 1% of the time, Pallas kernels for 0%

commit v1 on v0

v1 whole, which is shorter than its diff:
```python
import math

import jax
import jax.numpy as jnp
from jax import lax
from jax.sharding import Mesh, PartitionSpec as P

LAT = 512
QKD = 192
AXES = ("zh", "zl", "x", "y", "core")
DEV = ("zl", "x", "y", "core")
CHIPS = ("zh", "zl", "x", "y")
SIDE_CHIPS = ("zl", "x", "y")
SWAP = [(0, 1), (1, 0)]
F32 = jnp.float32
BF16 = jnp.bfloat16


def swap_halves(array, core, axis):
    half = array.shape[axis] // 2
    mine = lax.dynamic_slice_in_dim(array, core * half, half, axis)
    theirs = lax.dynamic_slice_in_dim(array, (1 - core) * half, half, axis)
    return mine, lax.ppermute(theirs, "core", SWAP)


def split_pair(value):
    high = lax.reduce_precision(value, 8, 7)
    low = lax.reduce_precision(value - high, 8, 7)
    return high, low


def local(
    query_latent,
    latent_cache,
    lengths,
    stream,
    norm_gain,
    value_up,
    out_proj,
    gate_proj,
    up_proj,
    down_proj,
):
    core = lax.axis_index("core")
    rows_own, width = stream.shape
    half = width // 2
    out_mine, out_theirs = swap_halves(out_proj, core, 1)
    down_mine, down_theirs = swap_halves(down_proj, core, 1)
    stream_mine, stream_theirs = swap_halves(stream, core, 1)
    first = core == 0
    stream_rows = jnp.concatenate(
        [
            jnp.where(first, stream_mine, stream_theirs),
            jnp.where(first, stream_theirs, stream_mine),
        ],
        axis=0,
    ).astype(F32)

    rows, heads, _ = query_latent.shape
    half_keys = latent_cache.shape[1]
    positions = lax.axis_index("zh") * half_keys + lax.iota(jnp.int32, half_keys)
    usable = (positions[None, :] < lengths[:, None])[:, None, :]
    scores = jnp.einsum(
        "rhc,rkc->rhk", query_latent, latent_cache, preferred_element_type=F32
    ) * (1.0 / math.sqrt(QKD))
    scores = jnp.where(usable, scores, F32(-1e30))
    peak_high, peak_low = split_pair(jnp.max(scores, axis=2))
    peak = peak_high + peak_low
    exponent = jnp.where(usable, jnp.exp(scores - peak[:, :, None]), F32(0.0))
    total_high, total_low = split_pair(jnp.sum(exponent, axis=2))
    weighted = jnp.einsum(
        "rhk,rkc->rhc",
        exponent.astype(BF16),
        latent_cache[:, :, :LAT],
        preferred_element_type=F32,
    ).astype(BF16)
    stats = jnp.stack([peak_high, peak_low, total_high, total_low]).astype(BF16)
    stats = stats.transpose(2, 0, 1).reshape(heads, 1, 4 * rows)
    stats = jnp.pad(stats, ((0, 0), (0, 1), (0, LAT - 4 * rows)))
    payload = jnp.concatenate([weighted.transpose(1, 0, 2), stats], axis=1)
    received = lax.all_to_all(payload, AXES, split_axis=0, concat_axis=0, tiled=True)

    devs = received.shape[0] // 2
    received = received.reshape(2, devs, rows + 2, LAT)
    stats = received[:, :, rows, : 4 * rows].reshape(2, devs, 4, rows).astype(F32)
    peaks = stats[:, :, 0] + stats[:, :, 1]
    totals = stats[:, :, 2] + stats[:, :, 3]
    factor = jnp.exp(peaks - jnp.max(peaks, axis=0, keepdims=True))
    factor = factor / jnp.sum(factor * totals, axis=0, keepdims=True)
    latent = jnp.sum(received[:, :, :rows].astype(F32) * factor[..., None], axis=0).astype(BF16)
    latent = latent.reshape(devs * rows, LAT)
    values = jnp.dot(latent, value_up[0], preferred_element_type=F32).astype(BF16)
    values_theirs = lax.ppermute(values, "core", SWAP)
    partial = jnp.dot(values, out_mine, preferred_element_type=F32) + jnp.dot(
        values_theirs, out_theirs, preferred_element_type=F32
    )

    chips = devs
    chunk = 2 * rows_own
    partial = partial.astype(BF16).reshape(chips, chunk * half // 128, 128)
    parts = lax.all_to_all(partial, CHIPS, split_axis=0, concat_axis=0, tiled=True)
    attended = jnp.sum(parts.astype(F32), axis=0).reshape(chunk, half)
    residual = stream_rows + attended
    squares = jnp.sum(residual * residual, axis=1)
    squares = squares + lax.ppermute(squares, "core", SWAP)
    scale = lax.rsqrt(squares / width + 1e-06)
    gain = lax.dynamic_slice_in_dim(norm_gain, core * half, half, 0)
    normalized = (residual * scale[:, None] * gain).astype(BF16)

    side_chips = chips // 2
    normalized = normalized.reshape(1, chunk * half // 128, 128)
    normalized = jnp.broadcast_to(normalized, (side_chips,) + normalized.shape[1:])
    piece = lax.all_to_all(normalized, SIDE_CHIPS, split_axis=0, concat_axis=0, tiled=True)
    piece = piece.reshape(side_chips * chunk, half)
    piece_theirs = lax.ppermute(piece, "core", SWAP)

    def hidden_units(weight):
        mine = lax.dynamic_slice_in_dim(weight, core * half, half, 0)
        theirs = lax.dynamic_slice_in_dim(weight, (1 - core) * half, half, 0)
        return jnp.dot(piece, mine, preferred_element_type=F32) + jnp.dot(
            piece_theirs, theirs, preferred_element_type=F32
        )

    hidden = (jax.nn.silu(hidden_units(gate_proj)) * hidden_units(up_proj)).astype(BF16)
    hidden_theirs = lax.ppermute(hidden, "core", SWAP)
    partial = jnp.dot(hidden, down_mine, preferred_element_type=F32) + jnp.dot(
        hidden_theirs, down_theirs, preferred_element_type=F32
    )
    partial = partial.astype(BF16).reshape(side_chips, chunk * half // 128, 128)
    parts = lax.all_to_all(partial, SIDE_CHIPS, split_axis=0, concat_axis=0, tiled=True)
    feed_out = jnp.sum(parts.astype(F32), axis=0).reshape(chunk, half)
    new_stream = (residual + feed_out).astype(BF16)
    mine = lax.dynamic_slice_in_dim(new_stream, core * rows_own, rows_own, 0)
    theirs = lax.dynamic_slice_in_dim(new_stream, (1 - core) * rows_own, rows_own, 0)
    theirs = lax.ppermute(theirs, "core", SWAP)
    return jnp.concatenate(
        [jnp.where(first, mine, theirs), jnp.where(first, theirs, mine)], axis=1
    )


def solution(mesh):
    fine = Mesh(mesh.devices.reshape(2, 2, 4, 4, 2), AXES)
    placed = (
        P(DEV, None, None),
        P(DEV, "zh", None),
        P(DEV),
        P(AXES, None),
        P(),
        P(AXES, None, None),
        P(AXES, None),
        P(None, DEV),
        P(None, DEV),
        P(DEV, None),
    )
    return jax.shard_map(
        local, mesh=fine, in_specs=placed, out_specs=P(AXES, None), check_vma=False
    )
```

time: 948 us -> 170 us (0.18)
  waiting for transfers between devices: 858 us -> 73.1 us
  starting transfers between devices: 0.17 us -> 30.5 us
  between operations: 13.9 us -> 0.38 us
  matrix products: 28.7 us -> 17 us
    unnamed x8 -> x0, waiting for transfers between devices: 731 us -> none
    all_gather x1 -> x0, waiting for transfers between devices: 104 us -> none  [local(): piece = lax.all_gather(normalized, 'dev', axis=0, tiled=True)]
    all_to_all x0 -> x3, waiting for transfers between devices: none -> 70.7 us  [the longest x1 34.5 us: local(): lax.all_to_all(partial, CHIPS, split_axis=0, concat_axis=0, tiled=True)]
    reduce_scatter x1 -> x0, waiting for transfers between devices: 22.9 us -> none  [local(): lax.psum_scatter(weighted.astype(jnp.bfloat16), 'side', scatter_dimension...]
    all_to_all x0 -> x3, starting transfers between devices: none -> 21.1 us  [the longest x1 11.5 us: local(): lax.all_to_all(payload, AXES, split_axis=0, concat_axis=0, tiled=True)]
    dot_general x4 -> x10, matrix products: 25.4 us -> 13.7 us  [the longest x2 3.85 us: hidden_units(): jnp.dot(piece, mine, preferred_element_type=F32)]
    reshape x0 -> x7, local copies, waits for them, and re-layouts: none -> 11.5 us  [the longest x1 6.42 us: local(): partial = partial.astype(BF16).reshape(chips, chunk * half // 128, 128)]
  transfers between devices with their start and end apart: 5 -> 11, of which waited for: 5 -> 7; matrix products, arithmetic and copies ran while one was open for 1% -> 7% of each run, Pallas kernels for 0% -> 0%
where the time goes in v1:
time: 170 us; the launch traced here: 169 us
  waiting for transfers between devices  73.1 us (43%)
  starting transfers between devices  30.5 us (18%)
  blocking collectives  24.5 us (14%)
  local copies, waits for them, and re-layouts  18.6 us (11%)
  matrix products  17 us (10%)
  other arithmetic  5.29 us (3%)
    all_to_all x1, waiting for transfers between devices, local(): lax.all_to_all(partial, CHIPS, split_axis=0, concat_axis=0, tiled=True)  34.5 us
    all_to_all x1, blocking collectives, local(): lax.all_to_all(normalized, SIDE_CHIPS, split_axis=0, concat_axis=0, tiled...  24.5 us
    all_to_all x1, waiting for transfers between devices, local(): lax.all_to_all(partial, SIDE_CHIPS, split_axis=0, concat_axis=0, tiled=True)  19.4 us
    all_to_all x1, waiting for transfers between devices, local(): lax.all_to_all(payload, AXES, split_axis=0, concat_axis=0, tiled=True)  16.8 us
    all_to_all x1, starting transfers between devices, local(): lax.all_to_all(payload, AXES, split_axis=0, concat_axis=0, tiled=True)  11.5 us
    reshape x1, local copies, waits for them, and re-layouts, local(): partial = partial.astype(BF16).reshape(chips, chunk * half // 128, 128)  6.42 us
    all_to_all x1, starting transfers between devices, local(): lax.all_to_all(partial, CHIPS, split_axis=0, concat_axis=0, tiled=True)  5.7 us
    all_to_all x1, starting transfers between devices, local(): lax.all_to_all(partial, SIDE_CHIPS, split_axis=0, concat_axis=0, tiled=True)  3.96 us
  transfers between devices with their start and end apart: 11, of which 7 were waited for; matrix products, arithmetic and copies ran while one was open for 7% of the time, Pallas kernels for 0%

profile of v1, /device:TPU:1, one launch (start us, length us, event | category | flops | bytes accessed | tf_op | source)
XLA Modules:
  0.0 169.5 jit_solution(525475101944362618)
XLA Ops:
  0.0 0.9 broadcast_compare_fusion
  0.9 3.4 %fusion.58 = (f32[6,128]{1,0:T(8,128)S(1)}, f32[6,128,512]{2,1,0:T(8,128)S(1)}) fusion(bf16[6,128,576]{1,2,0:T(8,128)(2,1)} %param.10, bf16[6,512,576]{1,2,0:T(8,128)(2,1)} %param.11, pred[6,512]{1,0:T(8,128)(4,1)S(1)} %broadcast_compare_fusion), kind=kOutput, calls=%fused_computation.84 | convolution fusion | flops 454163712 | bytes 6002688 | tf_op jit(solution)/shard_map/rhc,rkc->rhk/dot_general | solution.py:63
  4.3 0.5 fusion.21
  4.7 1.2 fusion.18
  6.0 0.1 copy.26
  6.1 0.1 fusion.29
  6.2 1.6 copy.27
  7.8 11.5 %all-to-all-start = ((bf16[128,8,512]{2,1,0:T(8,128)(2,1)}), bf16[128,8,512]{2,1,0:T(8,128)(2,1)S(1)}, u32[]{:S(2)}, u32[]{:S(2)}) async-start(bf16[128,8,512]{2,1,0:T(8,128)(2,1)} %copy.27), calls=%async_computation | async-start | bytes 2097152 | tf_op jit(solution)/shard_map/all_to_all | solution.py:81
  19.3 1.0 constant_dynamic-slice_fusion.2
  20.3 1.1 collective-permute-start.2
  21.4 16.8 %all-to-all-done = bf16[128,8,512]{2,1,0:T(8,128)(2,1)S(1)} async-done(((bf16[128,8,512]{2,1,0:T(8,128)(2,1)}), bf16[128,8,512]{2,1,0:T(8,128)(2,1)S(1)}, u32[]{:S(2)}, u32[]{:S(2)}) %all-to-all-start) | async-done | bytes 1048608 | tf_op jit(solution)/shard_map/all_to_all | solution.py:81
  38.2 0.1 slice.29
  38.2 0.1 copy.33
  38.4 0.3 multiply_reduce_fusion
  38.7 0.2 copy.30
  38.9 0.1 convert_element_type.84
  39.1 0.3 convolution_convert_fusion
  39.3 1.3 collective-permute-start.1
  40.7 0.9 fusion.30
  41.5 0.0 collective-permute-done.2
  41.5 0.1 collective-permute-done.1
  41.6 3.6 %fusion = bf16[384,3584]{1,0:T(8,128)(2,1)} fusion(f32[384,3584]{1,0:T(8,128)S(1)} %fusion.30, bf16[384,128]{1,0:T(8,128)(2,1)S(1)} %collective-permute-done.1, bf16[128,3584]{1,0:T(8,128)(2,1)} %collective-permute-done.2), kind=kOutput, calls=%fused_computation.1 | convolution fusion | flops 355074048 | bytes 9273344 | tf_op jit(solution)/shard_map/dot_general | solution.py:94
  45.2 6.4 %reshape.155 = bf16[64,168,128]{2,1,0:T(8,128)(2,1)} reshape(bf16[384,3584]{1,0:T(8,128)(2,1)} %fusion) | data formatting | bytes 5505024 | tf_op jit(solution)/shard_map/reshape | solution.py:100
  51.7 5.7 %all-to-all-start.1 = ((bf16[64,168,128]{2,1,0:T(8,128)(2,1)}), bf16[64,168,128]{2,1,0:T(8,128)(2,1)}, u32[]{:S(2)}, u32[]{:S(2)}) async-start(bf16[64,168,128]{2,1,0:T(8,128)(2,1)} %reshape.155), calls=%async_computation.1 | async-start | bytes 5505024 | tf_op jit(solution)/shard_map/all_to_all | solution.py:101
  57.4 0.4 collective-permute-start
  57.8 0.1 dynamic-slice_bitcast_fusion
  57.9 0.7 collective-permute-done
  58.8 34.5 %all-to-all-done.1 = bf16[64,168,128]{2,1,0:T(8,128)(2,1)} async-done(((bf16[64,168,128]{2,1,0:T(8,128)(2,1)}), bf16[64,168,128]{2,1,0:T(8,128)(2,1)}, u32[]{:S(2)}, u32[]{:S(2)}) %all-to-all-start.1) | async-done | bytes 2752544 | tf_op jit(solution)/shard_map/all_to_all | solution.py:101
  93.3 2.2 %convert_reduce_fusion = f32[168,128]{1,0:T(8,128)S(1)} fusion(bf16[64,168,128]{2,1,0:T(8,128)(2,1)} %all-to-all-done.1), kind=kLoop, calls=%fused_computation.2 | loop fusion | flops 2731008 | bytes 2838528 | tf_op jit(solution)/shard_map/reduce_sum | solution.py:102
  95.4 0.1 multiply_reduce_fusion.1
  95.6 0.1 reduce_sum.69
  95.6 0.1 reduce_sum.70
  95.8 2.0 %collective-permute-start.3 = (f32[6]{0:T(128)S(1)}, f32[6]{0:T(128)S(1)}, u32[]{:S(2)}, u32[]{:S(2)}) collective-permute-start(f32[6]{0:T(128)S(1)} %reduce_sum.70), channel_id=1, source_target_pairs={{0,1},{1,0},{2,3},{3,2},{4,5},{5,4},{6,7},{7,6},{8,9},{9,8},{10,11... | collective-permute-start | bytes 80 | tf_op jit(solution)/shard_map/ppermute | solution.py:105
  97.7 0.8 collective-permute-done.3
  98.6 0.1 mul.93
  98.6 0.1 mul.94
  98.7 0.1 multiply_convert_fusion.1
  98.8 0.2 broadcast_in_dim.35
  99.0 24.5 %all_to_all.20 = bf16[32,168,128]{2,1,0:T(8,128)(2,1)S(1)} all-to-all(bf16[32,168,128]{2,1,0:T(8,128)(2,1)S(1)} %broadcast_in_dim.35), channel_id=1, replica_groups=mesh['zh'=2,'zl'=2,'x'=4,'y'=4,'core'=2] {'zl','x','y'}, dimensions={0} | all-to-all | bytes 2752512 | tf_op jit(solution)/shard_map/all_to_all | solution.py:113
  123.6 2.4 %reshape.157 = bf16[192,3584]{1,0:T(8,128)(2,1)} reshape(bf16[32,168,128]{2,1,0:T(8,128)(2,1)S(1)} %all_to_all.20) | data formatting | bytes 2752512 | tf_op jit(solution)/shard_map/reshape | solution.py:114
  125.9 2.0 %collective-permute-start.4 = (bf16[192,3584]{1,0:T(8,128)(2,1)}, bf16[192,3584]{1,0:T(8,128)(2,1)S(1)}, u32[]{:S(2)}, u32[]{:S(2)}) collective-permute-start(bf16[192,3584]{1,0:T(8,128)(2,1)} %reshape.157), channel_id=1, source_target_pairs={{0,1},{1,0},{2,3},{3,2},{4,5},{5,4},{6,7},{7,6},{8,9},{9,8},{10,11... | collective-permute-start | bytes 4128776 | tf_op jit(solution)/shard_map/ppermute | solution.py:115
  127.9 1.7 %constant_dynamic-slice_fusion.1 = bf16[288,3584]{1,0:T(8,128)(2,1)S(1)} fusion(bf16[288,7168]{1,0:T(8,128)(2,1)} %param.19, s32[]{:T(128)S(6)} %select_n.50), kind=kLoop, calls=%fused_computation.70 | loop fusion | bytes 4128772 | tf_op jit(solution)/shard_map/dynamic_slice | solution.py:22
  129.6 0.0 copy-start.8
  129.6 0.2 collective-permute-start.6
  129.8 2.8 %fusion.13 = f32[192,288]{1,0:T(8,128)S(1)} fusion(bf16[192,3584]{1,0:T(8,128)(2,1)S(1)} %copy-done.3, bf16[7168,288]{0,1:T(8,128)(2,1)} %param.17, s32[]{:T(128)S(6)} %select_n.49), kind=kOutput, calls=%fused_computation.18 | convolution fusion | flops 396361728 | bytes 3661828 | tf_op jit(solution)/shard_map/dot_general | solution.py:120
  132.6 0.0 copy-start.7
  132.6 1.1 fusion.9
  133.7 0.0 collective-permute-done.4
  133.7 1.1 copy-done.7
  134.8 1.1 fusion.23
  135.9 0.0 copy-start.1
  135.9 1.1 multiply_convert_fusion
  137.0 0.6 collective-permute-start.5
  137.5 0.5 copy-done.1
  138.0 0.9 fusion.5
  138.9 0.0 collective-permute-done.5
  138.9 0.9 fusion.1
  139.8 2.6 %reshape.158 = bf16[32,168,128]{2,1,0:T(8,128)(2,1)} reshape(bf16[192,3584]{1,0:T(8,128)(2,1)S(1)} %fusion.1) | data formatting | bytes 2752512 | tf_op jit(solution)/shard_map/reshape | solution.py:129
  142.4 4.0 %all-to-all-start.3 = ((bf16[32,168,128]{2,1,0:T(8,128)(2,1)}), bf16[32,168,128]{2,1,0:T(8,128)(2,1)S(1)}, u32[]{:S(2)}, u32[]{:S(2)}) async-start(bf16[32,168,128]{2,1,0:T(8,128)(2,1)} %reshape.158), calls=%async_computation.3 | async-start | bytes 2752512 | tf_op jit(solution)/shard_map/all_to_all | solution.py:130
  146.4 19.4 %all-to-all-done.3 = bf16[32,168,128]{2,1,0:T(8,128)(2,1)S(1)} async-done(((bf16[32,168,128]{2,1,0:T(8,128)(2,1)}), bf16[32,168,128]{2,1,0:T(8,128)(2,1)S(1)}, u32[]{:S(2)}, u32[]{:S(2)}) %all-to-all-start.3) | async-done | bytes 1376288 | tf_op jit(solution)/shard_map/all_to_all | solution.py:130
  165.8 0.2 convert_reduce_fusion.1
  166.1 1.8 %collective-permute-start.7 = (bf16[3,3584]{1,0:T(4,128)(2,1)S(1)}, bf16[3,3584]{1,0:T(4,128)(2,1)S(1)}, u32[]{:S(2)}, u32[]{:S(2)}) collective-permute-start(bf16[3,3584]{1,0:T(4,128)(2,1)S(1)} %constant_dynamic-slice_fusion), channel_id=1, source_target_pairs={{0,1},{1,0},{2,3},{3,2},{4,5},{5,4},{6,7},{7,6},{8,9},{9,8},{10,11... | collective-permute-start | bytes 64520 | tf_op jit(solution)/shard_map/ppermute | solution.py:135
  167.9 0.9 collective-permute-done.7
  168.8 0.7 pad_maximum_fusion
  (34 shorter events, 0.4 us)
Async XLA Ops:
  0.0 19.3 %copy-start = (bf16[128,7168]{1,0:T(8,128)(2,1)S(1)}, bf16[128,7168]{1,0:T(8,128)(2,1)}, u32[]{:S(2)}) copy-start(bf16[128,7168]{1,0:T(8,128)(2,1)} %param.16) | copy-start | bytes 5505028
  0.9 3.9 %copy-start.2 = (bf16[6,512,576]{1,2,0:T(8,128)(2,1)S(1)}, bf16[6,512,576]{1,2,0:T(8,128)(2,1)}, u32[]{:S(2)}) copy-start(bf16[6,512,576]{1,2,0:T(8,128)(2,1)} %param.11) | copy-start | bytes 10616836
  7.8 30.4 %all-to-all-start = ((bf16[128,8,512]{2,1,0:T(8,128)(2,1)}), bf16[128,8,512]{2,1,0:T(8,128)(2,1)S(1)}, u32[]{:S(2)}, u32[]{:S(2)}) async-start(bf16[128,8,512]{2,1,0:T(8,128)(2,1)} %copy.27), calls=%async_computation | async-start | bytes 2097152 | tf_op jit(solution)/shard_map/all_to_all | solution.py:81
  20.3 18.7 %copy-start.4 = (bf16[1,512,128]{2,1,0:T(8,128)(2,1)S(1)}, bf16[1,512,128]{2,1,0:T(8,128)(2,1)}, u32[]{:S(2)}) copy-start(bf16[1,512,128]{2,1,0:T(8,128)(2,1)} %param.15) | copy-start | bytes 393220
  20.3 21.2 %collective-permute-start.2 = (bf16[128,3584]{1,0:T(8,128)(2,1)}, bf16[128,3584]{1,0:T(8,128)(2,1)}, u32[]{:S(2)}, u32[]{:S(2)}) collective-permute-start(bf16[128,3584]{1,0:T(8,128)(2,1)} %constant_dynamic-slice_fusion.2), channel_id=1, source_target_pairs={{0,1},{1,0},{2,3},{3,2},{4,5},{5,4},{6,7},{7,6},{8,9},{9,8},{10,11... | collective-permute-start | bytes 2752520 | tf_op jit(solution)/shard_map/ppermute | solution.py:23
  39.3 2.3 %collective-permute-start.1 = (bf16[384,128]{1,0:T(8,128)(2,1)S(1)}, bf16[384,128]{1,0:T(8,128)(2,1)S(1)}, u32[]{:S(2)}, u32[]{:S(2)}) collective-permute-start(bf16[384,128]{1,0:T(8,128)(2,1)S(1)} %convolution_convert_fusion), channel_id=1, source_target_pairs={{0,1},{1,0},{2,3},{3,2},{4,5},{5,4},{6,7},{7,6},{8,9},{9,8},{10,11... | collective-permute-start | bytes 294920 | tf_op jit(solution)/shard_map/ppermute | solution.py:93
  51.6 5.7 %copy-start.5 = (bf16[3,7168]{1,0:T(4,128)(2,1)S(1)}, bf16[3,7168]{1,0:T(4,128)(2,1)}, u32[]{:S(2)}) copy-start(bf16[3,7168]{1,0:T(4,128)(2,1)} %param.13) | copy-start | bytes 129028
  51.6 6.2 %copy-start.6 = (f32[7168]{0:T(1024)S(1)}, f32[7168]{0:T(1024)}, u32[]{:S(2)}) copy-start(f32[7168]{0:T(1024)} %param.14) | copy-start | bytes 86020
  51.7 41.6 %all-to-all-start.1 = ((bf16[64,168,128]{2,1,0:T(8,128)(2,1)}), bf16[64,168,128]{2,1,0:T(8,128)(2,1)}, u32[]{:S(2)}, u32[]{:S(2)}) async-start(bf16[64,168,128]{2,1,0:T(8,128)(2,1)} %reshape.155), calls=%async_computation.1 | async-start | bytes 5505024 | tf_op jit(solution)/shard_map/all_to_all | solution.py:101
  57.4 1.3 collective-permute-start
  95.8 2.8 %collective-permute-start.3 = (f32[6]{0:T(128)S(1)}, f32[6]{0:T(128)S(1)}, u32[]{:S(2)}, u32[]{:S(2)}) collective-permute-start(f32[6]{0:T(128)S(1)} %reduce_sum.70), channel_id=1, source_target_pairs={{0,1},{1,0},{2,3},{3,2},{4,5},{5,4},{6,7},{7,6},{8,9},{9,8},{10,11... | collective-permute-start | bytes 80 | tf_op jit(solution)/shard_map/ppermute | solution.py:105
  125.9 3.9 %copy-start.3 = (bf16[192,3584]{1,0:T(8,128)(2,1)S(1)}, bf16[192,3584]{1,0:T(8,128)(2,1)}, u32[]{:S(2)}) copy-start(bf16[192,3584]{1,0:T(8,128)(2,1)} %reshape.157) | copy-start | bytes 4128772
  125.9 7.8 %collective-permute-start.4 = (bf16[192,3584]{1,0:T(8,128)(2,1)}, bf16[192,3584]{1,0:T(8,128)(2,1)S(1)}, u32[]{:S(2)}, u32[]{:S(2)}) collective-permute-start(bf16[192,3584]{1,0:T(8,128)(2,1)} %reshape.157), channel_id=1, source_target_pairs={{0,1},{1,0},{2,3},{3,2},{4,5},{5,4},{6,7},{7,6},{8,9},{9,8},{10,11... | collective-permute-start | bytes 4128776 | tf_op jit(solution)/shard_map/ppermute | solution.py:115
  129.6 3.0 %copy-start.8 = (bf16[7168,288]{0,1:T(8,128)(2,1)S(1)}, bf16[7168,288]{0,1:T(8,128)(2,1)}, u32[]{:S(2)}) copy-start(bf16[7168,288]{0,1:T(8,128)(2,1)} %param.18) | copy-start | bytes 12386308
  129.6 9.3 %collective-permute-start.6 = (bf16[288,3584]{1,0:T(8,128)(2,1)S(1)}, bf16[288,3584]{1,0:T(8,128)(2,1)S(1)}, u32[]{:S(2)}, u32[]{:S(2)}) collective-permute-start(bf16[288,3584]{1,0:T(8,128)(2,1)S(1)} %constant_dynamic-slice_fusion.1), channel_id=1, source_target_pairs={{0,1},{1,0},{2,3},{3,2},{4,5},{5,4},{6,7},{7,6},{8,9},{9,8},{10,11... | collective-permute-start | bytes 6193160 | tf_op jit(solution)/shard_map/ppermute | solution.py:23
  132.6 2.2 %copy-start.7 = (bf16[7168,288]{0,1:T(8,128)(2,1)S(1)}, bf16[7168,288]{0,1:T(8,128)(2,1)}, u32[]{:S(2)}) copy-start(bf16[7168,288]{0,1:T(8,128)(2,1)} %param.17) | copy-start | bytes 12386308
  135.9 2.2 %copy-start.1 = (bf16[288,7168]{1,0:T(8,128)(2,1)S(1)}, bf16[288,7168]{1,0:T(8,128)(2,1)}, u32[]{:S(2)}) copy-start(bf16[288,7168]{1,0:T(8,128)(2,1)} %param.19) | copy-start | bytes 12386308
  137.0 2.0 %collective-permute-start.5 = (bf16[192,288]{1,0:T(8,128)(2,1)S(1)}, bf16[192,288]{1,0:T(8,128)(2,1)S(1)}, u32[]{:S(2)}, u32[]{:S(2)}) collective-permute-start(bf16[192,288]{1,0:T(8,128)(2,1)S(1)} %multiply_convert_fusion), channel_id=1, source_target_pairs={{0,1},{1,0},{2,3},{3,2},{4,5},{5,4},{6,7},{7,6},{8,9},{9,8},{10,11... | collective-permute-start | bytes 331784 | tf_op jit(solution)/shard_map/ppermute | solution.py:125
  142.4 23.4 %all-to-all-start.3 = ((bf16[32,168,128]{2,1,0:T(8,128)(2,1)}), bf16[32,168,128]{2,1,0:T(8,128)(2,1)S(1)}, u32[]{:S(2)}, u32[]{:S(2)}) async-start(bf16[32,168,128]{2,1,0:T(8,128)(2,1)} %reshape.158), calls=%async_computation.3 | async-start | bytes 2752512 | tf_op jit(solution)/shard_map/all_to_all | solution.py:130
  166.1 2.7 %collective-permute-start.7 = (bf16[3,3584]{1,0:T(4,128)(2,1)S(1)}, bf16[3,3584]{1,0:T(4,128)(2,1)S(1)}, u32[]{:S(2)}, u32[]{:S(2)}) collective-permute-start(bf16[3,3584]{1,0:T(4,128)(2,1)S(1)} %constant_dynamic-slice_fusion), channel_id=1, source_target_pairs={{0,1},{1,0},{2,3},{3,2},{4,5},{5,4},{6,7},{7,6},{8,9},{9,8},{10,11... | collective-permute-start | bytes 64520 | tf_op jit(solution)/shard_map/ppermute | solution.py:135

commit v2 on v1

v2 whole, which is shorter than its diff:
```python
import math

import jax
import jax.numpy as jnp
from jax import lax
from jax.sharding import Mesh, PartitionSpec as P

LAT = 512
QKD = 192
LANES = 128
AXES = ("zh", "zl", "x", "y", "core")
DEV = ("zl", "x", "y", "core")
RING = ("y", "core")
OUTER = ("zh", "zl", "x")
SIDE_CHIPS = ("zl", "x", "y")
SWAP = [(0, 1), (1, 0)]
F32 = jnp.float32
BF16 = jnp.bfloat16


def swap(array):
    return lax.ppermute(array, "core", SWAP)


def shift(array, step):
    return lax.ppermute(array, "y", [(i, (i + step) % 4) for i in range(4)])


def block(array, index, size, axis):
    return lax.dynamic_slice_in_dim(array, index * size, size, axis)


def swap_halves(array, core, axis):
    half = array.shape[axis] // 2
    return block(array, core, half, axis), swap(block(array, 1 - core, half, axis))


def split_pair(value):
    high = lax.reduce_precision(value, 8, 7)
    low = lax.reduce_precision(value - high, 8, 7)
    return high, low


def local(
    query_latent,
    latent_cache,
    lengths,
    stream,
    norm_gain,
    value_up,
    out_proj,
    gate_proj,
    up_proj,
    down_proj,
):
    core = lax.axis_index("core")
    ring = lax.axis_index("y")
    rows_own, width = stream.shape
    half = width // 2
    eighth = width // 8
    first = core == 0

    ring_up = lax.all_gather(value_up, RING, axis=0, tiled=True)
    out_mine, out_theirs = swap_halves(out_proj, core, 1)
    out_pair = jnp.stack([out_mine, out_theirs])
    out_parts = [block(out_pair, ring, eighth, 2)]
    for step in (1, 2, 3):
        out_parts.append(shift(block(out_pair, (ring + step) % 4, eighth, 2), step))
    ring_stream = lax.all_gather(stream, RING, axis=0, tiled=True)
    ring_stream = block(ring_stream, core * 4 + ring, eighth, 1).astype(F32)
    down_mine, down_theirs = swap_halves(down_proj, core, 1)

    rows, heads, _ = query_latent.shape
    half_keys = latent_cache.shape[1]
    positions = lax.axis_index("zh") * half_keys + lax.iota(jnp.int32, half_keys)
    usable = (positions[None, :] < lengths[:, None])[:, None, :]
    scores = jnp.einsum(
        "rhc,rkc->rhk", query_latent, latent_cache, preferred_element_type=F32
    ) * (1.0 / math.sqrt(QKD))
    scores = jnp.where(usable, scores, F32(-1e30))
    peak_high, peak_low = split_pair(jnp.max(scores, axis=2))
    peak = peak_high + peak_low
    exponent = jnp.where(usable, jnp.exp(scores - peak[:, :, None]), F32(0.0))
    total_high, total_low = split_pair(jnp.sum(exponent, axis=2))
    weighted = jnp.einsum(
        "rhk,rkc->rhc",
        exponent.astype(BF16),
        latent_cache[:, :, :LAT],
        preferred_element_type=F32,
    ).astype(BF16)
    stats = jnp.stack([peak_high, peak_low, total_high, total_low], axis=-1).astype(BF16)
    stats = stats.transpose(1, 0, 2).reshape(heads // 8, 1, 8, 4 * rows)
    stats = jnp.pad(stats, ((0, 0), (0, 0), (0, 0), (0, LANES - 4 * rows)))
    tiles = LAT // LANES
    weighted = weighted.reshape(rows, heads // 8, 8, tiles, LANES).transpose(1, 0, 3, 2, 4)
    weighted = weighted.reshape(heads // 8, rows * tiles, 8, LANES)
    payload = jnp.concatenate([weighted, stats], axis=1)
    received = lax.all_to_all(payload, OUTER, split_axis=0, concat_axis=0, tiled=True)

    stats = received[:, rows * tiles, :, : 4 * rows].astype(F32).reshape(2, 8, 8, rows, 4)
    peaks = stats[..., 0] + stats[..., 1]
    totals = stats[..., 2] + stats[..., 3]
    factor = jnp.exp(peaks - jnp.max(peaks, axis=0, keepdims=True))
    factor = factor / jnp.sum(factor * totals, axis=0, keepdims=True)
    factor = factor.transpose(0, 1, 3, 2)
    parts = received[:, : rows * tiles].reshape(2, 8, rows, tiles, 8, LANES)
    latent = jnp.sum(parts.astype(F32) * factor[:, :, :, None, :, None], axis=0).astype(BF16)
    latent = latent.transpose(0, 1, 3, 2, 4).reshape(8 * rows, 8, LAT)
    values = jnp.einsum("rhc,hcd->rhd", latent, ring_up, preferred_element_type=F32)
    values = values.astype(BF16).reshape(8 * rows, 8 * LANES)

    ring_values = jnp.stack([values] + [shift(values, step) for step in (1, 2, 3)])
    both = jnp.stack([ring_values, swap(ring_values)], axis=1)
    both = both.reshape(4, 2, 8, rows, 8 * LANES)
    back = (ring - jnp.arange(4)) % 4
    both = jnp.take(both, back, axis=0)
    both = jnp.take(both, jnp.stack([core, 1 - core]), axis=1)
    left = both.transpose(2, 0, 1, 3, 4).reshape(64 * rows, 8 * LANES)
    weight = jnp.take(jnp.stack(out_parts), back, axis=0)
    weight = jnp.take(weight, jnp.stack([core, 1 - core]), axis=1)
    weight = weight.reshape(8 * LANES, eighth)
    partial = jnp.dot(left, weight, preferred_element_type=F32).astype(BF16)
    partial = partial.reshape(16, -1, eighth)
    parts = lax.all_to_all(partial, OUTER, split_axis=0, concat_axis=0, tiled=True)
    residual = ring_stream + jnp.sum(parts.astype(F32), axis=0)

    group_rows = residual.shape[0]
    squares = jnp.stack(split_pair(jnp.sum(residual * residual, axis=1)), axis=1).astype(BF16)
    squares = jnp.pad(squares, ((0, 0), (0, LANES - 2)))
    gain = block(norm_gain, core * 4 + ring, eighth, 0)
    normalized = jnp.concatenate([(residual * gain).astype(BF16), squares], axis=1)
    normalized = jnp.broadcast_to(normalized, (32,) + normalized.shape)
    piece = lax.all_to_all(normalized, SIDE_CHIPS, split_axis=0, concat_axis=0, tiled=True)
    side_rows = 8 * group_rows

    def unpack(gathered):
        gathered = gathered.reshape(8, 4, group_rows, -1)
        squares = gathered[..., eighth : eighth + 2].astype(F32)
        squares = jnp.sum(squares, axis=(1, 3)).reshape(side_rows)
        data = gathered[..., :eighth].transpose(0, 2, 1, 3).reshape(side_rows, half)
        return data, squares

    mine, squares_mine = unpack(piece)
    theirs, squares_theirs = unpack(swap(piece))
    scale = lax.rsqrt((squares_mine + squares_theirs) / width + 1e-06)[:, None]

    def hidden_units(weight):
        own = jnp.dot(mine, block(weight, core, half, 0), preferred_element_type=F32)
        other = jnp.dot(theirs, block(weight, 1 - core, half, 0), preferred_element_type=F32)
        return (own + other) * scale

    hidden = (jax.nn.silu(hidden_units(gate_proj)) * hidden_units(up_proj)).astype(BF16)
    partial = jnp.dot(hidden, down_mine, preferred_element_type=F32) + jnp.dot(
        swap(hidden), down_theirs, preferred_element_type=F32
    )
    group = lax.axis_index("zl") * 4 + lax.axis_index("x")
    start = (group * group_rows, ring * eighth)
    held = lax.dynamic_slice(partial, start, residual.shape)
    partial = lax.dynamic_update_slice(partial, held + residual, start)
    chunk = 2 * rows_own
    partial = partial.astype(BF16).reshape(32, chunk * half // LANES, LANES)
    parts = lax.all_to_all(partial, SIDE_CHIPS, split_axis=0, concat_axis=0, tiled=True)
    new_stream = jnp.sum(parts.astype(F32), axis=0).reshape(chunk, half).astype(BF16)
    mine = block(new_stream, core, rows_own, 0)
    theirs = swap(block(new_stream, 1 - core, rows_own, 0))
    return jnp.concatenate(
        [jnp.where(first, mine, theirs), jnp.where(first, theirs, mine)], axis=1
    )


def solution(mesh):
    fine = Mesh(mesh.devices.reshape(2, 2, 4, 4, 2), AXES)
    placed = (
        P(DEV, None, None),
        P(DEV, "zh", None),
        P(DEV),
        P(AXES, None),
        P(),
        P(AXES, None, None),
        P(AXES, None),
        P(None, DEV),
        P(None, DEV),
        P(DEV, None),
    )
    return jax.shard_map(
        local, mesh=fine, in_specs=placed, out_specs=P(AXES, None), check_vma=False
    )
```

time: 170 us -> 200 us (1.18)
  waiting for transfers between devices: 73.1 us -> 41.2 us
  blocking collectives: 24.5 us -> 42.6 us
  starting transfers between devices: 30.5 us -> 46.6 us
  between operations: 0.38 us -> 13.9 us
  other arithmetic: 5.29 us -> 12.4 us
  local copies, waits for them, and re-layouts: 18.6 us -> 25.5 us
    all_to_all x2, waiting for transfers between devices: 51.3 us -> 9.05 us  [the longest x1 9.05 us: local(): lax.all_to_all(payload, OUTER, split_axis=0, concat_axis=0, tiled=True)]
    all_gather x0 -> x1, blocking collectives: none -> 13.4 us  [local(): ring_stream = lax.all_gather(stream, RING, axis=0, tiled=True)]
    ppermute x8 -> x12, starting transfers between devices: 9.36 us -> 21.6 us  [the longest x6 13.8 us: shift(): return lax.ppermute(array, 'y', [(i, (i + step) % 4) for i in range(4)])]
    all_gather x0 -> x1, waiting for transfers between devices: none -> 10.8 us  [local(): ring_up = lax.all_gather(value_up, RING, axis=0, tiled=True)]
    reshape x7 -> x6, local copies, waits for them, and re-layouts: 11.5 us -> 3.25 us  [the longest x1 2.61 us: local(): partial = partial.astype(BF16).reshape(32, chunk * half // LANES, LANES)]
    gather x0 -> x4, local copies, waits for them, and re-layouts: none -> 5.27 us  [the longest x1 2.02 us: local(): weight = jnp.take(weight, jnp.stack([core, 1 - core]), axis=1)]
    all_to_all x1, blocking collectives: 24.5 us -> 29.2 us  [local(): lax.all_to_all(normalized, SIDE_CHIPS, split_axis=0, concat_axis=0, tiled...]
    unnamed x19 -> x27, local copies, waits for them, and re-layouts: 1.71 us -> 6.34 us
  transfers between devices with their start and end apart: 11 -> 16, of which waited for: 7 -> 6; matrix products, arithmetic and copies ran while one was open for 7% -> 15% of each run, Pallas kernels for 0% -> 0%
where the time goes in v2:
time: 200 us; the launch traced here: 199 us
  starting transfers between devices  46.6 us (23%)
  blocking collectives  42.6 us (21%)
  waiting for transfers between devices  41.2 us (21%)
  local copies, waits for them, and re-layouts  25.5 us (13%)
  matrix products  16.9 us (8%)
  between operations  13.9 us (7%)
  other arithmetic  12.4 us (6%)
    all_to_all x1, blocking collectives, local(): lax.all_to_all(normalized, SIDE_CHIPS, split_axis=0, concat_axis=0, tiled...  29.2 us
    all_to_all x1, waiting for transfers between devices, local(): lax.all_to_all(partial, SIDE_CHIPS, split_axis=0, concat_axis=0, tiled=True)  19.3 us
    ppermute x6, starting transfers between devices, shift(): return lax.ppermute(array, 'y', [(i, (i + step) % 4) for i in range(4)])  13.8 us
    all_gather x1, blocking collectives, local(): ring_stream = lax.all_gather(stream, RING, axis=0, tiled=True)  13.4 us
    all_to_all x1, starting transfers between devices, local(): lax.all_to_all(partial, OUTER, split_axis=0, concat_axis=0, tiled=True)  12.5 us
    all_gather x1, waiting for transfers between devices, local(): ring_up = lax.all_gather(value_up, RING, axis=0, tiled=True)  10.8 us
    all_to_all x1, waiting for transfers between devices, local(): lax.all_to_all(payload, OUTER, split_axis=0, concat_axis=0, tiled=True)  9.05 us
    all_to_all x1, starting transfers between devices, local(): lax.all_to_all(payload, OUTER, split_axis=0, concat_axis=0, tiled=True)  8.43 us
  transfers between devices with their start and end apart: 16, of which 6 were waited for; matrix products, arithmetic and copies ran while one was open for 15% of the time, Pallas kernels for 0%

profile of v2, /device:TPU:1, one launch (start us, length us, event | category | flops | bytes accessed | tf_op | source)
XLA Modules:
  0.0 199.1 jit_solution(17030311262981921196)
XLA Ops:
  6.5 0.8 broadcast_compare_fusion
  7.3 0.4 copy-done
  7.7 3.1 %fusion.77 = (f32[6,128]{1,0:T(8,128)S(1)}, f32[6,128,512]{2,1,0:T(8,128)S(1)}) fusion(bf16[6,128,576]{1,2,0:T(8,128)(2,1)S(1)} %copy-done, bf16[6,512,576]{1,2,0:T(8,128)(2,1)} %param.11, pred[6,512]{1,0:T(8,128)(4,1)S(1)} %broadcast_compare_fusion), kind=kOutput, calls=%fused_computation.135 | convolution fusion | flops 454163712 | bytes 6002688 | tf_op jit(solution)/shard_map/rhc,rkc->rhk/dot_general | solution.py:77
  10.8 0.5 fusion.21
  11.3 1.2 fusion.18
  12.9 1.0 fusion.43
  13.9 8.4 %all-to-all-start = ((bf16[16,25,8,128]{3,2,1,0:T(8,128)(2,1)}), bf16[16,25,8,128]{3,2,1,0:T(8,128)(2,1)S(1)}, u32[]{:S(2)}, u32[]{:S(2)}) async-start(bf16[16,25,8,128]{3,2,1,0:T(8,128)(2,1)} %fusion.43), calls=%async_computation | async-start | bytes 1638400 | tf_op jit(solution)/shard_map/all_to_all | solution.py:98
  22.4 0.7 all-gather.3.cloned.1.call-update
  23.1 2.6 %constant_dynamic-slice_fusion.2 = (bf16[128,3584]{1,0:T(8,128)(2,1)}, bf16[1,128,3584]{2,1,0:T(8,128)(2,1)S(1)}) fusion(bf16[128,7168]{1,0:T(8,128)(2,1)} %param.16, s32[]{:T(128)S(6)} %select_n.171, s32[]{:T(128)S(6)} %select_n.170), kind=kLoop, calls=%fused_computation.98 | loop fusion | bytes 3670024 | tf_op jit(solution)/shard_map/dynamic_slice | solution.py:30
  25.6 1.0 collective-permute-start.4
  26.8 9.0 %all-to-all-done = bf16[16,25,8,128]{3,2,1,0:T(8,128)(2,1)S(1)} async-done(((bf16[16,25,8,128]{3,2,1,0:T(8,128)(2,1)}), bf16[16,25,8,128]{3,2,1,0:T(8,128)(2,1)S(1)}, u32[]{:S(2)}, u32[]{:S(2)}) %all-to-all-start) | async-done | bytes 819232 | tf_op jit(solution)/shard_map/all_to_all | solution.py:98
  36.8 1.2 fusion.50
  38.0 1.3 collective-permute-start.5
  39.3 2.6 %collective-permute-start.6 = (bf16[2,128,896]{2,1,0:T(8,128)(2,1)}, bf16[2,128,896]{2,1,0:T(8,128)(2,1)S(1)}, u32[]{:S(2)}, u32[]{:S(2)}) collective-permute-start(bf16[2,128,896]{2,1,0:T(8,128)(2,1)} %get-tuple-element.7), channel_id=1, source_target_pairs={{0,4},{2,6},{4,0},{6,2},{1,5},{3,7},{5,1},{7,3},{8,12},{10,14},{12... | collective-permute-start | bytes 1376264 | tf_op jit(solution)/shard_map/ppermute | solution.py:26
  41.9 1.1 collective-permute-start.7
  43.0 10.8 %all-gather.3.cloned.1.call-done = bf16[8,512,128]{2,1,0:T(8,128)(2,1)} async-done(((bf16[1,512,128]{2,1,0:T(8,128)(2,1)}), bf16[8,512,128]{2,1,0:T(8,128)(2,1)}) %all-gather.3.cloned.1.call-update) | async-done | bytes 1048592 | tf_op jit(solution)/shard_map/all_gather | solution.py:63
  53.8 1.6 convolution_convert_fusion.1
  55.4 6.3 %collective-permute-start = (bf16[48,1024]{1,0:T(8,128)(2,1)S(1)}, bf16[48,1024]{1,0:T(8,128)(2,1)S(1)}, u32[]{:S(2)}, u32[]{:S(2)}) collective-permute-start(bf16[48,1024]{1,0:T(8,128)(2,1)S(1)} %copy_bitcast_fusion), channel_id=1, source_target_pairs={{0,2},{2,4},{4,6},{6,0},{1,3},{3,5},{5,7},{7,1},{8,10},{10,12},{12... | collective-permute-start | bytes 294920 | tf_op jit(solution)/shard_map/ppermute | solution.py:26
  61.7 2.1 %collective-permute-start.1 = (bf16[48,1024]{1,0:T(8,128)(2,1)S(1)}, bf16[48,1024]{1,0:T(8,128)(2,1)S(1)}, u32[]{:S(2)}, u32[]{:S(2)}) collective-permute-start(bf16[48,1024]{1,0:T(8,128)(2,1)S(1)} %copy_bitcast_fusion), channel_id=1, source_target_pairs={{0,4},{2,6},{4,0},{6,2},{1,5},{3,7},{5,1},{7,3},{8,12},{10,14},{12... | collective-permute-start | bytes 294920 | tf_op jit(solution)/shard_map/ppermute | solution.py:26
  63.7 0.4 collective-permute-start.2
  64.5 0.7 copy-done.7
  65.3 1.6 pad_maximum_fusion
  66.9 2.0 %gather_fusion.2 = bf16[4,2,128,896]{3,2,1,0:T(8,128)(2,1)} fusion(bf16[4,2,128,896]{3,2,1,0:T(8,128)(2,1)S(1)} %pad_maximum_fusion, s32[1024]{0:T(1024)S(1)} %pad_clamp_fusion.1), kind=kCustom, calls=%fused_computation.2 | custom fusion | bytes 3670032 | tf_op jit(solution)/shard_map/jit(_take)/gather | solution.py:119
  69.0 0.3 collective-permute-done.1
  69.3 2.1 %collective-permute-start.3 = (bf16[4,48,1024]{2,1,0:T(8,128)(2,1)S(1)}, bf16[4,48,1024]{2,1,0:T(8,128)(2,1)S(1)}, u32[]{:S(2)}, u32[]{:S(2)}) collective-permute-start(bf16[4,48,1024]{2,1,0:T(8,128)(2,1)S(1)} %pad_maximum_fusion.2), channel_id=1, source_target_pairs={{0,1},{1,0},{2,3},{3,2},{4,5},{5,4},{6,7},{7,6},{8,9},{9,8},{10,11... | collective-permute-start | bytes 1179656 | tf_op jit(solution)/shard_map/ppermute | solution.py:22
  71.4 1.7 broadcast_select_fusion
  73.2 2.0 %gather_fusion.3 = bf16[2,4,128,896]{3,2,1,0:T(8,128)(2,1)} fusion(bf16[4,2,128,896]{3,2,1,0:T(8,128)(2,1)S(1)} %broadcast_select_fusion, s32[1024]{0:T(1024)S(1)} %pad_clamp_fusion), kind=kCustom, calls=%fused_computation.3 | custom fusion | bytes 3670024 | tf_op jit(solution)/shard_map/jit(_take)/gather | solution.py:120
  75.2 1.7 select_bitcast_fusion
  77.0 1.4 copy.81
  78.7 0.3 copy.78
  79.1 0.3 pad_maximum_fusion.1
  79.4 0.6 gather_fusion
  80.2 0.6 gather_fusion.1
  81.2 0.3 reshape.354
  81.4 3.3 %convolution_convert_fusion = bf16[384,896]{1,0:T(8,128)(2,1)} fusion(bf16[384,1024]{1,0:T(8,128)(2,1)S(1)} %reshape.354, bf16[1024,896]{1,0:T(8,128)(2,1)} %bitcast.100), kind=kOutput, calls=%fused_computation.39 | convolution fusion | flops 704987136 | bytes 3309568 | tf_op jit(solution)/shard_map/dot_general | solution.py:122
  84.8 12.5 %all-to-all-start.1 = ((bf16[16,24,896]{2,1,0:T(8,128)(2,1)}), bf16[16,24,896]{2,1,0:T(8,128)(2,1)S(1)}, u32[]{:S(2)}, u32[]{:S(2)}) async-start(bf16[16,24,896]{2,1,0:T(8,128)(2,1)} %bitcast.31), calls=%async_computation.1 | async-start | bytes 1376256 | tf_op jit(solution)/shard_map/all_to_all | solution.py:124
  97.3 13.4 %all-gather = bf16[8,3,7168]{2,1,0:T(4,128)(2,1)S(1)} all-gather(bf16[1,3,7168]{2,1,0:T(4,128)(2,1)S(1)} %bitcast.115), channel_id=1, replica_groups=mesh['zh'=2,'zl'=2,'x'=4,'y'=4,'core'=2] {'y','core'}, dimensions={0}, use_global_device_ids=true | all-gather | bytes 387072 | tf_op jit(solution)/shard_map/all_gather | solution.py:69
  110.7 0.3 reshape.396
  111.0 0.8 dynamic_slice.58
  112.3 29.2 %all_to_all.20 = bf16[32,24,1024]{2,1,0:T(8,128)(2,1)S(1)} all-to-all(bf16[32,24,1024]{2,1,0:T(8,128)(2,1)S(1)} %broadcast_in_dim.75), channel_id=1, replica_groups=mesh['zh'=2,'zl'=2,'x'=4,'y'=4,'core'=2] {'zl','x','y'}, dimensions={0} | all-to-all | bytes 3145728 | tf_op jit(solution)/shard_map/all_to_all | solution.py:133
  141.6 2.2 %collective-permute-start.8 = (bf16[32,24,1024]{2,1,0:T(8,128)(2,1)S(1)}, bf16[32,24,1024]{2,1,0:T(8,128)(2,1)}, u32[]{:S(2)}, u32[]{:S(2)}) collective-permute-start(bf16[32,24,1024]{2,1,0:T(8,128)(2,1)S(1)} %all_to_all.20), channel_id=1, source_target_pairs={{0,1},{1,0},{2,3},{3,2},{4,5},{5,4},{6,7},{7,6},{8,9},{9,8},{10,11... | collective-permute-start | bytes 4718600 | tf_op jit(solution)/shard_map/ppermute | solution.py:22
  143.8 1.5 constant_dynamic-slice_fusion.1
  145.5 0.5 copy.83
  146.1 1.3 copy.88
  147.3 1.0 convert_reduce_fusion.1
  148.5 1.5 slice_bitcast_fusion
  149.9 0.5 copy.84
  150.6 1.5 copy-done.10
  152.1 1.1 fusion.9
  153.2 1.1 copy-done.11
  154.3 1.1 fusion.5
  155.3 0.3 copy-done.5
  155.6 1.1 fusion.26
  156.7 1.1 fusion.38
  157.9 0.6 collective-permute-start.9
  158.4 0.4 copy-done.3
  158.9 0.9 fusion.3
  159.8 2.5 %convolution_add_fusion = f32[192,3584]{1,0:T(8,128)S(1)} fusion(f32[192,3584]{1,0:T(8,128)S(1)} %fusion.3, bf16[192,288]{1,0:T(8,128)(2,1)S(1)} %collective-permute-done.9, bf16[288,3584]{1,0:T(8,128)(2,1)} %collective-permute-done.10), kind=kOutput, calls=%fused_computation.5 | convolution fusion | flops 397049856 | bytes 7680000 | tf_op jit(solution)/shard_map/dot_general | solution.py:153
  162.5 2.6 %reshape.360 = bf16[32,168,128]{2,1,0:T(8,128)(2,1)} reshape(bf16[192,3584]{1,0:T(8,128)(2,1)S(1)} %convert_element_type.84) | data formatting | bytes 2752512 | tf_op jit(solution)/shard_map/reshape | solution.py:161
  165.1 4.0 %all-to-all-start.3 = ((bf16[32,168,128]{2,1,0:T(8,128)(2,1)}), bf16[32,168,128]{2,1,0:T(8,128)(2,1)S(1)}, u32[]{:S(2)}, u32[]{:S(2)}) async-start(bf16[32,168,128]{2,1,0:T(8,128)(2,1)} %reshape.360), calls=%async_computation.3 | async-start | bytes 2752512 | tf_op jit(solution)/shard_map/all_to_all | solution.py:162
  169.1 19.3 %all-to-all-done.3 = bf16[32,168,128]{2,1,0:T(8,128)(2,1)S(1)} async-done(((bf16[32,168,128]{2,1,0:T(8,128)(2,1)}), bf16[32,168,128]{2,1,0:T(8,128)(2,1)S(1)}, u32[]{:S(2)}, u32[]{:S(2)}) %all-to-all-start.3) | async-done | bytes 1376288 | tf_op jit(solution)/shard_map/all_to_all | solution.py:162
  188.7 2.0 %collective-permute-start.11 = (bf16[3,3584]{1,0:T(4,128)(2,1)S(1)}, bf16[3,3584]{1,0:T(4,128)(2,1)S(1)}, u32[]{:S(2)}, u32[]{:S(2)}) collective-permute-start(bf16[3,3584]{1,0:T(4,128)(2,1)S(1)} %constant_dynamic-slice_fusion), channel_id=1, source_target_pairs={{0,1},{1,0},{2,3},{3,2},{4,5},{5,4},{6,7},{7,6},{8,9},{9,8},{10,11... | collective-permute-start | bytes 64520 | tf_op jit(solution)/shard_map/ppermute | solution.py:22
  190.7 0.9 collective-permute-done.11
  191.6 0.7 pad_maximum_fusion.3
  (82 shorter events, 4.6 us)
Async XLA Ops:
  6.5 1.2 copy-start
  7.7 3.6 %copy-start.4 = (bf16[6,512,576]{1,2,0:T(8,128)(2,1)S(1)}, bf16[6,512,576]{1,2,0:T(8,128)(2,1)}, u32[]{:S(2)}) copy-start(bf16[6,512,576]{1,2,0:T(8,128)(2,1)} %param.11) | copy-start | bytes 10616836
  13.9 22.0 %all-to-all-start = ((bf16[16,25,8,128]{3,2,1,0:T(8,128)(2,1)}), bf16[16,25,8,128]{3,2,1,0:T(8,128)(2,1)S(1)}, u32[]{:S(2)}, u32[]{:S(2)}) async-start(bf16[16,25,8,128]{3,2,1,0:T(8,128)(2,1)} %fusion.43), calls=%async_computation | async-start | bytes 1638400 | tf_op jit(solution)/shard_map/all_to_all | solution.py:98
  22.3 31.4 %all-gather.3.cloned.1.call-start = ((), (), s32[]{:S(2)}) async-start(), calls=%async_computation.4 | async-start | bytes 1179648 | tf_op jit(solution)/shard_map/all_gather | solution.py:63
  25.6 11.1 %collective-permute-start.4 = (bf16[128,3584]{1,0:T(8,128)(2,1)}, bf16[128,3584]{1,0:T(8,128)(2,1)S(1)}, u32[]{:S(2)}, u32[]{:S(2)}) collective-permute-start(bf16[128,3584]{1,0:T(8,128)(2,1)} %get-tuple-element.9), channel_id=1, source_target_pairs={{0,1},{1,0},{2,3},{3,2},{4,5},{5,4},{6,7},{7,6},{8,9},{9,8},{10,11... | collective-permute-start | bytes 2752520 | tf_op jit(solution)/shard_map/ppermute | solution.py:22
  38.0 25.8 %collective-permute-start.5 = (bf16[2,128,896]{2,1,0:T(8,128)(2,1)}, bf16[2,128,896]{2,1,0:T(8,128)(2,1)S(1)}, u32[]{:S(2)}, u32[]{:S(2)}) collective-permute-start(bf16[2,128,896]{2,1,0:T(8,128)(2,1)} %get-tuple-element.6), channel_id=1, source_target_pairs={{0,2},{2,4},{4,6},{6,0},{1,3},{3,5},{5,7},{7,1},{8,10},{10,12},{12... | collective-permute-start | bytes 1376264 | tf_op jit(solution)/shard_map/ppermute | solution.py:26
  39.3 25.1 %collective-permute-start.6 = (bf16[2,128,896]{2,1,0:T(8,128)(2,1)}, bf16[2,128,896]{2,1,0:T(8,128)(2,1)S(1)}, u32[]{:S(2)}, u32[]{:S(2)}) collective-permute-start(bf16[2,128,896]{2,1,0:T(8,128)(2,1)} %get-tuple-element.7), channel_id=1, source_target_pairs={{0,4},{2,6},{4,0},{6,2},{1,5},{3,7},{5,1},{7,3},{8,12},{10,14},{12... | collective-permute-start | bytes 1376264 | tf_op jit(solution)/shard_map/ppermute | solution.py:26
  41.9 22.5 %collective-permute-start.7 = (bf16[2,128,896]{2,1,0:T(8,128)(2,1)S(1)}, bf16[2,128,896]{2,1,0:T(8,128)(2,1)S(1)}, u32[]{:S(2)}, u32[]{:S(2)}) collective-permute-start(bf16[2,128,896]{2,1,0:T(8,128)(2,1)S(1)} %get-tuple-element.8), channel_id=1, source_target_pairs={{0,6},{2,0},{4,2},{6,4},{1,7},{3,1},{5,3},{7,5},{8,14},{10,8},{12,... | collective-permute-start | bytes 1376264 | tf_op jit(solution)/shard_map/ppermute | solution.py:26
  55.4 13.6 %collective-permute-start = (bf16[48,1024]{1,0:T(8,128)(2,1)S(1)}, bf16[48,1024]{1,0:T(8,128)(2,1)S(1)}, u32[]{:S(2)}, u32[]{:S(2)}) collective-permute-start(bf16[48,1024]{1,0:T(8,128)(2,1)S(1)} %copy_bitcast_fusion), channel_id=1, source_target_pairs={{0,2},{2,4},{4,6},{6,0},{1,3},{3,5},{5,7},{7,1},{8,10},{10,12},{12... | collective-permute-start | bytes 294920 | tf_op jit(solution)/shard_map/ppermute | solution.py:26
  61.7 7.6 %collective-permute-start.1 = (bf16[48,1024]{1,0:T(8,128)(2,1)S(1)}, bf16[48,1024]{1,0:T(8,128)(2,1)S(1)}, u32[]{:S(2)}, u32[]{:S(2)}) collective-permute-start(bf16[48,1024]{1,0:T(8,128)(2,1)S(1)} %copy_bitcast_fusion), channel_id=1, source_target_pairs={{0,4},{2,6},{4,0},{6,2},{1,5},{3,7},{5,1},{7,3},{8,12},{10,14},{12... | collective-permute-start | bytes 294920 | tf_op jit(solution)/shard_map/ppermute | solution.py:26
  63.7 0.8 copy-start.6
  63.7 5.5 %collective-permute-start.2 = (bf16[48,1024]{1,0:T(8,128)(2,1)S(1)}, bf16[48,1024]{1,0:T(8,128)(2,1)S(1)}, u32[]{:S(2)}, u32[]{:S(2)}) collective-permute-start(bf16[48,1024]{1,0:T(8,128)(2,1)S(1)} %copy_bitcast_fusion), channel_id=1, source_target_pairs={{0,6},{2,0},{4,2},{6,4},{1,7},{3,1},{5,3},{7,5},{8,14},{10,8},{12,... | collective-permute-start | bytes 294920 | tf_op jit(solution)/shard_map/ppermute | solution.py:26
  64.4 0.8 copy-start.7
  64.4 0.9 copy-start.8
  69.3 9.3 %collective-permute-start.3 = (bf16[4,48,1024]{2,1,0:T(8,128)(2,1)S(1)}, bf16[4,48,1024]{2,1,0:T(8,128)(2,1)S(1)}, u32[]{:S(2)}, u32[]{:S(2)}) collective-permute-start(bf16[4,48,1024]{2,1,0:T(8,128)(2,1)S(1)} %pad_maximum_fusion.2), channel_id=1, source_target_pairs={{0,1},{1,0},{2,3},{3,2},{4,5},{5,4},{6,7},{7,6},{8,9},{9,8},{10,11... | collective-permute-start | bytes 1179656 | tf_op jit(solution)/shard_map/ppermute | solution.py:22
  81.4 15.9 %copy-start.9 = (bf16[3,7168]{1,0:T(4,128)(2,1)S(1)}, bf16[3,7168]{1,0:T(4,128)(2,1)}, u32[]{:S(2)}) copy-start(bf16[3,7168]{1,0:T(4,128)(2,1)} %param.13) | copy-start | bytes 129028
  84.8 27.0 %all-to-all-start.1 = ((bf16[16,24,896]{2,1,0:T(8,128)(2,1)}), bf16[16,24,896]{2,1,0:T(8,128)(2,1)S(1)}, u32[]{:S(2)}, u32[]{:S(2)}) async-start(bf16[16,24,896]{2,1,0:T(8,128)(2,1)} %bitcast.31), calls=%async_computation.1 | async-start | bytes 1376256 | tf_op jit(solution)/shard_map/all_to_all | solution.py:124
  112.1 31.6 %copy-start.2 = (bf16[288,7168]{1,0:T(8,128)(2,1)S(1)}, bf16[288,7168]{1,0:T(8,128)(2,1)}, u32[]{:S(2)}) copy-start(bf16[288,7168]{1,0:T(8,128)(2,1)} %param.19) | copy-start | bytes 12386308
  141.6 5.8 %collective-permute-start.8 = (bf16[32,24,1024]{2,1,0:T(8,128)(2,1)S(1)}, bf16[32,24,1024]{2,1,0:T(8,128)(2,1)}, u32[]{:S(2)}, u32[]{:S(2)}) collective-permute-start(bf16[32,24,1024]{2,1,0:T(8,128)(2,1)S(1)} %all_to_all.20), channel_id=1, source_target_pairs={{0,1},{1,0},{2,3},{3,2},{4,5},{5,4},{6,7},{7,6},{8,9},{9,8},{10,11... | collective-permute-start | bytes 4718600 | tf_op jit(solution)/shard_map/ppermute | solution.py:22
  145.2 14.5 %collective-permute-start.10 = (bf16[288,3584]{1,0:T(8,128)(2,1)}, bf16[288,3584]{1,0:T(8,128)(2,1)}, u32[]{:S(2)}, u32[]{:S(2)}) collective-permute-start(bf16[288,3584]{1,0:T(8,128)(2,1)} %constant_dynamic-slice_fusion.1), channel_id=1, source_target_pairs={{0,1},{1,0},{2,3},{3,2},{4,5},{5,4},{6,7},{7,6},{8,9},{9,8},{10,11... | collective-permute-start | bytes 6193160 | tf_op jit(solution)/shard_map/ppermute | solution.py:22
  149.9 2.2 %copy-start.10 = (bf16[7168,288]{0,1:T(8,128)(2,1)S(1)}, bf16[7168,288]{0,1:T(8,128)(2,1)}, u32[]{:S(2)}) copy-start(bf16[7168,288]{0,1:T(8,128)(2,1)} %param.17) | copy-start | bytes 12386308
  152.1 2.2 %copy-start.11 = (bf16[7168,288]{0,1:T(8,128)(2,1)S(1)}, bf16[7168,288]{0,1:T(8,128)(2,1)}, u32[]{:S(2)}) copy-start(bf16[7168,288]{0,1:T(8,128)(2,1)} %param.18) | copy-start | bytes 12386308
  154.3 1.3 copy-start.5
  156.7 2.2 %copy-start.3 = (bf16[288,7168]{1,0:T(8,128)(2,1)S(1)}, bf16[288,7168]{1,0:T(8,128)(2,1)}, u32[]{:S(2)}) copy-start(bf16[288,7168]{1,0:T(8,128)(2,1)} %param.19) | copy-start | bytes 12386308
  157.9 1.9 collective-permute-start.9
  162.5 29.8 %copy-start.1 = (bf16[6,128,576]{1,2,0:T(8,128)(2,1)S(1)}, bf16[6,128,576]{1,2,0:T(8,128)(2,1)}, u32[]{:S(2)}) copy-start(bf16[6,128,576]{1,2,0:T(8,128)(2,1)} %param.10) | copy-start | bytes 2654212
  165.1 23.3 %all-to-all-start.3 = ((bf16[32,168,128]{2,1,0:T(8,128)(2,1)}), bf16[32,168,128]{2,1,0:T(8,128)(2,1)S(1)}, u32[]{:S(2)}, u32[]{:S(2)}) async-start(bf16[32,168,128]{2,1,0:T(8,128)(2,1)} %reshape.360), calls=%async_computation.3 | async-start | bytes 2752512 | tf_op jit(solution)/shard_map/all_to_all | solution.py:162
  188.7 2.9 %collective-permute-start.11 = (bf16[3,3584]{1,0:T(4,128)(2,1)S(1)}, bf16[3,3584]{1,0:T(4,128)(2,1)S(1)}, u32[]{:S(2)}, u32[]{:S(2)}) collective-permute-start(bf16[3,3584]{1,0:T(4,128)(2,1)S(1)} %constant_dynamic-slice_fusion), channel_id=1, source_target_pairs={{0,1},{1,0},{2,3},{3,2},{4,5},{5,4},{6,7},{7,6},{8,9},{9,8},{10,11... | collective-permute-start | bytes 64520 | tf_op jit(solution)/shard_map/ppermute | solution.py:22
Sparse Core Ops, SparseCore 0:
  24.9 28.8 all-gather.2

commit v3 on v1

v3 whole, which is shorter than its diff:
```python
import functools
import math

import jax
import jax.numpy as jnp
import numpy as np
from jax import lax
from jax.experimental import pallas as pl
from jax.experimental.pallas import tpu as pltpu
from jax.sharding import Mesh, PartitionSpec as P

LAT = 512
QKD = 192
LANES = 128
SUB = 8
AXES = ("zh", "zl", "x", "y", "core")
DEV = ("zl", "x", "y", "core")
OUTER = ("zh", "zl", "x")
SIDE_CHIPS = ("zl", "x", "y")
SWAP = [(0, 1), (1, 0)]
F32 = jnp.float32
BF16 = jnp.bfloat16
VMEM_LIMIT = 40 * 1024 * 1024


def swap(array):
    return lax.ppermute(array, "core", SWAP)


def shift(array, step):
    return lax.ppermute(array, "y", [(i, (i + step) % 4) for i in range(4)])


def block(array, index, size, axis):
    return lax.dynamic_slice_in_dim(array, index * size, size, axis)


def swap_halves(array, core, axis):
    half = array.shape[axis] // 2
    return block(array, core, half, axis), swap(block(array, 1 - core, half, axis))


def spread(groups, rows):
    matrix = np.zeros((groups * SUB, groups * rows), np.float32)
    for group in range(groups):
        for row in range(rows):
            matrix[group * SUB + row, group * rows + row] = 1.0
    return matrix


def params(*semantics):
    return pltpu.CompilerParams(
        vmem_limit_bytes=VMEM_LIMIT, dimension_semantics=semantics or None
    )


def cost(flops, read):
    return pl.CostEstimate(flops=flops, bytes_accessed=read, transcendentals=0)


WHOLE = pl.BlockSpec(memory_space=pltpu.VMEM)


def rounded(value):
    return value.astype(BF16).astype(F32)


def attend_kernel(info_ref, query_ref, cache_ref, out_ref, held, stats):
    row = pl.program_id(0)
    rows = pl.num_programs(0)
    keys = cache_ref.shape[1]
    heads = query_ref.shape[1]
    cached = cache_ref[0]
    scores = lax.dot_general(
        query_ref[0], cached, (((1,), (1,)), ((), ())), preferred_element_type=F32
    ) * (1.0 / math.sqrt(QKD))
    position = lax.broadcasted_iota(jnp.int32, (1, keys), 1) + info_ref[rows]
    usable = position < info_ref[row]
    scores = jnp.where(usable, scores, F32(-1e30))
    top = jnp.max(scores, axis=1, keepdims=True)
    top_high = rounded(top)
    top_low = rounded(top - top_high)
    exponent = jnp.where(usable, jnp.exp(scores - (top_high + top_low)), F32(0.0))
    total = jnp.sum(exponent, axis=1, keepdims=True)
    total_high = rounded(total)
    total_low = rounded(total - total_high)
    weighted = jnp.dot(
        exponent.astype(BF16), cached[:, :LAT], preferred_element_type=F32
    )
    tiles = [slice(start, start + LANES) for start in range(0, LAT, LANES)]
    for index, tile in enumerate(tiles):
        held[index, pl.ds(row, heads, stride=SUB), :] = weighted[:, tile]
    lane = lax.broadcasted_iota(jnp.int32, (heads, LANES), 1)
    new = jnp.where(lane == row, top_high, stats[...])
    new = jnp.where(lane == row + SUB, top_low, new)
    new = jnp.where(lane == row + 2 * SUB, total_high, new)
    stats[...] = jnp.where(lane == row + 3 * SUB, total_low, new)

    @pl.when(row == rows - 1)
    def _():
        zero = jnp.zeros((heads, LANES), F32)
        for index, tile in enumerate(tiles):
            filler = zero if index else stats[...]
            held[index, pl.ds(SUB - 2, heads, stride=SUB), :] = filler
            held[index, pl.ds(SUB - 1, heads, stride=SUB), :] = zero
            out_ref[:, :, tile] = held[index].reshape(heads, SUB, LANES).astype(BF16)


def attend(info, query, cache):
    rows, heads, depth = query.shape
    keys = cache.shape[1]
    return pl.pallas_call(
        attend_kernel,
        out_shape=jax.ShapeDtypeStruct((heads, SUB, LAT), BF16),
        grid_spec=pltpu.PrefetchScalarGridSpec(
            num_scalar_prefetch=1,
            grid=(rows,),
            in_specs=[
                pl.BlockSpec((1, heads, depth), lambda r, info: (r, 0, 0)),
                pl.BlockSpec((1, keys, depth), lambda r, info: (r, 0, 0)),
            ],
            out_specs=pl.BlockSpec((heads, SUB, LAT), lambda r, info: (0, 0, 0)),
            scratch_shapes=[
                pltpu.VMEM((LAT // LANES, heads * SUB, LANES), F32),
                pltpu.VMEM((heads, LANES), F32),
            ],
        ),
        compiler_params=params("arbitrary"),
        cost_estimate=cost(2 * rows * heads * keys * (depth + LAT), 5_000_000),
        name="attend",
    )(info, query, cache)


def join_kernel(rows, recv_ref, up_ref, gather_ref, out_ref):
    devs = recv_ref.shape[0] // 2
    parts = recv_ref[...].astype(F32).reshape(2, devs, SUB, LAT)
    table = parts[:, :, SUB - 2 : SUB - 1, :LANES]
    lane = lax.broadcasted_iota(jnp.int32, (SUB, LANES), 1)
    sub = lax.broadcasted_iota(jnp.int32, (SUB, LANES), 0)

    def pick(first):
        chosen = (lane == sub + first) | (lane == sub + first + SUB)
        return jnp.sum(jnp.where(chosen & (sub < rows), table, F32(0.0)), axis=3, keepdims=True)

    peaks = pick(0)
    totals = pick(2 * SUB)
    factor = jnp.exp(peaks - jnp.maximum(peaks[:1], peaks[1:]))
    total = factor[0] * totals[0] + factor[1] * totals[1]
    valid = lax.broadcasted_iota(jnp.int32, (1, SUB, 1), 1) < rows
    scale = jnp.where(valid, 1.0 / jnp.where(valid, total, F32(1.0)), F32(0.0))
    latent = parts[0] * (factor[0] * scale) + parts[1] * (factor[1] * scale)
    latent = latent.reshape(devs * SUB, LAT).astype(BF16)
    values = jnp.dot(latent, up_ref[0], preferred_element_type=F32).astype(BF16)
    out_ref[...] = jnp.dot(gather_ref[...], values, preferred_element_type=F32).astype(BF16)


def join(received, value_up, rows):
    devs = received.shape[0] // 2
    gather = jnp.asarray(spread(devs, rows).T, BF16)
    return pl.pallas_call(
        functools.partial(join_kernel, rows),
        out_shape=jax.ShapeDtypeStruct((devs * rows, value_up.shape[2]), BF16),
        in_specs=[WHOLE] * 3,
        out_specs=WHOLE,
        compiler_params=params(),
        cost_estimate=cost(120_000_000, 1_500_000),
        name="join",
    )(received, value_up, gather)


def project_kernel(info_ref, *refs):
    values, theirs, out_ref = refs[:8], refs[8:16], refs[16]
    del info_ref
    left = jnp.concatenate([ref[...] for ref in values], axis=1)
    right = jnp.concatenate([ref[...] for ref in theirs], axis=0)
    total = jnp.dot(left, right, preferred_element_type=F32)
    out_ref[...] = total.reshape(out_ref.shape).astype(BF16)


def project(info, values, out_proj, parts, theirs, chips):
    rows, lanes = values[0].shape
    eighth = theirs[0].shape[1]
    full = lambda shape: pl.BlockSpec(shape, lambda i, info: (0,) * len(shape))
    held = pl.BlockSpec((lanes, eighth), lambda i, info: (0, info[1]))
    own = pl.BlockSpec((lanes, eighth), lambda i, info: (0, info[0]))
    return pl.pallas_call(
        project_kernel,
        out_shape=jax.ShapeDtypeStruct((chips, rows // chips, eighth), BF16),
        grid_spec=pltpu.PrefetchScalarGridSpec(
            num_scalar_prefetch=1,
            grid=(1,),
            in_specs=[full((rows, lanes))] * 8
            + [own]
            + [held] * 3
            + [full((lanes, eighth))] * 4,
            out_specs=full((chips, rows // chips, eighth)),
        ),
        compiler_params=params("arbitrary"),
        cost_estimate=cost(2 * rows * 8 * lanes * eighth, 3_500_000),
        name="project",
    )(info, *values, out_proj, *parts, *theirs)


def residual_kernel(parts_ref, stream_ref, gain_ref, residual_ref, out_ref):
    residual = stream_ref[...].astype(F32) + jnp.sum(parts_ref[...].astype(F32), axis=0)
    residual_ref[...] = residual
    rows, width = residual.shape
    squares = jnp.sum(residual * residual, axis=1, keepdims=True)
    high = rounded(squares)
    low = rounded(squares - high)
    lane = lax.broadcasted_iota(jnp.int32, (SUB, LANES), 1)
    table = jnp.zeros((SUB, LANES), F32)
    scaled = residual * gain_ref[...]
    groups = rows // SUB
    columns = width // LANES
    chips = out_ref.shape[0]
    for group in range(groups):
        span = slice(group * SUB, group * SUB + SUB)
        table = jnp.where(lane == group, high[span], table)
        table = jnp.where(lane == SUB + group, low[span], table)
    tiles = [
        scaled[group * SUB : group * SUB + SUB, column * LANES : column * LANES + LANES]
        for column in range(columns)
        for group in range(groups)
    ] + [table]
    for index, tile in enumerate(tiles):
        out_ref[:, index] = jnp.broadcast_to(tile.astype(BF16)[None], (chips, SUB, LANES))


def residual_rows(parts, stream, gain, chips):
    _, rows, width = parts.shape
    tiles = rows * width // (SUB * LANES) + 1
    return pl.pallas_call(
        residual_kernel,
        out_shape=(
            jax.ShapeDtypeStruct((rows, width), F32),
            jax.ShapeDtypeStruct((chips, tiles, SUB, LANES), BF16),
        ),
        in_specs=[WHOLE] * 3,
        out_specs=(WHOLE, WHOLE),
        compiler_params=params(),
        cost_estimate=cost(2_000_000, 2_500_000),
        name="residual",
    )(parts, stream, gain)


def units_kernel(groups, width, last, info_ref, *refs):
    if last:
        recv_ref, gate_ref, up_ref, gate_in, up_in, sq_in, out_ref, gate_acc, up_acc, sq_acc = refs
    else:
        recv_ref, gate_ref, up_ref, gate_acc, up_acc, sq_acc = refs
    step = pl.program_id(0)
    sides, _, tiles, _, _ = recv_ref.shape
    columns = (tiles - 1) // groups
    rows = sides * groups * SUB
    left = jnp.concatenate(
        [
            recv_ref[:, 0, column * groups : column * groups + groups]
            .astype(F32)
            .reshape(rows, LANES)
            for column in range(columns)
        ],
        axis=1,
    ).astype(BF16)
    gate = jnp.dot(left, gate_ref[...], preferred_element_type=F32)
    upper = jnp.dot(left, up_ref[...], preferred_element_type=F32)
    table = recv_ref[:, 0, tiles - 1].astype(F32)
    lane = lax.broadcasted_iota(jnp.int32, (SUB, LANES), 1)
    pieces = [
        jnp.sum(
            jnp.where((lane == group) | (lane == SUB + group), table, F32(0.0)),
            axis=2,
            keepdims=True,
        )
        for group in range(groups)
    ]
    squares = jnp.stack(pieces, axis=1).reshape(rows, 1)
    squares = jnp.broadcast_to(squares, (rows, LANES))

    @pl.when(step == 0)
    def _():
        if last:
            gate_acc[...] = gate_in[...] + gate
            up_acc[...] = up_in[...] + upper
            sq_acc[...] = sq_in[...] + squares
        else:
            gate_acc[...] = gate
            up_acc[...] = upper
            sq_acc[...] = squares

    @pl.when(step > 0)
    def _():
        gate_acc[...] += gate
        up_acc[...] += upper
        sq_acc[...] += squares

    if last:

        @pl.when(step == pl.num_programs(0) - 1)
        def _():
            scale = lax.rsqrt(sq_acc[:, :1] / width + 1e-06)
            gate = gate_acc[...] * scale
            out_ref[...] = (gate / (1.0 + jnp.exp(-gate)) * (up_acc[...] * scale)).astype(BF16)


def units(info, which, received, gate_proj, up_proj, groups, carry=None):
    sides, quarters, tiles = received.shape[:3]
    depth = (tiles - 1) // groups * LANES
    hidden = gate_proj.shape[1]
    rows = sides * groups * SUB
    whole = lambda shape: pl.BlockSpec(shape, lambda i, info: (0,) * len(shape))
    weight = pl.BlockSpec((depth, hidden), lambda i, info: (info[which] * quarters + i, 0))
    shapes = [(rows, hidden), (rows, hidden), (rows, LANES)]
    last = carry is not None
    return pl.pallas_call(
        functools.partial(units_kernel, groups, gate_proj.shape[0], last),
        out_shape=jax.ShapeDtypeStruct((rows, hidden), BF16)
        if last
        else [jax.ShapeDtypeStruct(shape, F32) for shape in shapes],
        grid_spec=pltpu.PrefetchScalarGridSpec(
            num_scalar_prefetch=1,
            grid=(quarters,),
            in_specs=[
                pl.BlockSpec(
                    (sides, 1, tiles, SUB, LANES), lambda i, info: (0, i, 0, 0, 0)
                ),
                weight,
                weight,
            ]
            + ([whole(shape) for shape in shapes] if last else []),
            out_specs=whole((rows, hidden)) if last else [whole(shape) for shape in shapes],
            scratch_shapes=[pltpu.VMEM(shape, F32) for shape in shapes] if last else [],
        ),
        compiler_params=params("arbitrary"),
        cost_estimate=cost(4 * rows * depth * quarters * hidden, 8_000_000),
        name="units_last" if last else "units_first",
    )(info, received, gate_proj, up_proj, *(carry or ()))


def down_kernel(info_ref, mine_ref, theirs_ref, spread_ref, own_ref, other_ref, held_ref, out_ref, left, right):
    @pl.when(pl.program_id(0) == 0)
    def _():
        left[...] = jnp.dot(
            spread_ref[...], mine_ref[...], preferred_element_type=F32
        ).astype(BF16)
        right[...] = jnp.dot(
            spread_ref[...], theirs_ref[...], preferred_element_type=F32
        ).astype(BF16)

    total = jnp.dot(left[...], own_ref[...], preferred_element_type=F32) + jnp.dot(
        right[...], other_ref[...], preferred_element_type=F32
    )
    span = held_ref.shape[0]
    place = lax.broadcasted_iota(jnp.int32, (total.shape[0] // span, 1, 1), 0) == info_ref[2]
    total = total.reshape(-1, span, total.shape[1])
    total = total + jnp.where(place, held_ref[...][None], F32(0.0))
    chips = out_ref.shape[0]
    total = total.reshape(chips, SUB, -1)
    quads = [total[:, :, tile * LANES : tile * LANES + LANES] for tile in range(4)]
    sub = lax.broadcasted_iota(jnp.int32, (1, SUB, LANES), 1)
    packed = [
        jnp.where(sub < 6, quads[tile], pltpu.roll(quads[3], 6 - 2 * tile, 1))
        for tile in range(3)
    ]
    out_ref[:, 0] = jnp.concatenate(packed, axis=1).astype(BF16)


def down(info, mine, theirs, down_proj, down_theirs, held, chips):
    rows, hidden = mine.shape
    half = down_theirs.shape[1]
    width = 4 * LANES
    steps = half // width
    put = jnp.asarray(spread(chips, rows // chips), BF16)
    whole = lambda shape: pl.BlockSpec(shape, lambda i, info: (0,) * len(shape))
    return pl.pallas_call(
        down_kernel,
        out_shape=jax.ShapeDtypeStruct((chips, steps, 3 * SUB, LANES), BF16),
        grid_spec=pltpu.PrefetchScalarGridSpec(
            num_scalar_prefetch=1,
            grid=(steps,),
            in_specs=[
                whole((rows, hidden)),
                whole((rows, hidden)),
                whole(put.shape),
                pl.BlockSpec((hidden, width), lambda i, info: (0, info[3] * steps + i)),
                pl.BlockSpec((hidden, width), lambda i, info: (0, i)),
                pl.BlockSpec((held.shape[0], width), lambda i, info: (0, i)),
            ],
            out_specs=pl.BlockSpec(
                (chips, 1, 3 * SUB, LANES), lambda i, info: (0, i, 0, 0)
            ),
            scratch_shapes=[pltpu.VMEM((chips * SUB, hidden), BF16)] * 2,
        ),
        compiler_params=params("arbitrary"),
        cost_estimate=cost(4 * chips * SUB * hidden * half, 6_000_000),
        name="down",
    )(info, mine, theirs, put, down_proj, down_theirs, held)


def finish_kernel(info_ref, parts_ref, mine_ref, theirs_ref):
    total = jnp.sum(parts_ref[...].astype(F32), axis=0)
    sub = lax.broadcasted_iota(jnp.int32, (SUB, LANES), 0)
    columns = []
    for step in range(total.shape[0]):
        quads = [total[step, tile * SUB : tile * SUB + SUB] for tile in range(3)]
        last = jnp.where(
            sub < 2,
            pltpu.roll(quads[0], 2, 0),
            jnp.where(sub < 4, pltpu.roll(quads[1], 4, 0), pltpu.roll(quads[2], 6, 0)),
        )
        columns += quads + [last]
    rows = jnp.concatenate(columns, axis=1)
    first, second = rows[0:3], rows[3:6]
    is_first = info_ref[3] == 0
    mine_ref[...] = jnp.where(is_first, first, second).astype(BF16)
    theirs_ref[...] = jnp.where(is_first, second, first).astype(BF16)


def finish(info, parts):
    shape = jax.ShapeDtypeStruct((3, parts.shape[1] * 4 * LANES), BF16)
    return pl.pallas_call(
        finish_kernel,
        out_shape=(shape, shape),
        in_specs=[pl.BlockSpec(memory_space=pltpu.SMEM), WHOLE],
        out_specs=(WHOLE, WHOLE),
        compiler_params=params(),
        cost_estimate=cost(1_000_000, 1_500_000),
        name="finish",
    )(info, parts)


def local(
    query_latent,
    latent_cache,
    lengths,
    stream,
    norm_gain,
    value_up,
    out_proj,
    gate_proj,
    up_proj,
    down_proj,
):
    core = lax.axis_index("core")
    ring = lax.axis_index("y")
    group = lax.axis_index("zl") * 4 + lax.axis_index("x")
    rows_own, width = stream.shape
    rows = query_latent.shape[0]
    half = width // 2
    eighth = width // 8
    first = core == 0
    info = jnp.stack([core * 4 + ring, core, group, core, 1 - core]).astype(jnp.int32)

    def ring_part(step):
        chip = (ring + step) % 4
        return jnp.concatenate(
            [
                lax.dynamic_slice_in_dim(out_proj, start + chip * eighth, eighth, 1)
                for start in (0, half)
            ],
            axis=1,
        )

    part_one, part_three = shift(ring_part(1), 1), shift(ring_part(3), 3)
    stream_mine, stream_theirs = swap_halves(stream, core, 1)
    stream_rows = jnp.concatenate(
        [
            jnp.where(first, stream_mine, stream_theirs),
            jnp.where(first, stream_theirs, stream_mine),
        ],
        axis=0,
    )
    stream_parts = [block(stream_rows, ring, eighth, 1)]
    for step in (1, 2, 3):
        stream_parts.append(shift(block(stream_rows, (ring + step) % 4, eighth, 1), step))
    back = (ring - jnp.arange(4)) % 4
    ring_stream = jnp.take(jnp.stack(stream_parts), back, axis=0)
    ring_stream = ring_stream.reshape(8 * rows_own, eighth)
    _, down_theirs = swap_halves(down_proj, core, 1)
    gain = block(norm_gain, core * 4 + ring, eighth, 0)[None]

    offset = lax.axis_index("zh") * latent_cache.shape[1]
    payload = attend(
        jnp.concatenate([lengths, offset[None].astype(jnp.int32)]), query_latent, latent_cache
    )
    payload, part_one, part_three = lax.optimization_barrier((payload, part_one, part_three))
    part_two = shift(lax.optimization_barrier((ring_part(2), part_one))[0], 2)
    received = lax.all_to_all(payload, AXES, split_axis=0, concat_axis=0, tiled=True)
    values = join(received, value_up, rows)

    ring_values = [values] + [shift(values, step) for step in (1, 2, 3)]
    parts = [part_one, part_two, part_three]
    theirs = [swap(block(out_proj, (1 - core) * 4 + ring, eighth, 1))]
    theirs += [swap(block(part, 1 - core, eighth, 1)) for part in parts]
    partial = project(
        info,
        ring_values + [swap(piece) for piece in ring_values],
        out_proj,
        parts,
        theirs,
        16,
    )
    parts = lax.all_to_all(partial, OUTER, split_axis=0, concat_axis=0, tiled=True)

    residual, payload = residual_rows(parts, ring_stream, gain, 32)
    held = residual.reshape(4, 2 * rows_own, eighth)
    held = jnp.pad(held, ((0, 0), (0, SUB - 2 * rows_own), (0, 0))).reshape(4 * SUB, eighth)
    held = lax.dynamic_update_slice(
        jnp.zeros((4 * SUB, half), F32), held, (0, ring * eighth)
    )
    piece = lax.all_to_all(payload, SIDE_CHIPS, split_axis=0, concat_axis=0, tiled=True)
    piece = piece.reshape((8, 4) + piece.shape[1:])
    other = swap(piece)
    groups = 8 * rows_own // SUB
    carry = units(info, 3, piece, gate_proj, up_proj, groups)
    hidden = units(info, 4, other, gate_proj, up_proj, groups, carry)
    partial = down(info, hidden, swap(hidden), down_proj, down_theirs, held, 32)
    parts = lax.all_to_all(partial, SIDE_CHIPS, split_axis=0, concat_axis=0, tiled=True)
    mine, theirs = finish(info, parts)
    theirs = swap(theirs)
    return jnp.concatenate(
        [jnp.where(first, mine, theirs), jnp.where(first, theirs, mine)], axis=1
    )


def solution(mesh):
    fine = Mesh(mesh.devices.reshape(2, 2, 4, 4, 2), AXES)
    placed = (
        P(DEV, None, None),
        P(DEV, "zh", None),
        P(DEV),
        P(AXES, None),
        P(),
        P(AXES, None, None),
        P(AXES, None),
        P(None, DEV),
        P(None, DEV),
        P(DEV, None),
    )
    return jax.shard_map(
        local, mesh=fine, in_specs=placed, out_specs=P(AXES, None), check_vma=False
    )
```

time: 170 us -> 193 us (1.14)
  local copies, waits for them, and re-layouts: 18.6 us -> 47.1 us
  waiting for transfers between devices: 73.1 us -> 46.6 us
  Pallas kernels: 0 us -> 26.3 us
  matrix products: 17 us -> 0 us
  starting transfers between devices: 30.5 us -> 43.3 us
    unnamed x19 -> x38, local copies, waits for them, and re-layouts: 1.71 us -> 35.2 us
    all_to_all x2, waiting for transfers between devices: 53.9 us -> 20.7 us  [the longest x1 15.5 us: local(): lax.all_to_all(payload, SIDE_CHIPS, split_axis=0, concat_axis=0, tiled=True)]
    pallas_call x0 -> x8, Pallas kernels: none -> 26.3 us  [the longest x2 8.11 us: units(): pl.pallas_call(functools.partial(units_kernel, groups, gate_proj.shape[0]...]
    ppermute x8 -> x22, waiting for transfers between devices: 2.5 us -> 25.9 us  [the longest x9 22.9 us: shift(): return lax.ppermute(array, 'y', [(i, (i + step) % 4) for i in range(4)])]
    dot_general x11 -> x0, matrix products: 17 us -> none  [the longest x2 3.85 us: hidden_units(): jnp.dot(piece, mine, preferred_element_type=F32)]
    all_to_all x1, waiting for transfers between devices: 16.8 us -> 0.01 us  [local(): lax.all_to_all(payload, AXES, split_axis=0, concat_axis=0, tiled=True)]
    ppermute x8 -> x22, starting transfers between devices: 9.36 us -> 22.5 us  [the longest x9 12.3 us: shift(): return lax.ppermute(array, 'y', [(i, (i + step) % 4) for i in range(4)])]
    reshape x7 -> x1, local copies, waits for them, and re-layouts: 11.5 us -> 0.01 us  [local(): held = residual.reshape(4, 2 * rows_own, eighth)]
  transfers between devices with their start and end apart: 11 -> 25, of which waited for: 7 -> 10; matrix products, arithmetic and copies ran while one was open for 7% -> 18% of each run, Pallas kernels for 0% -> 10%
where the time goes in v3:
time: 193 us; the launch traced here: 192 us
  local copies, waits for them, and re-layouts  47.1 us (24%)
  waiting for transfers between devices  46.6 us (24%)
  starting transfers between devices  43.3 us (22%)
  Pallas kernels  26.3 us (14%)
  blocking collectives  24.3 us (13%)
  other arithmetic  3.88 us (2%)
    unnamed x38, local copies, waits for them, and re-layouts  35.2 us
    all_to_all x1, blocking collectives, local(): lax.all_to_all(partial, SIDE_CHIPS, split_axis=0, concat_axis=0, tiled=True)  24.3 us
    ppermute x9, waiting for transfers between devices, shift(): return lax.ppermute(array, 'y', [(i, (i + step) % 4) for i in range(4)])  22.9 us
    all_to_all x1, waiting for transfers between devices, local(): lax.all_to_all(payload, SIDE_CHIPS, split_axis=0, concat_axis=0, tiled=True)  15.5 us
    ppermute x9, starting transfers between devices, shift(): return lax.ppermute(array, 'y', [(i, (i + step) % 4) for i in range(4)])  12.3 us
    dynamic_slice x7, local copies, waits for them, and re-layouts, block(): return lax.dynamic_slice_in_dim(array, index * size, size, axis)  11 us
    ppermute x13, starting transfers between devices, swap(): return lax.ppermute(array, 'core', SWAP)  10.2 us
    all_to_all x1, starting transfers between devices, local(): lax.all_to_all(payload, AXES, split_axis=0, concat_axis=0, tiled=True)  8.97 us
  transfers between devices with their start and end apart: 25, of which 10 were waited for; matrix products, arithmetic and copies ran while one was open for 18% of the time, Pallas kernels for 10%

profile of v3, /device:TPU:1, one launch (start us, length us, event | category | flops | bytes accessed | tf_op | source)
XLA Modules:
  0.0 191.7 jit_solution(11315770353096546324)
XLA Ops:
  0.0 2.5 %constant_dynamic-slice_fusion.5 = (bf16[128,896]{1,0:T(8,128)(2,1)}, bf16[128,896]{1,0:T(8,128)(2,1)}, bf16[128,896]{1,0:T(8,128)(2,1)}, bf16[128,896]{1,0:T(8,...) fusion(bf16[128,7168]{1,0:T(8,128)(2,1)} %refs_8_.1, ...), kind=kLoop, calls=%fused_computation.30 | loop fusion | bytes 3211292 | tf_op jit(solution)/shard_map/dynamic_slice | solution.py:35
  2.5 2.2 %collective-permute-start = (bf16[128,1792]{1,0:T(8,128)(2,1)S(1)}, bf16[128,1792]{1,0:T(8,128)(2,1)S(1)}, u32[]{:S(2)}, u32[]{:S(2)}) collective-permute-start(bf16[128,1792]{1,0:T(8,128)(2,1)S(1)} %pad_maximum_fusion), channel_id=1, source_target_pairs={{0,2},{2,4},{4,6},{6,0},{1,3},{3,5},{5,7},{7,1},{8,10},{10,12},{12... | collective-permute-start | bytes 1376264 | tf_op jit(solution)/shard_map/ppermute | solution.py:31
  4.7 0.8 pad_maximum_fusion.1
  5.5 1.5 collective-permute-start.1
  7.0 1.1 collective-permute-start.10
  8.1 0.6 copy.19.query_ref
  8.7 6.0 %copy.20.cache_ref = bf16[6,512,576]{2,1,0:T(8,128)(2,1)} copy(bf16[6,512,576]{1,2,0:T(8,128)(2,1)} %param.13) | data formatting | bytes 7077888 | tf_op args[1]
  14.8 2.1 %copy-done.3 = bf16[6,512,576]{2,1,0:T(8,128)(2,1)S(1)} copy-done((bf16[6,512,576]{2,1,0:T(8,128)(2,1)S(1)}, bf16[6,512,576]{2,1,0:T(8,128)(2,1)}, u32[]{:S(2)}) %copy-start.3) | copy-done | bytes 3538968
  16.9 5.8 %attend.1 = bf16[128,8,512]{2,1,0:T(8,128)(2,1)} custom-call(s32[7]{0:T(128)S(1)} %pad_add_fusion.info_ref, bf16[6,128,576]{2,1,0:T(8,128)(2,1)S(1)} %copy.19.query_ref, bf16[6,512,576]{2,1,0:T(8,128)(2,1)S(1)} %copy-done.3), custom_call_target="tpu_custom_call" | custom-call | flops 855638016 | bytes 5000000 | tf_op jit(solution)/shard_map/attend/pallas_call | solution.py:112
  22.8 0.8 copy-done.7
  23.5 9.0 %all-to-all-start = ((bf16[128,8,512]{2,1,0:T(8,128)(2,1)}), bf16[128,8,512]{2,1,0:T(8,128)(2,1)S(1)}, u32[]{:S(2)}, u32[]{:S(2)}) async-start(bf16[128,8,512]{2,1,0:T(8,128)(2,1)} %attend.1), calls=%async_computation | async-start | bytes 2097152 | tf_op jit(solution)/shard_map/all_to_all | solution.py:488
  32.5 2.0 %pad_maximum_fusion.2 = bf16[128,1792]{1,0:T(8,128)(2,1)} fusion(bf16[128,896]{1,0:T(8,128)(2,1)} %get-tuple-element.28, bf16[128,896]{1,0:T(8,128)(2,1)} %get-tuple-element.29), kind=kLoop, calls=%fused_computation.3 | loop fusion | flops 917504 | bytes 917504 | tf_op jit(solution)/shard_map/concatenate | solution.py:456
  34.5 2.9 %collective-permute-start.9 = (bf16[128,1792]{1,0:T(8,128)(2,1)}, bf16[128,1792]{1,0:T(8,128)(2,1)}, u32[]{:S(2)}, u32[]{:S(2)}) collective-permute-start(bf16[128,1792]{1,0:T(8,128)(2,1)} %pad_maximum_fusion.2), channel_id=1, source_target_pairs={{0,4},{2,6},{4,0},{6,2},{1,5},{3,7},{5,1},{7,3},{8,12},{10,14},{12... | collective-permute-start | bytes 1376264 | tf_op jit(solution)/shard_map/ppermute | solution.py:31
  37.4 0.6 constant_dynamic-slice_fusion.1
  38.1 0.7 constant_dynamic-slice_fusion.4
  38.8 0.6 collective-permute-start.11
  39.5 1.6 constant_dynamic-slice_fusion.2
  41.1 16.1 %collective-permute-done.9.refs_10_ = bf16[128,1792]{1,0:T(8,128)(2,1)} collective-permute-done((bf16[128,1792]{1,0:T(8,128)(2,1)}, bf16[128,1792]{1,0:T(8,128)(2,1)}, u32[]{:S(2)}, u32[]{:S(2)}) %collective-permute-start.9) | collective-permute-done | bytes 458784 | tf_op jit(solution)/shard_map/ppermute | solution.py:31
  57.3 1.7 constant_dynamic-slice_fusion.3
  58.9 0.8 collective-permute-start.12
  59.8 1.0 copy-done.9
  60.8 0.8 join.1.refs_0_
  61.7 1.5 collective-permute-start.3
  63.2 1.2 collective-permute-start.4
  64.5 0.6 collective-permute-start.5
  65.1 4.3 %collective-permute-done.2.refs_1_ = bf16[384,128]{1,0:T(8,128)(2,1)S(1)} collective-permute-done((bf16[384,128]{1,0:T(8,128)(2,1)S(1)}, bf16[384,128]{1,0:T(8,128)(2,1)S(1)}, u32[]{:S(2)}, u32[]{:S(2)}) %collective-permute-start.2) | collective-permute-done | bytes 98336 | tf_op jit(solution)/shard_map/ppermute | solution.py:31
  69.4 0.8 collective-permute-start.6
  70.2 0.6 collective-permute-start.8
  70.8 0.1 collective-permute-start.14
  70.9 0.2 collective-permute-done.6.refs_5_
  71.1 0.4 collective-permute-done.7.refs_6_
  71.5 0.3 collective-permute-done.8.refs_7_
  71.8 1.0 copy-done.8
  72.8 3.8 %project.1 = bf16[16,24,896]{2,1,0:T(8,128)(2,1)} custom-call(s32[5]{0:T(128)S(1)} %stack.35.info_ref, bf16[384,128]{1,0:T(8,128)(2,1)S(1)} %join.1.refs_0_, bf16[384,128]{1,0:T(8,128)(2,1)S(1)} %collective-permute-done.2.refs_1_, bf16[384,128]{1,0:T(8,128)(2,1)S(1)} %collective-permute-done.3.refs_2_, bf16[384,128]{1,0:T(8,128)(2,1)S(1)} %collective-permute-done.4.refs_3_, ...), custom_call_target="tpu_custom_call" | custom-call | flops 704643072 | bytes 3500000 | tf_op jit(solution)/shard_map/project/pallas_call | solution.py:186
  76.6 6.5 %all-to-all-start.1 = ((bf16[16,24,896]{2,1,0:T(8,128)(2,1)}), bf16[16,24,896]{2,1,0:T(8,128)(2,1)S(1)}, u32[]{:S(2)}, u32[]{:S(2)}) async-start(bf16[16,24,896]{2,1,0:T(8,128)(2,1)} %project.1), calls=%async_computation.1 | async-start | bytes 1376256 | tf_op jit(solution)/shard_map/all_to_all | solution.py:503
  83.1 0.1 fusion.2
  83.2 2.3 %collective-permute-start.17 = (bf16[6,896]{1,0:T(8,128)(2,1)S(1)}, bf16[6,896]{1,0:T(8,128)(2,1)S(1)}, u32[]{:S(2)}, u32[]{:S(2)}) collective-permute-start(bf16[6,896]{1,0:T(8,128)(2,1)S(1)} %get-tuple-element.41), channel_id=1, source_target_pairs={{0,6},{2,0},{4,2},{6,4},{1,7},{3,1},{5,3},{7,5},{8,14},{10,8},{12,... | collective-permute-start | bytes 32264 | tf_op jit(solution)/shard_map/ppermute | solution.py:31
  85.5 0.7 collective-permute-start.15
  86.3 0.1 broadcast_in_dim.25
  86.4 0.8 dynamic_slice.70
  87.1 2.4 %collective-permute-done.16 = bf16[6,896]{1,0:T(8,128)(2,1)S(1)} collective-permute-done((bf16[6,896]{1,0:T(8,128)(2,1)S(1)}, bf16[6,896]{1,0:T(8,128)(2,1)S(1)}, u32[]{:S(2)}, u32[]{:S(2)}) %collective-permute-start.16) | collective-permute-done | bytes 10784 | tf_op jit(solution)/shard_map/ppermute | solution.py:31
  89.6 0.6 gather_fusion
  90.3 5.3 %all-to-all-done.1.parts_ref = bf16[16,24,896]{2,1,0:T(8,128)(2,1)S(1)} async-done(((bf16[16,24,896]{2,1,0:T(8,128)(2,1)}), bf16[16,24,896]{2,1,0:T(8,128)(2,1)S(1)}, u32[]{:S(2)}, u32[]{:S(2)}) %all-to-all-start.1) | async-done | bytes 688160 | tf_op jit(solution)/shard_map/all_to_all | solution.py:503
  95.5 0.3 residual.1
  95.9 1.1 copy-done.6
  97.0 5.3 %all-to-all-start.2 = ((bf16[32,22,8,128]{3,2,1,0:T(8,128)(2,1)}), bf16[32,22,8,128]{3,2,1,0:T(8,128)(2,1)S(1)}, u32[]{:S(2)}, u32[]{:S(2)}) async-start(bf16[32,22,8,128]{3,2,1,0:T(8,128)(2,1)} %copy-done.6), calls=%async_computation.2 | async-start | bytes 2883584 | tf_op jit(solution)/shard_map/all_to_all | solution.py:511
  102.3 3.2 %constant_dynamic-slice_fusion = bf16[288,3584]{1,0:T(8,128)(2,1)} fusion(bf16[288,7168]{1,0:T(8,128)(2,1)} %own_ref.1, s32[]{:T(128)S(6)} %select_n.143), kind=kLoop, calls=%fused_computation.25 | loop fusion | bytes 4128772 | tf_op jit(solution)/shard_map/dynamic_slice | solution.py:35
  105.4 1.0 collective-permute-start.20
  106.4 15.5 %all-to-all-done.2 = bf16[32,22,8,128]{3,2,1,0:T(8,128)(2,1)S(1)} async-done(((bf16[32,22,8,128]{3,2,1,0:T(8,128)(2,1)}), bf16[32,22,8,128]{3,2,1,0:T(8,128)(2,1)S(1)}, u32[]{:S(2)}, u32[]{:S(2)}) %all-to-all-start.2) | async-done | bytes 1441824 | tf_op jit(solution)/shard_map/all_to_all | solution.py:511
  121.9 2.4 %collective-permute-start.18 = (bf16[8,4,22,8,128]{4,3,2,1,0:T(8,128)(2,1)S(1)}, bf16[8,4,22,8,128]{4,3,2,1,0:T(8,128)(2,1)}, u32[]{:S(2)}, u32[]{:S(2)}) collective-permute-start(bf16[8,4,22,8,128]{4,3,2,1,0:T(8,128)(2,1)S(1)} %bitcast.17), channel_id=1, source_target_pairs={{0,1},{1,0},{2,3},{3,2},{4,5},{5,4},{6,7},{7,6},{8,9},{9,8},{10,11... | collective-permute-start | bytes 4325384 | tf_op jit(solution)/shard_map/ppermute | solution.py:27
  124.3 7.3 %copy.23.refs_1_ = bf16[7168,288]{1,0:T(8,128)(2,1)} copy(bf16[7168,288]{0,1:T(8,128)(2,1)} %param.19) | data formatting | bytes 8257536 | tf_op args[7]
  131.7 7.4 %copy.24.refs_2_ = bf16[7168,288]{1,0:T(8,128)(2,1)} copy(bf16[7168,288]{0,1:T(8,128)(2,1)} %param.20) | data formatting | bytes 8257536 | tf_op args[8]
  139.1 2.6 %copy-done = bf16[7168,288]{1,0:T(8,128)(2,1)S(1)} copy-done((bf16[7168,288]{1,0:T(8,128)(2,1)S(1)}, bf16[7168,288]{1,0:T(8,128)(2,1)}, u32[]{:S(2)}) %copy-start) | copy-done | bytes 4128792
  141.7 2.6 %copy-done.1 = bf16[7168,288]{1,0:T(8,128)(2,1)S(1)} copy-done((bf16[7168,288]{1,0:T(8,128)(2,1)S(1)}, bf16[7168,288]{1,0:T(8,128)(2,1)}, u32[]{:S(2)}) %copy-start.1) | copy-done | bytes 4128792
  144.2 3.2 %units_first.1 = (f32[192,288]{1,0:T(8,128)S(1)}, f32[192,288]{1,0:T(8,128)S(1)}, f32[192,128]{1,0:T(8,128)S(1)}) custom-call(s32[5]{0:T(128)S(1)} %stack.35.info_ref, bf16[8,4,22,8,128]{4,3,2,1,0:T(8,128)(2,1)S(1)} %bitcast.18, bf16[7168,288]{1,0:T(8,128)(2,1)S(1)} %copy-done, bf16[7168,288]{1,0:T(8,128)(2,1)S(1)} %copy-done.1), custom_call_target="tpu_custom_call" | custom-call | flops 792723456 | bytes 8000000 | tf_op jit(solution)/shard_map/units_first/pallas_call | solution.py:315
  147.5 2.6 %copy-done.2 = bf16[7168,288]{1,0:T(8,128)(2,1)S(1)} copy-done((bf16[7168,288]{1,0:T(8,128)(2,1)S(1)}, bf16[7168,288]{1,0:T(8,128)(2,1)}, u32[]{:S(2)}) %copy-start.2) | copy-done | bytes 4128792
  150.0 4.9 %units_last.1.mine_ref = bf16[192,288]{1,0:T(8,128)(2,1)S(1)} custom-call(s32[5]{0:T(128)S(1)} %stack.35.info_ref, bf16[8,4,22,8,128]{4,3,2,1,0:T(8,128)(2,1)} %collective-permute-done.18.refs_0_, bf16[7168,288]{1,0:T(8,128)(2,1)S(1)} %bitcast.16, bf16[7168,288]{1,0:T(8,128)(2,1)S(1)} %copy-done.2, f32[192,288]{1,0:T(8,128)S(1)} %get-tuple-element.21.refs_3_, ...), custom_call_target="tpu_custom_call" | custom-call | flops 792723456 | bytes 8000000 | tf_op jit(solution)/shard_map/units_last/pallas_call | solution.py:315
  155.1 1.3 collective-permute-done.19.theirs_ref
  156.4 6.7 %down.1 = bf16[32,7,24,128]{3,2,1,0:T(8,128)(2,1)S(1)} custom-call(s32[5]{0:T(128)S(1)} %stack.35.info_ref, bf16[192,288]{1,0:T(8,128)(2,1)S(1)} %units_last.1.mine_ref, bf16[192,288]{1,0:T(8,128)(2,1)S(1)} %collective-permute-done.19.theirs_ref, bf16[256,192]{1,0:T(8,128)(2,1)S(1)} %copy-done.10, bf16[288,7168]{1,0:T(8,128)(2,1)S(1)} %copy-done.4, ...), custom_call_target="tpu_custom_call" | custom-call | flops 1056964608 | bytes 6000000 | tf_op jit(solution)/shard_map/down/pallas_call | solution.py:375
  163.1 24.3 %all_to_all.20.parts_ref = bf16[32,7,24,128]{3,2,1,0:T(8,128)(2,1)S(1)} all-to-all(bf16[32,7,24,128]{3,2,1,0:T(8,128)(2,1)S(1)} %down.1), channel_id=1, replica_groups=mesh['zh'=2,'zl'=2,'x'=4,'y'=4,'core'=2] {'zl','x','y'}, dimensions={0} | all-to-all | bytes 2752512 | tf_op jit(solution)/shard_map/all_to_all | solution.py:518
  187.4 0.8 finish.1
  188.2 2.0 %collective-permute-start.21 = (bf16[3,3584]{1,0:T(4,128)(2,1)S(1)}, bf16[3,3584]{1,0:T(4,128)(2,1)S(1)}, u32[]{:S(2)}, u32[]{:S(2)}) collective-permute-start(bf16[3,3584]{1,0:T(4,128)(2,1)S(1)} %get-tuple-element.26), channel_id=1, source_target_pairs={{0,1},{1,0},{2,3},{3,2},{4,5},{5,4},{6,7},{7,6},{8,9},{9,8},{10,11... | collective-permute-start | bytes 64520 | tf_op jit(solution)/shard_map/ppermute | solution.py:27
  190.2 0.9 collective-permute-done.21
  191.1 0.7 pad_maximum_fusion.4
  (63 shorter events, 0.8 us)
Async XLA Ops:
  0.0 8.1 %copy-start.12 = (bf16[6,128,576]{1,2,0:T(8,128)(2,1)S(1)}, bf16[6,128,576]{1,2,0:T(8,128)(2,1)}, u32[]{:S(2)}) copy-start(bf16[6,128,576]{1,2,0:T(8,128)(2,1)} %param.12) | copy-start | bytes 2654212
  2.5 20.2 %collective-permute-start = (bf16[128,1792]{1,0:T(8,128)(2,1)S(1)}, bf16[128,1792]{1,0:T(8,128)(2,1)S(1)}, u32[]{:S(2)}, u32[]{:S(2)}) collective-permute-start(bf16[128,1792]{1,0:T(8,128)(2,1)S(1)} %pad_maximum_fusion), channel_id=1, source_target_pairs={{0,2},{2,4},{4,6},{6,0},{1,3},{3,5},{5,7},{7,1},{8,10},{10,12},{12... | collective-permute-start | bytes 1376264 | tf_op jit(solution)/shard_map/ppermute | solution.py:31
  5.5 17.2 %collective-permute-start.1 = (bf16[128,1792]{1,0:T(8,128)(2,1)}, bf16[128,1792]{1,0:T(8,128)(2,1)S(1)}, u32[]{:S(2)}, u32[]{:S(2)}) collective-permute-start(bf16[128,1792]{1,0:T(8,128)(2,1)} %pad_maximum_fusion.1), channel_id=1, source_target_pairs={{0,6},{2,0},{4,2},{6,4},{1,7},{3,1},{5,3},{7,5},{8,14},{10,8},{12,... | collective-permute-start | bytes 1376264 | tf_op jit(solution)/shard_map/ppermute | solution.py:31
  7.0 54.7 %collective-permute-start.10 = (bf16[128,896]{1,0:T(8,128)(2,1)}, bf16[128,896]{1,0:T(8,128)(2,1)}, u32[]{:S(2)}, u32[]{:S(2)}) collective-permute-start(bf16[128,896]{1,0:T(8,128)(2,1)} %get-tuple-element.27), channel_id=1, source_target_pairs={{0,1},{1,0},{2,3},{3,2},{4,5},{5,4},{6,7},{7,6},{8,9},{9,8},{10,11... | collective-permute-start | bytes 688136 | tf_op jit(solution)/shard_map/ppermute | solution.py:27
  8.7 6.0 %copy-start.14 = (s32[6]{0:T(128)S(1)}, s32[6]{0:T(128)}, u32[]{:S(2)}) copy-start(s32[6]{0:T(128)} %param.14) | copy-start | bytes 76
  14.8 2.1 %copy-start.3 = (bf16[6,512,576]{2,1,0:T(8,128)(2,1)S(1)}, bf16[6,512,576]{2,1,0:T(8,128)(2,1)}, u32[]{:S(2)}) copy-start(bf16[6,512,576]{2,1,0:T(8,128)(2,1)} %copy.20.cache_ref) | copy-start | bytes 10616836
  22.7 14.7 %copy-start.13 = (bf16[3,7168]{1,0:T(4,128)(2,1)S(1)}, bf16[3,7168]{1,0:T(4,128)(2,1)}, u32[]{:S(2)}) copy-start(bf16[3,7168]{1,0:T(4,128)(2,1)} %param.15) | copy-start | bytes 129028
  22.7 37.0 %copy-start.11 = (bf16[1,512,128]{2,1,0:T(8,128)(2,1)S(1)}, bf16[1,512,128]{2,1,0:T(8,128)(2,1)}, u32[]{:S(2)}) copy-start(bf16[1,512,128]{2,1,0:T(8,128)(2,1)} %up_ref.1) | copy-start | bytes 393220
  22.7 0.8 copy-start.7
  23.5 36.2 %all-to-all-start = ((bf16[128,8,512]{2,1,0:T(8,128)(2,1)}), bf16[128,8,512]{2,1,0:T(8,128)(2,1)S(1)}, u32[]{:S(2)}, u32[]{:S(2)}) async-start(bf16[128,8,512]{2,1,0:T(8,128)(2,1)} %attend.1), calls=%async_computation | async-start | bytes 2097152 | tf_op jit(solution)/shard_map/all_to_all | solution.py:488
  32.5 39.3 %copy-start.5 = (bf16[128,7168]{1,0:T(8,128)(2,1)S(1)}, bf16[128,7168]{1,0:T(8,128)(2,1)}, u32[]{:S(2)}) copy-start(bf16[128,7168]{1,0:T(8,128)(2,1)} %refs_8_.1) | copy-start | bytes 5505028
  34.5 22.7 %collective-permute-start.9 = (bf16[128,1792]{1,0:T(8,128)(2,1)}, bf16[128,1792]{1,0:T(8,128)(2,1)}, u32[]{:S(2)}, u32[]{:S(2)}) collective-permute-start(bf16[128,1792]{1,0:T(8,128)(2,1)} %pad_maximum_fusion.2), channel_id=1, source_target_pairs={{0,4},{2,6},{4,0},{6,2},{1,5},{3,7},{5,1},{7,3},{8,12},{10,14},{12... | collective-permute-start | bytes 1376264 | tf_op jit(solution)/shard_map/ppermute | solution.py:31
  38.8 24.4 %collective-permute-start.11 = (bf16[128,896]{1,0:T(8,128)(2,1)}, bf16[128,896]{1,0:T(8,128)(2,1)}, u32[]{:S(2)}, u32[]{:S(2)}) collective-permute-start(bf16[128,896]{1,0:T(8,128)(2,1)} %constant_dynamic-slice_fusion.4), channel_id=1, source_target_pairs={{0,1},{1,0},{2,3},{3,2},{4,5},{5,4},{6,7},{7,6},{8,9},{9,8},{10,11... | collective-permute-start | bytes 688136 | tf_op jit(solution)/shard_map/ppermute | solution.py:27
  41.1 23.3 %collective-permute-start.13 = (bf16[128,896]{1,0:T(8,128)(2,1)}, bf16[128,896]{1,0:T(8,128)(2,1)}, u32[]{:S(2)}, u32[]{:S(2)}) collective-permute-start(bf16[128,896]{1,0:T(8,128)(2,1)} %constant_dynamic-slice_fusion.2), channel_id=1, source_target_pairs={{0,1},{1,0},{2,3},{3,2},{4,5},{5,4},{6,7},{7,6},{8,9},{9,8},{10,11... | collective-permute-start | bytes 688136 | tf_op jit(solution)/shard_map/ppermute | solution.py:27
  58.9 11.9 %collective-permute-start.12 = (bf16[128,896]{1,0:T(8,128)(2,1)}, bf16[128,896]{1,0:T(8,128)(2,1)}, u32[]{:S(2)}, u32[]{:S(2)}) collective-permute-start(bf16[128,896]{1,0:T(8,128)(2,1)} %constant_dynamic-slice_fusion.3), channel_id=1, source_target_pairs={{0,1},{1,0},{2,3},{3,2},{4,5},{5,4},{6,7},{7,6},{8,9},{9,8},{10,11... | collective-permute-start | bytes 688136 | tf_op jit(solution)/shard_map/ppermute | solution.py:27
  59.8 1.0 copy-start.9
  61.6 7.8 %collective-permute-start.2 = (bf16[384,128]{1,0:T(8,128)(2,1)S(1)}, bf16[384,128]{1,0:T(8,128)(2,1)S(1)}, u32[]{:S(2)}, u32[]{:S(2)}) collective-permute-start(bf16[384,128]{1,0:T(8,128)(2,1)S(1)} %join.1.refs_0_), channel_id=1, source_target_pairs={{0,2},{2,4},{4,6},{6,0},{1,3},{3,5},{5,7},{7,1},{8,10},{10,12},{12... | collective-permute-start | bytes 294920 | tf_op jit(solution)/shard_map/ppermute | solution.py:31
  61.7 8.5 %collective-permute-start.3 = (bf16[384,128]{1,0:T(8,128)(2,1)S(1)}, bf16[384,128]{1,0:T(8,128)(2,1)S(1)}, u32[]{:S(2)}, u32[]{:S(2)}) collective-permute-start(bf16[384,128]{1,0:T(8,128)(2,1)S(1)} %join.1.refs_0_), channel_id=1, source_target_pairs={{0,4},{2,6},{4,0},{6,2},{1,5},{3,7},{5,1},{7,3},{8,12},{10,14},{12... | collective-permute-start | bytes 294920 | tf_op jit(solution)/shard_map/ppermute | solution.py:31
  63.2 7.0 %collective-permute-start.4 = (bf16[384,128]{1,0:T(8,128)(2,1)S(1)}, bf16[384,128]{1,0:T(8,128)(2,1)S(1)}, u32[]{:S(2)}, u32[]{:S(2)}) collective-permute-start(bf16[384,128]{1,0:T(8,128)(2,1)S(1)} %join.1.refs_0_), channel_id=1, source_target_pairs={{0,6},{2,0},{4,2},{6,4},{1,7},{3,1},{5,3},{7,5},{8,14},{10,8},{12,... | collective-permute-start | bytes 294920 | tf_op jit(solution)/shard_map/ppermute | solution.py:31
  64.5 6.5 %collective-permute-start.5 = (bf16[384,128]{1,0:T(8,128)(2,1)S(1)}, bf16[384,128]{1,0:T(8,128)(2,1)S(1)}, u32[]{:S(2)}, u32[]{:S(2)}) collective-permute-start(bf16[384,128]{1,0:T(8,128)(2,1)S(1)} %join.1.refs_0_), channel_id=1, source_target_pairs={{0,1},{1,0},{2,3},{3,2},{4,5},{5,4},{6,7},{7,6},{8,9},{9,8},{10,11... | collective-permute-start | bytes 294920 | tf_op jit(solution)/shard_map/ppermute | solution.py:27
  69.4 1.7 collective-permute-start.6
  70.2 1.3 collective-permute-start.7
  70.2 1.6 collective-permute-start.8
  70.8 12.2 %collective-permute-start.14 = (bf16[3,3584]{1,0:T(4,128)(2,1)}, bf16[3,3584]{1,0:T(4,128)(2,1)S(1)}, u32[]{:S(2)}, u32[]{:S(2)}) collective-permute-start(bf16[3,3584]{1,0:T(4,128)(2,1)} %constant_dynamic-slice_fusion.1), channel_id=1, source_target_pairs={{0,1},{1,0},{2,3},{3,2},{4,5},{5,4},{6,7},{7,6},{8,9},{9,8},{10,11... | collective-permute-start | bytes 64520 | tf_op jit(solution)/shard_map/ppermute | solution.py:27
  71.8 1.0 copy-start.8
  76.6 19.0 %all-to-all-start.1 = ((bf16[16,24,896]{2,1,0:T(8,128)(2,1)}), bf16[16,24,896]{2,1,0:T(8,128)(2,1)S(1)}, u32[]{:S(2)}, u32[]{:S(2)}) async-start(bf16[16,24,896]{2,1,0:T(8,128)(2,1)} %project.1), calls=%async_computation.1 | async-start | bytes 1376256 | tf_op jit(solution)/shard_map/all_to_all | solution.py:503
  83.2 3.9 %collective-permute-start.17 = (bf16[6,896]{1,0:T(8,128)(2,1)S(1)}, bf16[6,896]{1,0:T(8,128)(2,1)S(1)}, u32[]{:S(2)}, u32[]{:S(2)}) collective-permute-start(bf16[6,896]{1,0:T(8,128)(2,1)S(1)} %get-tuple-element.41), channel_id=1, source_target_pairs={{0,6},{2,0},{4,2},{6,4},{1,7},{3,1},{5,3},{7,5},{8,14},{10,8},{12,... | collective-permute-start | bytes 32264 | tf_op jit(solution)/shard_map/ppermute | solution.py:31
  85.5 4.1 %collective-permute-start.16 = (bf16[6,896]{1,0:T(8,128)(2,1)S(1)}, bf16[6,896]{1,0:T(8,128)(2,1)S(1)}, u32[]{:S(2)}, u32[]{:S(2)}) collective-permute-start(bf16[6,896]{1,0:T(8,128)(2,1)S(1)} %get-tuple-element.40), channel_id=1, source_target_pairs={{0,4},{2,6},{4,0},{6,2},{1,5},{3,7},{5,1},{7,3},{8,12},{10,14},{12... | collective-permute-start | bytes 32264 | tf_op jit(solution)/shard_map/ppermute | solution.py:31
  85.5 4.1 %collective-permute-start.15 = (bf16[6,896]{1,0:T(8,128)(2,1)S(1)}, bf16[6,896]{1,0:T(8,128)(2,1)S(1)}, u32[]{:S(2)}, u32[]{:S(2)}) collective-permute-start(bf16[6,896]{1,0:T(8,128)(2,1)S(1)} %get-tuple-element.39), channel_id=1, source_target_pairs={{0,2},{2,4},{4,6},{6,0},{1,3},{3,5},{5,7},{7,1},{8,10},{10,12},{12... | collective-permute-start | bytes 32264 | tf_op jit(solution)/shard_map/ppermute | solution.py:31
  95.8 1.1 copy-start.6
  97.0 24.9 %all-to-all-start.2 = ((bf16[32,22,8,128]{3,2,1,0:T(8,128)(2,1)}), bf16[32,22,8,128]{3,2,1,0:T(8,128)(2,1)S(1)}, u32[]{:S(2)}, u32[]{:S(2)}) async-start(bf16[32,22,8,128]{3,2,1,0:T(8,128)(2,1)} %copy-done.6), calls=%async_computation.2 | async-start | bytes 2883584 | tf_op jit(solution)/shard_map/all_to_all | solution.py:511
  105.4 49.7 %collective-permute-start.20 = (bf16[288,3584]{1,0:T(8,128)(2,1)}, bf16[288,3584]{1,0:T(8,128)(2,1)}, u32[]{:S(2)}, u32[]{:S(2)}) collective-permute-start(bf16[288,3584]{1,0:T(8,128)(2,1)} %constant_dynamic-slice_fusion), channel_id=1, source_target_pairs={{0,1},{1,0},{2,3},{3,2},{4,5},{5,4},{6,7},{7,6},{8,9},{9,8},{10,11... | collective-permute-start | bytes 6193160 | tf_op jit(solution)/shard_map/ppermute | solution.py:27
  121.9 25.5 %collective-permute-start.18 = (bf16[8,4,22,8,128]{4,3,2,1,0:T(8,128)(2,1)S(1)}, bf16[8,4,22,8,128]{4,3,2,1,0:T(8,128)(2,1)}, u32[]{:S(2)}, u32[]{:S(2)}) collective-permute-start(bf16[8,4,22,8,128]{4,3,2,1,0:T(8,128)(2,1)S(1)} %bitcast.17), channel_id=1, source_target_pairs={{0,1},{1,0},{2,3},{3,2},{4,5},{5,4},{6,7},{7,6},{8,9},{9,8},{10,11... | collective-permute-start | bytes 4325384 | tf_op jit(solution)/shard_map/ppermute | solution.py:27
  131.7 15.8 %slice-start = ((s8[5505024]{0:T(1024)(128)(4,1)}), s8[1310720]{0:T(1024)(128)(4,1)S(1)}, s32[]{:S(2)}) async-start(s8[5505024]{0:T(1024)(128)(4,1)} %bitcast.15), calls=%async_computation.4 | async-start | bytes 2621440
  139.1 2.6 %copy-start = (bf16[7168,288]{1,0:T(8,128)(2,1)S(1)}, bf16[7168,288]{1,0:T(8,128)(2,1)}, u32[]{:S(2)}) copy-start(bf16[7168,288]{1,0:T(8,128)(2,1)} %copy.23.refs_1_) | copy-start | bytes 12386308
  141.7 2.6 %copy-start.1 = (bf16[7168,288]{1,0:T(8,128)(2,1)S(1)}, bf16[7168,288]{1,0:T(8,128)(2,1)}, u32[]{:S(2)}) copy-start(bf16[7168,288]{1,0:T(8,128)(2,1)} %copy.24.refs_2_) | copy-start | bytes 12386308
  144.2 3.2 %slice-start.1 = ((s8[5505024]{0:T(1024)(128)(4,1)}), s8[4194304]{0:T(1024)(128)(4,1)S(1)}, s32[]{:S(2)}) async-start(s8[5505024]{0:T(1024)(128)(4,1)} %bitcast.15), calls=%async_computation.5 | async-start | bytes 8388608
  147.5 2.6 %copy-start.2 = (bf16[7168,288]{1,0:T(8,128)(2,1)S(1)}, bf16[7168,288]{1,0:T(8,128)(2,1)}, u32[]{:S(2)}) copy-start(bf16[7168,288]{1,0:T(8,128)(2,1)} %copy.24.refs_2_) | copy-start | bytes 12386308
  150.0 6.4 %copy-start.4 = (bf16[288,7168]{1,0:T(8,128)(2,1)S(1)}, bf16[288,7168]{1,0:T(8,128)(2,1)}, u32[]{:S(2)}) copy-start(bf16[288,7168]{1,0:T(8,128)(2,1)} %own_ref.1) | copy-start | bytes 12386308
  150.0 6.4 %copy-start.10 = (bf16[256,192]{1,0:T(8,128)(2,1)S(1)}, bf16[256,192]{1,0:T(8,128)(2,1)}, u32[]{:S(2)}) copy-start(bf16[256,192]{1,0:T(8,128)(2,1)} %constant.97.clone.spread_ref) | copy-start | bytes 294916
  155.0 1.5 collective-permute-start.19
  188.2 2.9 %collective-permute-start.21 = (bf16[3,3584]{1,0:T(4,128)(2,1)S(1)}, bf16[3,3584]{1,0:T(4,128)(2,1)S(1)}, u32[]{:S(2)}, u32[]{:S(2)}) collective-permute-start(bf16[3,3584]{1,0:T(4,128)(2,1)S(1)} %get-tuple-element.26), channel_id=1, source_target_pairs={{0,1},{1,0},{2,3},{3,2},{4,5},{5,4},{6,7},{7,6},{8,9},{9,8},{10,11... | collective-permute-start | bytes 64520 | tf_op jit(solution)/shard_map/ppermute | solution.py:27

commit v4 on v3

v4 whole, which is shorter than its diff:
```python
import functools
import math

import jax
import jax.numpy as jnp
import numpy as np
from jax import lax
from jax.experimental import pallas as pl
from jax.experimental.pallas import tpu as pltpu
from jax.sharding import Mesh, PartitionSpec as P

LAT = 512
QKD = 192
LANES = 128
SUB = 8
AXES = ("zh", "zl", "x", "y", "core")
DEV = ("zl", "x", "y", "core")
OUTER = ("zh", "zl", "x")
SIDE_CHIPS = ("zl", "x", "y")
SWAP = [(0, 1), (1, 0)]
F32 = jnp.float32
BF16 = jnp.bfloat16
VMEM_MOST = 60 * 1024 * 1024
VMEM_SOME = 24 * 1024 * 1024


def swap(array):
    return lax.ppermute(array, "core", SWAP)


def shift(array, step):
    return lax.ppermute(array, "y", [(i, (i + step) % 4) for i in range(4)])


def block(array, index, size, axis):
    return lax.dynamic_slice_in_dim(array, index * size, size, axis)


def swap_halves(array, core, axis):
    half = array.shape[axis] // 2
    return block(array, core, half, axis), swap(block(array, 1 - core, half, axis))


def params(limit, *semantics):
    return pltpu.CompilerParams(
        vmem_limit_bytes=limit, dimension_semantics=semantics or None
    )


def cost(flops, read):
    return pl.CostEstimate(flops=flops, bytes_accessed=read, transcendentals=0)


WHOLE = pl.BlockSpec(memory_space=pltpu.VMEM)


def rounded(value):
    return value.astype(BF16).astype(F32)


def attend_kernel(rows, info_ref, query_ref, cache_ref, out_ref, stats):
    count, _, heads = query_ref.shape
    keys = cache_ref.shape[2]
    tiles = [slice(start, start + LANES) for start in range(0, LAT, LANES)]
    position = lax.broadcasted_iota(jnp.int32, (1, keys), 1) + info_ref[rows]
    lane = lax.broadcasted_iota(jnp.int32, (heads, LANES), 1)
    table = stats[...]
    for index in range(count):
        row = pl.program_id(0) * count + index
        cached = cache_ref[index]
        scores = lax.dot_general(
            query_ref[index], cached, (((0,), (0,)), ((), ())), preferred_element_type=F32
        ) * (1.0 / math.sqrt(QKD))
        usable = position < info_ref[row]
        scores = jnp.where(usable, scores, F32(-1e30))
        top = jnp.max(scores, axis=1, keepdims=True)
        top_high = rounded(top)
        top_low = rounded(top - top_high)
        exponent = jnp.where(usable, jnp.exp(scores - (top_high + top_low)), F32(0.0))
        total = jnp.sum(exponent, axis=1, keepdims=True)
        total_high = rounded(total)
        total_low = rounded(total - total_high)
        weighted = lax.dot_general(
            exponent.astype(BF16),
            cached[:LAT],
            (((1,), (1,)), ((), ())),
            preferred_element_type=F32,
        )
        for number, tile in enumerate(tiles):
            out_ref[:, row * len(tiles) + number] = (
                weighted[:, tile].reshape(heads // SUB, SUB, LANES).astype(BF16)
            )
        table = jnp.where(lane == row, top_high, table)
        table = jnp.where(lane == row + SUB, top_low, table)
        table = jnp.where(lane == row + 2 * SUB, total_high, table)
        table = jnp.where(lane == row + 3 * SUB, total_low, table)
    stats[...] = table

    @pl.when(pl.program_id(0) == pl.num_programs(0) - 1)
    def _():
        out_ref[:, rows * len(tiles)] = (
            stats[...].reshape(heads // SUB, SUB, LANES).astype(BF16)
        )


def attend(info, query, cache):
    rows, depth, heads = query.shape
    keys = cache.shape[2]
    count = 2
    shape = (heads // SUB, rows * (LAT // LANES) + 1, SUB, LANES)
    return pl.pallas_call(
        functools.partial(attend_kernel, rows),
        out_shape=jax.ShapeDtypeStruct(shape, BF16),
        grid_spec=pltpu.PrefetchScalarGridSpec(
            num_scalar_prefetch=1,
            grid=(rows // count,),
            in_specs=[
                pl.BlockSpec((count, depth, heads), lambda r, info: (r, 0, 0)),
                pl.BlockSpec((count, depth, keys), lambda r, info: (r, 0, 0)),
            ],
            out_specs=pl.BlockSpec(shape, lambda r, info: (0, 0, 0, 0)),
            scratch_shapes=[pltpu.VMEM((heads, LANES), F32)],
        ),
        compiler_params=params(VMEM_MOST, "arbitrary"),
        cost_estimate=cost(2 * rows * heads * keys * (depth + LAT), 5_000_000),
        name="attend",
    )(info, query, cache)


def cut_kernel(info_ref, up_ref, *refs):
    del info_ref
    blocks, outs = refs[:7], refs[7:]
    lanes = [slice(start, start + LANES) for start in range(0, blocks[0].shape[1], LANES)]
    ups = up_ref.shape[1] // LANES
    for step in range(4):
        outs[step][:ups] = up_ref[0].reshape(ups, LANES, LANES)
        for index, lane in enumerate(lanes):
            outs[step][ups + index] = blocks[step][:, lane]
    for step in range(3):
        for index, lane in enumerate(lanes):
            outs[4 + step][index] = blocks[4 + step][:, lane]


def cut(info, value_up, out_proj):
    rows, width = out_proj.shape
    eighth = width // 8
    columns = eighth // LANES
    ups = value_up.shape[1] // LANES
    first = (ups + columns, LANES, LANES)
    second = (columns, LANES, LANES)
    full = lambda shape: pl.BlockSpec(shape, lambda i, info: (0,) * len(shape))

    def column(side, step):
        return pl.BlockSpec(
            (rows, eighth),
            lambda i, info: (0, info[side] * 4 + lax.rem(info[5] + step, 4)),
        )

    return pl.pallas_call(
        cut_kernel,
        out_shape=[jax.ShapeDtypeStruct(first, BF16)] * 4
        + [jax.ShapeDtypeStruct(second, BF16)] * 3,
        grid_spec=pltpu.PrefetchScalarGridSpec(
            num_scalar_prefetch=1,
            grid=(1,),
            in_specs=[full(value_up.shape)]
            + [column(4, step) for step in range(4)]
            + [column(3, step) for step in range(1, 4)],
            out_specs=[full(first)] * 4 + [full(second)] * 3,
        ),
        compiler_params=params(VMEM_SOME, "arbitrary"),
        cost_estimate=cost(0, 4_000_000),
        name="cut",
    )(info, value_up, *([out_proj] * 7))


def join_kernel(rows, info_ref, recv_ref, own_ref, *refs):
    firsts, theirs, sum_ref, out_ref = refs[:3], refs[3:7], refs[7], refs[8]
    sides = 2
    devs = recv_ref.shape[0] // sides
    tiles = LAT // LANES
    table = recv_ref[:, rows * tiles].astype(F32).reshape(sides, devs, SUB, LANES)
    lane = lax.broadcasted_iota(jnp.int32, (SUB, LANES), 1)

    def pick(first):
        chosen = (lane == first) | (lane == first + SUB)
        return jnp.sum(jnp.where(chosen, table, F32(0.0)), axis=3, keepdims=True)

    latents = []
    for row in range(rows):
        peaks = pick(row)
        totals = pick(2 * SUB + row)
        factor = jnp.exp(peaks - jnp.maximum(peaks[:1], peaks[1:]))
        factor = factor / (factor[:1] * totals[:1] + factor[1:] * totals[1:])
        parts = [
            recv_ref[:, row * tiles + number].astype(F32).reshape(sides, devs, SUB, LANES)
            for number in range(tiles)
        ]
        joined = [part[0] * factor[0] + part[1] * factor[1] for part in parts]
        latents.append(
            jnp.concatenate([part.reshape(devs * SUB, LANES) for part in joined], axis=1)
        )
    latent = jnp.concatenate(latents, axis=0).astype(BF16)
    maps = [own_ref[0]]
    maps += [ref[:tiles].reshape(LAT, LANES) for ref in firsts]
    maps += [ref[:tiles].reshape(LAT, LANES) for ref in theirs]
    products = jnp.dot(
        latent, jnp.concatenate(maps, axis=1), preferred_element_type=F32
    ).reshape(rows * devs, SUB, len(maps) * LANES)
    sub = lax.broadcasted_iota(jnp.int32, (1, SUB, LANES), 1)
    masked = []
    for piece in range(len(maps)):
        chip = lax.rem(info_ref[5] + 4 - piece % 4, 4)
        head = chip * 2 + info_ref[3 + piece // 4]
        part = products[:, :, piece * LANES : piece * LANES + LANES]
        masked.append(jnp.where(sub == head, part, F32(0.0)))
    masked = jnp.concatenate(masked, axis=2).reshape(rows * devs * SUB, len(maps) * LANES)
    out_ref[...] = jnp.dot(
        sum_ref[...], masked.astype(BF16), preferred_element_type=F32
    ).astype(BF16)


def join(info, received, value_up, firsts, theirs, rows):
    devs = received.shape[0] // 2
    count = rows * devs
    sums = np.repeat(np.eye(count, dtype=np.float32), SUB, axis=1)
    return pl.pallas_call(
        functools.partial(join_kernel, rows),
        out_shape=jax.ShapeDtypeStruct((count, SUB * LANES), BF16),
        in_specs=[pl.BlockSpec(memory_space=pltpu.SMEM)] + [WHOLE] * 10,
        out_specs=WHOLE,
        compiler_params=params(VMEM_SOME),
        cost_estimate=cost(480_000_000, 3_000_000),
        name="join",
    )(info, received, value_up, *firsts, *theirs, jnp.asarray(sums, BF16))


def project_kernel(info_ref, place_ref, *refs):
    values, own_ref = refs[:8], refs[8]
    seconds, theirs, out_ref = refs[9:12], refs[12:16], refs[16]
    del info_ref
    rows = []
    for source, ref in enumerate(values):
        data = ref[...]
        lanes = []
        for piece in range(8):
            step = (piece - source) % 4
            side = piece // 4 ^ source // 4
            start = (side * 4 + step) * LANES
            lanes.append(data[:, start : start + LANES])
        rows.append(jnp.concatenate(lanes, axis=1))
    left = jnp.concatenate(rows, axis=0)
    count = left.shape[0]
    order = lax.broadcasted_iota(jnp.int32, (count, count), 0) == place_ref[...]
    order = jnp.where(order, F32(1.0), F32(0.0)).astype(BF16)
    left = jnp.dot(order, left, preferred_element_type=F32).astype(BF16)
    columns = own_ref.shape[1] // LANES
    right = [own_ref[...]]
    for ref in seconds + theirs:
        first = ref.shape[0] - columns
        right.append(
            jnp.concatenate([ref[first + column] for column in range(columns)], axis=1)
        )
    right = jnp.concatenate(right, axis=0)
    total = jnp.dot(left, right, preferred_element_type=F32)
    out_ref[...] = total.reshape(out_ref.shape).astype(BF16)


def project(info, place, values, out_proj, seconds, theirs, chips):
    rows = sum(value.shape[0] for value in values)
    lanes = out_proj.shape[0]
    eighth = out_proj.shape[1] // 8
    full = lambda shape: pl.BlockSpec(shape, lambda i, info: (0,) * len(shape))
    own = pl.BlockSpec((lanes, eighth), lambda i, info: (0, info[0]))
    return pl.pallas_call(
        project_kernel,
        out_shape=jax.ShapeDtypeStruct((chips, rows // chips, eighth), BF16),
        grid_spec=pltpu.PrefetchScalarGridSpec(
            num_scalar_prefetch=1,
            grid=(1,),
            in_specs=[full(place.shape)]
            + [full(value.shape) for value in values]
            + [own]
            + [full(part.shape) for part in seconds + theirs],
            out_specs=full((chips, rows // chips, eighth)),
        ),
        compiler_params=params(VMEM_SOME, "arbitrary"),
        cost_estimate=cost(2 * rows * 8 * lanes * eighth, 3_500_000),
        name="project",
    )(info, place, *values, out_proj, *seconds, *theirs)


def residual_kernel(parts_ref, stream_ref, gain_ref, residual_ref, out_ref):
    residual = stream_ref[...].astype(F32) + jnp.sum(parts_ref[...].astype(F32), axis=0)
    residual_ref[...] = residual
    rows, width = residual.shape
    squares = jnp.sum(residual * residual, axis=1, keepdims=True)
    high = rounded(squares)
    low = rounded(squares - high)
    lane = lax.broadcasted_iota(jnp.int32, (SUB, LANES), 1)
    table = jnp.zeros((SUB, LANES), F32)
    scaled = residual * gain_ref[...]
    groups = rows // SUB
    columns = width // LANES
    chips = out_ref.shape[0]
    for group in range(groups):
        span = slice(group * SUB, group * SUB + SUB)
        table = jnp.where(lane == group, high[span], table)
        table = jnp.where(lane == SUB + group, low[span], table)
    tiles = [
        scaled[group * SUB : group * SUB + SUB, column * LANES : column * LANES + LANES]
        for column in range(columns)
        for group in range(groups)
    ] + [table]
    for index, tile in enumerate(tiles):
        out_ref[:, index] = jnp.broadcast_to(tile.astype(BF16)[None], (chips, SUB, LANES))


def residual_rows(parts, stream, gain, chips):
    _, rows, width = parts.shape
    tiles = rows * width // (SUB * LANES) + 1
    return pl.pallas_call(
        residual_kernel,
        out_shape=(
            jax.ShapeDtypeStruct((rows, width), F32),
            jax.ShapeDtypeStruct((chips, tiles, SUB, LANES), BF16),
        ),
        in_specs=[WHOLE] * 3,
        out_specs=(WHOLE, WHOLE),
        compiler_params=params(VMEM_SOME),
        cost_estimate=cost(2_000_000, 2_500_000),
        name="residual",
    )(parts, stream, gain)


def units_kernel(groups, width, last, info_ref, *refs):
    if last:
        recv_ref, gate_ref, up_ref, acc_in, sq_in, out_ref, acc, sq_acc = refs
    else:
        recv_ref, gate_ref, up_ref, acc, sq_acc = refs
    step = pl.program_id(0)
    sides, _, tiles, _, _ = recv_ref.shape
    columns = (tiles - 1) // groups
    rows = sides * groups * SUB
    left = jnp.concatenate(
        [
            recv_ref[:, 0, column * groups : column * groups + groups]
            .astype(F32)
            .reshape(rows, LANES)
            for column in range(columns)
        ],
        axis=1,
    ).astype(BF16)
    both = jnp.concatenate([gate_ref[...], up_ref[...]], axis=0)
    total = lax.dot_general(
        left, both, (((1,), (1,)), ((), ())), preferred_element_type=F32
    )
    table = recv_ref[:, 0, tiles - 1].astype(F32)
    lane = lax.broadcasted_iota(jnp.int32, (SUB, LANES), 1)
    pieces = [
        jnp.sum(
            jnp.where((lane == group) | (lane == SUB + group), table, F32(0.0)),
            axis=2,
            keepdims=True,
        )
        for group in range(groups)
    ]
    squares = jnp.stack(pieces, axis=1).reshape(rows, 1)
    squares = jnp.broadcast_to(squares, (rows, LANES))

    @pl.when(step == 0)
    def _():
        acc[...] = acc_in[...] + total if last else total
        sq_acc[...] = sq_in[...] + squares if last else squares

    @pl.when(step > 0)
    def _():
        acc[...] += total
        sq_acc[...] += squares

    if last:

        @pl.when(step == pl.num_programs(0) - 1)
        def _():
            hidden = out_ref.shape[1]
            scale = lax.rsqrt(sq_acc[:, :1] / width + 1e-06)
            gate = acc[:, :hidden] * scale
            upper = acc[:, hidden:] * scale
            out_ref[...] = (gate / (1.0 + jnp.exp(-gate)) * upper).astype(BF16)


def units(info, which, received, gate_proj, up_proj, groups, carry=None):
    sides, quarters, tiles = received.shape[:3]
    depth = (tiles - 1) // groups * LANES
    hidden, width = gate_proj.shape
    rows = sides * groups * SUB
    whole = lambda shape: pl.BlockSpec(shape, lambda i, info: (0,) * len(shape))
    weight = pl.BlockSpec((hidden, depth), lambda i, info: (0, info[which] * quarters + i))
    shapes = [(rows, 2 * hidden), (rows, LANES)]
    last = carry is not None
    return pl.pallas_call(
        functools.partial(units_kernel, groups, width, last),
        out_shape=jax.ShapeDtypeStruct((rows, hidden), BF16)
        if last
        else [jax.ShapeDtypeStruct(shape, F32) for shape in shapes],
        grid_spec=pltpu.PrefetchScalarGridSpec(
            num_scalar_prefetch=1,
            grid=(quarters,),
            in_specs=[
                pl.BlockSpec(
                    (sides, 1, tiles, SUB, LANES), lambda i, info: (0, i, 0, 0, 0)
                ),
                weight,
                weight,
            ]
            + ([whole(shape) for shape in shapes] if last else []),
            out_specs=whole((rows, hidden)) if last else [whole(shape) for shape in shapes],
            scratch_shapes=[pltpu.VMEM(shape, F32) for shape in shapes] if last else [],
        ),
        compiler_params=params(VMEM_MOST, "arbitrary"),
        cost_estimate=cost(4 * rows * depth * quarters * hidden, 5_000_000),
        name="units_last" if last else "units_first",
    )(info, received, gate_proj, up_proj, *(carry or ()))


def down_kernel(info_ref, mine_ref, theirs_ref, own_ref, other_ref, held_ref, out_ref, left, total):
    chips = out_ref.shape[0]
    rows = mine_ref.shape[0]
    count = rows // chips
    hidden = mine_ref.shape[1]

    @pl.when(pl.program_id(0) == 0)
    def _():
        left[...] = jnp.concatenate(
            [mine_ref[...].astype(F32), theirs_ref[...].astype(F32)], axis=1
        ).astype(BF16)
        total[pl.ds(rows, SUB), :] = jnp.zeros((SUB, total.shape[1]), F32)

    weight = jnp.concatenate([own_ref[...], other_ref[...]], axis=0)
    total[pl.ds(0, rows), :] = jnp.dot(left[...], weight, preferred_element_type=F32)
    span = held_ref.shape[0]
    place = pl.ds(pl.multiple_of(info_ref[2] * span, SUB), span)
    total[place, :] += held_ref[...]
    sub = lax.broadcasted_iota(jnp.int32, (SUB, LANES), 0)
    for chip in range(chips):
        part = total[chip * count : chip * count + SUB, :]
        quads = [part[:, tile * LANES : tile * LANES + LANES] for tile in range(4)]
        packed = [
            jnp.where(sub < count, quads[tile], pltpu.roll(quads[3], count - 2 * tile, 0))
            for tile in range(3)
        ]
        out_ref[chip, 0] = jnp.concatenate(packed, axis=0).astype(BF16)


def down(info, mine, theirs, down_proj, down_theirs, held, chips):
    rows, hidden = mine.shape
    half = down_theirs.shape[1]
    width = 4 * LANES
    steps = half // width
    whole = lambda shape: pl.BlockSpec(shape, lambda i, info: (0,) * len(shape))
    return pl.pallas_call(
        down_kernel,
        out_shape=jax.ShapeDtypeStruct((chips, steps, 3 * SUB, LANES), BF16),
        grid_spec=pltpu.PrefetchScalarGridSpec(
            num_scalar_prefetch=1,
            grid=(steps,),
            in_specs=[
                whole((rows, hidden)),
                whole((rows, hidden)),
                pl.BlockSpec((hidden, width), lambda i, info: (0, info[3] * steps + i)),
                pl.BlockSpec((hidden, width), lambda i, info: (0, i)),
                pl.BlockSpec((held.shape[0], width), lambda i, info: (0, i)),
            ],
            out_specs=pl.BlockSpec(
                (chips, 1, 3 * SUB, LANES), lambda i, info: (0, i, 0, 0)
            ),
            scratch_shapes=[
                pltpu.VMEM((rows, 2 * hidden), BF16),
                pltpu.VMEM((rows + SUB, width), F32),
            ],
        ),
        compiler_params=params(VMEM_SOME, "arbitrary"),
        cost_estimate=cost(4 * rows * hidden * half, 6_000_000),
        name="down",
    )(info, mine, theirs, down_proj, down_theirs, held)


def finish_kernel(info_ref, parts_ref, mine_ref, theirs_ref):
    total = jnp.sum(parts_ref[...].astype(F32), axis=0)
    sub = lax.broadcasted_iota(jnp.int32, (SUB, LANES), 0)
    columns = []
    for step in range(total.shape[0]):
        quads = [total[step, tile * SUB : tile * SUB + SUB] for tile in range(3)]
        last = jnp.where(
            sub < 2,
            pltpu.roll(quads[0], 2, 0),
            jnp.where(sub < 4, pltpu.roll(quads[1], 4, 0), pltpu.roll(quads[2], 6, 0)),
        )
        columns += quads + [last]
    rows = jnp.concatenate(columns, axis=1)
    first, second = rows[0:3], rows[3:6]
    is_first = info_ref[3] == 0
    mine_ref[...] = jnp.where(is_first, first, second).astype(BF16)
    theirs_ref[...] = jnp.where(is_first, second, first).astype(BF16)


def finish(info, parts):
    shape = jax.ShapeDtypeStruct((3, parts.shape[1] * 4 * LANES), BF16)
    return pl.pallas_call(
        finish_kernel,
        out_shape=(shape, shape),
        in_specs=[pl.BlockSpec(memory_space=pltpu.SMEM), WHOLE],
        out_specs=(WHOLE, WHOLE),
        compiler_params=params(VMEM_SOME),
        cost_estimate=cost(1_000_000, 1_500_000),
        name="finish",
    )(info, parts)


def local(
    query_latent,
    latent_cache,
    lengths,
    stream,
    norm_gain,
    value_up,
    out_proj,
    gate_proj,
    up_proj,
    down_proj,
):
    core = lax.axis_index("core")
    ring = lax.axis_index("y")
    group = lax.axis_index("zl") * 4 + lax.axis_index("x")
    rows_own, width = stream.shape
    rows = query_latent.shape[0]
    half = width // 2
    eighth = width // 8
    first = core == 0
    info = jnp.stack([core * 4 + ring, core, group, core, 1 - core, ring]).astype(jnp.int32)

    cuts = cut(info, value_up, out_proj)
    own = cuts[0]
    first_one, first_three = shift(cuts[1], 1), shift(cuts[3], 3)
    stream_mine, stream_theirs = swap_halves(stream, core, 1)
    stream_rows = jnp.concatenate(
        [
            jnp.where(first, stream_mine, stream_theirs),
            jnp.where(first, stream_theirs, stream_mine),
        ],
        axis=0,
    )
    stream_parts = [block(stream_rows, ring, eighth, 1)]
    for step in (1, 2, 3):
        stream_parts.append(shift(block(stream_rows, (ring + step) % 4, eighth, 1), step))
    back = (ring - jnp.arange(4)) % 4
    ring_stream = jnp.take(jnp.stack(stream_parts), back, axis=0)
    ring_stream = ring_stream.reshape(8 * rows_own, eighth)
    _, down_theirs = swap_halves(down_proj, core, 1)
    gain = block(norm_gain, core * 4 + ring, eighth, 0)[None]

    offset = lax.axis_index("zh") * latent_cache.shape[1]
    payload = attend(
        jnp.concatenate([lengths, offset[None].astype(jnp.int32)]),
        query_latent.transpose(0, 2, 1),
        latent_cache.transpose(0, 2, 1),
    )
    payload, first_one, first_three = lax.optimization_barrier(
        (payload, first_one, first_three)
    )
    first_two = shift(lax.optimization_barrier((cuts[2], first_one))[0], 2)
    seconds = [shift(cuts[3 + step], step) for step in (1, 2, 3)]
    firsts = [first_one, first_two, first_three]
    theirs = [swap(part) for part in [own] + firsts]
    received = lax.all_to_all(payload, OUTER, split_axis=0, concat_axis=0, tiled=True)
    values = join(info, received, value_up, firsts, theirs, rows)

    ring_values = [values] + [shift(values, step) for step in (1, 2, 3)]
    row = jnp.arange(8 * rows)
    natural = jnp.tile(row % 8 * (8 * rows) + row // 8, 8).reshape(8, 8 * rows)
    chip = (ring - jnp.arange(8)) % 4
    side = jnp.where(jnp.arange(8) < 4, core, 1 - core)
    place = natural[:, : 8 * rows] + ((chip * 2 + side) * rows)[:, None]
    place = place.reshape(1, 64 * rows).astype(jnp.int32)
    partial = project(
        info,
        place,
        ring_values + [swap(piece) for piece in ring_values],
        out_proj,
        seconds,
        theirs,
        16,
    )
    parts = lax.all_to_all(partial, OUTER, split_axis=0, concat_axis=0, tiled=True)

    residual, payload = residual_rows(parts, ring_stream, gain, 32)
    held = lax.dynamic_update_slice(
        jnp.zeros((8 * rows_own, half), F32), residual, (0, ring * eighth)
    )
    piece = lax.all_to_all(payload, SIDE_CHIPS, split_axis=0, concat_axis=0, tiled=True)
    piece = piece.reshape((8, 4) + piece.shape[1:])
    other = swap(piece)
    groups = 8 * rows_own // SUB
    gate_proj, up_proj = gate_proj.T, up_proj.T
    carry = units(info, 3, piece, gate_proj, up_proj, groups)
    hidden = units(info, 4, other, gate_proj, up_proj, groups, carry)
    partial = down(info, hidden, swap(hidden), down_proj, down_theirs, held, 32)
    parts = lax.all_to_all(partial, SIDE_CHIPS, split_axis=0, concat_axis=0, tiled=True)
    mine, theirs = finish(info, parts)
    theirs = swap(theirs)
    return jnp.concatenate(
        [jnp.where(first, mine, theirs), jnp.where(first, theirs, mine)], axis=1
    )


def solution(mesh):
    fine = Mesh(mesh.devices.reshape(2, 2, 4, 4, 2), AXES)
    placed = (
        P(DEV, None, None),
        P(DEV, "zh", None),
        P(DEV),
        P(AXES, None),
        P(),
        P(AXES, None, None),
        P(AXES, None),
        P(None, DEV),
        P(None, DEV),
        P(DEV, None),
    )
    return jax.shard_map(
        local, mesh=fine, in_specs=placed, out_specs=P(AXES, None), check_vma=False
    )
```

time: 193 us -> 166 us (0.86)
  local copies, waits for them, and re-layouts: 47.1 us -> 16.3 us
  waiting for transfers between devices: 46.6 us -> 32.1 us
  starting transfers between devices: 43.3 us -> 54.4 us
  Pallas kernels: 26.3 us -> 36.1 us
  other arithmetic: 3.88 us -> 1.6 us
    unnamed x38 -> x44, local copies, waits for them, and re-layouts: 35.2 us -> 9.99 us
    ppermute x9 -> x12, waiting for transfers between devices: 22.9 us -> 9.89 us  [shift(): return lax.ppermute(array, 'y', [(i, (i + step) % 4) for i in range(4)])]
    ppermute x13, starting transfers between devices: 10.2 us -> 18 us  [swap(): return lax.ppermute(array, 'core', SWAP)]
    pallas_call x3 -> x4, Pallas kernels: 13.9 us -> 21.3 us  [the longest x2 12.9 us: units(): pl.pallas_call(functools.partial(units_kernel, groups, width, last), out_...]
    dynamic_slice x7 -> x3, local copies, waits for them, and re-layouts: 11 us -> 4.46 us  [block(): return lax.dynamic_slice_in_dim(array, index * size, size, axis)]
    ppermute x9 -> x12, starting transfers between devices: 12.3 us -> 16.7 us  [shift(): return lax.ppermute(array, 'y', [(i, (i + step) % 4) for i in range(4)])]
    concatenate x3 -> x0, other arithmetic: 2.85 us -> none  [ring_part(): jnp.concatenate([lax.dynamic_slice_in_dim(out_proj, start + chip * eighth...]
  transfers between devices with their start and end apart: 25 -> 28, of which waited for: 10 -> 10; matrix products, arithmetic and copies ran while one was open for 18% -> 4% of each run, Pallas kernels for 10% -> 16%
where the time goes in v4:
time: 166 us; the launch traced here: 165 us
  starting transfers between devices  54.4 us (33%)
  Pallas kernels  36.1 us (22%)
  waiting for transfers between devices  32.1 us (19%)
  blocking collectives  24.2 us (15%)
  local copies, waits for them, and re-layouts  16.3 us (10%)
    all_to_all x1, blocking collectives, local(): lax.all_to_all(partial, SIDE_CHIPS, split_axis=0, concat_axis=0, tiled=True)  24.2 us
    ppermute x13, starting transfers between devices, swap(): return lax.ppermute(array, 'core', SWAP)  18 us
    ppermute x12, starting transfers between devices, shift(): return lax.ppermute(array, 'y', [(i, (i + step) % 4) for i in range(4)])  16.7 us
    all_to_all x1, waiting for transfers between devices, local(): lax.all_to_all(payload, SIDE_CHIPS, split_axis=0, concat_axis=0, tiled=True)  15.5 us
    pallas_call x2, Pallas kernels, units(): pl.pallas_call(functools.partial(units_kernel, groups, width, last), out_...  12.9 us
    unnamed x44, local copies, waits for them, and re-layouts  9.99 us
    ppermute x12, waiting for transfers between devices, shift(): return lax.ppermute(array, 'y', [(i, (i + step) % 4) for i in range(4)])  9.89 us
    all_to_all x1, starting transfers between devices, local(): lax.all_to_all(payload, OUTER, split_axis=0, concat_axis=0, tiled=True)  7.6 us
  transfers between devices with their start and end apart: 28, of which 10 were waited for; matrix products, arithmetic and copies ran while one was open for 4% of the time, Pallas kernels for 16%

profile of v4, /device:TPU:1, one launch (start us, length us, event | category | flops | bytes accessed | tf_op | source)
XLA Modules:
  0.0 164.9 jit_solution(4255796264780876920)
XLA Ops:
  0.1 1.5 copy-done
  1.6 0.9 copy-done.4
  2.5 1.8 %cut.1 = (bf16[11,128,128]{2,1,0:T(8,128)(2,1)}, bf16[11,128,128]{2,1,0:T(8,128)(2,1)S(1)}, bf16[11,128,128]{2,1,0:T(8,128)(2,1)}, bf16[11,128,128]{2,1,0:T(8,12...) custom-call(s32[6]{0:T(128)S(1)} %stack.39.info_ref, ...), custom_call_target="tpu_custom_call" | custom-call | bytes 4000000 | tf_op jit(solution)/shard_map/cut/pallas_call | solution.py:159
  4.3 0.7 copy-done.15
  5.0 0.7 copy-done.16
  5.7 2.1 %collective-permute-start = (bf16[11,128,128]{2,1,0:T(8,128)(2,1)S(1)}, bf16[11,128,128]{2,1,0:T(8,128)(2,1)S(1)}, u32[]{:S(2)}, u32[]{:S(2)}) collective-permute-start(bf16[11,128,128]{2,1,0:T(8,128)(2,1)S(1)} %get-tuple-element.22), channel_id=1, source_target_pairs={{0,2},{2,4},{4,6},{6,0},{1,3},{3,5},{5,7},{7,1},{8,10},{10,12},{12... | collective-permute-start | bytes 1081352 | tf_op jit(solution)/shard_map/ppermute | solution.py:32
  7.8 1.4 collective-permute-start.1
  9.2 1.1 collective-permute-start.3
  10.3 0.2 collective-permute-start.14
  10.5 0.6 pad_add_fusion.info_ref
  11.1 6.5 %attend.1 = bf16[16,25,8,128]{3,2,1,0:T(8,128)(2,1)} custom-call(s32[7]{0:T(128)} %pad_add_fusion.info_ref, bf16[6,576,128]{2,1,0:T(8,128)(2,1)} %bitcast.25, bf16[6,576,512]{2,1,0:T(8,128)(2,1)} %bitcast.24), custom_call_target="tpu_custom_call" | custom-call | flops 855638016 | bytes 5000000 | tf_op jit(solution)/shard_map/attend/pallas_call | solution.py:111
  17.6 0.7 copy-done.6
  18.4 7.6 %all-to-all-start = ((bf16[16,25,8,128]{3,2,1,0:T(8,128)(2,1)}), bf16[16,25,8,128]{3,2,1,0:T(8,128)(2,1)S(1)}, u32[]{:S(2)}, u32[]{:S(2)}) async-start(bf16[16,25,8,128]{3,2,1,0:T(8,128)(2,1)} %attend.1), calls=%async_computation | async-start | bytes 1638400 | tf_op jit(solution)/shard_map/all_to_all | solution.py:575
  26.1 2.7 %collective-permute-start.2 = (bf16[11,128,128]{2,1,0:T(8,128)(2,1)}, bf16[11,128,128]{2,1,0:T(8,128)(2,1)}, u32[]{:S(2)}, u32[]{:S(2)}) collective-permute-start(bf16[11,128,128]{2,1,0:T(8,128)(2,1)} %get-tuple-element.27), channel_id=1, source_target_pairs={{0,4},{2,6},{4,0},{6,2},{1,5},{3,7},{5,1},{7,3},{8,12},{10,14},{12... | collective-permute-start | bytes 1081352 | tf_op jit(solution)/shard_map/ppermute | solution.py:32
  28.8 0.6 constant_dynamic-slice_fusion.1
  29.4 1.8 %collective-permute-start.4 = (bf16[11,128,128]{2,1,0:T(8,128)(2,1)}, bf16[11,128,128]{2,1,0:T(8,128)(2,1)S(1)}, u32[]{:S(2)}, u32[]{:S(2)}) collective-permute-start(bf16[11,128,128]{2,1,0:T(8,128)(2,1)} %copy-done.6), channel_id=1, source_target_pairs={{0,1},{1,0},{2,3},{3,2},{4,5},{5,4},{6,7},{7,6},{8,9},{9,8},{10,11... | collective-permute-start | bytes 1081352 | tf_op jit(solution)/shard_map/ppermute | solution.py:28
  31.1 4.3 %collective-permute-done.2.refs_1_ = bf16[11,128,128]{2,1,0:T(8,128)(2,1)} collective-permute-done((bf16[11,128,128]{2,1,0:T(8,128)(2,1)}, bf16[11,128,128]{2,1,0:T(8,128)(2,1)}, u32[]{:S(2)}, u32[]{:S(2)}) %collective-permute-start.2) | collective-permute-done | bytes 360480 | tf_op jit(solution)/shard_map/ppermute | solution.py:32
  35.5 3.3 %collective-permute-start.5 = (bf16[11,128,128]{2,1,0:T(8,128)(2,1)}, bf16[11,128,128]{2,1,0:T(8,128)(2,1)}, u32[]{:S(2)}, u32[]{:S(2)}) collective-permute-start(bf16[11,128,128]{2,1,0:T(8,128)(2,1)} %collective-permute-done.2.refs_1_), channel_id=1, source_target_pairs={{0,1},{1,0},{2,3},{3,2},{4,5},{5,4},{6,7},{7,6},{8,9},{9,8},{10,11... | collective-permute-start | bytes 1081352 | tf_op jit(solution)/shard_map/ppermute | solution.py:28
  38.8 2.7 %collective-permute-start.15 = (bf16[7,128,128]{2,1,0:T(8,128)(2,1)}, bf16[7,128,128]{2,1,0:T(8,128)(2,1)}, u32[]{:S(2)}, u32[]{:S(2)}) collective-permute-start(bf16[7,128,128]{2,1,0:T(8,128)(2,1)} %copy-done.16), channel_id=1, source_target_pairs={{0,4},{2,6},{4,0},{6,2},{1,5},{3,7},{5,1},{7,3},{8,12},{10,14},{12... | collective-permute-start | bytes 688136 | tf_op jit(solution)/shard_map/ppermute | solution.py:32
  41.7 1.1 collective-permute-start.16
  42.9 1.0 copy-done.7
  43.8 1.0 copy-done.9
  44.8 2.1 %join.1.refs_0_ = bf16[48,1024]{1,0:T(8,128)(2,1)S(1)} custom-call(s32[6]{0:T(128)S(1)} %stack.39.info_ref, bf16[16,25,8,128]{3,2,1,0:T(8,128)(2,1)S(1)} %all-to-all-done.recv_ref, bf16[1,512,128]{2,1,0:T(8,128)(2,1)S(1)} %copy-done.5, bf16[11,128,128]{2,1,0:T(8,128)(2,1)S(1)} %copy-done.7, bf16[11,128,128]{2,1,0:T(8,128)(2,1)} %collective-permute-done.2.refs_1_, ...), custom_call_target="tpu_custom_call" | custom-call | flops 480000000 | bytes 3000000 | tf_op jit(solution)/shard_map/join/pallas_call | solution.py:227
  46.9 0.5 collective-permute-start.7
  47.4 1.0 collective-permute-start.8
  48.4 2.0 %collective-permute-start.9 = (bf16[48,1024]{1,0:T(8,128)(2,1)S(1)}, bf16[48,1024]{1,0:T(8,128)(2,1)S(1)}, u32[]{:S(2)}, u32[]{:S(2)}) collective-permute-start(bf16[48,1024]{1,0:T(8,128)(2,1)S(1)} %join.1.refs_0_), channel_id=1, source_target_pairs={{0,6},{2,0},{4,2},{6,4},{1,7},{3,1},{5,3},{7,5},{8,14},{10,8},{12,... | collective-permute-start | bytes 294920 | tf_op jit(solution)/shard_map/ppermute | solution.py:32
  50.4 1.5 collective-permute-start.10
  51.8 0.9 collective-permute-done.7.refs_1_
  52.7 2.8 %collective-permute-start.11 = (bf16[48,1024]{1,0:T(8,128)(2,1)S(1)}, bf16[48,1024]{1,0:T(8,128)(2,1)S(1)}, u32[]{:S(2)}, u32[]{:S(2)}) collective-permute-start(bf16[48,1024]{1,0:T(8,128)(2,1)S(1)} %collective-permute-done.7.refs_1_), channel_id=1, source_target_pairs={{0,1},{1,0},{2,3},{3,2},{4,5},{5,4},{6,7},{7,6},{8,9},{9,8},{10,11... | collective-permute-start | bytes 294920 | tf_op jit(solution)/shard_map/ppermute | solution.py:28
  55.5 1.7 %collective-permute-done.9.refs_3_ = bf16[48,1024]{1,0:T(8,128)(2,1)S(1)} collective-permute-done((bf16[48,1024]{1,0:T(8,128)(2,1)S(1)}, bf16[48,1024]{1,0:T(8,128)(2,1)S(1)}, u32[]{:S(2)}, u32[]{:S(2)}) %collective-permute-start.9) | collective-permute-done | bytes 98336 | tf_op jit(solution)/shard_map/ppermute | solution.py:32
  57.3 0.8 collective-permute-start.13
  58.2 0.8 collective-permute-done.13.refs_7_
  59.0 4.2 %project.1 = bf16[16,24,896]{2,1,0:T(8,128)(2,1)} custom-call(s32[6]{0:T(128)S(1)} %stack.39.info_ref, s32[1,384]{1,0:T(1,128)S(1)} %add.146.place_ref, bf16[48,1024]{1,0:T(8,128)(2,1)S(1)} %join.1.refs_0_, bf16[48,1024]{1,0:T(8,128)(2,1)S(1)} %collective-permute-done.7.refs_1_, bf16[48,1024]{1,0:T(8,128)(2,1)S(1)} %collective-permute-done.8.refs_2_, ...), custom_call_target="tpu_custom_call" | custom-call | flops 704643072 | bytes 3500000 | tf_op jit(solution)/shard_map/project/pallas_call | solution.py:275
  63.1 6.6 %all-to-all-start.1 = ((bf16[16,24,896]{2,1,0:T(8,128)(2,1)}), bf16[16,24,896]{2,1,0:T(8,128)(2,1)S(1)}, u32[]{:S(2)}, u32[]{:S(2)}) async-start(bf16[16,24,896]{2,1,0:T(8,128)(2,1)} %project.1), calls=%async_computation.1 | async-start | bytes 1376256 | tf_op jit(solution)/shard_map/all_to_all | solution.py:594
  69.9 0.1 fusion.2
  70.0 2.4 %collective-permute-start.20 = (bf16[6,896]{1,0:T(8,128)(2,1)S(1)}, bf16[6,896]{1,0:T(8,128)(2,1)S(1)}, u32[]{:S(2)}, u32[]{:S(2)}) collective-permute-start(bf16[6,896]{1,0:T(8,128)(2,1)S(1)} %get-tuple-element.46), channel_id=1, source_target_pairs={{0,6},{2,0},{4,2},{6,4},{1,7},{3,1},{5,3},{7,5},{8,14},{10,8},{12,... | collective-permute-start | bytes 32264 | tf_op jit(solution)/shard_map/ppermute | solution.py:32
  72.4 0.5 collective-permute-start.19
  72.9 0.2 collective-permute-start.18
  73.2 0.8 dynamic_slice.30
  74.0 2.4 %collective-permute-done.19 = bf16[6,896]{1,0:T(8,128)(2,1)S(1)} collective-permute-done((bf16[6,896]{1,0:T(8,128)(2,1)S(1)}, bf16[6,896]{1,0:T(8,128)(2,1)S(1)}, u32[]{:S(2)}, u32[]{:S(2)}) %collective-permute-start.19) | collective-permute-done | bytes 10784 | tf_op jit(solution)/shard_map/ppermute | solution.py:32
  76.4 0.5 collective-permute-done.18
  77.0 0.6 gather_fusion
  77.6 4.7 %all-to-all-done.1.parts_ref = bf16[16,24,896]{2,1,0:T(8,128)(2,1)S(1)} async-done(((bf16[16,24,896]{2,1,0:T(8,128)(2,1)}), bf16[16,24,896]{2,1,0:T(8,128)(2,1)S(1)}, u32[]{:S(2)}, u32[]{:S(2)}) %all-to-all-start.1) | async-done | bytes 688160 | tf_op jit(solution)/shard_map/all_to_all | solution.py:594
  82.3 1.4 residual.1
  83.7 0.6 copy-done.10
  84.4 5.4 %all-to-all-start.2 = ((bf16[32,22,8,128]{3,2,1,0:T(8,128)(2,1)}), bf16[32,22,8,128]{3,2,1,0:T(8,128)(2,1)S(1)}, u32[]{:S(2)}, u32[]{:S(2)}) async-start(bf16[32,22,8,128]{3,2,1,0:T(8,128)(2,1)} %get-tuple-element.33), calls=%async_computation.2 | async-start | bytes 2883584 | tf_op jit(solution)/shard_map/all_to_all | solution.py:600
  89.8 3.1 %constant_dynamic-slice_fusion = bf16[288,3584]{1,0:T(8,128)(2,1)} fusion(bf16[288,7168]{1,0:T(8,128)(2,1)} %own_ref.3, s32[]{:T(128)S(6)} %select_n.141), kind=kLoop, calls=%fused_computation.23 | loop fusion | bytes 4128772 | tf_op jit(solution)/shard_map/dynamic_slice | solution.py:36
  92.8 1.0 collective-permute-start.23
  93.9 15.5 %all-to-all-done.2 = bf16[32,22,8,128]{3,2,1,0:T(8,128)(2,1)S(1)} async-done(((bf16[32,22,8,128]{3,2,1,0:T(8,128)(2,1)}), bf16[32,22,8,128]{3,2,1,0:T(8,128)(2,1)S(1)}, u32[]{:S(2)}, u32[]{:S(2)}) %all-to-all-start.2) | async-done | bytes 1441824 | tf_op jit(solution)/shard_map/all_to_all | solution.py:600
  109.4 2.4 %collective-permute-start.21 = (bf16[8,4,22,8,128]{4,3,2,1,0:T(8,128)(2,1)S(1)}, bf16[8,4,22,8,128]{4,3,2,1,0:T(8,128)(2,1)S(1)}, u32[]{:S(2)}, u32[]{:S(2)}) collective-permute-start(bf16[8,4,22,8,128]{4,3,2,1,0:T(8,128)(2,1)S(1)} %bitcast.22), channel_id=1, source_target_pairs={{0,1},{1,0},{2,3},{3,2},{4,5},{5,4},{6,7},{7,6},{8,9},{9,8},{10,11... | collective-permute-start | bytes 4325384 | tf_op jit(solution)/shard_map/ppermute | solution.py:28
  111.8 6.1 %units_first.1 = (f32[192,576]{1,0:T(8,128)}, f32[192,128]{1,0:T(8,128)}) custom-call(s32[6]{0:T(128)} %copy-done.12, bf16[8,4,22,8,128]{4,3,2,1,0:T(8,128)(2,1)} %bitcast.23, bf16[288,7168]{1,0:T(8,128)(2,1)} %bitcast.18, bf16[288,7168]{1,0:T(8,128)(2,1)} %bitcast.20), custom_call_target="tpu_custom_call" | custom-call | flops 792723456 | bytes 5000000 | tf_op jit(solution)/shard_map/units_first/pallas_call | solution.py:401
  117.9 1.1 copy-done.18
  119.1 6.9 %units_last.1.mine_ref = bf16[192,288]{1,0:T(8,128)(2,1)} custom-call(s32[6]{0:T(128)} %copy-done.12, bf16[8,4,22,8,128]{4,3,2,1,0:T(8,128)(2,1)} %copy-done.18, bf16[288,7168]{1,0:T(8,128)(2,1)} %bitcast.19, bf16[288,7168]{1,0:T(8,128)(2,1)} %bitcast.21, f32[192,576]{1,0:T(8,128)} %get-tuple-element.34.refs_3_, f32[192,128]{1,0:T(8,128)} %get-tuple-element.35.refs_4_), custom_call_target="tpu_custom_call" | custom-call | flops 792723456 | bytes 5000000 | tf_op jit(solution)/shard_map/units_last/pallas_call | solution.py:401
  125.9 1.1 collective-permute-start.22
  127.1 0.9 constant_dynamic-update-slice_fusion.held_ref
  128.0 0.3 collective-permute-done.22.theirs_ref
  128.3 0.9 copy-done.3
  129.2 0.7 copy-done.13
  129.9 6.4 %down.1 = bf16[32,7,24,128]{3,2,1,0:T(8,128)(2,1)S(1)} custom-call(s32[6]{0:T(128)S(1)} %copy-done.13, bf16[192,288]{1,0:T(8,128)(2,1)S(1)} %copy-done.3, bf16[192,288]{1,0:T(8,128)(2,1)S(1)} %collective-permute-done.22.theirs_ref, bf16[288,7168]{1,0:T(8,128)(2,1)S(1)} %copy-done.2, bf16[288,3584]{1,0:T(8,128)(2,1)} %collective-permute-done.23.other_ref, ...), custom_call_target="tpu_custom_call" | custom-call | flops 792723456 | bytes 6000000 | tf_op jit(solution)/shard_map/down/pallas_call | solution.py:461
  136.2 24.2 %all_to_all.20.parts_ref = bf16[32,7,24,128]{3,2,1,0:T(8,128)(2,1)S(1)} all-to-all(bf16[32,7,24,128]{3,2,1,0:T(8,128)(2,1)S(1)} %down.1), channel_id=1, replica_groups=mesh['zh'=2,'zl'=2,'x'=4,'y'=4,'core'=2] {'zl','x','y'}, dimensions={0} | all-to-all | bytes 2752512 | tf_op jit(solution)/shard_map/all_to_all | solution.py:608
  160.4 0.8 finish.1
  161.3 2.1 %collective-permute-start.24 = (bf16[3,3584]{1,0:T(4,128)(2,1)S(1)}, bf16[3,3584]{1,0:T(4,128)(2,1)S(1)}, u32[]{:S(2)}, u32[]{:S(2)}) collective-permute-start(bf16[3,3584]{1,0:T(4,128)(2,1)S(1)} %get-tuple-element.38), channel_id=1, source_target_pairs={{0,1},{1,0},{2,3},{3,2},{4,5},{5,4},{6,7},{7,6},{8,9},{9,8},{10,11... | collective-permute-start | bytes 64520 | tf_op jit(solution)/shard_map/ppermute | solution.py:28
  163.4 0.9 collective-permute-done.24
  164.3 0.7 pad_maximum_fusion.1
  (71 shorter events, 1.0 us)
Async XLA Ops:
  0.1 1.5 copy-start
  1.6 0.9 copy-start.4
  2.5 56.5 %copy-start.12 = (s32[6]{0:T(128)}, s32[6]{0:T(128)S(1)}, u32[]{:S(2)}) copy-start(s32[6]{0:T(128)S(1)} %stack.39.info_ref) | copy-start | bytes 76
  2.5 8.0 %copy-start.21 = (s32[6]{0:T(128)S(1)}, s32[6]{0:T(128)}, u32[]{:S(2)}) copy-start(s32[6]{0:T(128)} %param.13) | copy-start | bytes 76
  4.3 0.7 copy-start.15
  5.0 0.7 copy-start.16
  5.7 11.9 %collective-permute-start = (bf16[11,128,128]{2,1,0:T(8,128)(2,1)S(1)}, bf16[11,128,128]{2,1,0:T(8,128)(2,1)S(1)}, u32[]{:S(2)}, u32[]{:S(2)}) collective-permute-start(bf16[11,128,128]{2,1,0:T(8,128)(2,1)S(1)} %get-tuple-element.22), channel_id=1, source_target_pairs={{0,2},{2,4},{4,6},{6,0},{1,3},{3,5},{5,7},{7,1},{8,10},{10,12},{12... | collective-permute-start | bytes 1081352 | tf_op jit(solution)/shard_map/ppermute | solution.py:32
  7.8 9.8 %collective-permute-start.1 = (bf16[11,128,128]{2,1,0:T(8,128)(2,1)S(1)}, bf16[11,128,128]{2,1,0:T(8,128)(2,1)S(1)}, u32[]{:S(2)}, u32[]{:S(2)}) collective-permute-start(bf16[11,128,128]{2,1,0:T(8,128)(2,1)S(1)} %get-tuple-element.23), channel_id=1, source_target_pairs={{0,6},{2,0},{4,2},{6,4},{1,7},{3,1},{5,3},{7,5},{8,14},{10,8},{12,... | collective-permute-start | bytes 1081352 | tf_op jit(solution)/shard_map/ppermute | solution.py:32
  9.2 29.6 %collective-permute-start.3 = (bf16[11,128,128]{2,1,0:T(8,128)(2,1)}, bf16[11,128,128]{2,1,0:T(8,128)(2,1)S(1)}, u32[]{:S(2)}, u32[]{:S(2)}) collective-permute-start(bf16[11,128,128]{2,1,0:T(8,128)(2,1)} %get-tuple-element.29), channel_id=1, source_target_pairs={{0,1},{1,0},{2,3},{3,2},{4,5},{5,4},{6,7},{7,6},{8,9},{9,8},{10,11... | collective-permute-start | bytes 1081352 | tf_op jit(solution)/shard_map/ppermute | solution.py:28
  10.3 38.0 %collective-permute-start.14 = (bf16[7,128,128]{2,1,0:T(8,128)(2,1)}, bf16[7,128,128]{2,1,0:T(8,128)(2,1)}, u32[]{:S(2)}, u32[]{:S(2)}) collective-permute-start(bf16[7,128,128]{2,1,0:T(8,128)(2,1)} %get-tuple-element.30), channel_id=1, source_target_pairs={{0,2},{2,4},{4,6},{6,0},{1,3},{3,5},{5,7},{7,1},{8,10},{10,12},{12... | collective-permute-start | bytes 688136 | tf_op jit(solution)/shard_map/ppermute | solution.py:32
  11.1 17.7 %copy-start.19 = (bf16[3,7168]{1,0:T(4,128)(2,1)S(1)}, bf16[3,7168]{1,0:T(4,128)(2,1)}, u32[]{:S(2)}) copy-start(bf16[3,7168]{1,0:T(4,128)(2,1)} %param.14) | copy-start | bytes 129028
  11.1 31.8 %copy-start.5 = (bf16[1,512,128]{2,1,0:T(8,128)(2,1)S(1)}, bf16[1,512,128]{2,1,0:T(8,128)(2,1)}, u32[]{:S(2)}) copy-start(bf16[1,512,128]{2,1,0:T(8,128)(2,1)} %own_ref.2) | copy-start | bytes 393220
  11.1 31.8 %copy-start.11 = (bf16[48,384]{1,0:T(8,128)(2,1)S(1)}, bf16[48,384]{1,0:T(8,128)(2,1)}, u32[]{:S(2)}) copy-start(bf16[48,384]{1,0:T(8,128)(2,1)} %constant.123.clone.refs_7_) | copy-start | bytes 110596
  17.6 0.8 copy-start.6
  17.6 0.8 copy-start.8
  18.4 24.4 %all-to-all-start = ((bf16[16,25,8,128]{3,2,1,0:T(8,128)(2,1)}), bf16[16,25,8,128]{3,2,1,0:T(8,128)(2,1)S(1)}, u32[]{:S(2)}, u32[]{:S(2)}) async-start(bf16[16,25,8,128]{3,2,1,0:T(8,128)(2,1)} %attend.1), calls=%async_computation | async-start | bytes 1638400 | tf_op jit(solution)/shard_map/all_to_all | solution.py:575
  26.0 32.9 %copy-start.1 = (bf16[128,7168]{1,0:T(8,128)(2,1)S(1)}, bf16[128,7168]{1,0:T(8,128)(2,1)}, u32[]{:S(2)}) copy-start(bf16[128,7168]{1,0:T(8,128)(2,1)} %refs_8_.1) | copy-start | bytes 5505028
  26.1 9.4 %collective-permute-start.2 = (bf16[11,128,128]{2,1,0:T(8,128)(2,1)}, bf16[11,128,128]{2,1,0:T(8,128)(2,1)}, u32[]{:S(2)}, u32[]{:S(2)}) collective-permute-start(bf16[11,128,128]{2,1,0:T(8,128)(2,1)} %get-tuple-element.27), channel_id=1, source_target_pairs={{0,4},{2,6},{4,0},{6,2},{1,5},{3,7},{5,1},{7,3},{8,12},{10,14},{12... | collective-permute-start | bytes 1081352 | tf_op jit(solution)/shard_map/ppermute | solution.py:32
  29.4 12.3 %collective-permute-start.4 = (bf16[11,128,128]{2,1,0:T(8,128)(2,1)}, bf16[11,128,128]{2,1,0:T(8,128)(2,1)S(1)}, u32[]{:S(2)}, u32[]{:S(2)}) collective-permute-start(bf16[11,128,128]{2,1,0:T(8,128)(2,1)} %copy-done.6), channel_id=1, source_target_pairs={{0,1},{1,0},{2,3},{3,2},{4,5},{5,4},{6,7},{7,6},{8,9},{9,8},{10,11... | collective-permute-start | bytes 1081352 | tf_op jit(solution)/shard_map/ppermute | solution.py:28
  31.1 11.7 %collective-permute-start.6 = (bf16[11,128,128]{2,1,0:T(8,128)(2,1)}, bf16[11,128,128]{2,1,0:T(8,128)(2,1)}, u32[]{:S(2)}, u32[]{:S(2)}) collective-permute-start(bf16[11,128,128]{2,1,0:T(8,128)(2,1)} %copy-done.8), channel_id=1, source_target_pairs={{0,1},{1,0},{2,3},{3,2},{4,5},{5,4},{6,7},{7,6},{8,9},{9,8},{10,11... | collective-permute-start | bytes 1081352 | tf_op jit(solution)/shard_map/ppermute | solution.py:28
  35.5 7.3 %collective-permute-start.5 = (bf16[11,128,128]{2,1,0:T(8,128)(2,1)}, bf16[11,128,128]{2,1,0:T(8,128)(2,1)}, u32[]{:S(2)}, u32[]{:S(2)}) collective-permute-start(bf16[11,128,128]{2,1,0:T(8,128)(2,1)} %collective-permute-done.2.refs_1_), channel_id=1, source_target_pairs={{0,1},{1,0},{2,3},{3,2},{4,5},{5,4},{6,7},{7,6},{8,9},{9,8},{10,11... | collective-permute-start | bytes 1081352 | tf_op jit(solution)/shard_map/ppermute | solution.py:28
  38.8 11.5 %collective-permute-start.15 = (bf16[7,128,128]{2,1,0:T(8,128)(2,1)}, bf16[7,128,128]{2,1,0:T(8,128)(2,1)}, u32[]{:S(2)}, u32[]{:S(2)}) collective-permute-start(bf16[7,128,128]{2,1,0:T(8,128)(2,1)} %copy-done.16), channel_id=1, source_target_pairs={{0,4},{2,6},{4,0},{6,2},{1,5},{3,7},{5,1},{7,3},{8,12},{10,14},{12... | collective-permute-start | bytes 688136 | tf_op jit(solution)/shard_map/ppermute | solution.py:32
  41.7 16.4 %collective-permute-start.16 = (bf16[7,128,128]{2,1,0:T(8,128)(2,1)}, bf16[7,128,128]{2,1,0:T(8,128)(2,1)}, u32[]{:S(2)}, u32[]{:S(2)}) collective-permute-start(bf16[7,128,128]{2,1,0:T(8,128)(2,1)} %copy-done.15), channel_id=1, source_target_pairs={{0,6},{2,0},{4,2},{6,4},{1,7},{3,1},{5,3},{7,5},{8,14},{10,8},{12,... | collective-permute-start | bytes 688136 | tf_op jit(solution)/shard_map/ppermute | solution.py:32
  42.8 1.0 copy-start.7
  43.8 1.0 copy-start.9
  46.9 5.8 %collective-permute-start.7 = (bf16[48,1024]{1,0:T(8,128)(2,1)S(1)}, bf16[48,1024]{1,0:T(8,128)(2,1)S(1)}, u32[]{:S(2)}, u32[]{:S(2)}) collective-permute-start(bf16[48,1024]{1,0:T(8,128)(2,1)S(1)} %join.1.refs_0_), channel_id=1, source_target_pairs={{0,2},{2,4},{4,6},{6,0},{1,3},{3,5},{5,7},{7,1},{8,10},{10,12},{12... | collective-permute-start | bytes 294920 | tf_op jit(solution)/shard_map/ppermute | solution.py:32
  47.4 8.1 %collective-permute-start.8 = (bf16[48,1024]{1,0:T(8,128)(2,1)S(1)}, bf16[48,1024]{1,0:T(8,128)(2,1)S(1)}, u32[]{:S(2)}, u32[]{:S(2)}) collective-permute-start(bf16[48,1024]{1,0:T(8,128)(2,1)S(1)} %join.1.refs_0_), channel_id=1, source_target_pairs={{0,4},{2,6},{4,0},{6,2},{1,5},{3,7},{5,1},{7,3},{8,12},{10,14},{12... | collective-permute-start | bytes 294920 | tf_op jit(solution)/shard_map/ppermute | solution.py:32
  48.4 8.9 %collective-permute-start.9 = (bf16[48,1024]{1,0:T(8,128)(2,1)S(1)}, bf16[48,1024]{1,0:T(8,128)(2,1)S(1)}, u32[]{:S(2)}, u32[]{:S(2)}) collective-permute-start(bf16[48,1024]{1,0:T(8,128)(2,1)S(1)} %join.1.refs_0_), channel_id=1, source_target_pairs={{0,6},{2,0},{4,2},{6,4},{1,7},{3,1},{5,3},{7,5},{8,14},{10,8},{12,... | collective-permute-start | bytes 294920 | tf_op jit(solution)/shard_map/ppermute | solution.py:32
  50.4 7.8 %collective-permute-start.10 = (bf16[48,1024]{1,0:T(8,128)(2,1)S(1)}, bf16[48,1024]{1,0:T(8,128)(2,1)S(1)}, u32[]{:S(2)}, u32[]{:S(2)}) collective-permute-start(bf16[48,1024]{1,0:T(8,128)(2,1)S(1)} %join.1.refs_0_), channel_id=1, source_target_pairs={{0,1},{1,0},{2,3},{3,2},{4,5},{5,4},{6,7},{7,6},{8,9},{9,8},{10,11... | collective-permute-start | bytes 294920 | tf_op jit(solution)/shard_map/ppermute | solution.py:28
  52.7 5.5 %collective-permute-start.11 = (bf16[48,1024]{1,0:T(8,128)(2,1)S(1)}, bf16[48,1024]{1,0:T(8,128)(2,1)S(1)}, u32[]{:S(2)}, u32[]{:S(2)}) collective-permute-start(bf16[48,1024]{1,0:T(8,128)(2,1)S(1)} %collective-permute-done.7.refs_1_), channel_id=1, source_target_pairs={{0,1},{1,0},{2,3},{3,2},{4,5},{5,4},{6,7},{7,6},{8,9},{9,8},{10,11... | collective-permute-start | bytes 294920 | tf_op jit(solution)/shard_map/ppermute | solution.py:28
  55.5 2.7 %collective-permute-start.12 = (bf16[48,1024]{1,0:T(8,128)(2,1)S(1)}, bf16[48,1024]{1,0:T(8,128)(2,1)S(1)}, u32[]{:S(2)}, u32[]{:S(2)}) collective-permute-start(bf16[48,1024]{1,0:T(8,128)(2,1)S(1)} %collective-permute-done.8.refs_2_), channel_id=1, source_target_pairs={{0,1},{1,0},{2,3},{3,2},{4,5},{5,4},{6,7},{7,6},{8,9},{9,8},{10,11... | collective-permute-start | bytes 294920 | tf_op jit(solution)/shard_map/ppermute | solution.py:28
  57.3 1.7 %collective-permute-start.13 = (bf16[48,1024]{1,0:T(8,128)(2,1)S(1)}, bf16[48,1024]{1,0:T(8,128)(2,1)S(1)}, u32[]{:S(2)}, u32[]{:S(2)}) collective-permute-start(bf16[48,1024]{1,0:T(8,128)(2,1)S(1)} %collective-permute-done.9.refs_3_), channel_id=1, source_target_pairs={{0,1},{1,0},{2,3},{3,2},{4,5},{5,4},{6,7},{7,6},{8,9},{9,8},{10,11... | collective-permute-start | bytes 294920 | tf_op jit(solution)/shard_map/ppermute | solution.py:28
  58.1 11.8 %copy-start.20 = (bf16[3,7168]{1,0:T(4,128)(2,1)S(1)}, bf16[3,7168]{1,0:T(4,128)(2,1)}, u32[]{:S(2)}) copy-start(bf16[3,7168]{1,0:T(4,128)(2,1)} %param.14) | copy-start | bytes 129028
  58.1 11.7 %collective-permute-start.17 = (bf16[3,3584]{1,0:T(4,128)(2,1)}, bf16[3,3584]{1,0:T(4,128)(2,1)S(1)}, u32[]{:S(2)}, u32[]{:S(2)}) collective-permute-start(bf16[3,3584]{1,0:T(4,128)(2,1)} %constant_dynamic-slice_fusion.1), channel_id=1, source_target_pairs={{0,1},{1,0},{2,3},{3,2},{4,5},{5,4},{6,7},{7,6},{8,9},{9,8},{10,11... | collective-permute-start | bytes 64520 | tf_op jit(solution)/shard_map/ppermute | solution.py:28
  63.1 19.1 %all-to-all-start.1 = ((bf16[16,24,896]{2,1,0:T(8,128)(2,1)}), bf16[16,24,896]{2,1,0:T(8,128)(2,1)S(1)}, u32[]{:S(2)}, u32[]{:S(2)}) async-start(bf16[16,24,896]{2,1,0:T(8,128)(2,1)} %project.1), calls=%async_computation.1 | async-start | bytes 1376256 | tf_op jit(solution)/shard_map/all_to_all | solution.py:594
  70.0 4.0 %collective-permute-start.20 = (bf16[6,896]{1,0:T(8,128)(2,1)S(1)}, bf16[6,896]{1,0:T(8,128)(2,1)S(1)}, u32[]{:S(2)}, u32[]{:S(2)}) collective-permute-start(bf16[6,896]{1,0:T(8,128)(2,1)S(1)} %get-tuple-element.46), channel_id=1, source_target_pairs={{0,6},{2,0},{4,2},{6,4},{1,7},{3,1},{5,3},{7,5},{8,14},{10,8},{12,... | collective-permute-start | bytes 32264 | tf_op jit(solution)/shard_map/ppermute | solution.py:32
  72.4 4.1 %collective-permute-start.19 = (bf16[6,896]{1,0:T(8,128)(2,1)S(1)}, bf16[6,896]{1,0:T(8,128)(2,1)S(1)}, u32[]{:S(2)}, u32[]{:S(2)}) collective-permute-start(bf16[6,896]{1,0:T(8,128)(2,1)S(1)} %get-tuple-element.45), channel_id=1, source_target_pairs={{0,4},{2,6},{4,0},{6,2},{1,5},{3,7},{5,1},{7,3},{8,12},{10,14},{12... | collective-permute-start | bytes 32264 | tf_op jit(solution)/shard_map/ppermute | solution.py:32
  72.9 4.1 %collective-permute-start.18 = (bf16[6,896]{1,0:T(8,128)(2,1)S(1)}, bf16[6,896]{1,0:T(8,128)(2,1)S(1)}, u32[]{:S(2)}, u32[]{:S(2)}) collective-permute-start(bf16[6,896]{1,0:T(8,128)(2,1)S(1)} %get-tuple-element.44), channel_id=1, source_target_pairs={{0,2},{2,4},{4,6},{6,0},{1,3},{3,5},{5,7},{7,1},{8,10},{10,12},{12... | collective-permute-start | bytes 32264 | tf_op jit(solution)/shard_map/ppermute | solution.py:32
  83.7 0.6 copy-start.10
  84.4 25.0 %all-to-all-start.2 = ((bf16[32,22,8,128]{3,2,1,0:T(8,128)(2,1)}), bf16[32,22,8,128]{3,2,1,0:T(8,128)(2,1)S(1)}, u32[]{:S(2)}, u32[]{:S(2)}) async-start(bf16[32,22,8,128]{3,2,1,0:T(8,128)(2,1)} %get-tuple-element.33), calls=%async_computation.2 | async-start | bytes 2883584 | tf_op jit(solution)/shard_map/all_to_all | solution.py:600
  92.8 35.1 %collective-permute-start.23 = (bf16[288,3584]{1,0:T(8,128)(2,1)}, bf16[288,3584]{1,0:T(8,128)(2,1)}, u32[]{:S(2)}, u32[]{:S(2)}) collective-permute-start(bf16[288,3584]{1,0:T(8,128)(2,1)} %constant_dynamic-slice_fusion), channel_id=1, source_target_pairs={{0,1},{1,0},{2,3},{3,2},{4,5},{5,4},{6,7},{7,6},{8,9},{9,8},{10,11... | collective-permute-start | bytes 6193160 | tf_op jit(solution)/shard_map/ppermute | solution.py:28
  109.4 2.4 %copy-start.17 = (bf16[32,22,8,128]{3,2,1,0:T(8,128)(2,1)}, bf16[32,22,8,128]{3,2,1,0:T(8,128)(2,1)S(1)}, u32[]{:S(2)}) copy-start(bf16[32,22,8,128]{3,2,1,0:T(8,128)(2,1)S(1)} %all-to-all-done.2) | copy-start | bytes 4325380
  109.4 8.5 %collective-permute-start.21 = (bf16[8,4,22,8,128]{4,3,2,1,0:T(8,128)(2,1)S(1)}, bf16[8,4,22,8,128]{4,3,2,1,0:T(8,128)(2,1)S(1)}, u32[]{:S(2)}, u32[]{:S(2)}) collective-permute-start(bf16[8,4,22,8,128]{4,3,2,1,0:T(8,128)(2,1)S(1)} %bitcast.22), channel_id=1, source_target_pairs={{0,1},{1,0},{2,3},{3,2},{4,5},{5,4},{6,7},{7,6},{8,9},{9,8},{10,11... | collective-permute-start | bytes 4325384 | tf_op jit(solution)/shard_map/ppermute | solution.py:28
  117.9 1.1 copy-start.18
  119.1 9.2 %copy-start.2 = (bf16[288,7168]{1,0:T(8,128)(2,1)S(1)}, bf16[288,7168]{1,0:T(8,128)(2,1)}, u32[]{:S(2)}) copy-start(bf16[288,7168]{1,0:T(8,128)(2,1)} %own_ref.3) | copy-start | bytes 12386308
  125.9 2.4 %collective-permute-start.22 = (bf16[192,288]{1,0:T(8,128)(2,1)}, bf16[192,288]{1,0:T(8,128)(2,1)S(1)}, u32[]{:S(2)}, u32[]{:S(2)}) collective-permute-start(bf16[192,288]{1,0:T(8,128)(2,1)} %units_last.1.mine_ref), channel_id=1, source_target_pairs={{0,1},{1,0},{2,3},{3,2},{4,5},{5,4},{6,7},{7,6},{8,9},{9,8},{10,11... | collective-permute-start | bytes 331784 | tf_op jit(solution)/shard_map/ppermute | solution.py:28
  128.3 0.9 copy-start.3
  129.2 0.7 copy-start.13
  136.2 24.2 %copy-start.14 = (s32[6]{0:T(128)S(1)}, s32[6]{0:T(128)}, u32[]{:S(2)}) copy-start(s32[6]{0:T(128)} %copy-done.12) | copy-start | bytes 76
  161.3 3.0 %collective-permute-start.24 = (bf16[3,3584]{1,0:T(4,128)(2,1)S(1)}, bf16[3,3584]{1,0:T(4,128)(2,1)S(1)}, u32[]{:S(2)}, u32[]{:S(2)}) collective-permute-start(bf16[3,3584]{1,0:T(4,128)(2,1)S(1)} %get-tuple-element.38), channel_id=1, source_target_pairs={{0,1},{1,0},{2,3},{3,2},{4,5},{5,4},{6,7},{7,6},{8,9},{9,8},{10,11... | collective-permute-start | bytes 64520 | tf_op jit(solution)/shard_map/ppermute | solution.py:28

commit v5 on v4

--- a/solution.py
+++ b/solution.py
@@ -34,11 +34,6 @@
 
 def block(array, index, size, axis):
     return lax.dynamic_slice_in_dim(array, index * size, size, axis)
-
-
-def swap_halves(array, core, axis):
-    half = array.shape[axis] // 2
-    return block(array, core, half, axis), swap(block(array, 1 - core, half, axis))
 
 
 def params(limit, *semantics):
@@ -127,28 +122,49 @@
     )(info, query, cache)
 
 
-def cut_kernel(info_ref, up_ref, *refs):
+def early_kernel(info_ref, up_ref, stream_ref, *outs):
+    rows, width = stream_ref.shape
+    eighth = width // 8
+    ups = up_ref.shape[1] // LANES
+    for step, out_ref in enumerate(outs):
+        out_ref[:ups] = up_ref[0].reshape(ups, LANES, LANES)
+        chip = lax.rem(info_ref[5] + step, 4)
+        lines = []
+        for side in (3, 4):
+            start = pl.multiple_of((info_ref[side] * 4 + chip) * eighth, LANES)
+            data = stream_ref[:, pl.ds(start, eighth)].astype(F32)
+            for lane in range(0, eighth, LANES):
+                lines.append(data[:, lane : lane + LANES])
+                lines.append(jnp.zeros((SUB - rows, LANES), F32))
+            lines.append(jnp.zeros((LANES // 2 - eighth // LANES * SUB, LANES), F32))
+        out_ref[ups] = jnp.concatenate(lines, axis=0).astype(BF16)
+
+
+def early(info, value_up, stream):
+    shape = (value_up.shape[1] // LANES + 1, LANES, LANES)
+    return pl.pallas_call(
+        early_kernel,
+        out_shape=[jax.ShapeDtypeStruct(shape, BF16)] * 4,
+        in_specs=[pl.BlockSpec(memory_space=pltpu.SMEM), WHOLE, WHOLE],
+        out_specs=[WHOLE] * 4,
+        compiler_params=params(VMEM_SOME),
+        cost_estimate=cost(0, 800_000),
+        name="early",
+    )(info, value_up, stream)
+
+
+def cut_kernel(info_ref, *refs):
     del info_ref
-    blocks, outs = refs[:7], refs[7:]
-    lanes = [slice(start, start + LANES) for start in range(0, blocks[0].shape[1], LANES)]
-    ups = up_ref.shape[1] // LANES
-    for step in range(4):
-        outs[step][:ups] = up_ref[0].reshape(ups, LANES, LANES)
-        for index, lane in enumerate(lanes):
-            outs[step][ups + index] = blocks[step][:, lane]
-    for step in range(3):
-        for index, lane in enumerate(lanes):
-            outs[4 + step][index] = blocks[4 + step][:, lane]
-
-
-def cut(info, value_up, out_proj):
+    count = len(refs) // 2
+    for source, out_ref in zip(refs[:count], refs[count:]):
+        for index in range(out_ref.shape[0]):
+            out_ref[index] = source[:, index * LANES : index * LANES + LANES]
+
+
+def cut(info, out_proj):
     rows, width = out_proj.shape
     eighth = width // 8
-    columns = eighth // LANES
-    ups = value_up.shape[1] // LANES
-    first = (ups + columns, LANES, LANES)
-    second = (columns, LANES, LANES)
-    full = lambda shape: pl.BlockSpec(shape, lambda i, info: (0,) * len(shape))
+    shape = (eighth // LANES, rows, LANES)
 
     def column(side, step):
         return pl.BlockSpec(
@@ -158,20 +174,55 @@
 
     return pl.pallas_call(
         cut_kernel,
-        out_shape=[jax.ShapeDtypeStruct(first, BF16)] * 4
-        + [jax.ShapeDtypeStruct(second, BF16)] * 3,
+        out_shape=[jax.ShapeDtypeStruct(shape, BF16)] * 7,
         grid_spec=pltpu.PrefetchScalarGridSpec(
             num_scalar_prefetch=1,
             grid=(1,),
-            in_specs=[full(value_up.shape)]
-            + [column(4, step) for step in range(4)]
+            in_specs=[column(4, step) for step in range(4)]
             + [column(3, step) for step in range(1, 4)],
-            out_specs=[full(first)] * 4 + [full(second)] * 3,
+            out_specs=[pl.BlockSpec(shape, lambda i, info: (0, 0, 0))] * 7,
         ),
-        compiler_params=params(VMEM_SOME, "arbitrary"),
+        compiler_params=params(VMEM_MOST, "arbitrary"),
         cost_estimate=cost(0, 4_000_000),
         name="cut",
-    )(info, value_up, *([out_proj] * 7))
+    )(info, *([out_proj] * 7))
+
+
+def stage_kernel(info_ref, first_ref, second_ref, out_ref, sems):
+    rows, width = first_ref.shape
+    columns = out_ref.shape[1]
+    lines = rows // 9
+    copies = []
+    for index, ref in enumerate((first_ref, second_ref)):
+        for piece in range(9):
+            span = pl.ds(piece * lines, lines)
+            place = pl.ds(index * rows + piece * lines, lines)
+            if ref.shape[1] == columns:
+                source = ref.at[span, :]
+            else:
+                start = pl.multiple_of(info_ref[3] * columns, LANES)
+                source = ref.at[span, pl.ds(start, columns)]
+            copies.append(
+                pltpu.make_async_copy(source, out_ref.at[place, :], sems.at[index * 9 + piece])
+            )
+    for copy in copies:
+        copy.start()
+    for copy in copies:
+        copy.wait()
+
+
+def stage(info, first, second):
+    anywhere = pl.BlockSpec(memory_space=pl.ANY)
+    return pl.pallas_call(
+        stage_kernel,
+        out_shape=jax.ShapeDtypeStruct((2 * first.shape[0], second.shape[1]), BF16),
+        in_specs=[pl.BlockSpec(memory_space=pltpu.SMEM), anywhere, anywhere],
+        out_specs=WHOLE,
+        scratch_shapes=[pltpu.SemaphoreType.DMA((18,))],
+        compiler_params=params(VMEM_SOME),
+        cost_estimate=cost(0, 2 * second.size * 2),
+        name="stage",
+    )(info, first, second)
 
 
 def join_kernel(rows, info_ref, recv_ref, own_ref, *refs):
@@ -290,10 +341,28 @@
     )(info, place, *values, out_proj, *seconds, *theirs)
 
 
-def residual_kernel(parts_ref, stream_ref, gain_ref, residual_ref, out_ref):
-    residual = stream_ref[...].astype(F32) + jnp.sum(parts_ref[...].astype(F32), axis=0)
+def residual_kernel(parts_ref, place_ref, gain_ref, *refs):
+    blocks, residual_ref, out_ref = refs[:8], refs[8], refs[9]
+    rows, width = residual_ref.shape
+    stream = []
+    for index, ref in enumerate(blocks):
+        lines = ref[ref.shape[0] - 1].astype(F32)
+        base = LANES // 2 * (index // 4)
+        stream.append(
+            jnp.concatenate(
+                [
+                    lines[base + SUB * column : base + SUB * column + SUB]
+                    for column in range(width // LANES)
+                ],
+                axis=1,
+            )
+        )
+    stream = jnp.concatenate(stream, axis=0).astype(BF16)
+    order = lax.broadcasted_iota(jnp.int32, (rows, stream.shape[0]), 0) == place_ref[...]
+    order = jnp.where(order, F32(1.0), F32(0.0)).astype(BF16)
+    residual = jnp.dot(order, stream, preferred_element_type=F32)
+    residual = residual + jnp.sum(parts_ref[...].astype(F32), axis=0)
     residual_ref[...] = residual
-    rows, width = residual.shape
     squares = jnp.sum(residual * residual, axis=1, keepdims=True)
     high = rounded(squares)
     low = rounded(squares - high)
@@ -316,7 +385,7 @@
         out_ref[:, index] = jnp.broadcast_to(tile.astype(BF16)[None], (chips, SUB, LANES))
 
 
-def residual_rows(parts, stream, gain, chips):
+def residual_rows(parts, place, gain, blocks, chips):
     _, rows, width = parts.shape
     tiles = rows * width // (SUB * LANES) + 1
     return pl.pallas_call(
@@ -325,164 +394,132 @@
             jax.ShapeDtypeStruct((rows, width), F32),
             jax.ShapeDtypeStruct((chips, tiles, SUB, LANES), BF16),
         ),
-        in_specs=[WHOLE] * 3,
+        in_specs=[WHOLE] * 11,
         out_specs=(WHOLE, WHOLE),
         compiler_params=params(VMEM_SOME),
         cost_estimate=cost(2_000_000, 2_500_000),
         name="residual",
-    )(parts, stream, gain)
-
-
-def units_kernel(groups, width, last, info_ref, *refs):
-    if last:
-        recv_ref, gate_ref, up_ref, acc_in, sq_in, out_ref, acc, sq_acc = refs
-    else:
-        recv_ref, gate_ref, up_ref, acc, sq_acc = refs
-    step = pl.program_id(0)
-    sides, _, tiles, _, _ = recv_ref.shape
+    )(parts, place, gain, *blocks)
+
+
+def units_kernel(groups, last, info_ref, recv_ref, weight_ref, *refs):
+    sides, quarters, tiles, _, _ = recv_ref.shape
     columns = (tiles - 1) // groups
     rows = sides * groups * SUB
-    left = jnp.concatenate(
-        [
-            recv_ref[:, 0, column * groups : column * groups + groups]
-            .astype(F32)
-            .reshape(rows, LANES)
-            for column in range(columns)
-        ],
-        axis=1,
-    ).astype(BF16)
-    both = jnp.concatenate([gate_ref[...], up_ref[...]], axis=0)
-    total = lax.dot_general(
-        left, both, (((1,), (1,)), ((), ())), preferred_element_type=F32
-    )
-    table = recv_ref[:, 0, tiles - 1].astype(F32)
+    depth = columns * LANES
+    which = 4 if last else 3
     lane = lax.broadcasted_iota(jnp.int32, (SUB, LANES), 1)
-    pieces = [
-        jnp.sum(
-            jnp.where((lane == group) | (lane == SUB + group), table, F32(0.0)),
-            axis=2,
-            keepdims=True,
-        )
-        for group in range(groups)
-    ]
-    squares = jnp.stack(pieces, axis=1).reshape(rows, 1)
-    squares = jnp.broadcast_to(squares, (rows, LANES))
-
-    @pl.when(step == 0)
-    def _():
-        acc[...] = acc_in[...] + total if last else total
-        sq_acc[...] = sq_in[...] + squares if last else squares
-
-    @pl.when(step > 0)
-    def _():
-        acc[...] += total
-        sq_acc[...] += squares
-
-    if last:
-
-        @pl.when(step == pl.num_programs(0) - 1)
-        def _():
-            hidden = out_ref.shape[1]
-            scale = lax.rsqrt(sq_acc[:, :1] / width + 1e-06)
-            gate = acc[:, :hidden] * scale
-            upper = acc[:, hidden:] * scale
-            out_ref[...] = (gate / (1.0 + jnp.exp(-gate)) * upper).astype(BF16)
-
-
-def units(info, which, received, gate_proj, up_proj, groups, carry=None):
+    total = squares = None
+    for quarter in range(quarters):
+        left = jnp.concatenate(
+            [
+                recv_ref[:, quarter, column * groups : column * groups + groups]
+                .astype(F32)
+                .reshape(rows, LANES)
+                for column in range(columns)
+            ],
+            axis=1,
+        ).astype(BF16)
+        start = pl.multiple_of((info_ref[which] * quarters + quarter) * depth, LANES)
+        part = lax.dot_general(
+            left,
+            weight_ref[:, pl.ds(start, depth)],
+            (((1,), (1,)), ((), ())),
+            preferred_element_type=F32,
+        )
+        total = part if total is None else total + part
+        table = recv_ref[:, quarter, tiles - 1].astype(F32)
+        pieces = [
+            jnp.sum(
+                jnp.where((lane == group) | (lane == SUB + group), table, F32(0.0)),
+                axis=2,
+                keepdims=True,
+            )
+            for group in range(groups)
+        ]
+        part = jnp.stack(pieces, axis=1).reshape(rows, 1)
+        squares = part if squares is None else squares + part
+    if not last:
+        acc_ref, sq_ref = refs
+        acc_ref[...] = total
+        sq_ref[...] = jnp.broadcast_to(squares, (rows, LANES))
+    else:
+        acc_ref, sq_ref, out_ref = refs
+        hidden = out_ref.shape[1]
+        scale = lax.rsqrt((sq_ref[:, :1] + squares) / weight_ref.shape[1] + 1e-06)
+        total = total + acc_ref[...]
+        gate = total[:, :hidden] * scale
+        upper = total[:, hidden:] * scale
+        out_ref[...] = (gate / (1.0 + jnp.exp(-gate)) * upper).astype(BF16)
+
+
+def units(info, received, weight, groups, carry=()):
     sides, quarters, tiles = received.shape[:3]
-    depth = (tiles - 1) // groups * LANES
-    hidden, width = gate_proj.shape
+    hidden = weight.shape[0] // 2
     rows = sides * groups * SUB
-    whole = lambda shape: pl.BlockSpec(shape, lambda i, info: (0,) * len(shape))
-    weight = pl.BlockSpec((hidden, depth), lambda i, info: (0, info[which] * quarters + i))
-    shapes = [(rows, 2 * hidden), (rows, LANES)]
-    last = carry is not None
-    return pl.pallas_call(
-        functools.partial(units_kernel, groups, width, last),
+    last = bool(carry)
+    return pl.pallas_call(
+        functools.partial(units_kernel, groups, last),
         out_shape=jax.ShapeDtypeStruct((rows, hidden), BF16)
         if last
-        else [jax.ShapeDtypeStruct(shape, F32) for shape in shapes],
-        grid_spec=pltpu.PrefetchScalarGridSpec(
-            num_scalar_prefetch=1,
-            grid=(quarters,),
-            in_specs=[
-                pl.BlockSpec(
-                    (sides, 1, tiles, SUB, LANES), lambda i, info: (0, i, 0, 0, 0)
-                ),
-                weight,
-                weight,
-            ]
-            + ([whole(shape) for shape in shapes] if last else []),
-            out_specs=whole((rows, hidden)) if last else [whole(shape) for shape in shapes],
-            scratch_shapes=[pltpu.VMEM(shape, F32) for shape in shapes] if last else [],
-        ),
-        compiler_params=params(VMEM_MOST, "arbitrary"),
-        cost_estimate=cost(4 * rows * depth * quarters * hidden, 5_000_000),
+        else [
+            jax.ShapeDtypeStruct((rows, 2 * hidden), F32),
+            jax.ShapeDtypeStruct((rows, LANES), F32),
+        ],
+        in_specs=[pl.BlockSpec(memory_space=pltpu.SMEM)] + [WHOLE] * (2 + len(carry)),
+        out_specs=WHOLE if last else [WHOLE, WHOLE],
+        compiler_params=params(VMEM_SOME),
+        cost_estimate=cost(2 * rows * weight.size // 2, 5_000_000),
         name="units_last" if last else "units_first",
-    )(info, received, gate_proj, up_proj, *(carry or ()))
-
-
-def down_kernel(info_ref, mine_ref, theirs_ref, own_ref, other_ref, held_ref, out_ref, left, total):
-    chips = out_ref.shape[0]
+    )(info, received, weight, *carry)
+
+
+def down_kernel(info_ref, mine_ref, theirs_ref, weight_ref, held_ref, out_ref, total):
+    chips, steps = out_ref.shape[:2]
     rows = mine_ref.shape[0]
     count = rows // chips
-    hidden = mine_ref.shape[1]
-
-    @pl.when(pl.program_id(0) == 0)
-    def _():
-        left[...] = jnp.concatenate(
-            [mine_ref[...].astype(F32), theirs_ref[...].astype(F32)], axis=1
-        ).astype(BF16)
-        total[pl.ds(rows, SUB), :] = jnp.zeros((SUB, total.shape[1]), F32)
-
-    weight = jnp.concatenate([own_ref[...], other_ref[...]], axis=0)
-    total[pl.ds(0, rows), :] = jnp.dot(left[...], weight, preferred_element_type=F32)
-    span = held_ref.shape[0]
-    place = pl.ds(pl.multiple_of(info_ref[2] * span, SUB), span)
-    total[place, :] += held_ref[...]
+    left = jnp.concatenate(
+        [mine_ref[...].astype(F32), theirs_ref[...].astype(F32)], axis=1
+    ).astype(BF16)
+    width = 4 * LANES
+    for step in range(steps):
+        span = slice(step * width, step * width + width)
+        total[:rows, span] = jnp.dot(
+            left, weight_ref[:, span], preferred_element_type=F32
+        )
+    total[pl.ds(rows, SUB), :] = jnp.zeros((SUB, total.shape[1]), F32)
+    lines, columns = held_ref.shape
+    place = pl.ds(pl.multiple_of(info_ref[2] * lines, SUB), lines)
+    across = pl.ds(pl.multiple_of(info_ref[5] * columns, LANES), columns)
+    total[place, across] += held_ref[...]
     sub = lax.broadcasted_iota(jnp.int32, (SUB, LANES), 0)
     for chip in range(chips):
-        part = total[chip * count : chip * count + SUB, :]
-        quads = [part[:, tile * LANES : tile * LANES + LANES] for tile in range(4)]
-        packed = [
-            jnp.where(sub < count, quads[tile], pltpu.roll(quads[3], count - 2 * tile, 0))
-            for tile in range(3)
-        ]
-        out_ref[chip, 0] = jnp.concatenate(packed, axis=0).astype(BF16)
-
-
-def down(info, mine, theirs, down_proj, down_theirs, held, chips):
-    rows, hidden = mine.shape
-    half = down_theirs.shape[1]
-    width = 4 * LANES
-    steps = half // width
-    whole = lambda shape: pl.BlockSpec(shape, lambda i, info: (0,) * len(shape))
+        for step in range(steps):
+            span = slice(step * width, step * width + width)
+            part = total[chip * count : chip * count + SUB, span]
+            quads = [part[:, tile * LANES : tile * LANES + LANES] for tile in range(4)]
+            packed = [
+                jnp.where(
+                    sub < count, quads[tile], pltpu.roll(quads[3], count - 2 * tile, 0)
+                )
+                for tile in range(3)
+            ]
+            out_ref[chip, step] = jnp.concatenate(packed, axis=0).astype(BF16)
+
+
+def down(info, mine, theirs, weight, held, chips):
+    rows = mine.shape[0]
+    half = weight.shape[1]
     return pl.pallas_call(
         down_kernel,
-        out_shape=jax.ShapeDtypeStruct((chips, steps, 3 * SUB, LANES), BF16),
-        grid_spec=pltpu.PrefetchScalarGridSpec(
-            num_scalar_prefetch=1,
-            grid=(steps,),
-            in_specs=[
-                whole((rows, hidden)),
-                whole((rows, hidden)),
-                pl.BlockSpec((hidden, width), lambda i, info: (0, info[3] * steps + i)),
-                pl.BlockSpec((hidden, width), lambda i, info: (0, i)),
-                pl.BlockSpec((held.shape[0], width), lambda i, info: (0, i)),
-            ],
-            out_specs=pl.BlockSpec(
-                (chips, 1, 3 * SUB, LANES), lambda i, info: (0, i, 0, 0)
-            ),
-            scratch_shapes=[
-                pltpu.VMEM((rows, 2 * hidden), BF16),
-                pltpu.VMEM((rows + SUB, width), F32),
-            ],
-        ),
-        compiler_params=params(VMEM_SOME, "arbitrary"),
-        cost_estimate=cost(4 * rows * hidden * half, 6_000_000),
+        out_shape=jax.ShapeDtypeStruct((chips, half // (4 * LANES), 3 * SUB, LANES), BF16),
+        in_specs=[pl.BlockSpec(memory_space=pltpu.SMEM)] + [WHOLE] * 4,
+        out_specs=WHOLE,
+        scratch_shapes=[pltpu.VMEM((rows + SUB, half), F32)],
+        compiler_params=params(VMEM_SOME),
+        cost_estimate=cost(2 * rows * weight.size, 6_000_000),
         name="down",
-    )(info, mine, theirs, down_proj, down_theirs, held)
+    )(info, mine, theirs, weight, held)
 
 
 def finish_kernel(info_ref, parts_ref, mine_ref, theirs_ref):
@@ -539,24 +576,8 @@
     first = core == 0
     info = jnp.stack([core * 4 + ring, core, group, core, 1 - core, ring]).astype(jnp.int32)
 
-    cuts = cut(info, value_up, out_proj)
-    own = cuts[0]
-    first_one, first_three = shift(cuts[1], 1), shift(cuts[3], 3)
-    stream_mine, stream_theirs = swap_halves(stream, core, 1)
-    stream_rows = jnp.concatenate(
-        [
-            jnp.where(first, stream_mine, stream_theirs),
-            jnp.where(first, stream_theirs, stream_mine),
-        ],
-        axis=0,
-    )
-    stream_parts = [block(stream_rows, ring, eighth, 1)]
-    for step in (1, 2, 3):
-        stream_parts.append(shift(block(stream_rows, (ring + step) % 4, eighth, 1), step))
-    back = (ring - jnp.arange(4)) % 4
-    ring_stream = jnp.take(jnp.stack(stream_parts), back, axis=0)
-    ring_stream = ring_stream.reshape(8 * rows_own, eighth)
-    _, down_theirs = swap_halves(down_proj, core, 1)
+    own, *starts = early(info, value_up, stream)
+    firsts = [shift(part, step) for step, part in zip((1, 2, 3), starts)]
     gain = block(norm_gain, core * 4 + ring, eighth, 0)[None]
 
     offset = lax.axis_index("zh") * latent_cache.shape[1]
@@ -565,15 +586,14 @@
         query_latent.transpose(0, 2, 1),
         latent_cache.transpose(0, 2, 1),
     )
-    payload, first_one, first_three = lax.optimization_barrier(
-        (payload, first_one, first_three)
-    )
-    first_two = shift(lax.optimization_barrier((cuts[2], first_one))[0], 2)
-    seconds = [shift(cuts[3 + step], step) for step in (1, 2, 3)]
-    firsts = [first_one, first_two, first_three]
-    theirs = [swap(part) for part in [own] + firsts]
+    payload, out_proj, *firsts = lax.optimization_barrier((payload, out_proj, *firsts))
+    firsts_theirs = [swap(part) for part in [own] + firsts]
+    cuts = cut(info, out_proj)
+    others = [cuts[0]] + [shift(part, step) for step, part in zip((1, 2, 3), cuts[1:4])]
+    seconds = [shift(part, step) for step, part in zip((1, 2, 3), cuts[4:])]
+    theirs = [swap(part) for part in others]
     received = lax.all_to_all(payload, OUTER, split_axis=0, concat_axis=0, tiled=True)
-    values = join(info, received, value_up, firsts, theirs, rows)
+    values = join(info, received, value_up, firsts, firsts_theirs, rows)
 
     ring_values = [values] + [shift(values, step) for step in (1, 2, 3)]
     row = jnp.arange(8 * rows)
@@ -582,6 +602,10 @@
     side = jnp.where(jnp.arange(8) < 4, core, 1 - core)
     place = natural[:, : 8 * rows] + ((chip * 2 + side) * rows)[:, None]
     place = place.reshape(1, 64 * rows).astype(jnp.int32)
+    line = jnp.arange(SUB)[None]
+    stream_place = ((chip * 2 + side) * rows_own)[:, None] + line
+    stream_place = jnp.where(line < rows_own, stream_place, -1)
+    stream_place = stream_place.reshape(1, 8 * SUB).astype(jnp.int32)
     partial = project(
         info,
         place,
@@ -593,18 +617,21 @@
     )
     parts = lax.all_to_all(partial, OUTER, split_axis=0, concat_axis=0, tiled=True)
 
-    residual, payload = residual_rows(parts, ring_stream, gain, 32)
-    held = lax.dynamic_update_slice(
-        jnp.zeros((8 * rows_own, half), F32), residual, (0, ring * eighth)
+    residual, payload = residual_rows(
+        parts, stream_place, gain, [own] + firsts + firsts_theirs, 32
+    )
+    payload, gate_proj, up_proj, down_proj = lax.optimization_barrier(
+        (payload, gate_proj, up_proj, down_proj)
     )
     piece = lax.all_to_all(payload, SIDE_CHIPS, split_axis=0, concat_axis=0, tiled=True)
     piece = piece.reshape((8, 4) + piece.shape[1:])
     other = swap(piece)
+    down_theirs = swap(block(down_proj, 1 - core, half, 1))
+    weight = stage(info, gate_proj.T, up_proj.T)
     groups = 8 * rows_own // SUB
-    gate_proj, up_proj = gate_proj.T, up_proj.T
-    carry = units(info, 3, piece, gate_proj, up_proj, groups)
-    hidden = units(info, 4, other, gate_proj, up_proj, groups, carry)
-    partial = down(info, hidden, swap(hidden), down_proj, down_theirs, held, 32)
+    carry = units(info, piece, weight, groups)
+    hidden = units(info, other, weight, groups, carry)
+    partial = down(info, hidden, swap(hidden), stage(info, down_proj, down_theirs), residual, 32)
     parts = lax.all_to_all(partial, SIDE_CHIPS, split_axis=0, concat_axis=0, tiled=True)
     mine, theirs = finish(info, parts)
     theirs = swap(theirs)

time: 166 us -> 177 us (1.066)
  waiting for transfers between devices: 32.1 us -> 46.1 us
  starting transfers between devices: 54.4 us -> 48.4 us
    ppermute x12, waiting for transfers between devices: 9.89 us -> 17.2 us  [shift(): return lax.ppermute(array, 'y', [(i, (i + step) % 4) for i in range(4)])]
    all_to_all x1, waiting for transfers between devices: 4.65 us -> 11.5 us  [local(): lax.all_to_all(partial, OUTER, split_axis=0, concat_axis=0, tiled=True)]
    ppermute x13 -> x16, starting transfers between devices: 18 us -> 14.4 us  [swap(): return lax.ppermute(array, 'core', SWAP)]
    unnamed x44, local copies, waits for them, and re-layouts: 9.99 us -> 13.4 us
    ppermute x12, starting transfers between devices: 16.7 us -> 14 us  [shift(): return lax.ppermute(array, 'y', [(i, (i + step) % 4) for i in range(4)])]
    dynamic_slice x3 -> x2, local copies, waits for them, and re-layouts: 4.46 us -> 3.83 us  [block(): return lax.dynamic_slice_in_dim(array, index * size, size, axis)]
    pallas_call x4 -> x7, Pallas kernels: 21.1 us -> 21.6 us  [the longest x2 9.66 us: stage(): pl.pallas_call(stage_kernel, out_shape=jax.ShapeDtypeStruct((2 * first.sh...]
  transfers between devices with their start and end apart: 28 -> 31, of which waited for: 10 -> 9; matrix products, arithmetic and copies ran while one was open for 4% -> 3% of each run, Pallas kernels for 16% -> 15%
where the time goes in v5:
time: 177 us; the launch traced here: 176 us
  starting transfers between devices  48.4 us (27%)
  waiting for transfers between devices  46.1 us (26%)
  Pallas kernels  37.4 us (21%)
  blocking collectives  23.8 us (13%)
  local copies, waits for them, and re-layouts  17.5 us (10%)
  other arithmetic  2.08 us (1%)
    all_to_all x1, blocking collectives, local(): lax.all_to_all(partial, SIDE_CHIPS, split_axis=0, concat_axis=0, tiled=True)  23.8 us
    ppermute x12, waiting for transfers between devices, shift(): return lax.ppermute(array, 'y', [(i, (i + step) % 4) for i in range(4)])  17.2 us
    all_to_all x1, waiting for transfers between devices, local(): lax.all_to_all(payload, SIDE_CHIPS, split_axis=0, concat_axis=0, tiled=True)  15.3 us
    ppermute x16, starting transfers between devices, swap(): return lax.ppermute(array, 'core', SWAP)  14.4 us
    ppermute x12, starting transfers between devices, shift(): return lax.ppermute(array, 'y', [(i, (i + step) % 4) for i in range(4)])  14 us
    unnamed x44, local copies, waits for them, and re-layouts  13.4 us
    all_to_all x1, waiting for transfers between devices, local(): lax.all_to_all(partial, OUTER, split_axis=0, concat_axis=0, tiled=True)  11.5 us
    pallas_call x2, Pallas kernels, stage(): pl.pallas_call(stage_kernel, out_shape=jax.ShapeDtypeStruct((2 * first.sh...  9.66 us
  transfers between devices with their start and end apart: 31, of which 9 were waited for; matrix products, arithmetic and copies ran while one was open for 3% of the time, Pallas kernels for 15%

profile of v5, /device:TPU:1, one launch (start us, length us, event | category | flops | bytes accessed | tf_op | source)
XLA Modules:
  0.0 175.7 jit_solution(3520261767212780333)
XLA Ops:
  0.1 0.9 copy-done.10
  1.0 0.8 copy-done.20
  1.8 1.3 early.1
  3.1 2.1 %collective-permute-start = (bf16[5,128,128]{2,1,0:T(8,128)(2,1)S(1)}, bf16[5,128,128]{2,1,0:T(8,128)(2,1)S(1)}, u32[]{:S(2)}, u32[]{:S(2)}) collective-permute-start(bf16[5,128,128]{2,1,0:T(8,128)(2,1)S(1)} %get-tuple-element.31), channel_id=1, source_target_pairs={{0,2},{2,4},{4,6},{6,0},{1,3},{3,5},{5,7},{7,1},{8,10},{10,12},{12... | collective-permute-start | bytes 491528 | tf_op jit(solution)/shard_map/ppermute | solution.py:32
  5.2 2.6 %collective-permute-start.1 = (bf16[5,128,128]{2,1,0:T(8,128)(2,1)S(1)}, bf16[5,128,128]{2,1,0:T(8,128)(2,1)S(1)}, u32[]{:S(2)}, u32[]{:S(2)}) collective-permute-start(bf16[5,128,128]{2,1,0:T(8,128)(2,1)S(1)} %get-tuple-element.32), channel_id=1, source_target_pairs={{0,4},{2,6},{4,0},{6,2},{1,5},{3,7},{5,1},{7,3},{8,12},{10,14},{12... | collective-permute-start | bytes 491528 | tf_op jit(solution)/shard_map/ppermute | solution.py:32
  7.8 1.1 collective-permute-start.2
  8.9 1.2 pad_add_fusion.info_ref
  10.1 6.4 %attend.1 = bf16[16,25,8,128]{3,2,1,0:T(8,128)(2,1)} custom-call(s32[7]{0:T(128)} %pad_add_fusion.info_ref, bf16[6,576,128]{2,1,0:T(8,128)(2,1)} %bitcast.16, bf16[6,576,512]{2,1,0:T(8,128)(2,1)} %bitcast.15), custom_call_target="tpu_custom_call" | custom-call | flops 855638016 | bytes 5000000 | tf_op jit(solution)/shard_map/attend/pallas_call | solution.py:106
  16.5 7.6 %all-to-all-start = ((bf16[16,25,8,128]{3,2,1,0:T(8,128)(2,1)}), bf16[16,25,8,128]{3,2,1,0:T(8,128)(2,1)S(1)}, u32[]{:S(2)}, u32[]{:S(2)}) async-start(bf16[16,25,8,128]{3,2,1,0:T(8,128)(2,1)} %attend.1), calls=%async_computation | async-start | bytes 1638400 | tf_op jit(solution)/shard_map/all_to_all | solution.py:595
  24.2 1.9 %collective-permute-start.3 = (bf16[5,128,128]{2,1,0:T(8,128)(2,1)}, bf16[5,128,128]{2,1,0:T(8,128)(2,1)S(1)}, u32[]{:S(2)}, u32[]{:S(2)}) collective-permute-start(bf16[5,128,128]{2,1,0:T(8,128)(2,1)} %get-tuple-element.38.refs_0_), channel_id=1, source_target_pairs={{0,1},{1,0},{2,3},{3,2},{4,5},{5,4},{6,7},{7,6},{8,9},{9,8},{10,11... | collective-permute-start | bytes 491528 | tf_op jit(solution)/shard_map/ppermute | solution.py:28
  26.1 0.4 collective-permute-start.5
  26.6 3.6 %cut.1 = (bf16[7,128,128]{2,1,0:T(8,128)(2,1)}, bf16[7,128,128]{2,1,0:T(8,128)(2,1)}, bf16[7,128,128]{2,1,0:T(8,128)(2,1)}, bf16[7,128,128]{2,1,0:T(8,128)(2,1)}...) custom-call(s32[6]{0:T(128)} %copy-done.18, bf16[128,7168]{1,0:T(8,128)(2,1)} %refs_8_, ...), custom_call_target="tpu_custom_call" | custom-call | bytes 4000000 | tf_op jit(solution)/shard_map/cut/pallas_call | solution.py:175
  30.2 0.4 collective-permute-start.14
  30.6 1.0 collective-permute-start.15
  31.6 1.9 %collective-permute-start.18 = (bf16[7,128,128]{2,1,0:T(8,128)(2,1)}, bf16[7,128,128]{2,1,0:T(8,128)(2,1)}, u32[]{:S(2)}, u32[]{:S(2)}) collective-permute-start(bf16[7,128,128]{2,1,0:T(8,128)(2,1)} %get-tuple-element.44), channel_id=1, source_target_pairs={{0,2},{2,4},{4,6},{6,0},{1,3},{3,5},{5,7},{7,1},{8,10},{10,12},{12... | collective-permute-start | bytes 688136 | tf_op jit(solution)/shard_map/ppermute | solution.py:32
  33.5 0.9 collective-permute-start.6
  34.4 0.7 copy-done.4
  35.0 0.7 collective-permute-start.20
  35.8 0.7 copy-done.7
  36.5 1.5 collective-permute-start.22
  37.9 5.8 %collective-permute-done.14.refs_9_ = bf16[7,128,128]{2,1,0:T(8,128)(2,1)S(1)} collective-permute-done((bf16[7,128,128]{2,1,0:T(8,128)(2,1)}, bf16[7,128,128]{2,1,0:T(8,128)(2,1)S(1)}, u32[]{:S(2)}, u32[]{:S(2)}) %collective-permute-start.14) | collective-permute-done | bytes 229408 | tf_op jit(solution)/shard_map/ppermute | solution.py:32
  43.7 0.7 copy-done.12
  44.4 0.7 copy-done.14
  45.1 1.3 collective-permute-start.17
  46.4 7.2 %collective-permute-done.18 = bf16[7,128,128]{2,1,0:T(8,128)(2,1)} collective-permute-done((bf16[7,128,128]{2,1,0:T(8,128)(2,1)}, bf16[7,128,128]{2,1,0:T(8,128)(2,1)}, u32[]{:S(2)}, u32[]{:S(2)}) %collective-permute-start.18) | collective-permute-done | bytes 229408 | tf_op jit(solution)/shard_map/ppermute | solution.py:32
  53.6 0.9 collective-permute-start.19
  54.6 0.9 copy-done.5
  55.5 0.9 copy-done.8
  56.4 0.9 copy-done.11
  57.3 2.1 %join.1.refs_0_ = bf16[48,1024]{1,0:T(8,128)(2,1)} custom-call(s32[6]{0:T(128)S(1)} %copy-done.19, bf16[16,25,8,128]{3,2,1,0:T(8,128)(2,1)S(1)} %all-to-all-done.recv_ref, bf16[1,512,128]{2,1,0:T(8,128)(2,1)S(1)} %copy-done.11, bf16[5,128,128]{2,1,0:T(8,128)(2,1)S(1)} %collective-permute-done.refs_0_.refs_1_, ...), custom_call_target="tpu_custom_call" | custom-call | flops 480000000 | bytes 3000000 | tf_op jit(solution)/shard_map/join/pallas_call | solution.py:278
  59.4 0.5 collective-permute-start.23
  59.9 0.5 collective-permute-start.8
  60.4 2.3 %collective-permute-start.9 = (bf16[48,1024]{1,0:T(8,128)(2,1)}, bf16[48,1024]{1,0:T(8,128)(2,1)}, u32[]{:S(2)}, u32[]{:S(2)}) collective-permute-start(bf16[48,1024]{1,0:T(8,128)(2,1)} %join.1.refs_0_), channel_id=1, source_target_pairs={{0,6},{2,0},{4,2},{6,4},{1,7},{3,1},{5,3},{7,5},{8,14},{10,8},{12,... | collective-permute-start | bytes 294920 | tf_op jit(solution)/shard_map/ppermute | solution.py:32
  62.6 0.9 collective-permute-start.10
  63.5 4.2 %collective-permute-done.7.refs_1_ = bf16[48,1024]{1,0:T(8,128)(2,1)S(1)} collective-permute-done((bf16[48,1024]{1,0:T(8,128)(2,1)}, bf16[48,1024]{1,0:T(8,128)(2,1)S(1)}, u32[]{:S(2)}, u32[]{:S(2)}) %collective-permute-start.7) | collective-permute-done | bytes 98336 | tf_op jit(solution)/shard_map/ppermute | solution.py:32
  67.8 0.8 collective-permute-start.11
  68.6 0.7 collective-permute-start.13
  69.5 0.2 collective-permute-done.11.refs_5_
  69.7 0.4 collective-permute-done.12.refs_6_
  70.1 0.6 collective-permute-done.13.refs_7_
  70.6 0.9 copy-done.13
  71.6 0.9 copy-done.15
  72.5 4.2 %project.1 = bf16[16,24,896]{2,1,0:T(8,128)(2,1)} custom-call(s32[6]{0:T(128)S(1)} %copy-done.19, s32[1,384]{1,0:T(1,128)S(1)} %add.106.place_ref, bf16[48,1024]{1,0:T(8,128)(2,1)} %join.1.refs_0_, bf16[48,1024]{1,0:T(8,128)(2,1)S(1)} %collective-permute-done.7.refs_1_, bf16[48,1024]{1,0:T(8,128)(2,1)S(1)} %collective-permute-done.8.refs_2_, ...), custom_call_target="tpu_custom_call" | custom-call | flops 704643072 | bytes 3500000 | tf_op jit(solution)/shard_map/project/pallas_call | solution.py:326
  76.7 6.9 %all-to-all-start.1 = ((bf16[16,24,896]{2,1,0:T(8,128)(2,1)}), bf16[16,24,896]{2,1,0:T(8,128)(2,1)S(1)}, u32[]{:S(2)}, u32[]{:S(2)}) async-start(bf16[16,24,896]{2,1,0:T(8,128)(2,1)} %project.1), calls=%async_computation.1 | async-start | bytes 1376256 | tf_op jit(solution)/shard_map/all_to_all | solution.py:618
  83.8 0.8 dynamic_slice.6
  84.6 11.5 %all-to-all-done.1.parts_ref = bf16[16,24,896]{2,1,0:T(8,128)(2,1)S(1)} async-done(((bf16[16,24,896]{2,1,0:T(8,128)(2,1)}), bf16[16,24,896]{2,1,0:T(8,128)(2,1)S(1)}, u32[]{:S(2)}, u32[]{:S(2)}) %all-to-all-start.1) | async-done | bytes 688160 | tf_op jit(solution)/shard_map/all_to_all | solution.py:618
  96.2 2.4 %residual.1 = (f32[24,896]{1,0:T(8,128)S(1)}, bf16[32,22,8,128]{3,2,1,0:T(8,128)(2,1)}) custom-call(bf16[16,24,896]{2,1,0:T(8,128)(2,1)S(1)} %all-to-all-done.1.parts_ref, s32[1,64]{1,0:T(1,128)S(1)} %select_n.82.place_ref, f32[1,896]{1,0:T(1,128)S(1)} %broadcast_in_dim.34.gain_ref, bf16[5,128,128]{2,1,0:T(8,128)(2,1)} %get-tuple-element.38.refs_0_, ...), custom_call_target="tpu_custom_call" | custom-call | flops 2000000 | bytes 2500000 | tf_op jit(solution)/shard_map/residual/pallas_call | solution.py:391
  98.5 5.4 %all-to-all-start.2 = ((bf16[32,22,8,128]{3,2,1,0:T(8,128)(2,1)}), bf16[32,22,8,128]{3,2,1,0:T(8,128)(2,1)S(1)}, u32[]{:S(2)}, u32[]{:S(2)}) async-start(bf16[32,22,8,128]{3,2,1,0:T(8,128)(2,1)} %get-tuple-element.48), calls=%async_computation.2 | async-start | bytes 2883584 | tf_op jit(solution)/shard_map/all_to_all | solution.py:626
  103.9 3.1 %constant_dynamic-slice_fusion = bf16[288,3584]{1,0:T(8,128)(2,1)} fusion(bf16[288,7168]{1,0:T(8,128)(2,1)} %first_ref, s32[]{:T(128)S(6)} %select_n.84), kind=kLoop, calls=%fused_computation.23 | loop fusion | bytes 4128772 | tf_op jit(solution)/shard_map/dynamic_slice | solution.py:36
  107.0 1.0 collective-permute-start.26
  108.0 15.3 %all-to-all-done.2 = bf16[32,22,8,128]{3,2,1,0:T(8,128)(2,1)S(1)} async-done(((bf16[32,22,8,128]{3,2,1,0:T(8,128)(2,1)}), bf16[32,22,8,128]{3,2,1,0:T(8,128)(2,1)S(1)}, u32[]{:S(2)}, u32[]{:S(2)}) %all-to-all-start.2) | async-done | bytes 1441824 | tf_op jit(solution)/shard_map/all_to_all | solution.py:626
  123.4 2.4 %collective-permute-start.24 = (bf16[8,4,22,8,128]{4,3,2,1,0:T(8,128)(2,1)S(1)}, bf16[8,4,22,8,128]{4,3,2,1,0:T(8,128)(2,1)S(1)}, u32[]{:S(2)}, u32[]{:S(2)}) collective-permute-start(bf16[8,4,22,8,128]{4,3,2,1,0:T(8,128)(2,1)S(1)} %bitcast.11), channel_id=1, source_target_pairs={{0,1},{1,0},{2,3},{3,2},{4,5},{5,4},{6,7},{7,6},{8,9},{9,8},{10,11... | collective-permute-start | bytes 4325384 | tf_op jit(solution)/shard_map/ppermute | solution.py:28
  125.8 2.2 %copy-done.2 = bf16[7168,288]{0,1:T(8,128)(2,1)S(1)} copy-done((bf16[7168,288]{0,1:T(8,128)(2,1)S(1)}, bf16[7168,288]{0,1:T(8,128)(2,1)}, u32[]{:S(2)}) %copy-start.2) | copy-done | bytes 4128792
  128.0 2.2 %copy-done.3 = bf16[7168,288]{0,1:T(8,128)(2,1)S(1)} copy-done((bf16[7168,288]{0,1:T(8,128)(2,1)S(1)}, bf16[7168,288]{0,1:T(8,128)(2,1)}, u32[]{:S(2)}) %copy-start.3) | copy-done | bytes 4128792
  130.1 5.6 %stage.2.weight_ref = bf16[576,7168]{1,0:T(8,128)(2,1)S(1)} custom-call(s32[6]{0:T(128)S(1)} %copy-done.19, bf16[288,7168]{1,0:T(8,128)(2,1)S(1)} %bitcast.13, bf16[288,7168]{1,0:T(8,128)(2,1)S(1)} %bitcast.14), custom_call_target="tpu_custom_call" | custom-call | bytes 8257536 | tf_op jit(solution)/shard_map/stage/pallas_call | solution.py:216
  135.7 2.3 %units_first.1 = (f32[192,576]{1,0:T(8,128)S(1)}, f32[192,128]{1,0:T(8,128)S(1)}) custom-call(s32[6]{0:T(128)S(1)} %copy-done.19, bf16[8,4,22,8,128]{4,3,2,1,0:T(8,128)(2,1)S(1)} %bitcast.12, bf16[576,7168]{1,0:T(8,128)(2,1)S(1)} %stage.2.weight_ref), custom_call_target="tpu_custom_call" | custom-call | flops 792723456 | bytes 5000000 | tf_op jit(solution)/shard_map/units_first/pallas_call | solution.py:461
  138.1 2.4 %units_last.1.mine_ref = bf16[192,288]{1,0:T(8,128)(2,1)S(1)} custom-call(s32[6]{0:T(128)S(1)} %copy-done.19, bf16[8,4,22,8,128]{4,3,2,1,0:T(8,128)(2,1)S(1)} %collective-permute-done.24.recv_ref, bf16[576,7168]{1,0:T(8,128)(2,1)S(1)} %stage.2.weight_ref, f32[192,576]{1,0:T(8,128)S(1)} %get-tuple-element.51.refs_0_, f32[192,128]{1,0:T(8,128)S(1)} %get-tuple-element.52.refs_1_), custom_call_target="tpu_custom_call" | custom-call | flops 792723456 | bytes 5000000 | tf_op jit(solution)/shard_map/units_last/pallas_call | solution.py:461
  140.6 4.1 %stage.3.weight_ref = bf16[576,3584]{1,0:T(8,128)(2,1)S(1)} custom-call(s32[6]{0:T(128)S(1)} %copy-done.19, bf16[288,7168]{1,0:T(8,128)(2,1)S(1)} %copy-done.1, bf16[288,3584]{1,0:T(8,128)(2,1)S(1)} %collective-permute-done.26.second_ref), custom_call_target="tpu_custom_call" | custom-call | bytes 4128768 | tf_op jit(solution)/shard_map/stage/pallas_call | solution.py:216
  144.7 2.3 %down.1 = bf16[32,7,24,128]{3,2,1,0:T(8,128)(2,1)S(1)} custom-call(s32[6]{0:T(128)S(1)} %copy-done.19, bf16[192,288]{1,0:T(8,128)(2,1)S(1)} %units_last.1.mine_ref, bf16[192,288]{1,0:T(8,128)(2,1)S(1)} %collective-permute-done.25.theirs_ref, bf16[576,3584]{1,0:T(8,128)(2,1)S(1)} %stage.3.weight_ref, f32[24,896]{1,0:T(8,128)S(1)} %copy-done.17), custom_call_target="tpu_custom_call" | custom-call | flops 792723456 | bytes 6000000 | tf_op jit(solution)/shard_map/down/pallas_call | solution.py:513
  147.0 23.8 %all_to_all.20.parts_ref = bf16[32,7,24,128]{3,2,1,0:T(8,128)(2,1)S(1)} all-to-all(bf16[32,7,24,128]{3,2,1,0:T(8,128)(2,1)S(1)} %down.1), channel_id=1, replica_groups=mesh['zh'=2,'zl'=2,'x'=4,'y'=4,'core'=2] {'zl','x','y'}, dimensions={0} | all-to-all | bytes 2752512 | tf_op jit(solution)/shard_map/all_to_all | solution.py:635
  170.9 0.8 finish.1
  171.7 2.4 %collective-permute-start.27 = (bf16[3,3584]{1,0:T(4,128)(2,1)S(1)}, bf16[3,3584]{1,0:T(4,128)(2,1)S(1)}, u32[]{:S(2)}, u32[]{:S(2)}) collective-permute-start(bf16[3,3584]{1,0:T(4,128)(2,1)S(1)} %get-tuple-element.56), channel_id=1, source_target_pairs={{0,1},{1,0},{2,3},{3,2},{4,5},{5,4},{6,7},{7,6},{8,9},{9,8},{10,11... | collective-permute-start | bytes 64520 | tf_op jit(solution)/shard_map/ppermute | solution.py:28
  174.1 0.9 collective-permute-done.27
  175.0 0.7 pad_maximum_fusion
  (69 shorter events, 0.8 us)
Async XLA Ops:
  0.1 0.9 copy-start.10
  1.0 0.8 copy-start.20
  1.8 14.7 %copy-start.18 = (s32[6]{0:T(128)}, s32[6]{0:T(128)S(1)}, u32[]{:S(2)}) copy-start(s32[6]{0:T(128)S(1)} %stack.24.info_ref) | copy-start | bytes 76
  3.1 13.4 %collective-permute-start = (bf16[5,128,128]{2,1,0:T(8,128)(2,1)S(1)}, bf16[5,128,128]{2,1,0:T(8,128)(2,1)S(1)}, u32[]{:S(2)}, u32[]{:S(2)}) collective-permute-start(bf16[5,128,128]{2,1,0:T(8,128)(2,1)S(1)} %get-tuple-element.31), channel_id=1, source_target_pairs={{0,2},{2,4},{4,6},{6,0},{1,3},{3,5},{5,7},{7,1},{8,10},{10,12},{12... | collective-permute-start | bytes 491528 | tf_op jit(solution)/shard_map/ppermute | solution.py:32
  5.2 11.3 %collective-permute-start.1 = (bf16[5,128,128]{2,1,0:T(8,128)(2,1)S(1)}, bf16[5,128,128]{2,1,0:T(8,128)(2,1)S(1)}, u32[]{:S(2)}, u32[]{:S(2)}) collective-permute-start(bf16[5,128,128]{2,1,0:T(8,128)(2,1)S(1)} %get-tuple-element.32), channel_id=1, source_target_pairs={{0,4},{2,6},{4,0},{6,2},{1,5},{3,7},{5,1},{7,3},{8,12},{10,14},{12... | collective-permute-start | bytes 491528 | tf_op jit(solution)/shard_map/ppermute | solution.py:32
  7.8 8.7 %collective-permute-start.2 = (bf16[5,128,128]{2,1,0:T(8,128)(2,1)S(1)}, bf16[5,128,128]{2,1,0:T(8,128)(2,1)S(1)}, u32[]{:S(2)}, u32[]{:S(2)}) collective-permute-start(bf16[5,128,128]{2,1,0:T(8,128)(2,1)S(1)} %get-tuple-element.33), channel_id=1, source_target_pairs={{0,6},{2,0},{4,2},{6,4},{1,7},{3,1},{5,3},{7,5},{8,14},{10,8},{12,... | collective-permute-start | bytes 491528 | tf_op jit(solution)/shard_map/ppermute | solution.py:32
  16.5 38.0 %all-to-all-start = ((bf16[16,25,8,128]{3,2,1,0:T(8,128)(2,1)}), bf16[16,25,8,128]{3,2,1,0:T(8,128)(2,1)S(1)}, u32[]{:S(2)}, u32[]{:S(2)}) async-start(bf16[16,25,8,128]{3,2,1,0:T(8,128)(2,1)} %attend.1), calls=%async_computation | async-start | bytes 1638400 | tf_op jit(solution)/shard_map/all_to_all | solution.py:595
  24.2 30.4 %copy-start.19 = (s32[6]{0:T(128)S(1)}, s32[6]{0:T(128)}, u32[]{:S(2)}) copy-start(s32[6]{0:T(128)} %copy-done.18) | copy-start | bytes 76
  24.2 30.4 %copy-start.21 = (bf16[48,384]{1,0:T(8,128)(2,1)S(1)}, bf16[48,384]{1,0:T(8,128)(2,1)}, u32[]{:S(2)}) copy-start(bf16[48,384]{1,0:T(8,128)(2,1)} %constant.85.clone.refs_7_) | copy-start | bytes 110596
  24.2 7.4 %collective-permute-start.3 = (bf16[5,128,128]{2,1,0:T(8,128)(2,1)}, bf16[5,128,128]{2,1,0:T(8,128)(2,1)S(1)}, u32[]{:S(2)}, u32[]{:S(2)}) collective-permute-start(bf16[5,128,128]{2,1,0:T(8,128)(2,1)} %get-tuple-element.38.refs_0_), channel_id=1, source_target_pairs={{0,1},{1,0},{2,3},{3,2},{4,5},{5,4},{6,7},{7,6},{8,9},{9,8},{10,11... | collective-permute-start | bytes 491528 | tf_op jit(solution)/shard_map/ppermute | solution.py:28
  26.1 7.4 %collective-permute-start.4 = (bf16[5,128,128]{2,1,0:T(8,128)(2,1)S(1)}, bf16[5,128,128]{2,1,0:T(8,128)(2,1)S(1)}, u32[]{:S(2)}, u32[]{:S(2)}) collective-permute-start(bf16[5,128,128]{2,1,0:T(8,128)(2,1)S(1)} %collective-permute-done.refs_0_.refs_1_), channel_id=1, source_target_pairs={{0,1},{1,0},{2,3},{3,2},{4,5},{5,4},{6,7},{7,6},{8,9},{9,8},{10,11... | collective-permute-start | bytes 491528 | tf_op jit(solution)/shard_map/ppermute | solution.py:28
  26.1 8.2 %collective-permute-start.5 = (bf16[5,128,128]{2,1,0:T(8,128)(2,1)S(1)}, bf16[5,128,128]{2,1,0:T(8,128)(2,1)S(1)}, u32[]{:S(2)}, u32[]{:S(2)}) collective-permute-start(bf16[5,128,128]{2,1,0:T(8,128)(2,1)S(1)} %collective-permute-done.1.refs_1_.refs_2_), channel_id=1, source_target_pairs={{0,1},{1,0},{2,3},{3,2},{4,5},{5,4},{6,7},{7,6},{8,9},{9,8},{10,11... | collective-permute-start | bytes 491528 | tf_op jit(solution)/shard_map/ppermute | solution.py:28
  30.2 40.4 %copy-start = (bf16[128,7168]{1,0:T(8,128)(2,1)S(1)}, bf16[128,7168]{1,0:T(8,128)(2,1)}, u32[]{:S(2)}) copy-start(bf16[128,7168]{1,0:T(8,128)(2,1)} %refs_8_) | copy-start | bytes 5505028
  30.2 13.5 %collective-permute-start.14 = (bf16[7,128,128]{2,1,0:T(8,128)(2,1)}, bf16[7,128,128]{2,1,0:T(8,128)(2,1)S(1)}, u32[]{:S(2)}, u32[]{:S(2)}) collective-permute-start(bf16[7,128,128]{2,1,0:T(8,128)(2,1)} %get-tuple-element.40), channel_id=1, source_target_pairs={{0,2},{2,4},{4,6},{6,0},{1,3},{3,5},{5,7},{7,1},{8,10},{10,12},{12... | collective-permute-start | bytes 688136 | tf_op jit(solution)/shard_map/ppermute | solution.py:32
  30.6 13.8 %collective-permute-start.15 = (bf16[7,128,128]{2,1,0:T(8,128)(2,1)}, bf16[7,128,128]{2,1,0:T(8,128)(2,1)S(1)}, u32[]{:S(2)}, u32[]{:S(2)}) collective-permute-start(bf16[7,128,128]{2,1,0:T(8,128)(2,1)} %get-tuple-element.41), channel_id=1, source_target_pairs={{0,4},{2,6},{4,0},{6,2},{1,5},{3,7},{5,1},{7,3},{8,12},{10,14},{12... | collective-permute-start | bytes 688136 | tf_op jit(solution)/shard_map/ppermute | solution.py:32
  31.6 22.0 %collective-permute-start.18 = (bf16[7,128,128]{2,1,0:T(8,128)(2,1)}, bf16[7,128,128]{2,1,0:T(8,128)(2,1)}, u32[]{:S(2)}, u32[]{:S(2)}) collective-permute-start(bf16[7,128,128]{2,1,0:T(8,128)(2,1)} %get-tuple-element.44), channel_id=1, source_target_pairs={{0,2},{2,4},{4,6},{6,0},{1,3},{3,5},{5,7},{7,1},{8,10},{10,12},{12... | collective-permute-start | bytes 688136 | tf_op jit(solution)/shard_map/ppermute | solution.py:32
  33.5 2.3 %collective-permute-start.6 = (bf16[5,128,128]{2,1,0:T(8,128)(2,1)S(1)}, bf16[5,128,128]{2,1,0:T(8,128)(2,1)S(1)}, u32[]{:S(2)}, u32[]{:S(2)}) collective-permute-start(bf16[5,128,128]{2,1,0:T(8,128)(2,1)S(1)} %collective-permute-done.2.refs_2_.refs_3_), channel_id=1, source_target_pairs={{0,1},{1,0},{2,3},{3,2},{4,5},{5,4},{6,7},{7,6},{8,9},{9,8},{10,11... | collective-permute-start | bytes 491528 | tf_op jit(solution)/shard_map/ppermute | solution.py:28
  34.4 0.7 copy-start.4
  35.0 19.5 %collective-permute-start.20 = (bf16[7,128,128]{2,1,0:T(8,128)(2,1)}, bf16[7,128,128]{2,1,0:T(8,128)(2,1)}, u32[]{:S(2)}, u32[]{:S(2)}) collective-permute-start(bf16[7,128,128]{2,1,0:T(8,128)(2,1)} %get-tuple-element.45), channel_id=1, source_target_pairs={{0,4},{2,6},{4,0},{6,2},{1,5},{3,7},{5,1},{7,3},{8,12},{10,14},{12... | collective-permute-start | bytes 688136 | tf_op jit(solution)/shard_map/ppermute | solution.py:32
  35.8 0.7 copy-start.7
  36.5 22.9 %collective-permute-start.22 = (bf16[7,128,128]{2,1,0:T(8,128)(2,1)}, bf16[7,128,128]{2,1,0:T(8,128)(2,1)}, u32[]{:S(2)}, u32[]{:S(2)}) collective-permute-start(bf16[7,128,128]{2,1,0:T(8,128)(2,1)} %get-tuple-element.46), channel_id=1, source_target_pairs={{0,6},{2,0},{4,2},{6,4},{1,7},{3,1},{5,3},{7,5},{8,14},{10,8},{12,... | collective-permute-start | bytes 688136 | tf_op jit(solution)/shard_map/ppermute | solution.py:32
  43.7 0.7 copy-start.12
  44.4 15.5 %collective-permute-start.16 = (bf16[7,128,128]{2,1,0:T(8,128)(2,1)}, bf16[7,128,128]{2,1,0:T(8,128)(2,1)}, u32[]{:S(2)}, u32[]{:S(2)}) collective-permute-start(bf16[7,128,128]{2,1,0:T(8,128)(2,1)} %get-tuple-element.42), channel_id=1, source_target_pairs={{0,6},{2,0},{4,2},{6,4},{1,7},{3,1},{5,3},{7,5},{8,14},{10,8},{12,... | collective-permute-start | bytes 688136 | tf_op jit(solution)/shard_map/ppermute | solution.py:32
  44.4 0.7 copy-start.14
  45.1 14.8 %collective-permute-start.17 = (bf16[7,128,128]{2,1,0:T(8,128)(2,1)}, bf16[7,128,128]{2,1,0:T(8,128)(2,1)}, u32[]{:S(2)}, u32[]{:S(2)}) collective-permute-start(bf16[7,128,128]{2,1,0:T(8,128)(2,1)} %get-tuple-element.43), channel_id=1, source_target_pairs={{0,1},{1,0},{2,3},{3,2},{4,5},{5,4},{6,7},{7,6},{8,9},{9,8},{10,11... | collective-permute-start | bytes 688136 | tf_op jit(solution)/shard_map/ppermute | solution.py:28
  53.6 6.7 %collective-permute-start.19 = (bf16[7,128,128]{2,1,0:T(8,128)(2,1)}, bf16[7,128,128]{2,1,0:T(8,128)(2,1)}, u32[]{:S(2)}, u32[]{:S(2)}) collective-permute-start(bf16[7,128,128]{2,1,0:T(8,128)(2,1)} %collective-permute-done.18), channel_id=1, source_target_pairs={{0,1},{1,0},{2,3},{3,2},{4,5},{5,4},{6,7},{7,6},{8,9},{9,8},{10,11... | collective-permute-start | bytes 688136 | tf_op jit(solution)/shard_map/ppermute | solution.py:28
  54.5 8.1 %collective-permute-start.21 = (bf16[7,128,128]{2,1,0:T(8,128)(2,1)}, bf16[7,128,128]{2,1,0:T(8,128)(2,1)}, u32[]{:S(2)}, u32[]{:S(2)}) collective-permute-start(bf16[7,128,128]{2,1,0:T(8,128)(2,1)} %collective-permute-done.20), channel_id=1, source_target_pairs={{0,1},{1,0},{2,3},{3,2},{4,5},{5,4},{6,7},{7,6},{8,9},{9,8},{10,11... | collective-permute-start | bytes 688136 | tf_op jit(solution)/shard_map/ppermute | solution.py:28
  54.5 0.9 copy-start.5
  55.5 0.9 copy-start.8
  56.4 0.9 copy-start.11
  59.4 10.2 %collective-permute-start.23 = (bf16[7,128,128]{2,1,0:T(8,128)(2,1)}, bf16[7,128,128]{2,1,0:T(8,128)(2,1)S(1)}, u32[]{:S(2)}, u32[]{:S(2)}) collective-permute-start(bf16[7,128,128]{2,1,0:T(8,128)(2,1)} %collective-permute-done.22), channel_id=1, source_target_pairs={{0,1},{1,0},{2,3},{3,2},{4,5},{5,4},{6,7},{7,6},{8,9},{9,8},{10,11... | collective-permute-start | bytes 688136 | tf_op jit(solution)/shard_map/ppermute | solution.py:28
  59.9 7.9 %collective-permute-start.7 = (bf16[48,1024]{1,0:T(8,128)(2,1)}, bf16[48,1024]{1,0:T(8,128)(2,1)S(1)}, u32[]{:S(2)}, u32[]{:S(2)}) collective-permute-start(bf16[48,1024]{1,0:T(8,128)(2,1)} %join.1.refs_0_), channel_id=1, source_target_pairs={{0,2},{2,4},{4,6},{6,0},{1,3},{3,5},{5,7},{7,1},{8,10},{10,12},{12... | collective-permute-start | bytes 294920 | tf_op jit(solution)/shard_map/ppermute | solution.py:32
  59.9 8.7 %collective-permute-start.8 = (bf16[48,1024]{1,0:T(8,128)(2,1)}, bf16[48,1024]{1,0:T(8,128)(2,1)S(1)}, u32[]{:S(2)}, u32[]{:S(2)}) collective-permute-start(bf16[48,1024]{1,0:T(8,128)(2,1)} %join.1.refs_0_), channel_id=1, source_target_pairs={{0,4},{2,6},{4,0},{6,2},{1,5},{3,7},{5,1},{7,3},{8,12},{10,14},{12... | collective-permute-start | bytes 294920 | tf_op jit(solution)/shard_map/ppermute | solution.py:32
  60.4 8.3 %collective-permute-start.9 = (bf16[48,1024]{1,0:T(8,128)(2,1)}, bf16[48,1024]{1,0:T(8,128)(2,1)}, u32[]{:S(2)}, u32[]{:S(2)}) collective-permute-start(bf16[48,1024]{1,0:T(8,128)(2,1)} %join.1.refs_0_), channel_id=1, source_target_pairs={{0,6},{2,0},{4,2},{6,4},{1,7},{3,1},{5,3},{7,5},{8,14},{10,8},{12,... | collective-permute-start | bytes 294920 | tf_op jit(solution)/shard_map/ppermute | solution.py:32
  62.6 6.9 %collective-permute-start.10 = (bf16[48,1024]{1,0:T(8,128)(2,1)}, bf16[48,1024]{1,0:T(8,128)(2,1)}, u32[]{:S(2)}, u32[]{:S(2)}) collective-permute-start(bf16[48,1024]{1,0:T(8,128)(2,1)} %join.1.refs_0_), channel_id=1, source_target_pairs={{0,1},{1,0},{2,3},{3,2},{4,5},{5,4},{6,7},{7,6},{8,9},{9,8},{10,11... | collective-permute-start | bytes 294920 | tf_op jit(solution)/shard_map/ppermute | solution.py:28
  67.8 1.9 %collective-permute-start.11 = (bf16[48,1024]{1,0:T(8,128)(2,1)S(1)}, bf16[48,1024]{1,0:T(8,128)(2,1)}, u32[]{:S(2)}, u32[]{:S(2)}) collective-permute-start(bf16[48,1024]{1,0:T(8,128)(2,1)S(1)} %collective-permute-done.7.refs_1_), channel_id=1, source_target_pairs={{0,1},{1,0},{2,3},{3,2},{4,5},{5,4},{6,7},{7,6},{8,9},{9,8},{10,11... | collective-permute-start | bytes 294920 | tf_op jit(solution)/shard_map/ppermute | solution.py:28
  68.6 1.4 collective-permute-start.12
  68.6 2.0 %collective-permute-start.13 = (bf16[48,1024]{1,0:T(8,128)(2,1)}, bf16[48,1024]{1,0:T(8,128)(2,1)}, u32[]{:S(2)}, u32[]{:S(2)}) collective-permute-start(bf16[48,1024]{1,0:T(8,128)(2,1)} %collective-permute-done.9.refs_3_), channel_id=1, source_target_pairs={{0,1},{1,0},{2,3},{3,2},{4,5},{5,4},{6,7},{7,6},{8,9},{9,8},{10,11... | collective-permute-start | bytes 294920 | tf_op jit(solution)/shard_map/ppermute | solution.py:28
  69.5 26.7 %copy-start.6 = (bf16[5,128,128]{2,1,0:T(8,128)(2,1)S(1)}, bf16[5,128,128]{2,1,0:T(8,128)(2,1)}, u32[]{:S(2)}) copy-start(bf16[5,128,128]{2,1,0:T(8,128)(2,1)} %copy-done.4) | copy-start | bytes 491524
  69.5 26.7 %copy-start.9 = (bf16[5,128,128]{2,1,0:T(8,128)(2,1)S(1)}, bf16[5,128,128]{2,1,0:T(8,128)(2,1)}, u32[]{:S(2)}) copy-start(bf16[5,128,128]{2,1,0:T(8,128)(2,1)} %copy-done.7) | copy-start | bytes 491524
  70.6 0.9 copy-start.13
  71.6 0.9 copy-start.15
  76.7 19.4 %all-to-all-start.1 = ((bf16[16,24,896]{2,1,0:T(8,128)(2,1)}), bf16[16,24,896]{2,1,0:T(8,128)(2,1)S(1)}, u32[]{:S(2)}, u32[]{:S(2)}) async-start(bf16[16,24,896]{2,1,0:T(8,128)(2,1)} %project.1), calls=%async_computation.1 | async-start | bytes 1376256 | tf_op jit(solution)/shard_map/all_to_all | solution.py:618
  98.5 5.4 %copy-start.16 = (f32[24,896]{1,0:T(8,128)}, f32[24,896]{1,0:T(8,128)S(1)}, u32[]{:S(2)}) copy-start(f32[24,896]{1,0:T(8,128)S(1)} %get-tuple-element.54.held_ref) | copy-start | bytes 258052
  98.5 24.8 %all-to-all-start.2 = ((bf16[32,22,8,128]{3,2,1,0:T(8,128)(2,1)}), bf16[32,22,8,128]{3,2,1,0:T(8,128)(2,1)S(1)}, u32[]{:S(2)}, u32[]{:S(2)}) async-start(bf16[32,22,8,128]{3,2,1,0:T(8,128)(2,1)} %get-tuple-element.48), calls=%async_computation.2 | async-start | bytes 2883584 | tf_op jit(solution)/shard_map/all_to_all | solution.py:626
  107.0 33.6 %collective-permute-start.26 = (bf16[288,3584]{1,0:T(8,128)(2,1)}, bf16[288,3584]{1,0:T(8,128)(2,1)S(1)}, u32[]{:S(2)}, u32[]{:S(2)}) collective-permute-start(bf16[288,3584]{1,0:T(8,128)(2,1)} %constant_dynamic-slice_fusion), channel_id=1, source_target_pairs={{0,1},{1,0},{2,3},{3,2},{4,5},{5,4},{6,7},{7,6},{8,9},{9,8},{10,11... | collective-permute-start | bytes 6193160 | tf_op jit(solution)/shard_map/ppermute | solution.py:28
  123.4 14.7 %collective-permute-start.24 = (bf16[8,4,22,8,128]{4,3,2,1,0:T(8,128)(2,1)S(1)}, bf16[8,4,22,8,128]{4,3,2,1,0:T(8,128)(2,1)S(1)}, u32[]{:S(2)}, u32[]{:S(2)}) collective-permute-start(bf16[8,4,22,8,128]{4,3,2,1,0:T(8,128)(2,1)S(1)} %bitcast.11), channel_id=1, source_target_pairs={{0,1},{1,0},{2,3},{3,2},{4,5},{5,4},{6,7},{7,6},{8,9},{9,8},{10,11... | collective-permute-start | bytes 4325384 | tf_op jit(solution)/shard_map/ppermute | solution.py:28
  125.8 2.2 %copy-start.2 = (bf16[7168,288]{0,1:T(8,128)(2,1)S(1)}, bf16[7168,288]{0,1:T(8,128)(2,1)}, u32[]{:S(2)}) copy-start(bf16[7168,288]{0,1:T(8,128)(2,1)} %param.18) | copy-start | bytes 12386308
  128.0 2.2 %copy-start.3 = (bf16[7168,288]{0,1:T(8,128)(2,1)S(1)}, bf16[7168,288]{0,1:T(8,128)(2,1)}, u32[]{:S(2)}) copy-start(bf16[7168,288]{0,1:T(8,128)(2,1)} %param.19) | copy-start | bytes 12386308
  138.1 2.5 %copy-start.1 = (bf16[288,7168]{1,0:T(8,128)(2,1)S(1)}, bf16[288,7168]{1,0:T(8,128)(2,1)}, u32[]{:S(2)}) copy-start(bf16[288,7168]{1,0:T(8,128)(2,1)} %first_ref) | copy-start | bytes 12386308
  140.5 4.2 %copy-start.17 = (f32[24,896]{1,0:T(8,128)S(1)}, f32[24,896]{1,0:T(8,128)}, u32[]{:S(2)}) copy-start(f32[24,896]{1,0:T(8,128)} %copy-done.16) | copy-start | bytes 258052
  140.5 4.2 %collective-permute-start.25 = (bf16[192,288]{1,0:T(8,128)(2,1)S(1)}, bf16[192,288]{1,0:T(8,128)(2,1)S(1)}, u32[]{:S(2)}, u32[]{:S(2)}) collective-permute-start(bf16[192,288]{1,0:T(8,128)(2,1)S(1)} %units_last.1.mine_ref), channel_id=1, source_target_pairs={{0,1},{1,0},{2,3},{3,2},{4,5},{5,4},{6,7},{7,6},{8,9},{9,8},{10,11... | collective-permute-start | bytes 331784 | tf_op jit(solution)/shard_map/ppermute | solution.py:28
  171.7 3.3 %collective-permute-start.27 = (bf16[3,3584]{1,0:T(4,128)(2,1)S(1)}, bf16[3,3584]{1,0:T(4,128)(2,1)S(1)}, u32[]{:S(2)}, u32[]{:S(2)}) collective-permute-start(bf16[3,3584]{1,0:T(4,128)(2,1)S(1)} %get-tuple-element.56), channel_id=1, source_target_pairs={{0,1},{1,0},{2,3},{3,2},{4,5},{5,4},{6,7},{7,6},{8,9},{9,8},{10,11... | collective-permute-start | bytes 64520 | tf_op jit(solution)/shard_map/ppermute | solution.py:28

commit v6 on v5

--- a/solution.py
+++ b/solution.py
@@ -21,7 +21,6 @@
 F32 = jnp.float32
 BF16 = jnp.bfloat16
 VMEM_MOST = 60 * 1024 * 1024
-VMEM_SOME = 24 * 1024 * 1024
 
 
 def swap(array):
@@ -36,37 +35,67 @@
     return lax.dynamic_slice_in_dim(array, index * size, size, axis)
 
 
-def params(limit, *semantics):
-    return pltpu.CompilerParams(
-        vmem_limit_bytes=limit, dimension_semantics=semantics or None
-    )
-
-
-def cost(flops, read):
-    return pl.CostEstimate(flops=flops, bytes_accessed=read, transcendentals=0)
-
-
-WHOLE = pl.BlockSpec(memory_space=pltpu.VMEM)
+ANYWHERE = pl.BlockSpec(memory_space=pl.ANY)
+
+
+def full(shape):
+    return pl.BlockSpec(shape, lambda i, *info: (0,) * len(shape))
+
+
+def call(kernel, name, scalars, arrays, specs, outs, scratch=(), work=None):
+    single = not isinstance(outs, list)
+    shapes = [outs] if single else outs
+    return pl.pallas_call(
+        kernel,
+        out_shape=outs,
+        grid_spec=pltpu.PrefetchScalarGridSpec(
+            num_scalar_prefetch=len(scalars),
+            grid=(1,),
+            in_specs=[full(a.shape) if s is None else s for a, s in zip(arrays, specs)],
+            out_specs=full(outs.shape) if single else [full(o.shape) for o in outs],
+            scratch_shapes=list(scratch),
+        ),
+        compiler_params=pltpu.CompilerParams(
+            vmem_limit_bytes=VMEM_MOST, dimension_semantics=("arbitrary",)
+        ),
+        cost_estimate=pl.CostEstimate(
+            flops=work or 0,
+            bytes_accessed=2 * sum(math.prod(a.shape) for a in list(arrays) + shapes),
+            transcendentals=0,
+        ),
+        name=name,
+    )(*scalars, *arrays)
 
 
 def rounded(value):
     return value.astype(BF16).astype(F32)
 
 
-def attend_kernel(rows, info_ref, query_ref, cache_ref, out_ref, stats):
-    count, _, heads = query_ref.shape
+def attend_kernel(info_ref, lengths_ref, query_hbm, cache_hbm, out_ref, query_ref, cache_ref, sems):
+    rows, _, heads = query_ref.shape
     keys = cache_ref.shape[2]
+    pairs = rows // 2
+    copies = [pltpu.make_async_copy(query_hbm, query_ref, sems.at[pairs])] + [
+        pltpu.make_async_copy(
+            cache_hbm.at[pl.ds(2 * pair, 2)], cache_ref.at[pl.ds(2 * pair, 2)], sems.at[pair]
+        )
+        for pair in range(pairs)
+    ]
+    for copy in copies:
+        copy.start()
+    copies[0].wait()
     tiles = [slice(start, start + LANES) for start in range(0, LAT, LANES)]
-    position = lax.broadcasted_iota(jnp.int32, (1, keys), 1) + info_ref[rows]
+    position = lax.broadcasted_iota(jnp.int32, (1, keys), 1) + info_ref[6] * keys
     lane = lax.broadcasted_iota(jnp.int32, (heads, LANES), 1)
-    table = stats[...]
-    for index in range(count):
-        row = pl.program_id(0) * count + index
-        cached = cache_ref[index]
+    table = jnp.zeros((heads, LANES), F32)
+    for row in range(rows):
+        if row % 2 == 0:
+            copies[1 + row // 2].wait()
+        cached = cache_ref[row]
         scores = lax.dot_general(
-            query_ref[index], cached, (((0,), (0,)), ((), ())), preferred_element_type=F32
+            query_ref[row], cached, (((0,), (0,)), ((), ())), preferred_element_type=F32
         ) * (1.0 / math.sqrt(QKD))
-        usable = position < info_ref[row]
+        usable = position < lengths_ref[row]
         scores = jnp.where(usable, scores, F32(-1e30))
         top = jnp.max(scores, axis=1, keepdims=True)
         top_high = rounded(top)
@@ -89,40 +118,31 @@
         table = jnp.where(lane == row + SUB, top_low, table)
         table = jnp.where(lane == row + 2 * SUB, total_high, table)
         table = jnp.where(lane == row + 3 * SUB, total_low, table)
-    stats[...] = table
-
-    @pl.when(pl.program_id(0) == pl.num_programs(0) - 1)
-    def _():
-        out_ref[:, rows * len(tiles)] = (
-            stats[...].reshape(heads // SUB, SUB, LANES).astype(BF16)
-        )
-
-
-def attend(info, query, cache):
+    out_ref[:, rows * len(tiles)] = table.reshape(heads // SUB, SUB, LANES).astype(BF16)
+
+
+def attend(info, lengths, query, cache):
     rows, depth, heads = query.shape
     keys = cache.shape[2]
-    count = 2
     shape = (heads // SUB, rows * (LAT // LANES) + 1, SUB, LANES)
-    return pl.pallas_call(
-        functools.partial(attend_kernel, rows),
-        out_shape=jax.ShapeDtypeStruct(shape, BF16),
-        grid_spec=pltpu.PrefetchScalarGridSpec(
-            num_scalar_prefetch=1,
-            grid=(rows // count,),
-            in_specs=[
-                pl.BlockSpec((count, depth, heads), lambda r, info: (r, 0, 0)),
-                pl.BlockSpec((count, depth, keys), lambda r, info: (r, 0, 0)),
-            ],
-            out_specs=pl.BlockSpec(shape, lambda r, info: (0, 0, 0, 0)),
-            scratch_shapes=[pltpu.VMEM((heads, LANES), F32)],
-        ),
-        compiler_params=params(VMEM_MOST, "arbitrary"),
-        cost_estimate=cost(2 * rows * heads * keys * (depth + LAT), 5_000_000),
-        name="attend",
-    )(info, query, cache)
-
-
-def early_kernel(info_ref, up_ref, stream_ref, *outs):
+    return call(
+        attend_kernel,
+        "attend",
+        [info, lengths],
+        [query, cache],
+        [ANYWHERE, ANYWHERE],
+        jax.ShapeDtypeStruct(shape, BF16),
+        [
+            pltpu.VMEM(query.shape, BF16),
+            pltpu.VMEM(cache.shape, BF16),
+            pltpu.SemaphoreType.DMA((rows // 2 + 1,)),
+        ],
+        2 * rows * heads * keys * (depth + LAT),
+    )
+
+
+def early_kernel(info_ref, up_ref, stream_ref, half_ref, send_ref, *outs):
+    send_ref[...] = half_ref[...]
     rows, width = stream_ref.shape
     eighth = width // 8
     ups = up_ref.shape[1] // LANES
@@ -140,31 +160,35 @@
         out_ref[ups] = jnp.concatenate(lines, axis=0).astype(BF16)
 
 
-def early(info, value_up, stream):
-    shape = (value_up.shape[1] // LANES + 1, LANES, LANES)
-    return pl.pallas_call(
+def early(info, value_up, stream, out_proj):
+    part = jax.ShapeDtypeStruct((value_up.shape[1] // LANES + 1, LANES, LANES), BF16)
+    half = (out_proj.shape[0], out_proj.shape[1] // 2)
+    return call(
         early_kernel,
-        out_shape=[jax.ShapeDtypeStruct(shape, BF16)] * 4,
-        in_specs=[pl.BlockSpec(memory_space=pltpu.SMEM), WHOLE, WHOLE],
-        out_specs=[WHOLE] * 4,
-        compiler_params=params(VMEM_SOME),
-        cost_estimate=cost(0, 800_000),
-        name="early",
-    )(info, value_up, stream)
+        "early",
+        [info],
+        [value_up, stream, out_proj],
+        [None, None, pl.BlockSpec(half, lambda i, info: (0, info[4]))],
+        [jax.ShapeDtypeStruct(half, BF16)] + [part] * 4,
+    )
 
 
 def cut_kernel(info_ref, *refs):
     del info_ref
-    count = len(refs) // 2
-    for source, out_ref in zip(refs[:count], refs[count:]):
-        for index in range(out_ref.shape[0]):
-            out_ref[index] = source[:, index * LANES : index * LANES + LANES]
-
-
-def cut(info, out_proj):
-    rows, width = out_proj.shape
-    eighth = width // 8
-    shape = (eighth // LANES, rows, LANES)
+    steps = len(refs) // 3
+    for step in range(steps):
+        out_ref = refs[2 * steps + step]
+        columns = out_ref.shape[0] // 2
+        for side in range(2):
+            for column in range(columns):
+                span = slice(column * LANES, column * LANES + LANES)
+                out_ref[side * columns + column] = refs[side * steps + step][:, span]
+
+
+def cut(info, mine, theirs):
+    rows, half = theirs.shape
+    eighth = half // 4
+    part = jax.ShapeDtypeStruct((2 * eighth // LANES, rows, LANES), BF16)
 
     def column(side, step):
         return pl.BlockSpec(
@@ -172,57 +196,14 @@
             lambda i, info: (0, info[side] * 4 + lax.rem(info[5] + step, 4)),
         )
 
-    return pl.pallas_call(
+    return call(
         cut_kernel,
-        out_shape=[jax.ShapeDtypeStruct(shape, BF16)] * 7,
-        grid_spec=pltpu.PrefetchScalarGridSpec(
-            num_scalar_prefetch=1,
-            grid=(1,),
-            in_specs=[column(4, step) for step in range(4)]
-            + [column(3, step) for step in range(1, 4)],
-            out_specs=[pl.BlockSpec(shape, lambda i, info: (0, 0, 0))] * 7,
-        ),
-        compiler_params=params(VMEM_MOST, "arbitrary"),
-        cost_estimate=cost(0, 4_000_000),
-        name="cut",
-    )(info, *([out_proj] * 7))
-
-
-def stage_kernel(info_ref, first_ref, second_ref, out_ref, sems):
-    rows, width = first_ref.shape
-    columns = out_ref.shape[1]
-    lines = rows // 9
-    copies = []
-    for index, ref in enumerate((first_ref, second_ref)):
-        for piece in range(9):
-            span = pl.ds(piece * lines, lines)
-            place = pl.ds(index * rows + piece * lines, lines)
-            if ref.shape[1] == columns:
-                source = ref.at[span, :]
-            else:
-                start = pl.multiple_of(info_ref[3] * columns, LANES)
-                source = ref.at[span, pl.ds(start, columns)]
-            copies.append(
-                pltpu.make_async_copy(source, out_ref.at[place, :], sems.at[index * 9 + piece])
-            )
-    for copy in copies:
-        copy.start()
-    for copy in copies:
-        copy.wait()
-
-
-def stage(info, first, second):
-    anywhere = pl.BlockSpec(memory_space=pl.ANY)
-    return pl.pallas_call(
-        stage_kernel,
-        out_shape=jax.ShapeDtypeStruct((2 * first.shape[0], second.shape[1]), BF16),
-        in_specs=[pl.BlockSpec(memory_space=pltpu.SMEM), anywhere, anywhere],
-        out_specs=WHOLE,
-        scratch_shapes=[pltpu.SemaphoreType.DMA((18,))],
-        compiler_params=params(VMEM_SOME),
-        cost_estimate=cost(0, 2 * second.size * 2),
-        name="stage",
-    )(info, first, second)
+        "cut",
+        [info],
+        [mine] * 3 + [theirs] * 3,
+        [column(3, step) for step in (1, 2, 3)] + [column(7, step) for step in (1, 2, 3)],
+        [part] * 3,
+    )
 
 
 def join_kernel(rows, info_ref, recv_ref, own_ref, *refs):
@@ -275,20 +256,21 @@
     devs = received.shape[0] // 2
     count = rows * devs
     sums = np.repeat(np.eye(count, dtype=np.float32), SUB, axis=1)
-    return pl.pallas_call(
+    arrays = [received, value_up, *firsts, *theirs, jnp.asarray(sums, BF16)]
+    return call(
         functools.partial(join_kernel, rows),
-        out_shape=jax.ShapeDtypeStruct((count, SUB * LANES), BF16),
-        in_specs=[pl.BlockSpec(memory_space=pltpu.SMEM)] + [WHOLE] * 10,
-        out_specs=WHOLE,
-        compiler_params=params(VMEM_SOME),
-        cost_estimate=cost(480_000_000, 3_000_000),
-        name="join",
-    )(info, received, value_up, *firsts, *theirs, jnp.asarray(sums, BF16))
+        "join",
+        [info],
+        arrays,
+        [None] * len(arrays),
+        jax.ShapeDtypeStruct((count, SUB * LANES), BF16),
+        work=480_000_000,
+    )
 
 
 def project_kernel(info_ref, place_ref, *refs):
-    values, own_ref = refs[:8], refs[8]
-    seconds, theirs, out_ref = refs[9:12], refs[12:16], refs[16]
+    values, own_ref, theirs_ref = refs[:8], refs[8], refs[9]
+    parts, out_ref = refs[10:13], refs[13]
     del info_ref
     rows = []
     for source, ref in enumerate(values):
@@ -306,39 +288,32 @@
     order = jnp.where(order, F32(1.0), F32(0.0)).astype(BF16)
     left = jnp.dot(order, left, preferred_element_type=F32).astype(BF16)
     columns = own_ref.shape[1] // LANES
-    right = [own_ref[...]]
-    for ref in seconds + theirs:
-        first = ref.shape[0] - columns
-        right.append(
-            jnp.concatenate([ref[first + column] for column in range(columns)], axis=1)
-        )
+    right = []
+    for side, held_ref in enumerate((own_ref, theirs_ref)):
+        right.append(held_ref[...])
+        for ref in parts:
+            tiles = [ref[side * columns + column] for column in range(columns)]
+            right.append(jnp.concatenate(tiles, axis=1))
     right = jnp.concatenate(right, axis=0)
     total = jnp.dot(left, right, preferred_element_type=F32)
     out_ref[...] = total.reshape(out_ref.shape).astype(BF16)
 
 
-def project(info, place, values, out_proj, seconds, theirs, chips):
+def project(info, place, values, out_proj, out_theirs, parts, chips):
     rows = sum(value.shape[0] for value in values)
     lanes = out_proj.shape[0]
     eighth = out_proj.shape[1] // 8
-    full = lambda shape: pl.BlockSpec(shape, lambda i, info: (0,) * len(shape))
     own = pl.BlockSpec((lanes, eighth), lambda i, info: (0, info[0]))
-    return pl.pallas_call(
+    other = pl.BlockSpec((lanes, eighth), lambda i, info: (0, info[5]))
+    return call(
         project_kernel,
-        out_shape=jax.ShapeDtypeStruct((chips, rows // chips, eighth), BF16),
-        grid_spec=pltpu.PrefetchScalarGridSpec(
-            num_scalar_prefetch=1,
-            grid=(1,),
-            in_specs=[full(place.shape)]
-            + [full(value.shape) for value in values]
-            + [own]
-            + [full(part.shape) for part in seconds + theirs],
-            out_specs=full((chips, rows // chips, eighth)),
-        ),
-        compiler_params=params(VMEM_SOME, "arbitrary"),
-        cost_estimate=cost(2 * rows * 8 * lanes * eighth, 3_500_000),
-        name="project",
-    )(info, place, *values, out_proj, *seconds, *theirs)
+        "project",
+        [info],
+        [place, *values, out_proj, out_theirs, *parts],
+        [None] * 9 + [own, other] + [None] * 3,
+        jax.ShapeDtypeStruct((chips, rows // chips, eighth), BF16),
+        work=2 * rows * 8 * lanes * eighth,
+    )
 
 
 def residual_kernel(parts_ref, place_ref, gain_ref, *refs):
@@ -388,26 +363,44 @@
 def residual_rows(parts, place, gain, blocks, chips):
     _, rows, width = parts.shape
     tiles = rows * width // (SUB * LANES) + 1
-    return pl.pallas_call(
+    last = blocks[0].shape[0] - 1
+    line = pl.BlockSpec((1, LANES, LANES), lambda i: (last, 0, 0))
+    return call(
         residual_kernel,
-        out_shape=(
+        "residual",
+        [],
+        [parts, place, gain, *blocks],
+        [None] * 3 + [line] * 8,
+        [
             jax.ShapeDtypeStruct((rows, width), F32),
             jax.ShapeDtypeStruct((chips, tiles, SUB, LANES), BF16),
-        ),
-        in_specs=[WHOLE] * 11,
-        out_specs=(WHOLE, WHOLE),
-        compiler_params=params(VMEM_SOME),
-        cost_estimate=cost(2_000_000, 2_500_000),
-        name="residual",
-    )(parts, place, gain, *blocks)
-
-
-def units_kernel(groups, last, info_ref, recv_ref, weight_ref, *refs):
+        ],
+    )
+
+
+def units_kernel(groups, last, info_ref, recv_ref, gate_hbm, up_hbm, *refs):
+    weight_ref, sems = refs[-2:]
+    refs = refs[:-2]
     sides, quarters, tiles, _, _ = recv_ref.shape
     columns = (tiles - 1) // groups
     rows = sides * groups * SUB
     depth = columns * LANES
     which = 4 if last else 3
+    hidden = gate_hbm.shape[0]
+    copies = []
+    for quarter in range(quarters):
+        start = pl.multiple_of((info_ref[which] * quarters + quarter) * depth, LANES)
+        for index, ref in enumerate((gate_hbm, up_hbm)):
+            target = weight_ref.at[
+                pl.ds(index * hidden, hidden), pl.ds(quarter * depth, depth)
+            ]
+            copies.append(
+                pltpu.make_async_copy(
+                    ref.at[:, pl.ds(start, depth)], target, sems.at[2 * quarter + index]
+                )
+            )
+    for copy in copies:
+        copy.start()
     lane = lax.broadcasted_iota(jnp.int32, (SUB, LANES), 1)
     total = squares = None
     for quarter in range(quarters):
@@ -420,10 +413,11 @@
             ],
             axis=1,
         ).astype(BF16)
-        start = pl.multiple_of((info_ref[which] * quarters + quarter) * depth, LANES)
+        copies[2 * quarter].wait()
+        copies[2 * quarter + 1].wait()
         part = lax.dot_general(
             left,
-            weight_ref[:, pl.ds(start, depth)],
+            weight_ref[:, quarter * depth : quarter * depth + depth],
             (((1,), (1,)), ((), ())),
             preferred_element_type=F32,
         )
@@ -445,45 +439,66 @@
         sq_ref[...] = jnp.broadcast_to(squares, (rows, LANES))
     else:
         acc_ref, sq_ref, out_ref = refs
-        hidden = out_ref.shape[1]
-        scale = lax.rsqrt((sq_ref[:, :1] + squares) / weight_ref.shape[1] + 1e-06)
+        scale = lax.rsqrt((sq_ref[:, :1] + squares) / gate_hbm.shape[1] + 1e-06)
         total = total + acc_ref[...]
         gate = total[:, :hidden] * scale
         upper = total[:, hidden:] * scale
         out_ref[...] = (gate / (1.0 + jnp.exp(-gate)) * upper).astype(BF16)
 
 
-def units(info, received, weight, groups, carry=()):
+def units(info, received, gate, up, groups, carry=()):
     sides, quarters, tiles = received.shape[:3]
-    hidden = weight.shape[0] // 2
+    hidden, width = gate.shape
     rows = sides * groups * SUB
     last = bool(carry)
-    return pl.pallas_call(
+    return call(
         functools.partial(units_kernel, groups, last),
-        out_shape=jax.ShapeDtypeStruct((rows, hidden), BF16)
+        "units_last" if last else "units_first",
+        [info],
+        [received, gate, up, *carry],
+        [None, ANYWHERE, ANYWHERE] + [None] * len(carry),
+        jax.ShapeDtypeStruct((rows, hidden), BF16)
         if last
         else [
             jax.ShapeDtypeStruct((rows, 2 * hidden), F32),
             jax.ShapeDtypeStruct((rows, LANES), F32),
         ],
-        in_specs=[pl.BlockSpec(memory_space=pltpu.SMEM)] + [WHOLE] * (2 + len(carry)),
-        out_specs=WHOLE if last else [WHOLE, WHOLE],
-        compiler_params=params(VMEM_SOME),
-        cost_estimate=cost(2 * rows * weight.size // 2, 5_000_000),
-        name="units_last" if last else "units_first",
-    )(info, received, weight, *carry)
-
-
-def down_kernel(info_ref, mine_ref, theirs_ref, weight_ref, held_ref, out_ref, total):
+        [
+            pltpu.VMEM((2 * hidden, width // 2), BF16),
+            pltpu.SemaphoreType.DMA((2 * quarters,)),
+        ],
+        2 * rows * hidden * width,
+    )
+
+
+def down_kernel(
+    info_ref, mine_ref, theirs_ref, own_hbm, other_hbm, held_ref, out_ref, total, weight_ref, sems
+):
     chips, steps = out_ref.shape[:2]
     rows = mine_ref.shape[0]
     count = rows // chips
+    hidden, half = other_hbm.shape
+    width = 4 * LANES
+    copies = []
+    for piece in range(0, half, width):
+        for index, ref in enumerate((own_hbm, other_hbm)):
+            start = info_ref[3] * half + piece if index == 0 else piece
+            copies.append(
+                pltpu.make_async_copy(
+                    ref.at[:, pl.ds(pl.multiple_of(start, LANES), width)],
+                    weight_ref.at[pl.ds(index * hidden, hidden), pl.ds(piece, width)],
+                    sems.at[len(copies)],
+                )
+            )
+    for copy in copies:
+        copy.start()
     left = jnp.concatenate(
         [mine_ref[...].astype(F32), theirs_ref[...].astype(F32)], axis=1
     ).astype(BF16)
-    width = 4 * LANES
     for step in range(steps):
         span = slice(step * width, step * width + width)
+        copies[2 * step].wait()
+        copies[2 * step + 1].wait()
         total[:rows, span] = jnp.dot(
             left, weight_ref[:, span], preferred_element_type=F32
         )
@@ -507,19 +522,24 @@
             out_ref[chip, step] = jnp.concatenate(packed, axis=0).astype(BF16)
 
 
-def down(info, mine, theirs, weight, held, chips):
+def down(info, mine, theirs, down_proj, other, held, chips):
     rows = mine.shape[0]
-    half = weight.shape[1]
-    return pl.pallas_call(
+    hidden, half = other.shape
+    steps = half // (4 * LANES)
+    return call(
         down_kernel,
-        out_shape=jax.ShapeDtypeStruct((chips, half // (4 * LANES), 3 * SUB, LANES), BF16),
-        in_specs=[pl.BlockSpec(memory_space=pltpu.SMEM)] + [WHOLE] * 4,
-        out_specs=WHOLE,
-        scratch_shapes=[pltpu.VMEM((rows + SUB, half), F32)],
-        compiler_params=params(VMEM_SOME),
-        cost_estimate=cost(2 * rows * weight.size, 6_000_000),
-        name="down",
-    )(info, mine, theirs, weight, held)
+        "down",
+        [info],
+        [mine, theirs, down_proj, other, held],
+        [None, None, ANYWHERE, ANYWHERE, None],
+        jax.ShapeDtypeStruct((chips, steps, 3 * SUB, LANES), BF16),
+        [
+            pltpu.VMEM((rows + SUB, half), F32),
+            pltpu.VMEM((2 * hidden, half), BF16),
+            pltpu.SemaphoreType.DMA((2 * steps,)),
+        ],
+        4 * rows * hidden * half,
+    )
 
 
 def finish_kernel(info_ref, parts_ref, mine_ref, theirs_ref):
@@ -543,15 +563,7 @@
 
 def finish(info, parts):
     shape = jax.ShapeDtypeStruct((3, parts.shape[1] * 4 * LANES), BF16)
-    return pl.pallas_call(
-        finish_kernel,
-        out_shape=(shape, shape),
-        in_specs=[pl.BlockSpec(memory_space=pltpu.SMEM), WHOLE],
-        out_specs=(WHOLE, WHOLE),
-        compiler_params=params(VMEM_SOME),
-        cost_estimate=cost(1_000_000, 1_500_000),
-        name="finish",
-    )(info, parts)
+    return call(finish_kernel, "finish", [info], [parts], [None], [shape, shape])
 
 
 def local(
@@ -574,24 +586,22 @@
     half = width // 2
     eighth = width // 8
     first = core == 0
-    info = jnp.stack([core * 4 + ring, core, group, core, 1 - core, ring]).astype(jnp.int32)
-
-    own, *starts = early(info, value_up, stream)
+    info = [core * 4 + ring, core, group, core, 1 - core, ring, lax.axis_index("zh"), 0]
+    info = jnp.stack(info).astype(jnp.int32)
+
+    out_send, own, *starts = early(info, value_up, stream, out_proj)
+    out_theirs = swap(out_send)
     firsts = [shift(part, step) for step, part in zip((1, 2, 3), starts)]
     gain = block(norm_gain, core * 4 + ring, eighth, 0)[None]
 
-    offset = lax.axis_index("zh") * latent_cache.shape[1]
     payload = attend(
-        jnp.concatenate([lengths, offset[None].astype(jnp.int32)]),
-        query_latent.transpose(0, 2, 1),
-        latent_cache.transpose(0, 2, 1),
-    )
-    payload, out_proj, *firsts = lax.optimization_barrier((payload, out_proj, *firsts))
+        info, lengths, query_latent.transpose(0, 2, 1), latent_cache.transpose(0, 2, 1)
+    )
+    payload, out_theirs, *firsts = lax.optimization_barrier((payload, out_theirs, *firsts))
     firsts_theirs = [swap(part) for part in [own] + firsts]
-    cuts = cut(info, out_proj)
-    others = [cuts[0]] + [shift(part, step) for step, part in zip((1, 2, 3), cuts[1:4])]
-    seconds = [shift(part, step) for step, part in zip((1, 2, 3), cuts[4:])]
-    theirs = [swap(part) for part in others]
+    parts = [
+        shift(part, step) for step, part in zip((1, 2, 3), cut(info, out_proj, out_theirs))
+    ]
     received = lax.all_to_all(payload, OUTER, split_axis=0, concat_axis=0, tiled=True)
     values = join(info, received, value_up, firsts, firsts_theirs, rows)
 
@@ -611,8 +621,8 @@
         place,
         ring_values + [swap(piece) for piece in ring_values],
         out_proj,
-        seconds,
-        theirs,
+        out_theirs,
+        parts,
         16,
     )
     parts = lax.all_to_all(partial, OUTER, split_axis=0, concat_axis=0, tiled=True)
@@ -627,11 +637,11 @@
     piece = piece.reshape((8, 4) + piece.shape[1:])
     other = swap(piece)
     down_theirs = swap(block(down_proj, 1 - core, half, 1))
-    weight = stage(info, gate_proj.T, up_proj.T)
+    gate_proj, up_proj = gate_proj.T, up_proj.T
     groups = 8 * rows_own // SUB
-    carry = units(info, piece, weight, groups)
-    hidden = units(info, other, weight, groups, carry)
-    partial = down(info, hidden, swap(hidden), stage(info, down_proj, down_theirs), residual, 32)
+    carry = units(info, piece, gate_proj, up_proj, groups)
+    hidden = units(info, other, gate_proj, up_proj, groups, carry)
+    partial = down(info, hidden, swap(hidden), down_proj, down_theirs, residual, 32)
     parts = lax.all_to_all(partial, SIDE_CHIPS, split_axis=0, concat_axis=0, tiled=True)
     mine, theirs = finish(info, parts)
     theirs = swap(theirs)

time: 177 us -> 172 us (0.972)
  Pallas kernels: 37.4 us -> 47 us
  local copies, waits for them, and re-layouts: 17.5 us -> 9.85 us
  waiting for transfers between devices: 46.1 us -> 39.8 us
    unnamed x44 -> x46, local copies, waits for them, and re-layouts: 13.4 us -> 3.58 us
    ppermute x12 -> x9, waiting for transfers between devices: 17.2 us -> 7.62 us  [shift(): return lax.ppermute(array, 'y', [(i, (i + step) % 4) for i in range(4)])]
    pallas_call x12 -> x10, Pallas kernels: 37.4 us -> 47 us  [call(): pl.pallas_call(kernel, out_shape=outs, grid_spec=pltpu.PrefetchScalarGrid...]
    all_to_all x1, waiting for transfers between devices: 0.01 us -> 2.68 us  [local(): lax.all_to_all(payload, OUTER, split_axis=0, concat_axis=0, tiled=True)]
    ppermute x16 -> x13, starting transfers between devices: 14.4 us -> 16 us  [swap(): return lax.ppermute(array, 'core', SWAP)]
    ppermute x12 -> x9, starting transfers between devices: 14 us -> 12.6 us  [shift(): return lax.ppermute(array, 'y', [(i, (i + step) % 4) for i in range(4)])]
  transfers between devices with their start and end apart: 31 -> 25, of which waited for: 9 -> 11; matrix products, arithmetic and copies ran while one was open for 3% -> 3% of each run, Pallas kernels for 15% -> 16%
where the time goes in v6:
time: 172 us; the launch traced here: 171 us
  starting transfers between devices  48.3 us (28%)
  Pallas kernels  47 us (27%)
  waiting for transfers between devices  39.8 us (23%)
  blocking collectives  24.6 us (14%)
  local copies, waits for them, and re-layouts  9.85 us (6%)
    pallas_call x10, Pallas kernels, call(): pl.pallas_call(kernel, out_shape=outs, grid_spec=pltpu.PrefetchScalarGrid...  47 us
    all_to_all x1, blocking collectives, local(): lax.all_to_all(partial, SIDE_CHIPS, split_axis=0, concat_axis=0, tiled=True)  24.6 us
    ppermute x13, starting transfers between devices, swap(): return lax.ppermute(array, 'core', SWAP)  16 us
    all_to_all x1, waiting for transfers between devices, local(): lax.all_to_all(payload, SIDE_CHIPS, split_axis=0, concat_axis=0, tiled=True)  15.7 us
    ppermute x9, starting transfers between devices, shift(): return lax.ppermute(array, 'y', [(i, (i + step) % 4) for i in range(4)])  12.6 us
    all_to_all x1, waiting for transfers between devices, local(): lax.all_to_all(partial, OUTER, split_axis=0, concat_axis=0, tiled=True)  10.8 us
    ppermute x9, waiting for transfers between devices, shift(): return lax.ppermute(array, 'y', [(i, (i + step) % 4) for i in range(4)])  7.62 us
    all_to_all x1, starting transfers between devices, local(): lax.all_to_all(payload, OUTER, split_axis=0, concat_axis=0, tiled=True)  7.61 us
  transfers between devices with their start and end apart: 25, of which 11 were waited for; matrix products, arithmetic and copies ran while one was open for 3% of the time, Pallas kernels for 16%

profile of v6, /device:TPU:1, one launch (start us, length us, event | category | flops | bytes accessed | tf_op | source)
XLA Modules:
  0.0 171.4 jit_solution(9151255734161306240)
XLA Ops:
  0.0 0.6 stack.28.info_ref
  0.6 3.1 %early.1 = (bf16[128,3584]{1,0:T(8,128)(2,1)}, bf16[5,128,128]{2,1,0:T(8,128)(2,1)}, bf16[5,128,128]{2,1,0:T(8,128)(2,1)}, bf16[5,128,128]{2,1,0:T(8,128)(2,1)}, bf16[5,128,128]{2,1,0:T(8,128)(2,1)}) custom-call(s32[8]{0:T(128)} %stack.28.info_ref, bf16[1,512,128]{2,1,0:T(8,128)(2,1)} %own_ref.1, bf16[3,7168]{1,0:T(4,128)(2,1)} %stream_ref.1, ...), custom_call_target="tpu_custom_call" | custom-call | bytes 3581952 | tf_op jit(solution)/shard_map/early/pallas_call | solution.py:48
  3.8 1.4 collective-permute-start
  5.2 1.4 collective-permute-start.1
  6.6 2.6 %collective-permute-start.2 = (bf16[5,128,128]{2,1,0:T(8,128)(2,1)}, bf16[5,128,128]{2,1,0:T(8,128)(2,1)S(1)}, u32[]{:S(2)}, u32[]{:S(2)}) collective-permute-start(bf16[5,128,128]{2,1,0:T(8,128)(2,1)} %get-tuple-element.30), channel_id=1, source_target_pairs={{0,4},{2,6},{4,0},{6,2},{1,5},{3,7},{5,1},{7,3},{8,12},{10,14},{12... | collective-permute-start | bytes 491528 | tf_op jit(solution)/shard_map/ppermute | solution.py:31
  9.2 1.1 collective-permute-start.3
  10.3 6.2 %attend.1 = bf16[16,25,8,128]{3,2,1,0:T(8,128)(2,1)} custom-call(s32[8]{0:T(128)} %stack.28.info_ref, s32[6]{0:T(128)} %lengths_ref.1, bf16[6,576,128]{2,1,0:T(8,128)(2,1)} %bitcast.18, bf16[6,576,512]{2,1,0:T(8,128)(2,1)} %bitcast.17), custom_call_target="tpu_custom_call" | custom-call | flops 855638016 | bytes 5242880 | tf_op jit(solution)/shard_map/attend/pallas_call | solution.py:48
  16.5 0.8 collective-permute-done.2.refs_1_.refs_2_
  17.3 7.6 %all-to-all-start = ((bf16[16,25,8,128]{3,2,1,0:T(8,128)(2,1)}), bf16[16,25,8,128]{3,2,1,0:T(8,128)(2,1)S(1)}, u32[]{:S(2)}, u32[]{:S(2)}) async-start(bf16[16,25,8,128]{3,2,1,0:T(8,128)(2,1)} %attend.1), calls=%async_computation | async-start | bytes 1638400 | tf_op jit(solution)/shard_map/all_to_all | solution.py:605
  24.9 3.6 %cut.1 = (bf16[14,128,128]{2,1,0:T(8,128)(2,1)}, bf16[14,128,128]{2,1,0:T(8,128)(2,1)}, bf16[14,128,128]{2,1,0:T(8,128)(2,1)}) custom-call(s32[8]{0:T(128)} %stack.28.info_ref, bf16[128,7168]{1,0:T(8,128)(2,1)} %refs_8_.1, bf16[128,7168]{1,0:T(8,128)(2,1)} %refs_8_.1, bf16[128,7168]{1,0:T(8,128)(2,1)} %refs_8_.1, bf16[128,3584]{1,0:T(8,128)(2,1)} %copy-done, ...), custom_call_target="tpu_custom_call" | custom-call | bytes 9633792 | tf_op jit(solution)/shard_map/cut/pallas_call | solution.py:48
  28.5 0.4 collective-permute-start.15
  28.9 1.8 %collective-permute-start.4 = (bf16[5,128,128]{2,1,0:T(8,128)(2,1)S(1)}, bf16[5,128,128]{2,1,0:T(8,128)(2,1)S(1)}, u32[]{:S(2)}, u32[]{:S(2)}) collective-permute-start(bf16[5,128,128]{2,1,0:T(8,128)(2,1)S(1)} %copy-done.14), channel_id=1, source_target_pairs={{0,1},{1,0},{2,3},{3,2},{4,5},{5,4},{6,7},{7,6},{8,9},{9,8},{10,11... | collective-permute-start | bytes 491528 | tf_op jit(solution)/shard_map/ppermute | solution.py:27
  30.7 2.1 %collective-permute-start.16 = (bf16[14,128,128]{2,1,0:T(8,128)(2,1)}, bf16[14,128,128]{2,1,0:T(8,128)(2,1)S(1)}, u32[]{:S(2)}, u32[]{:S(2)}) collective-permute-start(bf16[14,128,128]{2,1,0:T(8,128)(2,1)} %get-tuple-element.39), channel_id=1, source_target_pairs={{0,4},{2,6},{4,0},{6,2},{1,5},{3,7},{5,1},{7,3},{8,12},{10,14},{12... | collective-permute-start | bytes 1376264 | tf_op jit(solution)/shard_map/ppermute | solution.py:31
  32.8 0.3 collective-permute-start.5
  33.1 0.2 collective-permute-start.6
  33.3 0.4 collective-permute-start.7
  33.7 0.5 collective-permute-done.5.refs_4_.refs_5_
  34.2 1.4 collective-permute-start.17
  35.7 2.7 %all-to-all-done.recv_ref = bf16[16,25,8,128]{3,2,1,0:T(8,128)(2,1)S(1)} async-done(((bf16[16,25,8,128]{3,2,1,0:T(8,128)(2,1)}), bf16[16,25,8,128]{3,2,1,0:T(8,128)(2,1)S(1)}, u32[]{:S(2)}, u32[]{:S(2)}) %all-to-all-start) | async-done | bytes 819232 | tf_op jit(solution)/shard_map/all_to_all | solution.py:605
  38.4 0.9 copy-done.2
  39.2 3.8 %join.1.refs_0_ = bf16[48,1024]{1,0:T(8,128)(2,1)} custom-call(s32[8]{0:T(128)} %stack.28.info_ref, bf16[16,25,8,128]{3,2,1,0:T(8,128)(2,1)} %copy-done.2, bf16[1,512,128]{2,1,0:T(8,128)(2,1)} %own_ref.1, bf16[5,128,128]{2,1,0:T(8,128)(2,1)} %copy-done.5, bf16[5,128,128]{2,1,0:T(8,128)(2,1)} %copy-done.6, bf16[5,128,128]{2,1,0:T(8,128)(2,1)} %copy-done.7, ...), custom_call_target="tpu_custom_call" | custom-call | flops 480000000 | bytes 2232320 | tf_op jit(solution)/shard_map/join/pallas_call | solution.py:48
  43.1 3.6 %collective-permute-start.9 = (bf16[48,1024]{1,0:T(8,128)(2,1)}, bf16[48,1024]{1,0:T(8,128)(2,1)S(1)}, u32[]{:S(2)}, u32[]{:S(2)}) collective-permute-start(bf16[48,1024]{1,0:T(8,128)(2,1)} %join.1.refs_0_), channel_id=1, source_target_pairs={{0,4},{2,6},{4,0},{6,2},{1,5},{3,7},{5,1},{7,3},{8,12},{10,14},{12... | collective-permute-start | bytes 294920 | tf_op jit(solution)/shard_map/ppermute | solution.py:31
  46.6 0.1 collective-permute-start.10
  46.8 4.9 %collective-permute-done.16.refs_11_ = bf16[14,128,128]{2,1,0:T(8,128)(2,1)S(1)} collective-permute-done((bf16[14,128,128]{2,1,0:T(8,128)(2,1)}, bf16[14,128,128]{2,1,0:T(8,128)(2,1)S(1)}, u32[]{:S(2)}, u32[]{:S(2)}) %collective-permute-start.16) | collective-permute-done | bytes 458784 | tf_op jit(solution)/shard_map/ppermute | solution.py:31
  51.6 3.0 %collective-permute-start.11 = (bf16[48,1024]{1,0:T(8,128)(2,1)}, bf16[48,1024]{1,0:T(8,128)(2,1)S(1)}, u32[]{:S(2)}, u32[]{:S(2)}) collective-permute-start(bf16[48,1024]{1,0:T(8,128)(2,1)} %join.1.refs_0_), channel_id=1, source_target_pairs={{0,1},{1,0},{2,3},{3,2},{4,5},{5,4},{6,7},{7,6},{8,9},{9,8},{10,11... | collective-permute-start | bytes 294920 | tf_op jit(solution)/shard_map/ppermute | solution.py:27
  54.6 1.3 collective-permute-done.8.refs_1_
  55.9 0.5 collective-permute-start.12
  56.4 1.1 collective-permute-start.13
  57.5 0.6 collective-permute-done.10.refs_3_
  58.1 0.8 collective-permute-start.14
  58.9 0.1 broadcast_add_fusion
  59.0 0.6 add.106.place_ref
  59.7 0.2 collective-permute-done.14.refs_7_
  59.9 0.4 copy-done.19
  60.3 0.1 copy-done.20
  60.3 0.0 copy-done.21
  60.4 0.6 copy-done.22
  61.0 4.7 %project.1 = bf16[16,24,896]{2,1,0:T(8,128)(2,1)} custom-call(s32[8]{0:T(128)} %stack.28.info_ref, s32[1,384]{1,0:T(1,128)} %add.106.place_ref, bf16[48,1024]{1,0:T(8,128)(2,1)} %join.1.refs_0_, bf16[48,1024]{1,0:T(8,128)(2,1)} %copy-done.16, bf16[48,1024]{1,0:T(8,128)(2,1)} %copy-done.17, bf16[48,1024]{1,0:T(8,128)(2,1)} %copy-done.18, ...), custom_call_target="tpu_custom_call" | custom-call | flops 704643072 | bytes 5604096 | tf_op jit(solution)/shard_map/project/pallas_call | solution.py:48
  65.7 6.9 %all-to-all-start.1 = ((bf16[16,24,896]{2,1,0:T(8,128)(2,1)}), bf16[16,24,896]{2,1,0:T(8,128)(2,1)S(1)}, u32[]{:S(2)}, u32[]{:S(2)}) async-start(bf16[16,24,896]{2,1,0:T(8,128)(2,1)} %project.1), calls=%async_computation.1 | async-start | bytes 1376256 | tf_op jit(solution)/shard_map/all_to_all | solution.py:628
  72.7 0.1 add_select_fusion
  72.7 0.6 select_n.82.place_ref
  73.3 0.8 dynamic_slice.6
  74.1 0.6 broadcast_in_dim.30.gain_ref
  74.7 10.8 %all-to-all-done.1.parts_ref = bf16[16,24,896]{2,1,0:T(8,128)(2,1)S(1)} async-done(((bf16[16,24,896]{2,1,0:T(8,128)(2,1)}), bf16[16,24,896]{2,1,0:T(8,128)(2,1)S(1)}, u32[]{:S(2)}, u32[]{:S(2)}) %all-to-all-start.1) | async-done | bytes 688160 | tf_op jit(solution)/shard_map/all_to_all | solution.py:628
  85.5 0.9 copy-done.3
  86.4 2.6 %residual.1 = (f32[24,896]{1,0:T(8,128)}, bf16[32,22,8,128]{3,2,1,0:T(8,128)(2,1)}) custom-call(bf16[16,24,896]{2,1,0:T(8,128)(2,1)} %copy-done.3, s32[1,64]{1,0:T(1,128)} %select_n.82.place_ref, f32[1,896]{1,0:T(1,128)} %broadcast_in_dim.30.gain_ref, bf16[5,128,128]{2,1,0:T(8,128)(2,1)} %get-tuple-element.36.refs_0_, bf16[5,128,128]{2,1,0:T(8,128)(2,1)} %copy-done.5, ...), custom_call_target="tpu_custom_call" | custom-call | bytes 3485568 | tf_op jit(solution)/shard_map/residual/pallas_call | solution.py:48
  89.0 5.1 %all-to-all-start.2 = ((bf16[32,22,8,128]{3,2,1,0:T(8,128)(2,1)}), bf16[32,22,8,128]{3,2,1,0:T(8,128)(2,1)S(1)}, u32[]{:S(2)}, u32[]{:S(2)}) async-start(bf16[32,22,8,128]{3,2,1,0:T(8,128)(2,1)} %get-tuple-element.42), calls=%async_computation.2 | async-start | bytes 2883584 | tf_op jit(solution)/shard_map/all_to_all | solution.py:636
  94.1 3.0 %constant_dynamic-slice_fusion = bf16[288,3584]{1,0:T(8,128)(2,1)} fusion(bf16[288,7168]{1,0:T(8,128)(2,1)} %own_hbm, s32[]{:T(128)S(6)} %select_n.84), kind=kLoop, calls=%fused_computation.22 | loop fusion | bytes 4128772 | tf_op jit(solution)/shard_map/dynamic_slice | solution.py:35
  97.2 1.0 collective-permute-start.20
  98.2 15.7 %all-to-all-done.2 = bf16[32,22,8,128]{3,2,1,0:T(8,128)(2,1)S(1)} async-done(((bf16[32,22,8,128]{3,2,1,0:T(8,128)(2,1)}), bf16[32,22,8,128]{3,2,1,0:T(8,128)(2,1)S(1)}, u32[]{:S(2)}, u32[]{:S(2)}) %all-to-all-start.2) | async-done | bytes 1441824 | tf_op jit(solution)/shard_map/all_to_all | solution.py:636
  113.9 2.3 %collective-permute-start.18 = (bf16[8,4,22,8,128]{4,3,2,1,0:T(8,128)(2,1)S(1)}, bf16[8,4,22,8,128]{4,3,2,1,0:T(8,128)(2,1)}, u32[]{:S(2)}, u32[]{:S(2)}) collective-permute-start(bf16[8,4,22,8,128]{4,3,2,1,0:T(8,128)(2,1)S(1)} %bitcast.15), channel_id=1, source_target_pairs={{0,1},{1,0},{2,3},{3,2},{4,5},{5,4},{6,7},{7,6},{8,9},{9,8},{10,11... | collective-permute-start | bytes 4325384 | tf_op jit(solution)/shard_map/ppermute | solution.py:27
  116.2 6.6 %units_first.1 = (f32[192,576]{1,0:T(8,128)}, f32[192,128]{1,0:T(8,128)}) custom-call(s32[8]{0:T(128)} %stack.28.info_ref, bf16[8,4,22,8,128]{4,3,2,1,0:T(8,128)(2,1)} %bitcast.16, bf16[288,7168]{1,0:T(8,128)(2,1)} %bitcast.11, bf16[288,7168]{1,0:T(8,128)(2,1)} %bitcast.13), custom_call_target="tpu_custom_call" | custom-call | flops 792723456 | bytes 9969664 | tf_op jit(solution)/shard_map/units_first/pallas_call | solution.py:48
  122.8 6.7 %units_last.1.mine_ref = bf16[192,288]{1,0:T(8,128)(2,1)} custom-call(s32[8]{0:T(128)} %stack.28.info_ref, bf16[8,4,22,8,128]{4,3,2,1,0:T(8,128)(2,1)} %collective-permute-done.18.recv_ref, bf16[288,7168]{1,0:T(8,128)(2,1)} %bitcast.12, bf16[288,7168]{1,0:T(8,128)(2,1)} %bitcast.14, f32[192,576]{1,0:T(8,128)} %get-tuple-element.45.refs_0_, ...), custom_call_target="tpu_custom_call" | custom-call | flops 792723456 | bytes 10080256 | tf_op jit(solution)/shard_map/units_last/pallas_call | solution.py:48
  129.6 1.2 collective-permute-start.19
  130.8 1.2 collective-permute-done.19.theirs_ref
  132.0 0.1 copy-done.4
  132.1 0.5 copy-done.15
  132.6 6.8 %down.1 = bf16[32,7,24,128]{3,2,1,0:T(8,128)(2,1)} custom-call(s32[8]{0:T(128)} %stack.28.info_ref, bf16[192,288]{1,0:T(8,128)(2,1)} %units_last.1.mine_ref, bf16[192,288]{1,0:T(8,128)(2,1)} %copy-done.15, bf16[288,7168]{1,0:T(8,128)(2,1)} %own_hbm, bf16[288,3584]{1,0:T(8,128)(2,1)} %copy-done.4, f32[24,896]{1,0:T(8,128)} %get-tuple-element.48.held_ref), custom_call_target="tpu_custom_call" | custom-call | flops 792723456 | bytes 7833600 | tf_op jit(solution)/shard_map/down/pallas_call | solution.py:48
  139.4 24.6 %all_to_all.20.parts_ref = bf16[32,7,24,128]{3,2,1,0:T(8,128)(2,1)} all-to-all(bf16[32,7,24,128]{3,2,1,0:T(8,128)(2,1)} %down.1), channel_id=1, replica_groups=mesh['zh'=2,'zl'=2,'x'=4,'y'=4,'core'=2] {'zl','x','y'}, dimensions={0} | all-to-all | bytes 2752512 | tf_op jit(solution)/shard_map/all_to_all | solution.py:645
  164.1 2.9 %finish.1 = (bf16[3,3584]{1,0:T(4,128)(2,1)}, bf16[3,3584]{1,0:T(4,128)(2,1)}) custom-call(s32[8]{0:T(128)} %stack.28.info_ref, bf16[32,7,24,128]{3,2,1,0:T(8,128)(2,1)} %all_to_all.20.parts_ref), custom_call_target="tpu_custom_call" | custom-call | bytes 1419264 | tf_op jit(solution)/shard_map/finish/pallas_call | solution.py:48
  167.0 2.0 %collective-permute-start.21 = (bf16[3,3584]{1,0:T(4,128)(2,1)}, bf16[3,3584]{1,0:T(4,128)(2,1)S(1)}, u32[]{:S(2)}, u32[]{:S(2)}) collective-permute-start(bf16[3,3584]{1,0:T(4,128)(2,1)} %get-tuple-element.50), channel_id=1, source_target_pairs={{0,1},{1,0},{2,3},{3,2},{4,5},{5,4},{6,7},{7,6},{8,9},{9,8},{10,11... | collective-permute-start | bytes 64520 | tf_op jit(solution)/shard_map/ppermute | solution.py:27
  168.9 1.1 collective-permute-done.21
  170.0 0.8 broadcast_select_fusion.1
  170.8 0.7 pad_maximum_fusion
  (56 shorter events, 0.2 us)
Async XLA Ops:
  3.8 13.5 %collective-permute-start = (bf16[128,3584]{1,0:T(8,128)(2,1)}, bf16[128,3584]{1,0:T(8,128)(2,1)S(1)}, u32[]{:S(2)}, u32[]{:S(2)}) collective-permute-start(bf16[128,3584]{1,0:T(8,128)(2,1)} %get-tuple-element.28), channel_id=1, source_target_pairs={{0,1},{1,0},{2,3},{3,2},{4,5},{5,4},{6,7},{7,6},{8,9},{9,8},{10,11... | collective-permute-start | bytes 2752520 | tf_op jit(solution)/shard_map/ppermute | solution.py:27
  5.2 11.3 %collective-permute-start.1 = (bf16[5,128,128]{2,1,0:T(8,128)(2,1)}, bf16[5,128,128]{2,1,0:T(8,128)(2,1)S(1)}, u32[]{:S(2)}, u32[]{:S(2)}) collective-permute-start(bf16[5,128,128]{2,1,0:T(8,128)(2,1)} %get-tuple-element.29), channel_id=1, source_target_pairs={{0,2},{2,4},{4,6},{6,0},{1,3},{3,5},{5,7},{7,1},{8,10},{10,12},{12... | collective-permute-start | bytes 491528 | tf_op jit(solution)/shard_map/ppermute | solution.py:31
  6.6 10.7 %collective-permute-start.2 = (bf16[5,128,128]{2,1,0:T(8,128)(2,1)}, bf16[5,128,128]{2,1,0:T(8,128)(2,1)S(1)}, u32[]{:S(2)}, u32[]{:S(2)}) collective-permute-start(bf16[5,128,128]{2,1,0:T(8,128)(2,1)} %get-tuple-element.30), channel_id=1, source_target_pairs={{0,4},{2,6},{4,0},{6,2},{1,5},{3,7},{5,1},{7,3},{8,12},{10,14},{12... | collective-permute-start | bytes 491528 | tf_op jit(solution)/shard_map/ppermute | solution.py:31
  9.2 8.1 %collective-permute-start.3 = (bf16[5,128,128]{2,1,0:T(8,128)(2,1)}, bf16[5,128,128]{2,1,0:T(8,128)(2,1)S(1)}, u32[]{:S(2)}, u32[]{:S(2)}) collective-permute-start(bf16[5,128,128]{2,1,0:T(8,128)(2,1)} %get-tuple-element.31), channel_id=1, source_target_pairs={{0,6},{2,0},{4,2},{6,4},{1,7},{3,1},{5,3},{7,5},{8,14},{10,8},{12,... | collective-permute-start | bytes 491528 | tf_op jit(solution)/shard_map/ppermute | solution.py:31
  16.5 16.3 %copy-start.5 = (bf16[5,128,128]{2,1,0:T(8,128)(2,1)}, bf16[5,128,128]{2,1,0:T(8,128)(2,1)S(1)}, u32[]{:S(2)}) copy-start(bf16[5,128,128]{2,1,0:T(8,128)(2,1)S(1)} %collective-permute-done.1.refs_0_.refs_1_) | copy-start | bytes 491524
  17.3 15.8 %copy-start.6 = (bf16[5,128,128]{2,1,0:T(8,128)(2,1)}, bf16[5,128,128]{2,1,0:T(8,128)(2,1)S(1)}, u32[]{:S(2)}) copy-start(bf16[5,128,128]{2,1,0:T(8,128)(2,1)S(1)} %collective-permute-done.2.refs_1_.refs_2_) | copy-start | bytes 491524
  17.3 16.0 %copy-start.7 = (bf16[5,128,128]{2,1,0:T(8,128)(2,1)}, bf16[5,128,128]{2,1,0:T(8,128)(2,1)S(1)}, u32[]{:S(2)}) copy-start(bf16[5,128,128]{2,1,0:T(8,128)(2,1)S(1)} %collective-permute-done.3.refs_2_.refs_3_) | copy-start | bytes 491524
  17.3 7.6 %copy-start = (bf16[128,3584]{1,0:T(8,128)(2,1)}, bf16[128,3584]{1,0:T(8,128)(2,1)S(1)}, u32[]{:S(2)}) copy-start(bf16[128,3584]{1,0:T(8,128)(2,1)S(1)} %collective-permute-done.refs_3_.refs_4_.refs_5_.refs_9_) | copy-start | bytes 2752516
  17.3 21.0 %all-to-all-start = ((bf16[16,25,8,128]{3,2,1,0:T(8,128)(2,1)}), bf16[16,25,8,128]{3,2,1,0:T(8,128)(2,1)S(1)}, u32[]{:S(2)}, u32[]{:S(2)}) async-start(bf16[16,25,8,128]{3,2,1,0:T(8,128)(2,1)} %attend.1), calls=%async_computation | async-start | bytes 1638400 | tf_op jit(solution)/shard_map/all_to_all | solution.py:605
  24.9 3.9 %copy-start.14 = (bf16[5,128,128]{2,1,0:T(8,128)(2,1)S(1)}, bf16[5,128,128]{2,1,0:T(8,128)(2,1)}, u32[]{:S(2)}) copy-start(bf16[5,128,128]{2,1,0:T(8,128)(2,1)} %get-tuple-element.36.refs_0_) | copy-start | bytes 491524
  28.5 18.1 %collective-permute-start.15 = (bf16[14,128,128]{2,1,0:T(8,128)(2,1)}, bf16[14,128,128]{2,1,0:T(8,128)(2,1)S(1)}, u32[]{:S(2)}, u32[]{:S(2)}) collective-permute-start(bf16[14,128,128]{2,1,0:T(8,128)(2,1)} %get-tuple-element.38), channel_id=1, source_target_pairs={{0,2},{2,4},{4,6},{6,0},{1,3},{3,5},{5,7},{7,1},{8,10},{10,12},{12... | collective-permute-start | bytes 1376264 | tf_op jit(solution)/shard_map/ppermute | solution.py:31
  28.9 4.5 %collective-permute-start.4 = (bf16[5,128,128]{2,1,0:T(8,128)(2,1)S(1)}, bf16[5,128,128]{2,1,0:T(8,128)(2,1)S(1)}, u32[]{:S(2)}, u32[]{:S(2)}) collective-permute-start(bf16[5,128,128]{2,1,0:T(8,128)(2,1)S(1)} %copy-done.14), channel_id=1, source_target_pairs={{0,1},{1,0},{2,3},{3,2},{4,5},{5,4},{6,7},{7,6},{8,9},{9,8},{10,11... | collective-permute-start | bytes 491528 | tf_op jit(solution)/shard_map/ppermute | solution.py:27
  30.7 20.9 %collective-permute-start.16 = (bf16[14,128,128]{2,1,0:T(8,128)(2,1)}, bf16[14,128,128]{2,1,0:T(8,128)(2,1)S(1)}, u32[]{:S(2)}, u32[]{:S(2)}) collective-permute-start(bf16[14,128,128]{2,1,0:T(8,128)(2,1)} %get-tuple-element.39), channel_id=1, source_target_pairs={{0,4},{2,6},{4,0},{6,2},{1,5},{3,7},{5,1},{7,3},{8,12},{10,14},{12... | collective-permute-start | bytes 1376264 | tf_op jit(solution)/shard_map/ppermute | solution.py:31
  32.8 1.4 collective-permute-start.5
  33.1 2.5 %collective-permute-start.6 = (bf16[5,128,128]{2,1,0:T(8,128)(2,1)S(1)}, bf16[5,128,128]{2,1,0:T(8,128)(2,1)S(1)}, u32[]{:S(2)}, u32[]{:S(2)}) collective-permute-start(bf16[5,128,128]{2,1,0:T(8,128)(2,1)S(1)} %collective-permute-done.2.refs_1_.refs_2_), channel_id=1, source_target_pairs={{0,1},{1,0},{2,3},{3,2},{4,5},{5,4},{6,7},{7,6},{8,9},{9,8},{10,11... | collective-permute-start | bytes 491528 | tf_op jit(solution)/shard_map/ppermute | solution.py:27
  33.3 5.0 %copy-start.8 = (bf16[5,128,128]{2,1,0:T(8,128)(2,1)}, bf16[5,128,128]{2,1,0:T(8,128)(2,1)S(1)}, u32[]{:S(2)}) copy-start(bf16[5,128,128]{2,1,0:T(8,128)(2,1)S(1)} %collective-permute-done.4.refs_3_.refs_4_) | copy-start | bytes 491524
  33.3 2.3 %collective-permute-start.7 = (bf16[5,128,128]{2,1,0:T(8,128)(2,1)S(1)}, bf16[5,128,128]{2,1,0:T(8,128)(2,1)S(1)}, u32[]{:S(2)}, u32[]{:S(2)}) collective-permute-start(bf16[5,128,128]{2,1,0:T(8,128)(2,1)S(1)} %collective-permute-done.3.refs_2_.refs_3_), channel_id=1, source_target_pairs={{0,1},{1,0},{2,3},{3,2},{4,5},{5,4},{6,7},{7,6},{8,9},{9,8},{10,11... | collective-permute-start | bytes 491528 | tf_op jit(solution)/shard_map/ppermute | solution.py:27
  34.2 4.1 %copy-start.9 = (bf16[5,128,128]{2,1,0:T(8,128)(2,1)}, bf16[5,128,128]{2,1,0:T(8,128)(2,1)S(1)}, u32[]{:S(2)}) copy-start(bf16[5,128,128]{2,1,0:T(8,128)(2,1)S(1)} %collective-permute-done.5.refs_4_.refs_5_) | copy-start | bytes 491524
  34.2 25.4 %collective-permute-start.17 = (bf16[14,128,128]{2,1,0:T(8,128)(2,1)}, bf16[14,128,128]{2,1,0:T(8,128)(2,1)}, u32[]{:S(2)}, u32[]{:S(2)}) collective-permute-start(bf16[14,128,128]{2,1,0:T(8,128)(2,1)} %get-tuple-element.40), channel_id=1, source_target_pairs={{0,6},{2,0},{4,2},{6,4},{1,7},{3,1},{5,3},{7,5},{8,14},{10,8},{12,... | collective-permute-start | bytes 1376264 | tf_op jit(solution)/shard_map/ppermute | solution.py:31
  35.6 2.7 %copy-start.10 = (bf16[5,128,128]{2,1,0:T(8,128)(2,1)}, bf16[5,128,128]{2,1,0:T(8,128)(2,1)S(1)}, u32[]{:S(2)}) copy-start(bf16[5,128,128]{2,1,0:T(8,128)(2,1)S(1)} %collective-permute-done.6.refs_5_.refs_6_) | copy-start | bytes 491524
  35.6 2.7 %copy-start.11 = (bf16[5,128,128]{2,1,0:T(8,128)(2,1)}, bf16[5,128,128]{2,1,0:T(8,128)(2,1)S(1)}, u32[]{:S(2)}) copy-start(bf16[5,128,128]{2,1,0:T(8,128)(2,1)S(1)} %collective-permute-done.7.refs_6_.refs_7_) | copy-start | bytes 491524
  38.4 0.9 copy-start.2
  43.1 12.9 %collective-permute-start.8 = (bf16[48,1024]{1,0:T(8,128)(2,1)}, bf16[48,1024]{1,0:T(8,128)(2,1)S(1)}, u32[]{:S(2)}, u32[]{:S(2)}) collective-permute-start(bf16[48,1024]{1,0:T(8,128)(2,1)} %join.1.refs_0_), channel_id=1, source_target_pairs={{0,2},{2,4},{4,6},{6,0},{1,3},{3,5},{5,7},{7,1},{8,10},{10,12},{12... | collective-permute-start | bytes 294920 | tf_op jit(solution)/shard_map/ppermute | solution.py:31
  43.1 13.4 %collective-permute-start.9 = (bf16[48,1024]{1,0:T(8,128)(2,1)}, bf16[48,1024]{1,0:T(8,128)(2,1)S(1)}, u32[]{:S(2)}, u32[]{:S(2)}) collective-permute-start(bf16[48,1024]{1,0:T(8,128)(2,1)} %join.1.refs_0_), channel_id=1, source_target_pairs={{0,4},{2,6},{4,0},{6,2},{1,5},{3,7},{5,1},{7,3},{8,12},{10,14},{12... | collective-permute-start | bytes 294920 | tf_op jit(solution)/shard_map/ppermute | solution.py:31
  46.6 13.2 %copy-start.12 = (bf16[14,128,128]{2,1,0:T(8,128)(2,1)}, bf16[14,128,128]{2,1,0:T(8,128)(2,1)S(1)}, u32[]{:S(2)}) copy-start(bf16[14,128,128]{2,1,0:T(8,128)(2,1)S(1)} %collective-permute-done.15.refs_10_) | copy-start | bytes 1376260
  46.6 11.5 %collective-permute-start.10 = (bf16[48,1024]{1,0:T(8,128)(2,1)}, bf16[48,1024]{1,0:T(8,128)(2,1)S(1)}, u32[]{:S(2)}, u32[]{:S(2)}) collective-permute-start(bf16[48,1024]{1,0:T(8,128)(2,1)} %join.1.refs_0_), channel_id=1, source_target_pairs={{0,6},{2,0},{4,2},{6,4},{1,7},{3,1},{5,3},{7,5},{8,14},{10,8},{12,... | collective-permute-start | bytes 294920 | tf_op jit(solution)/shard_map/ppermute | solution.py:31
  51.6 8.2 %copy-start.13 = (bf16[14,128,128]{2,1,0:T(8,128)(2,1)}, bf16[14,128,128]{2,1,0:T(8,128)(2,1)S(1)}, u32[]{:S(2)}) copy-start(bf16[14,128,128]{2,1,0:T(8,128)(2,1)S(1)} %collective-permute-done.16.refs_11_) | copy-start | bytes 1376260
  51.6 8.0 %collective-permute-start.11 = (bf16[48,1024]{1,0:T(8,128)(2,1)}, bf16[48,1024]{1,0:T(8,128)(2,1)S(1)}, u32[]{:S(2)}, u32[]{:S(2)}) collective-permute-start(bf16[48,1024]{1,0:T(8,128)(2,1)} %join.1.refs_0_), channel_id=1, source_target_pairs={{0,1},{1,0},{2,3},{3,2},{4,5},{5,4},{6,7},{7,6},{8,9},{9,8},{10,11... | collective-permute-start | bytes 294920 | tf_op jit(solution)/shard_map/ppermute | solution.py:27
  55.9 3.9 %copy-start.16 = (bf16[48,1024]{1,0:T(8,128)(2,1)}, bf16[48,1024]{1,0:T(8,128)(2,1)S(1)}, u32[]{:S(2)}) copy-start(bf16[48,1024]{1,0:T(8,128)(2,1)S(1)} %collective-permute-done.8.refs_1_) | copy-start | bytes 294916
  55.9 3.7 %collective-permute-start.12 = (bf16[48,1024]{1,0:T(8,128)(2,1)S(1)}, bf16[48,1024]{1,0:T(8,128)(2,1)S(1)}, u32[]{:S(2)}, u32[]{:S(2)}) collective-permute-start(bf16[48,1024]{1,0:T(8,128)(2,1)S(1)} %collective-permute-done.8.refs_1_), channel_id=1, source_target_pairs={{0,1},{1,0},{2,3},{3,2},{4,5},{5,4},{6,7},{7,6},{8,9},{9,8},{10,11... | collective-permute-start | bytes 294920 | tf_op jit(solution)/shard_map/ppermute | solution.py:27
  56.4 3.5 %copy-start.17 = (bf16[48,1024]{1,0:T(8,128)(2,1)}, bf16[48,1024]{1,0:T(8,128)(2,1)S(1)}, u32[]{:S(2)}) copy-start(bf16[48,1024]{1,0:T(8,128)(2,1)S(1)} %collective-permute-done.9.refs_2_) | copy-start | bytes 294916
  56.4 3.2 %collective-permute-start.13 = (bf16[48,1024]{1,0:T(8,128)(2,1)S(1)}, bf16[48,1024]{1,0:T(8,128)(2,1)S(1)}, u32[]{:S(2)}, u32[]{:S(2)}) collective-permute-start(bf16[48,1024]{1,0:T(8,128)(2,1)S(1)} %collective-permute-done.9.refs_2_), channel_id=1, source_target_pairs={{0,1},{1,0},{2,3},{3,2},{4,5},{5,4},{6,7},{7,6},{8,9},{9,8},{10,11... | collective-permute-start | bytes 294920 | tf_op jit(solution)/shard_map/ppermute | solution.py:27
  58.1 1.7 %copy-start.18 = (bf16[48,1024]{1,0:T(8,128)(2,1)}, bf16[48,1024]{1,0:T(8,128)(2,1)S(1)}, u32[]{:S(2)}) copy-start(bf16[48,1024]{1,0:T(8,128)(2,1)S(1)} %collective-permute-done.10.refs_3_) | copy-start | bytes 294916
  58.1 1.7 %collective-permute-start.14 = (bf16[48,1024]{1,0:T(8,128)(2,1)S(1)}, bf16[48,1024]{1,0:T(8,128)(2,1)S(1)}, u32[]{:S(2)}, u32[]{:S(2)}) collective-permute-start(bf16[48,1024]{1,0:T(8,128)(2,1)S(1)} %collective-permute-done.10.refs_3_), channel_id=1, source_target_pairs={{0,1},{1,0},{2,3},{3,2},{4,5},{5,4},{6,7},{7,6},{8,9},{9,8},{10,11... | collective-permute-start | bytes 294920 | tf_op jit(solution)/shard_map/ppermute | solution.py:27
  59.6 0.6 copy-start.19
  59.7 0.7 copy-start.20
  59.7 0.7 copy-start.21
  60.4 0.6 copy-start.22
  65.7 19.8 %all-to-all-start.1 = ((bf16[16,24,896]{2,1,0:T(8,128)(2,1)}), bf16[16,24,896]{2,1,0:T(8,128)(2,1)S(1)}, u32[]{:S(2)}, u32[]{:S(2)}) async-start(bf16[16,24,896]{2,1,0:T(8,128)(2,1)} %project.1), calls=%async_computation.1 | async-start | bytes 1376256 | tf_op jit(solution)/shard_map/all_to_all | solution.py:628
  85.5 0.9 copy-start.3
  89.0 24.9 %all-to-all-start.2 = ((bf16[32,22,8,128]{3,2,1,0:T(8,128)(2,1)}), bf16[32,22,8,128]{3,2,1,0:T(8,128)(2,1)S(1)}, u32[]{:S(2)}, u32[]{:S(2)}) async-start(bf16[32,22,8,128]{3,2,1,0:T(8,128)(2,1)} %get-tuple-element.42), calls=%async_computation.2 | async-start | bytes 2883584 | tf_op jit(solution)/shard_map/all_to_all | solution.py:636
  97.2 33.6 %collective-permute-start.20 = (bf16[288,3584]{1,0:T(8,128)(2,1)}, bf16[288,3584]{1,0:T(8,128)(2,1)S(1)}, u32[]{:S(2)}, u32[]{:S(2)}) collective-permute-start(bf16[288,3584]{1,0:T(8,128)(2,1)} %constant_dynamic-slice_fusion), channel_id=1, source_target_pairs={{0,1},{1,0},{2,3},{3,2},{4,5},{5,4},{6,7},{7,6},{8,9},{9,8},{10,11... | collective-permute-start | bytes 6193160 | tf_op jit(solution)/shard_map/ppermute | solution.py:27
  113.9 2.3 %copy-start.1 = (bf16[32,22,8,128]{3,2,1,0:T(8,128)(2,1)}, bf16[32,22,8,128]{3,2,1,0:T(8,128)(2,1)S(1)}, u32[]{:S(2)}) copy-start(bf16[32,22,8,128]{3,2,1,0:T(8,128)(2,1)S(1)} %all-to-all-done.2) | copy-start | bytes 4325380
  113.9 8.9 %collective-permute-start.18 = (bf16[8,4,22,8,128]{4,3,2,1,0:T(8,128)(2,1)S(1)}, bf16[8,4,22,8,128]{4,3,2,1,0:T(8,128)(2,1)}, u32[]{:S(2)}, u32[]{:S(2)}) collective-permute-start(bf16[8,4,22,8,128]{4,3,2,1,0:T(8,128)(2,1)S(1)} %bitcast.15), channel_id=1, source_target_pairs={{0,1},{1,0},{2,3},{3,2},{4,5},{5,4},{6,7},{7,6},{8,9},{9,8},{10,11... | collective-permute-start | bytes 4325384 | tf_op jit(solution)/shard_map/ppermute | solution.py:27
  129.6 2.4 %collective-permute-start.19 = (bf16[192,288]{1,0:T(8,128)(2,1)}, bf16[192,288]{1,0:T(8,128)(2,1)S(1)}, u32[]{:S(2)}, u32[]{:S(2)}) collective-permute-start(bf16[192,288]{1,0:T(8,128)(2,1)} %units_last.1.mine_ref), channel_id=1, source_target_pairs={{0,1},{1,0},{2,3},{3,2},{4,5},{5,4},{6,7},{7,6},{8,9},{9,8},{10,11... | collective-permute-start | bytes 331784 | tf_op jit(solution)/shard_map/ppermute | solution.py:27
  130.8 1.3 copy-start.4
  132.0 0.7 copy-start.15
  167.0 3.1 %collective-permute-start.21 = (bf16[3,3584]{1,0:T(4,128)(2,1)}, bf16[3,3584]{1,0:T(4,128)(2,1)S(1)}, u32[]{:S(2)}, u32[]{:S(2)}) collective-permute-start(bf16[3,3584]{1,0:T(4,128)(2,1)} %get-tuple-element.50), channel_id=1, source_target_pairs={{0,1},{1,0},{2,3},{3,2},{4,5},{5,4},{6,7},{7,6},{8,9},{9,8},{10,11... | collective-permute-start | bytes 64520 | tf_op jit(solution)/shard_map/ppermute | solution.py:27

commit v7 on v6

--- a/solution.py
+++ b/solution.py
@@ -21,6 +21,8 @@
 F32 = jnp.float32
 BF16 = jnp.bfloat16
 VMEM_MOST = 60 * 1024 * 1024
+VMEM_STAGE = 44 * 1024 * 1024
+VMEM_SOME = 24 * 1024 * 1024
 
 
 def swap(array):
@@ -35,6 +37,7 @@
     return lax.dynamic_slice_in_dim(array, index * size, size, axis)
 
 
+WHOLE = pl.BlockSpec(memory_space=pltpu.VMEM)
 ANYWHERE = pl.BlockSpec(memory_space=pl.ANY)
 
 
@@ -42,7 +45,7 @@
     return pl.BlockSpec(shape, lambda i, *info: (0,) * len(shape))
 
 
-def call(kernel, name, scalars, arrays, specs, outs, scratch=(), work=None):
+def call(kernel, name, scalars, arrays, specs, outs, scratch=(), work=None, limit=VMEM_SOME, out_specs=None):
     single = not isinstance(outs, list)
     shapes = [outs] if single else outs
     return pl.pallas_call(
@@ -52,11 +55,12 @@
             num_scalar_prefetch=len(scalars),
             grid=(1,),
             in_specs=[full(a.shape) if s is None else s for a, s in zip(arrays, specs)],
-            out_specs=full(outs.shape) if single else [full(o.shape) for o in outs],
+            out_specs=out_specs
+            or (full(outs.shape) if single else [full(o.shape) for o in outs]),
             scratch_shapes=list(scratch),
         ),
         compiler_params=pltpu.CompilerParams(
-            vmem_limit_bytes=VMEM_MOST, dimension_semantics=("arbitrary",)
+            vmem_limit_bytes=limit, dimension_semantics=("arbitrary",)
         ),
         cost_estimate=pl.CostEstimate(
             flops=work or 0,
@@ -71,7 +75,12 @@
     return value.astype(BF16).astype(F32)
 
 
-def attend_kernel(info_ref, lengths_ref, query_hbm, cache_hbm, out_ref, query_ref, cache_ref, sems):
+def attend_kernel(
+    info_ref, lengths_ref, query_hbm, cache_hbm, out_proj_hbm, theirs_hbm, out_ref, *refs
+):
+    cuts, (query_ref, cache_ref, weight_ref, sems) = refs[:3], refs[3:]
+    half = theirs_hbm.shape[1]
+    mine = out_proj_hbm.at[:, pl.ds(pl.multiple_of(info_ref[3] * half, LANES), half)]
     rows, _, heads = query_ref.shape
     keys = cache_ref.shape[2]
     pairs = rows // 2
@@ -81,6 +90,10 @@
         )
         for pair in range(pairs)
     ]
+    for side, ref in enumerate((mine, theirs_hbm)):
+        copies.append(
+            pltpu.make_async_copy(ref, weight_ref.at[side], sems.at[pairs + 1 + side])
+        )
     for copy in copies:
         copy.start()
     copies[0].wait()
@@ -119,25 +132,38 @@
         table = jnp.where(lane == row + 2 * SUB, total_high, table)
         table = jnp.where(lane == row + 3 * SUB, total_low, table)
     out_ref[:, rows * len(tiles)] = table.reshape(heads // SUB, SUB, LANES).astype(BF16)
-
-
-def attend(info, lengths, query, cache):
+    copies[-2].wait()
+    copies[-1].wait()
+    for step, cut_ref in enumerate(cuts):
+        columns = cut_ref.shape[0] // 2
+        first = lax.rem(info_ref[5] + step + 1, 4) * columns
+        for side in range(2):
+            for column in range(columns):
+                start = pl.multiple_of((first + column) * LANES, LANES)
+                cut_ref[side * columns + column] = weight_ref[side, :, pl.ds(start, LANES)]
+
+
+def attend(info, lengths, query, cache, out_proj, theirs):
     rows, depth, heads = query.shape
     keys = cache.shape[2]
     shape = (heads // SUB, rows * (LAT // LANES) + 1, SUB, LANES)
+    columns = out_proj.shape[1] // 8 // LANES
     return call(
         attend_kernel,
         "attend",
         [info, lengths],
-        [query, cache],
-        [ANYWHERE, ANYWHERE],
-        jax.ShapeDtypeStruct(shape, BF16),
+        [query, cache, out_proj, theirs],
+        [ANYWHERE] * 4,
+        [jax.ShapeDtypeStruct(shape, BF16)]
+        + [jax.ShapeDtypeStruct((2 * columns, LANES, LANES), BF16)] * 3,
         [
             pltpu.VMEM(query.shape, BF16),
             pltpu.VMEM(cache.shape, BF16),
-            pltpu.SemaphoreType.DMA((rows // 2 + 1,)),
+            pltpu.VMEM((2,) + theirs.shape, BF16),
+            pltpu.SemaphoreType.DMA((rows // 2 + 3,)),
         ],
         2 * rows * heads * keys * (depth + LAT),
+        VMEM_MOST,
     )
 
 
@@ -170,44 +196,63 @@
         [value_up, stream, out_proj],
         [None, None, pl.BlockSpec(half, lambda i, info: (0, info[4]))],
         [jax.ShapeDtypeStruct(half, BF16)] + [part] * 4,
-    )
-
-
-def cut_kernel(info_ref, *refs):
-    del info_ref
-    steps = len(refs) // 3
-    for step in range(steps):
-        out_ref = refs[2 * steps + step]
-        columns = out_ref.shape[0] // 2
-        for side in range(2):
-            for column in range(columns):
-                span = slice(column * LANES, column * LANES + LANES)
-                out_ref[side * columns + column] = refs[side * steps + step][:, span]
-
-
-def cut(info, mine, theirs):
-    rows, half = theirs.shape
-    eighth = half // 4
-    part = jax.ShapeDtypeStruct((2 * eighth // LANES, rows, LANES), BF16)
-
-    def column(side, step):
-        return pl.BlockSpec(
-            (rows, eighth),
-            lambda i, info: (0, info[side] * 4 + lax.rem(info[5] + step, 4)),
+        limit=VMEM_MOST,
+    )
+
+
+def stage_kernel(info_ref, gate_ref, up_ref, down_ref, out_ref, own_ref, send_ref, sems):
+    rows = gate_ref.shape[0]
+    half = own_ref.shape[1]
+    sides = [
+        down_ref.at[:, pl.ds(pl.multiple_of(info_ref[side] * half, LANES), half)]
+        for side in (4, 3)
+    ]
+    copies = [
+        pltpu.make_async_copy(source, target, sems.at[index])
+        for index, (source, target) in enumerate(
+            [
+                (sides[0], send_ref),
+                (gate_ref, out_ref.at[pl.ds(0, rows), :]),
+                (up_ref, out_ref.at[pl.ds(rows, rows), :]),
+                (sides[1], own_ref),
+            ]
         )
-
-    return call(
-        cut_kernel,
-        "cut",
+    ]
+    for copy in copies:
+        copy.start()
+    for copy in copies:
+        copy.wait()
+
+
+def stage(info, gate, up, down_proj):
+    rows, width = gate.shape
+    half = jax.ShapeDtypeStruct((down_proj.shape[0], down_proj.shape[1] // 2), BF16)
+    return call(
+        stage_kernel,
+        "stage",
         [info],
-        [mine] * 3 + [theirs] * 3,
-        [column(3, step) for step in (1, 2, 3)] + [column(7, step) for step in (1, 2, 3)],
-        [part] * 3,
-    )
-
-
-def join_kernel(rows, info_ref, recv_ref, own_ref, *refs):
-    firsts, theirs, sum_ref, out_ref = refs[:3], refs[3:7], refs[7], refs[8]
+        [gate, up, down_proj],
+        [ANYWHERE] * 3,
+        [jax.ShapeDtypeStruct((2 * rows, width), BF16), half, half],
+        [pltpu.SemaphoreType.DMA((4,))],
+        limit=VMEM_STAGE,
+        out_specs=[WHOLE] * 3,
+    )
+
+
+def join_kernel(rows, info_ref, recv_ref, own_ref, place_ref, *refs):
+    blocks, sum_ref, out_ref, stream_ref = refs[:8], refs[8], refs[9], refs[10]
+    stream = []
+    for index, ref in enumerate(blocks):
+        lines = ref[ref.shape[0] - 1].astype(F32)
+        base = LANES // 2 * (index // 4)
+        spans = range(base, base + stream_ref.shape[1] // LANES * SUB, SUB)
+        stream.append(jnp.concatenate([lines[span : span + SUB] for span in spans], axis=1))
+    stream = jnp.concatenate(stream, axis=0).astype(BF16)
+    shape = (stream_ref.shape[0], stream.shape[0])
+    order = lax.broadcasted_iota(jnp.int32, shape, 0) == place_ref[...]
+    order = jnp.where(order, F32(1.0), F32(0.0)).astype(BF16)
+    stream_ref[...] = jnp.dot(order, stream, preferred_element_type=F32)
     sides = 2
     devs = recv_ref.shape[0] // sides
     tiles = LAT // LANES
@@ -234,8 +279,7 @@
         )
     latent = jnp.concatenate(latents, axis=0).astype(BF16)
     maps = [own_ref[0]]
-    maps += [ref[:tiles].reshape(LAT, LANES) for ref in firsts]
-    maps += [ref[:tiles].reshape(LAT, LANES) for ref in theirs]
+    maps += [ref[:tiles].reshape(LAT, LANES) for ref in blocks[1:]]
     products = jnp.dot(
         latent, jnp.concatenate(maps, axis=1), preferred_element_type=F32
     ).reshape(rows * devs, SUB, len(maps) * LANES)
@@ -252,19 +296,23 @@
     ).astype(BF16)
 
 
-def join(info, received, value_up, firsts, theirs, rows):
+def join(info, received, value_up, place, blocks, rows, eighth):
     devs = received.shape[0] // 2
     count = rows * devs
     sums = np.repeat(np.eye(count, dtype=np.float32), SUB, axis=1)
-    arrays = [received, value_up, *firsts, *theirs, jnp.asarray(sums, BF16)]
+    arrays = [received, value_up, place, *blocks, jnp.asarray(sums, BF16)]
     return call(
         functools.partial(join_kernel, rows),
         "join",
         [info],
         arrays,
         [None] * len(arrays),
-        jax.ShapeDtypeStruct((count, SUB * LANES), BF16),
+        [
+            jax.ShapeDtypeStruct((count, SUB * LANES), BF16),
+            jax.ShapeDtypeStruct((4 * rows, eighth), F32),
+        ],
         work=480_000_000,
+        limit=VMEM_MOST,
     )
 
 
@@ -316,27 +364,9 @@
     )
 
 
-def residual_kernel(parts_ref, place_ref, gain_ref, *refs):
-    blocks, residual_ref, out_ref = refs[:8], refs[8], refs[9]
+def residual_kernel(parts_ref, stream_ref, gain_ref, residual_ref, out_ref):
     rows, width = residual_ref.shape
-    stream = []
-    for index, ref in enumerate(blocks):
-        lines = ref[ref.shape[0] - 1].astype(F32)
-        base = LANES // 2 * (index // 4)
-        stream.append(
-            jnp.concatenate(
-                [
-                    lines[base + SUB * column : base + SUB * column + SUB]
-                    for column in range(width // LANES)
-                ],
-                axis=1,
-            )
-        )
-    stream = jnp.concatenate(stream, axis=0).astype(BF16)
-    order = lax.broadcasted_iota(jnp.int32, (rows, stream.shape[0]), 0) == place_ref[...]
-    order = jnp.where(order, F32(1.0), F32(0.0)).astype(BF16)
-    residual = jnp.dot(order, stream, preferred_element_type=F32)
-    residual = residual + jnp.sum(parts_ref[...].astype(F32), axis=0)
+    residual = stream_ref[...] + jnp.sum(parts_ref[...].astype(F32), axis=0)
     residual_ref[...] = residual
     squares = jnp.sum(residual * residual, axis=1, keepdims=True)
     high = rounded(squares)
@@ -360,17 +390,15 @@
         out_ref[:, index] = jnp.broadcast_to(tile.astype(BF16)[None], (chips, SUB, LANES))
 
 
-def residual_rows(parts, place, gain, blocks, chips):
+def residual_rows(parts, stream, gain, chips):
     _, rows, width = parts.shape
     tiles = rows * width // (SUB * LANES) + 1
-    last = blocks[0].shape[0] - 1
-    line = pl.BlockSpec((1, LANES, LANES), lambda i: (last, 0, 0))
     return call(
         residual_kernel,
         "residual",
         [],
-        [parts, place, gain, *blocks],
-        [None] * 3 + [line] * 8,
+        [parts, stream, gain],
+        [None] * 3,
         [
             jax.ShapeDtypeStruct((rows, width), F32),
             jax.ShapeDtypeStruct((chips, tiles, SUB, LANES), BF16),
@@ -378,29 +406,12 @@
     )
 
 
-def units_kernel(groups, last, info_ref, recv_ref, gate_hbm, up_hbm, *refs):
-    weight_ref, sems = refs[-2:]
-    refs = refs[:-2]
+def units_kernel(groups, last, info_ref, recv_ref, weight_ref, *refs):
     sides, quarters, tiles, _, _ = recv_ref.shape
     columns = (tiles - 1) // groups
     rows = sides * groups * SUB
     depth = columns * LANES
     which = 4 if last else 3
-    hidden = gate_hbm.shape[0]
-    copies = []
-    for quarter in range(quarters):
-        start = pl.multiple_of((info_ref[which] * quarters + quarter) * depth, LANES)
-        for index, ref in enumerate((gate_hbm, up_hbm)):
-            target = weight_ref.at[
-                pl.ds(index * hidden, hidden), pl.ds(quarter * depth, depth)
-            ]
-            copies.append(
-                pltpu.make_async_copy(
-                    ref.at[:, pl.ds(start, depth)], target, sems.at[2 * quarter + index]
-                )
-            )
-    for copy in copies:
-        copy.start()
     lane = lax.broadcasted_iota(jnp.int32, (SUB, LANES), 1)
     total = squares = None
     for quarter in range(quarters):
@@ -413,11 +424,10 @@
             ],
             axis=1,
         ).astype(BF16)
-        copies[2 * quarter].wait()
-        copies[2 * quarter + 1].wait()
+        start = pl.multiple_of((info_ref[which] * quarters + quarter) * depth, LANES)
         part = lax.dot_general(
             left,
-            weight_ref[:, quarter * depth : quarter * depth + depth],
+            weight_ref[:, pl.ds(start, depth)],
             (((1,), (1,)), ((), ())),
             preferred_element_type=F32,
         )
@@ -439,69 +449,48 @@
         sq_ref[...] = jnp.broadcast_to(squares, (rows, LANES))
     else:
         acc_ref, sq_ref, out_ref = refs
-        scale = lax.rsqrt((sq_ref[:, :1] + squares) / gate_hbm.shape[1] + 1e-06)
+        hidden = out_ref.shape[1]
+        scale = lax.rsqrt((sq_ref[:, :1] + squares) / weight_ref.shape[1] + 1e-06)
         total = total + acc_ref[...]
         gate = total[:, :hidden] * scale
         upper = total[:, hidden:] * scale
         out_ref[...] = (gate / (1.0 + jnp.exp(-gate)) * upper).astype(BF16)
 
 
-def units(info, received, gate, up, groups, carry=()):
+def units(info, received, weight, groups, carry=()):
     sides, quarters, tiles = received.shape[:3]
-    hidden, width = gate.shape
+    hidden = weight.shape[0] // 2
     rows = sides * groups * SUB
     last = bool(carry)
+    single = jax.ShapeDtypeStruct((rows, hidden), BF16)
+    double = [
+        jax.ShapeDtypeStruct((rows, 2 * hidden), F32),
+        jax.ShapeDtypeStruct((rows, LANES), F32),
+    ]
     return call(
         functools.partial(units_kernel, groups, last),
         "units_last" if last else "units_first",
         [info],
-        [received, gate, up, *carry],
-        [None, ANYWHERE, ANYWHERE] + [None] * len(carry),
-        jax.ShapeDtypeStruct((rows, hidden), BF16)
-        if last
-        else [
-            jax.ShapeDtypeStruct((rows, 2 * hidden), F32),
-            jax.ShapeDtypeStruct((rows, LANES), F32),
-        ],
-        [
-            pltpu.VMEM((2 * hidden, width // 2), BF16),
-            pltpu.SemaphoreType.DMA((2 * quarters,)),
-        ],
-        2 * rows * hidden * width,
-    )
-
-
-def down_kernel(
-    info_ref, mine_ref, theirs_ref, own_hbm, other_hbm, held_ref, out_ref, total, weight_ref, sems
-):
+        [received, weight, *carry],
+        [WHOLE] * (2 + len(carry)),
+        single if last else double,
+        work=rows * weight.size,
+        out_specs=WHOLE if last else [WHOLE] * 2,
+    )
+
+
+def down_kernel(info_ref, mine_ref, theirs_ref, own_ref, other_ref, held_ref, out_ref, total):
     chips, steps = out_ref.shape[:2]
     rows = mine_ref.shape[0]
     count = rows // chips
-    hidden, half = other_hbm.shape
-    width = 4 * LANES
-    copies = []
-    for piece in range(0, half, width):
-        for index, ref in enumerate((own_hbm, other_hbm)):
-            start = info_ref[3] * half + piece if index == 0 else piece
-            copies.append(
-                pltpu.make_async_copy(
-                    ref.at[:, pl.ds(pl.multiple_of(start, LANES), width)],
-                    weight_ref.at[pl.ds(index * hidden, hidden), pl.ds(piece, width)],
-                    sems.at[len(copies)],
-                )
-            )
-    for copy in copies:
-        copy.start()
     left = jnp.concatenate(
         [mine_ref[...].astype(F32), theirs_ref[...].astype(F32)], axis=1
     ).astype(BF16)
+    width = 4 * LANES
     for step in range(steps):
         span = slice(step * width, step * width + width)
-        copies[2 * step].wait()
-        copies[2 * step + 1].wait()
-        total[:rows, span] = jnp.dot(
-            left, weight_ref[:, span], preferred_element_type=F32
-        )
+        weight = jnp.concatenate([own_ref[:, span], other_ref[:, span]], axis=0)
+        total[:rows, span] = jnp.dot(left, weight, preferred_element_type=F32)
     total[pl.ds(rows, SUB), :] = jnp.zeros((SUB, total.shape[1]), F32)
     lines, columns = held_ref.shape
     place = pl.ds(pl.multiple_of(info_ref[2] * lines, SUB), lines)
@@ -522,23 +511,19 @@
             out_ref[chip, step] = jnp.concatenate(packed, axis=0).astype(BF16)
 
 
-def down(info, mine, theirs, down_proj, other, held, chips):
+def down(info, mine, theirs, own, other, held, chips):
     rows = mine.shape[0]
-    hidden, half = other.shape
-    steps = half // (4 * LANES)
+    half = own.shape[1]
     return call(
         down_kernel,
         "down",
         [info],
-        [mine, theirs, down_proj, other, held],
-        [None, None, ANYWHERE, ANYWHERE, None],
-        jax.ShapeDtypeStruct((chips, steps, 3 * SUB, LANES), BF16),
-        [
-            pltpu.VMEM((rows + SUB, half), F32),
-            pltpu.VMEM((2 * hidden, half), BF16),
-            pltpu.SemaphoreType.DMA((2 * steps,)),
-        ],
-        4 * rows * hidden * half,
+        [mine, theirs, own, other, held],
+        [WHOLE] * 5,
+        jax.ShapeDtypeStruct((chips, half // (4 * LANES), 3 * SUB, LANES), BF16),
+        [pltpu.VMEM((rows + SUB, half), F32)],
+        4 * rows * own.size,
+        out_specs=WHOLE,
     )
 
 
@@ -563,7 +548,15 @@
 
 def finish(info, parts):
     shape = jax.ShapeDtypeStruct((3, parts.shape[1] * 4 * LANES), BF16)
-    return call(finish_kernel, "finish", [info], [parts], [None], [shape, shape])
+    return call(
+        finish_kernel,
+        "finish",
+        [info],
+        [parts],
+        [WHOLE],
+        [shape, shape],
+        out_specs=[WHOLE] * 2,
+    )
 
 
 def local(
@@ -594,32 +587,38 @@
     firsts = [shift(part, step) for step, part in zip((1, 2, 3), starts)]
     gain = block(norm_gain, core * 4 + ring, eighth, 0)[None]
 
-    payload = attend(
-        info, lengths, query_latent.transpose(0, 2, 1), latent_cache.transpose(0, 2, 1)
-    )
-    payload, out_theirs, *firsts = lax.optimization_barrier((payload, out_theirs, *firsts))
+    payload, *cuts = attend(
+        info,
+        lengths,
+        query_latent.transpose(0, 2, 1),
+        latent_cache.transpose(0, 2, 1),
+        out_proj,
+        out_theirs,
+    )
+    payload, *firsts = lax.optimization_barrier((payload, *firsts))
     firsts_theirs = [swap(part) for part in [own] + firsts]
-    parts = [
-        shift(part, step) for step, part in zip((1, 2, 3), cut(info, out_proj, out_theirs))
-    ]
+    parts = [shift(part, step) for step, part in zip((1, 2, 3), cuts)]
     received = lax.all_to_all(payload, OUTER, split_axis=0, concat_axis=0, tiled=True)
-    values = join(info, received, value_up, firsts, firsts_theirs, rows)
-
-    ring_values = [values] + [shift(values, step) for step in (1, 2, 3)]
+    chip = (ring - jnp.arange(8)) % 4
+    side = jnp.where(jnp.arange(8) < 4, core, 1 - core)
+    line = jnp.arange(SUB)[None]
+    place = ((chip * 2 + side) * rows_own)[:, None] + line
+    place = jnp.where(line < rows_own, place, -1).reshape(1, 8 * SUB).astype(jnp.int32)
+    blocks = [own] + firsts + firsts_theirs
+    values, stream_rows = join(info, received, value_up, place, blocks, rows, eighth)
+
+    last, parts[0] = lax.optimization_barrier((values, parts[0]))
+    ring_values = [values, shift(values, 1), shift(values, 2), shift(last, 3)]
+    late, _ = lax.optimization_barrier((values, ring_values[1]))
+    both_values = ring_values + [swap(piece) for piece in [late] + ring_values[1:]]
     row = jnp.arange(8 * rows)
     natural = jnp.tile(row % 8 * (8 * rows) + row // 8, 8).reshape(8, 8 * rows)
-    chip = (ring - jnp.arange(8)) % 4
-    side = jnp.where(jnp.arange(8) < 4, core, 1 - core)
     place = natural[:, : 8 * rows] + ((chip * 2 + side) * rows)[:, None]
     place = place.reshape(1, 64 * rows).astype(jnp.int32)
-    line = jnp.arange(SUB)[None]
-    stream_place = ((chip * 2 + side) * rows_own)[:, None] + line
-    stream_place = jnp.where(line < rows_own, stream_place, -1)
-    stream_place = stream_place.reshape(1, 8 * SUB).astype(jnp.int32)
     partial = project(
         info,
         place,
-        ring_values + [swap(piece) for piece in ring_values],
+        both_values,
         out_proj,
         out_theirs,
         parts,
@@ -627,21 +626,19 @@
     )
     parts = lax.all_to_all(partial, OUTER, split_axis=0, concat_axis=0, tiled=True)
 
-    residual, payload = residual_rows(
-        parts, stream_place, gain, [own] + firsts + firsts_theirs, 32
-    )
+    residual, payload = residual_rows(parts, stream_rows, gain, 32)
     payload, gate_proj, up_proj, down_proj = lax.optimization_barrier(
         (payload, gate_proj, up_proj, down_proj)
     )
     piece = lax.all_to_all(payload, SIDE_CHIPS, split_axis=0, concat_axis=0, tiled=True)
     piece = piece.reshape((8, 4) + piece.shape[1:])
     other = swap(piece)
-    down_theirs = swap(block(down_proj, 1 - core, half, 1))
-    gate_proj, up_proj = gate_proj.T, up_proj.T
+    weight, down_own, down_send = stage(info, gate_proj.T, up_proj.T, down_proj)
+    down_theirs = swap(down_send)
     groups = 8 * rows_own // SUB
-    carry = units(info, piece, gate_proj, up_proj, groups)
-    hidden = units(info, other, gate_proj, up_proj, groups, carry)
-    partial = down(info, hidden, swap(hidden), down_proj, down_theirs, residual, 32)
+    carry = units(info, piece, weight, groups)
+    hidden = units(info, other, weight, groups, carry)
+    partial = down(info, hidden, swap(hidden), down_own, down_theirs, residual, 32)
     parts = lax.all_to_all(partial, SIDE_CHIPS, split_axis=0, concat_axis=0, tiled=True)
     mine, theirs = finish(info, parts)
     theirs = swap(theirs)

time: 172 us -> 157 us (0.913)
  Pallas kernels: 47 us -> 37 us
  starting transfers between devices: 48.3 us -> 44 us
  waiting for transfers between devices: 39.8 us -> 37.2 us
  local copies, waits for them, and re-layouts: 9.85 us -> 12.3 us
    pallas_call x10, Pallas kernels: 47 us -> 37 us  [call(): pl.pallas_call(kernel, out_shape=outs, grid_spec=pltpu.PrefetchScalarGrid...]
    all_to_all x1, waiting for transfers between devices: 15.7 us -> 6.9 us  [local(): lax.all_to_all(payload, SIDE_CHIPS, split_axis=0, concat_axis=0, tiled=True)]
    unnamed x46 -> x34, local copies, waits for them, and re-layouts: 3.58 us -> 10.1 us
    all_to_all x1, waiting for transfers between devices: 2.68 us -> 5.99 us  [local(): lax.all_to_all(payload, OUTER, split_axis=0, concat_axis=0, tiled=True)]
    dynamic_slice x2 -> x1, local copies, waits for them, and re-layouts: 3.82 us -> 0.78 us  [block(): return lax.dynamic_slice_in_dim(array, index * size, size, axis)]
    ppermute x9, starting transfers between devices: 12.6 us -> 9.86 us  [shift(): return lax.ppermute(array, 'y', [(i, (i + step) % 4) for i in range(4)])]
    ppermute x9, waiting for transfers between devices: 7.62 us -> 9.44 us  [shift(): return lax.ppermute(array, 'y', [(i, (i + step) % 4) for i in range(4)])]
  transfers between devices with their start and end apart: 25 -> 25, of which waited for: 11 -> 8; matrix products, arithmetic and copies ran while one was open for 3% -> 1% of each run, Pallas kernels for 16% -> 15%
where the time goes in v7:
time: 157 us; the launch traced here: 156 us
  starting transfers between devices  44 us (28%)
  waiting for transfers between devices  37.2 us (24%)
  Pallas kernels  37 us (24%)
  blocking collectives  24.6 us (16%)
  local copies, waits for them, and re-layouts  12.3 us (8%)
    pallas_call x10, Pallas kernels, call(): pl.pallas_call(kernel, out_shape=outs, grid_spec=pltpu.PrefetchScalarGrid...  37 us
    all_to_all x1, blocking collectives, local(): lax.all_to_all(partial, SIDE_CHIPS, split_axis=0, concat_axis=0, tiled=True)  24.6 us
    ppermute x13, starting transfers between devices, swap(): return lax.ppermute(array, 'core', SWAP)  15.3 us
    all_to_all x1, waiting for transfers between devices, local(): lax.all_to_all(partial, OUTER, split_axis=0, concat_axis=0, tiled=True)  11.7 us
    unnamed x34, local copies, waits for them, and re-layouts  10.1 us
    ppermute x9, starting transfers between devices, shift(): return lax.ppermute(array, 'y', [(i, (i + step) % 4) for i in range(4)])  9.86 us
    ppermute x9, waiting for transfers between devices, shift(): return lax.ppermute(array, 'y', [(i, (i + step) % 4) for i in range(4)])  9.44 us
    all_to_all x1, starting transfers between devices, local(): lax.all_to_all(payload, OUTER, split_axis=0, concat_axis=0, tiled=True)  7.92 us
  transfers between devices with their start and end apart: 25, of which 8 were waited for; matrix products, arithmetic and copies ran while one was open for 1% of the time, Pallas kernels for 15%

profile of v7, /device:TPU:1, one launch (start us, length us, event | category | flops | bytes accessed | tf_op | source)
XLA Modules:
  0.0 156.1 jit_solution(8626379224431864907)
XLA Ops:
  0.0 0.7 stack.28.info_ref
  0.7 3.2 %early.1 = (bf16[128,3584]{1,0:T(8,128)(2,1)}, bf16[5,128,128]{2,1,0:T(8,128)(2,1)}, bf16[5,128,128]{2,1,0:T(8,128)(2,1)}, bf16[5,128,128]{2,1,0:T(8,128)(2,1)}, bf16[5,128,128]{2,1,0:T(8,128)(2,1)}) custom-call(s32[8]{0:T(128)} %stack.28.info_ref, bf16[1,512,128]{2,1,0:T(8,128)(2,1)} %own_ref.1, bf16[3,7168]{1,0:T(4,128)(2,1)} %stream_ref.1, ...), custom_call_target="tpu_custom_call" | custom-call | bytes 3581952 | tf_op jit(solution)/shard_map/early/pallas_call | solution.py:51
  3.9 1.4 collective-permute-start
  5.3 1.4 collective-permute-start.1
  6.7 2.6 %collective-permute-start.2 = (bf16[5,128,128]{2,1,0:T(8,128)(2,1)}, bf16[5,128,128]{2,1,0:T(8,128)(2,1)S(1)}, u32[]{:S(2)}, u32[]{:S(2)}) collective-permute-start(bf16[5,128,128]{2,1,0:T(8,128)(2,1)} %get-tuple-element.39), channel_id=1, source_target_pairs={{0,4},{2,6},{4,0},{6,2},{1,5},{3,7},{5,1},{7,3},{8,12},{10,14},{12... | collective-permute-start | bytes 491528 | tf_op jit(solution)/shard_map/ppermute | solution.py:33
  9.3 1.1 collective-permute-start.3
  10.4 0.0 collective-permute-done.theirs_hbm.refs_9_
  10.4 1.0 copy-done.3
  11.3 7.0 %attend.1 = (bf16[16,25,8,128]{3,2,1,0:T(8,128)(2,1)}, bf16[14,128,128]{2,1,0:T(8,128)(2,1)}, bf16[14,128,128]{2,1,0:T(8,128)(2,1)}, bf16[14,128,128]{2,1,0:T(8,128)(2,1)}) custom-call(s32[8]{0:T(128)} %stack.28.info_ref, s32[6]{0:T(128)} %lengths_ref.1, bf16[6,576,128]{2,1,0:T(8,128)(2,1)} %bitcast.16, bf16[6,576,512]{2,1,0:T(8,128)(2,1)} %bitcast.15, ...), custom_call_target="tpu_custom_call" | custom-call | flops 855638016 | bytes 9371648 | tf_op jit(solution)/shard_map/attend/pallas_call | solution.py:51
  18.3 0.0 copy-start.1
  18.4 0.0 collective-permute-done.2.refs_2_
  18.4 0.0 collective-permute-done.3.refs_3_
  18.4 7.9 %all-to-all-start = ((bf16[16,25,8,128]{3,2,1,0:T(8,128)(2,1)}), bf16[16,25,8,128]{3,2,1,0:T(8,128)(2,1)}, u32[]{:S(2)}, u32[]{:S(2)}) async-start(bf16[16,25,8,128]{3,2,1,0:T(8,128)(2,1)} %get-tuple-element.41), calls=%async_computation | async-start | bytes 1638400 | tf_op jit(solution)/shard_map/all_to_all | solution.py:601
  26.4 1.2 collective-permute-start.4
  27.6 0.1 collective-permute-start.5
  27.7 0.4 collective-permute-start.10
  28.1 1.3 collective-permute-start.16
  29.4 1.0 collective-permute-start.6
  30.3 0.1 collective-permute-start.7
  30.4 0.6 copy-done.14
  31.0 0.7 copy-done.15
  31.7 1.4 collective-permute-start.17
  33.1 0.1 add_select_fusion
  33.1 0.6 select_n.79.place_ref
  33.8 0.0 collective-permute-done.6.refs_6_
  33.8 6.0 %all-to-all-done.recv_ref = bf16[16,25,8,128]{3,2,1,0:T(8,128)(2,1)} async-done(((bf16[16,25,8,128]{3,2,1,0:T(8,128)(2,1)}), bf16[16,25,8,128]{3,2,1,0:T(8,128)(2,1)}, u32[]{:S(2)}, u32[]{:S(2)}) %all-to-all-start) | async-done | bytes 819232 | tf_op jit(solution)/shard_map/all_to_all | solution.py:601
  39.8 3.9 %join.1 = (bf16[48,1024]{1,0:T(8,128)(2,1)}, f32[24,896]{1,0:T(8,128)}) custom-call(s32[8]{0:T(128)} %stack.28.info_ref, bf16[16,25,8,128]{3,2,1,0:T(8,128)(2,1)} %all-to-all-done.recv_ref, bf16[1,512,128]{2,1,0:T(8,128)(2,1)} %own_ref.1, s32[1,64]{1,0:T(1,128)} %select_n.79.place_ref, bf16[5,128,128]{2,1,0:T(8,128)(2,1)} %get-tuple-element.42.refs_0_, ...), custom_call_target="tpu_custom_call" | custom-call | flops 480000000 | bytes 2439296 | tf_op jit(solution)/shard_map/join/pallas_call | solution.py:51
  43.7 0.7 collective-permute-start.9
  44.3 1.1 collective-permute-start.8
  45.4 6.6 %collective-permute-done.10.refs_10_ = bf16[14,128,128]{2,1,0:T(8,128)(2,1)S(1)} collective-permute-done((bf16[14,128,128]{2,1,0:T(8,128)(2,1)}, bf16[14,128,128]{2,1,0:T(8,128)(2,1)S(1)}, u32[]{:S(2)}, u32[]{:S(2)}) %collective-permute-start.10) | collective-permute-done | bytes 458784 | tf_op jit(solution)/shard_map/ppermute | solution.py:33
  52.0 2.8 %collective-permute-done.8.refs_1_ = bf16[48,1024]{1,0:T(8,128)(2,1)S(1)} collective-permute-done((bf16[48,1024]{1,0:T(8,128)(2,1)}, bf16[48,1024]{1,0:T(8,128)(2,1)S(1)}, u32[]{:S(2)}, u32[]{:S(2)}) %collective-permute-start.8) | collective-permute-done | bytes 98336 | tf_op jit(solution)/shard_map/ppermute | solution.py:33
  54.8 1.3 collective-permute-start.12
  56.1 0.0 collective-permute-start.13
  56.1 0.5 collective-permute-start.14
  56.6 3.0 %collective-permute-start.15 = (bf16[48,1024]{1,0:T(8,128)(2,1)S(1)}, bf16[48,1024]{1,0:T(8,128)(2,1)}, u32[]{:S(2)}, u32[]{:S(2)}) collective-permute-start(bf16[48,1024]{1,0:T(8,128)(2,1)S(1)} %collective-permute-done.11.refs_3_), channel_id=1, source_target_pairs={{0,1},{1,0},{2,3},{3,2},{4,5},{5,4},{6,7},{7,6},{8,9},{9,8},{10,11... | collective-permute-start | bytes 294920 | tf_op jit(solution)/shard_map/ppermute | solution.py:29
  59.6 0.1 broadcast_add_fusion
  59.7 0.1 add.103.place_ref
  59.8 0.9 collective-permute-done.15.refs_7_
  60.7 0.9 copy-done.5
  61.6 4.2 %project.1 = bf16[16,24,896]{2,1,0:T(8,128)(2,1)} custom-call(s32[8]{0:T(128)S(1)} %copy-done.9, s32[1,384]{1,0:T(1,128)S(1)} %add.103.place_ref, bf16[48,1024]{1,0:T(8,128)(2,1)S(1)} %copy-done.5, bf16[48,1024]{1,0:T(8,128)(2,1)S(1)} %collective-permute-done.8.refs_1_, bf16[48,1024]{1,0:T(8,128)(2,1)S(1)} %collective-permute-done.9.refs_2_, ...), custom_call_target="tpu_custom_call" | custom-call | flops 704643072 | bytes 5604096 | tf_op jit(solution)/shard_map/project/pallas_call | solution.py:51
  65.8 6.9 %all-to-all-start.1 = ((bf16[16,24,896]{2,1,0:T(8,128)(2,1)}), bf16[16,24,896]{2,1,0:T(8,128)(2,1)S(1)}, u32[]{:S(2)}, u32[]{:S(2)}) async-start(bf16[16,24,896]{2,1,0:T(8,128)(2,1)} %project.1), calls=%async_computation.1 | async-start | bytes 1376256 | tf_op jit(solution)/shard_map/all_to_all | solution.py:627
  72.7 0.8 dynamic_slice.3
  73.5 11.7 %all-to-all-done.1.parts_ref = bf16[16,24,896]{2,1,0:T(8,128)(2,1)S(1)} async-done(((bf16[16,24,896]{2,1,0:T(8,128)(2,1)}), bf16[16,24,896]{2,1,0:T(8,128)(2,1)S(1)}, u32[]{:S(2)}, u32[]{:S(2)}) %all-to-all-start.1) | async-done | bytes 688160 | tf_op jit(solution)/shard_map/all_to_all | solution.py:627
  85.2 0.9 copy-done.6
  86.1 1.4 residual.1
  87.5 0.6 copy-done.7
  88.1 4.0 %all-to-all-start.2 = ((bf16[32,22,8,128]{3,2,1,0:T(8,128)(2,1)}), bf16[32,22,8,128]{3,2,1,0:T(8,128)(2,1)S(1)}, u32[]{:S(2)}, u32[]{:S(2)}) async-start(bf16[32,22,8,128]{3,2,1,0:T(8,128)(2,1)} %get-tuple-element.55), calls=%async_computation.2 | async-start | bytes 2883584 | tf_op jit(solution)/shard_map/all_to_all | solution.py:633
  92.1 0.0 copy-start.2
  92.1 2.2 %copy-done.2 = bf16[7168,288]{0,1:T(8,128)(2,1)S(1)} copy-done((bf16[7168,288]{0,1:T(8,128)(2,1)S(1)}, bf16[7168,288]{0,1:T(8,128)(2,1)}, u32[]{:S(2)}) %copy-start.2) | copy-done | bytes 4128792
  94.3 7.9 %stage.1 = (bf16[576,7168]{1,0:T(8,128)(2,1)}, bf16[288,3584]{1,0:T(8,128)(2,1)S(1)}, bf16[288,3584]{1,0:T(8,128)(2,1)}) custom-call(s32[8]{0:T(128)S(1)} %copy-done.9, bf16[288,7168]{1,0:T(8,128)(2,1)S(1)} %bitcast.13, bf16[288,7168]{1,0:T(8,128)(2,1)} %bitcast.14, bf16[288,7168]{1,0:T(8,128)(2,1)} %down_ref), custom_call_target="tpu_custom_call" | custom-call | bytes 24772608 | tf_op jit(solution)/shard_map/stage/pallas_call | solution.py:51
  102.2 1.8 %collective-permute-start.20 = (bf16[288,3584]{1,0:T(8,128)(2,1)}, bf16[288,3584]{1,0:T(8,128)(2,1)}, u32[]{:S(2)}, u32[]{:S(2)}) collective-permute-start(bf16[288,3584]{1,0:T(8,128)(2,1)} %get-tuple-element.63), channel_id=1, source_target_pairs={{0,1},{1,0},{2,3},{3,2},{4,5},{5,4},{6,7},{7,6},{8,9},{9,8},{10,11... | collective-permute-start | bytes 6193160 | tf_op jit(solution)/shard_map/ppermute | solution.py:29
  104.0 6.9 %all-to-all-done.2 = bf16[32,22,8,128]{3,2,1,0:T(8,128)(2,1)S(1)} async-done(((bf16[32,22,8,128]{3,2,1,0:T(8,128)(2,1)}), bf16[32,22,8,128]{3,2,1,0:T(8,128)(2,1)S(1)}, u32[]{:S(2)}, u32[]{:S(2)}) %all-to-all-start.2) | async-done | bytes 1441824 | tf_op jit(solution)/shard_map/all_to_all | solution.py:633
  110.9 2.8 %collective-permute-start.18 = (bf16[8,4,22,8,128]{4,3,2,1,0:T(8,128)(2,1)S(1)}, bf16[8,4,22,8,128]{4,3,2,1,0:T(8,128)(2,1)S(1)}, u32[]{:S(2)}, u32[]{:S(2)}) collective-permute-start(bf16[8,4,22,8,128]{4,3,2,1,0:T(8,128)(2,1)S(1)} %bitcast.11), channel_id=1, source_target_pairs={{0,1},{1,0},{2,3},{3,2},{4,5},{5,4},{6,7},{7,6},{8,9},{9,8},{10,11... | collective-permute-start | bytes 4325384 | tf_op jit(solution)/shard_map/ppermute | solution.py:29
  113.7 3.3 %copy-done = bf16[576,7168]{1,0:T(8,128)(2,1)S(1)} copy-done((bf16[576,7168]{1,0:T(8,128)(2,1)S(1)}, bf16[576,7168]{1,0:T(8,128)(2,1)}, u32[]{:S(2)}) %copy-start) | copy-done | bytes 8257560
  117.1 2.3 %units_first.1 = (f32[192,576]{1,0:T(8,128)S(1)}, f32[192,128]{1,0:T(8,128)S(1)}) custom-call(s32[8]{0:T(128)S(1)} %copy-done.9, bf16[8,4,22,8,128]{4,3,2,1,0:T(8,128)(2,1)S(1)} %bitcast.12, bf16[576,7168]{1,0:T(8,128)(2,1)S(1)} %copy-done), custom_call_target="tpu_custom_call" | custom-call | flops 792723456 | bytes 9969664 | tf_op jit(solution)/shard_map/units_first/pallas_call | solution.py:51
  119.4 2.4 %units_last.1.mine_ref = bf16[192,288]{1,0:T(8,128)(2,1)S(1)} custom-call(s32[8]{0:T(128)S(1)} %copy-done.9, bf16[8,4,22,8,128]{4,3,2,1,0:T(8,128)(2,1)S(1)} %collective-permute-done.18.recv_ref, bf16[576,7168]{1,0:T(8,128)(2,1)S(1)} %copy-done, f32[192,576]{1,0:T(8,128)S(1)} %get-tuple-element.60.refs_0_, f32[192,128]{1,0:T(8,128)S(1)} %get-tuple-element.61.refs_1_), custom_call_target="tpu_custom_call" | custom-call | flops 792723456 | bytes 10080256 | tf_op jit(solution)/shard_map/units_last/pallas_call | solution.py:51
  121.8 0.1 collective-permute-start.19
  121.9 1.3 collective-permute-done.19.theirs_ref
  123.2 3.9 %down.1 = bf16[32,7,24,128]{3,2,1,0:T(8,128)(2,1)S(1)} custom-call(s32[8]{0:T(128)S(1)} %copy-done.9, bf16[192,288]{1,0:T(8,128)(2,1)S(1)} %units_last.1.mine_ref, bf16[192,288]{1,0:T(8,128)(2,1)S(1)} %collective-permute-done.19.theirs_ref, bf16[288,3584]{1,0:T(8,128)(2,1)S(1)} %get-tuple-element.62.own_ref, ...), custom_call_target="tpu_custom_call" | custom-call | flops 792723456 | bytes 5769216 | tf_op jit(solution)/shard_map/down/pallas_call | solution.py:51
  127.2 24.6 %all_to_all.20.parts_ref = bf16[32,7,24,128]{3,2,1,0:T(8,128)(2,1)S(1)} all-to-all(bf16[32,7,24,128]{3,2,1,0:T(8,128)(2,1)S(1)} %down.1), channel_id=1, replica_groups=mesh['zh'=2,'zl'=2,'x'=4,'y'=4,'core'=2] {'zl','x','y'}, dimensions={0} | all-to-all | bytes 2752512 | tf_op jit(solution)/shard_map/all_to_all | solution.py:642
  151.7 0.8 finish.1
  152.6 2.0 %collective-permute-start.21 = (bf16[3,3584]{1,0:T(4,128)(2,1)S(1)}, bf16[3,3584]{1,0:T(4,128)(2,1)S(1)}, u32[]{:S(2)}, u32[]{:S(2)}) collective-permute-start(bf16[3,3584]{1,0:T(4,128)(2,1)S(1)} %get-tuple-element.66), channel_id=1, source_target_pairs={{0,1},{1,0},{2,3},{3,2},{4,5},{5,4},{6,7},{7,6},{8,9},{9,8},{10,11... | collective-permute-start | bytes 64520 | tf_op jit(solution)/shard_map/ppermute | solution.py:29
  154.6 0.9 collective-permute-done.21
  155.5 0.7 pad_maximum_fusion
  (43 shorter events, 0.1 us)
Async XLA Ops:
  3.9 6.5 %collective-permute-start = (bf16[128,3584]{1,0:T(8,128)(2,1)}, bf16[128,3584]{1,0:T(8,128)(2,1)S(1)}, u32[]{:S(2)}, u32[]{:S(2)}) collective-permute-start(bf16[128,3584]{1,0:T(8,128)(2,1)} %get-tuple-element.36), channel_id=1, source_target_pairs={{0,1},{1,0},{2,3},{3,2},{4,5},{5,4},{6,7},{7,6},{8,9},{9,8},{10,11... | collective-permute-start | bytes 2752520 | tf_op jit(solution)/shard_map/ppermute | solution.py:29
  5.3 13.1 %collective-permute-start.1 = (bf16[5,128,128]{2,1,0:T(8,128)(2,1)}, bf16[5,128,128]{2,1,0:T(8,128)(2,1)S(1)}, u32[]{:S(2)}, u32[]{:S(2)}) collective-permute-start(bf16[5,128,128]{2,1,0:T(8,128)(2,1)} %get-tuple-element.38), channel_id=1, source_target_pairs={{0,2},{2,4},{4,6},{6,0},{1,3},{3,5},{5,7},{7,1},{8,10},{10,12},{12... | collective-permute-start | bytes 491528 | tf_op jit(solution)/shard_map/ppermute | solution.py:33
  6.7 11.7 %collective-permute-start.2 = (bf16[5,128,128]{2,1,0:T(8,128)(2,1)}, bf16[5,128,128]{2,1,0:T(8,128)(2,1)S(1)}, u32[]{:S(2)}, u32[]{:S(2)}) collective-permute-start(bf16[5,128,128]{2,1,0:T(8,128)(2,1)} %get-tuple-element.39), channel_id=1, source_target_pairs={{0,4},{2,6},{4,0},{6,2},{1,5},{3,7},{5,1},{7,3},{8,12},{10,14},{12... | collective-permute-start | bytes 491528 | tf_op jit(solution)/shard_map/ppermute | solution.py:33
  9.3 9.1 %collective-permute-start.3 = (bf16[5,128,128]{2,1,0:T(8,128)(2,1)}, bf16[5,128,128]{2,1,0:T(8,128)(2,1)S(1)}, u32[]{:S(2)}, u32[]{:S(2)}) collective-permute-start(bf16[5,128,128]{2,1,0:T(8,128)(2,1)} %get-tuple-element.40), channel_id=1, source_target_pairs={{0,6},{2,0},{4,2},{6,4},{1,7},{3,1},{5,3},{7,5},{8,14},{10,8},{12,... | collective-permute-start | bytes 491528 | tf_op jit(solution)/shard_map/ppermute | solution.py:33
  10.4 1.0 copy-start.3
  11.3 15.0 %copy-start.10 = (bf16[5,128,128]{2,1,0:T(8,128)(2,1)S(1)}, bf16[5,128,128]{2,1,0:T(8,128)(2,1)}, u32[]{:S(2)}) copy-start(bf16[5,128,128]{2,1,0:T(8,128)(2,1)} %get-tuple-element.42.refs_0_) | copy-start | bytes 491524
  18.3 42.4 %copy-start.1 = (bf16[128,7168]{1,0:T(8,128)(2,1)S(1)}, bf16[128,7168]{1,0:T(8,128)(2,1)}, u32[]{:S(2)}) copy-start(bf16[128,7168]{1,0:T(8,128)(2,1)} %refs_8_.2) | copy-start | bytes 5505028
  18.3 42.4 %copy-start.4 = (bf16[128,3584]{1,0:T(8,128)(2,1)S(1)}, bf16[128,3584]{1,0:T(8,128)(2,1)}, u32[]{:S(2)}) copy-start(bf16[128,3584]{1,0:T(8,128)(2,1)} %copy-done.3) | copy-start | bytes 2752516
  18.4 42.4 %copy-start.9 = (s32[8]{0:T(128)S(1)}, s32[8]{0:T(128)}, u32[]{:S(2)}) copy-start(s32[8]{0:T(128)} %stack.28.info_ref) | copy-start | bytes 100
  18.4 21.4 %copy-start.11 = (bf16[5,128,128]{2,1,0:T(8,128)(2,1)}, bf16[5,128,128]{2,1,0:T(8,128)(2,1)S(1)}, u32[]{:S(2)}) copy-start(bf16[5,128,128]{2,1,0:T(8,128)(2,1)S(1)} %collective-permute-done.1.refs_1_) | copy-start | bytes 491524
  18.4 9.3 %copy-start.12 = (bf16[5,128,128]{2,1,0:T(8,128)(2,1)}, bf16[5,128,128]{2,1,0:T(8,128)(2,1)S(1)}, u32[]{:S(2)}) copy-start(bf16[5,128,128]{2,1,0:T(8,128)(2,1)S(1)} %collective-permute-done.2.refs_2_) | copy-start | bytes 491524
  18.4 9.2 %copy-start.13 = (bf16[5,128,128]{2,1,0:T(8,128)(2,1)}, bf16[5,128,128]{2,1,0:T(8,128)(2,1)S(1)}, u32[]{:S(2)}) copy-start(bf16[5,128,128]{2,1,0:T(8,128)(2,1)S(1)} %collective-permute-done.3.refs_3_) | copy-start | bytes 491524
  18.4 21.3 %all-to-all-start = ((bf16[16,25,8,128]{3,2,1,0:T(8,128)(2,1)}), bf16[16,25,8,128]{3,2,1,0:T(8,128)(2,1)}, u32[]{:S(2)}, u32[]{:S(2)}) async-start(bf16[16,25,8,128]{3,2,1,0:T(8,128)(2,1)} %get-tuple-element.41), calls=%async_computation | async-start | bytes 1638400 | tf_op jit(solution)/shard_map/all_to_all | solution.py:601
  26.4 4.0 %collective-permute-start.4 = (bf16[5,128,128]{2,1,0:T(8,128)(2,1)S(1)}, bf16[5,128,128]{2,1,0:T(8,128)(2,1)S(1)}, u32[]{:S(2)}, u32[]{:S(2)}) collective-permute-start(bf16[5,128,128]{2,1,0:T(8,128)(2,1)S(1)} %copy-done.10), channel_id=1, source_target_pairs={{0,1},{1,0},{2,3},{3,2},{4,5},{5,4},{6,7},{7,6},{8,9},{9,8},{10,11... | collective-permute-start | bytes 491528 | tf_op jit(solution)/shard_map/ppermute | solution.py:29
  27.6 2.9 %collective-permute-start.5 = (bf16[5,128,128]{2,1,0:T(8,128)(2,1)S(1)}, bf16[5,128,128]{2,1,0:T(8,128)(2,1)S(1)}, u32[]{:S(2)}, u32[]{:S(2)}) collective-permute-start(bf16[5,128,128]{2,1,0:T(8,128)(2,1)S(1)} %collective-permute-done.1.refs_1_), channel_id=1, source_target_pairs={{0,1},{1,0},{2,3},{3,2},{4,5},{5,4},{6,7},{7,6},{8,9},{9,8},{10,11... | collective-permute-start | bytes 491528 | tf_op jit(solution)/shard_map/ppermute | solution.py:29
  27.7 24.4 %collective-permute-start.10 = (bf16[14,128,128]{2,1,0:T(8,128)(2,1)}, bf16[14,128,128]{2,1,0:T(8,128)(2,1)S(1)}, u32[]{:S(2)}, u32[]{:S(2)}) collective-permute-start(bf16[14,128,128]{2,1,0:T(8,128)(2,1)} %get-tuple-element.47), channel_id=1, source_target_pairs={{0,2},{2,4},{4,6},{6,0},{1,3},{3,5},{5,7},{7,1},{8,10},{10,12},{12... | collective-permute-start | bytes 1376264 | tf_op jit(solution)/shard_map/ppermute | solution.py:33
  28.1 28.0 %collective-permute-start.16 = (bf16[14,128,128]{2,1,0:T(8,128)(2,1)}, bf16[14,128,128]{2,1,0:T(8,128)(2,1)}, u32[]{:S(2)}, u32[]{:S(2)}) collective-permute-start(bf16[14,128,128]{2,1,0:T(8,128)(2,1)} %get-tuple-element.51), channel_id=1, source_target_pairs={{0,4},{2,6},{4,0},{6,2},{1,5},{3,7},{5,1},{7,3},{8,12},{10,14},{12... | collective-permute-start | bytes 1376264 | tf_op jit(solution)/shard_map/ppermute | solution.py:33
  29.4 4.4 %collective-permute-start.6 = (bf16[5,128,128]{2,1,0:T(8,128)(2,1)}, bf16[5,128,128]{2,1,0:T(8,128)(2,1)}, u32[]{:S(2)}, u32[]{:S(2)}) collective-permute-start(bf16[5,128,128]{2,1,0:T(8,128)(2,1)} %copy-done.12), channel_id=1, source_target_pairs={{0,1},{1,0},{2,3},{3,2},{4,5},{5,4},{6,7},{7,6},{8,9},{9,8},{10,11... | collective-permute-start | bytes 491528 | tf_op jit(solution)/shard_map/ppermute | solution.py:29
  30.3 0.7 copy-start.14
  30.3 3.4 %collective-permute-start.7 = (bf16[5,128,128]{2,1,0:T(8,128)(2,1)}, bf16[5,128,128]{2,1,0:T(8,128)(2,1)S(1)}, u32[]{:S(2)}, u32[]{:S(2)}) collective-permute-start(bf16[5,128,128]{2,1,0:T(8,128)(2,1)} %copy-done.13), channel_id=1, source_target_pairs={{0,1},{1,0},{2,3},{3,2},{4,5},{5,4},{6,7},{7,6},{8,9},{9,8},{10,11... | collective-permute-start | bytes 491528 | tf_op jit(solution)/shard_map/ppermute | solution.py:29
  31.0 0.7 copy-start.15
  31.7 28.1 %collective-permute-start.17 = (bf16[14,128,128]{2,1,0:T(8,128)(2,1)}, bf16[14,128,128]{2,1,0:T(8,128)(2,1)}, u32[]{:S(2)}, u32[]{:S(2)}) collective-permute-start(bf16[14,128,128]{2,1,0:T(8,128)(2,1)} %get-tuple-element.52), channel_id=1, source_target_pairs={{0,6},{2,0},{4,2},{6,4},{1,7},{3,1},{5,3},{7,5},{8,14},{10,8},{12,... | collective-permute-start | bytes 1376264 | tf_op jit(solution)/shard_map/ppermute | solution.py:33
  33.8 6.0 %copy-start.16 = (bf16[5,128,128]{2,1,0:T(8,128)(2,1)}, bf16[5,128,128]{2,1,0:T(8,128)(2,1)S(1)}, u32[]{:S(2)}) copy-start(bf16[5,128,128]{2,1,0:T(8,128)(2,1)S(1)} %collective-permute-done.7.refs_7_) | copy-start | bytes 491524
  43.7 12.4 %collective-permute-start.9 = (bf16[48,1024]{1,0:T(8,128)(2,1)}, bf16[48,1024]{1,0:T(8,128)(2,1)S(1)}, u32[]{:S(2)}, u32[]{:S(2)}) collective-permute-start(bf16[48,1024]{1,0:T(8,128)(2,1)} %get-tuple-element.49.refs_0_), channel_id=1, source_target_pairs={{0,4},{2,6},{4,0},{6,2},{1,5},{3,7},{5,1},{7,3},{8,12},{10,14},{12... | collective-permute-start | bytes 294920 | tf_op jit(solution)/shard_map/ppermute | solution.py:33
  44.3 10.5 %collective-permute-start.8 = (bf16[48,1024]{1,0:T(8,128)(2,1)}, bf16[48,1024]{1,0:T(8,128)(2,1)S(1)}, u32[]{:S(2)}, u32[]{:S(2)}) collective-permute-start(bf16[48,1024]{1,0:T(8,128)(2,1)} %get-tuple-element.49.refs_0_), channel_id=1, source_target_pairs={{0,2},{2,4},{4,6},{6,0},{1,3},{3,5},{5,7},{7,1},{8,10},{10,12},{12... | collective-permute-start | bytes 294920 | tf_op jit(solution)/shard_map/ppermute | solution.py:33
  52.0 4.6 %collective-permute-start.11 = (bf16[48,1024]{1,0:T(8,128)(2,1)}, bf16[48,1024]{1,0:T(8,128)(2,1)S(1)}, u32[]{:S(2)}, u32[]{:S(2)}) collective-permute-start(bf16[48,1024]{1,0:T(8,128)(2,1)} %get-tuple-element.49.refs_0_), channel_id=1, source_target_pairs={{0,6},{2,0},{4,2},{6,4},{1,7},{3,1},{5,3},{7,5},{8,14},{10,8},{12,... | collective-permute-start | bytes 294920 | tf_op jit(solution)/shard_map/ppermute | solution.py:33
  54.8 5.0 %collective-permute-start.12 = (bf16[48,1024]{1,0:T(8,128)(2,1)}, bf16[48,1024]{1,0:T(8,128)(2,1)}, u32[]{:S(2)}, u32[]{:S(2)}) collective-permute-start(bf16[48,1024]{1,0:T(8,128)(2,1)} %get-tuple-element.49.refs_0_), channel_id=1, source_target_pairs={{0,1},{1,0},{2,3},{3,2},{4,5},{5,4},{6,7},{7,6},{8,9},{9,8},{10,11... | collective-permute-start | bytes 294920 | tf_op jit(solution)/shard_map/ppermute | solution.py:29
  56.1 3.8 %collective-permute-start.13 = (bf16[48,1024]{1,0:T(8,128)(2,1)S(1)}, bf16[48,1024]{1,0:T(8,128)(2,1)}, u32[]{:S(2)}, u32[]{:S(2)}) collective-permute-start(bf16[48,1024]{1,0:T(8,128)(2,1)S(1)} %collective-permute-done.8.refs_1_), channel_id=1, source_target_pairs={{0,1},{1,0},{2,3},{3,2},{4,5},{5,4},{6,7},{7,6},{8,9},{9,8},{10,11... | collective-permute-start | bytes 294920 | tf_op jit(solution)/shard_map/ppermute | solution.py:29
  56.1 3.7 %collective-permute-start.14 = (bf16[48,1024]{1,0:T(8,128)(2,1)S(1)}, bf16[48,1024]{1,0:T(8,128)(2,1)}, u32[]{:S(2)}, u32[]{:S(2)}) collective-permute-start(bf16[48,1024]{1,0:T(8,128)(2,1)S(1)} %collective-permute-done.9.refs_2_), channel_id=1, source_target_pairs={{0,1},{1,0},{2,3},{3,2},{4,5},{5,4},{6,7},{7,6},{8,9},{9,8},{10,11... | collective-permute-start | bytes 294920 | tf_op jit(solution)/shard_map/ppermute | solution.py:29
  56.6 4.1 %collective-permute-start.15 = (bf16[48,1024]{1,0:T(8,128)(2,1)S(1)}, bf16[48,1024]{1,0:T(8,128)(2,1)}, u32[]{:S(2)}, u32[]{:S(2)}) collective-permute-start(bf16[48,1024]{1,0:T(8,128)(2,1)S(1)} %collective-permute-done.11.refs_3_), channel_id=1, source_target_pairs={{0,1},{1,0},{2,3},{3,2},{4,5},{5,4},{6,7},{7,6},{8,9},{9,8},{10,11... | collective-permute-start | bytes 294920 | tf_op jit(solution)/shard_map/ppermute | solution.py:29
  60.7 0.9 copy-start.5
  65.8 19.4 %all-to-all-start.1 = ((bf16[16,24,896]{2,1,0:T(8,128)(2,1)}), bf16[16,24,896]{2,1,0:T(8,128)(2,1)S(1)}, u32[]{:S(2)}, u32[]{:S(2)}) async-start(bf16[16,24,896]{2,1,0:T(8,128)(2,1)} %project.1), calls=%async_computation.1 | async-start | bytes 1376256 | tf_op jit(solution)/shard_map/all_to_all | solution.py:627
  85.2 0.9 copy-start.6
  87.5 0.6 copy-start.7
  88.1 22.8 %all-to-all-start.2 = ((bf16[32,22,8,128]{3,2,1,0:T(8,128)(2,1)}), bf16[32,22,8,128]{3,2,1,0:T(8,128)(2,1)S(1)}, u32[]{:S(2)}, u32[]{:S(2)}) async-start(bf16[32,22,8,128]{3,2,1,0:T(8,128)(2,1)} %get-tuple-element.55), calls=%async_computation.2 | async-start | bytes 2883584 | tf_op jit(solution)/shard_map/all_to_all | solution.py:633
  92.1 2.2 %copy-start.2 = (bf16[7168,288]{0,1:T(8,128)(2,1)S(1)}, bf16[7168,288]{0,1:T(8,128)(2,1)}, u32[]{:S(2)}) copy-start(bf16[7168,288]{0,1:T(8,128)(2,1)} %param.18) | copy-start | bytes 12386308
  102.2 19.6 %collective-permute-start.20 = (bf16[288,3584]{1,0:T(8,128)(2,1)}, bf16[288,3584]{1,0:T(8,128)(2,1)}, u32[]{:S(2)}, u32[]{:S(2)}) collective-permute-start(bf16[288,3584]{1,0:T(8,128)(2,1)} %get-tuple-element.63), channel_id=1, source_target_pairs={{0,1},{1,0},{2,3},{3,2},{4,5},{5,4},{6,7},{7,6},{8,9},{9,8},{10,11... | collective-permute-start | bytes 6193160 | tf_op jit(solution)/shard_map/ppermute | solution.py:29
  110.9 8.5 %collective-permute-start.18 = (bf16[8,4,22,8,128]{4,3,2,1,0:T(8,128)(2,1)S(1)}, bf16[8,4,22,8,128]{4,3,2,1,0:T(8,128)(2,1)S(1)}, u32[]{:S(2)}, u32[]{:S(2)}) collective-permute-start(bf16[8,4,22,8,128]{4,3,2,1,0:T(8,128)(2,1)S(1)} %bitcast.11), channel_id=1, source_target_pairs={{0,1},{1,0},{2,3},{3,2},{4,5},{5,4},{6,7},{7,6},{8,9},{9,8},{10,11... | collective-permute-start | bytes 4325384 | tf_op jit(solution)/shard_map/ppermute | solution.py:29
  113.7 3.3 %copy-start = (bf16[576,7168]{1,0:T(8,128)(2,1)S(1)}, bf16[576,7168]{1,0:T(8,128)(2,1)}, u32[]{:S(2)}) copy-start(bf16[576,7168]{1,0:T(8,128)(2,1)} %get-tuple-element.59.weight_ref) | copy-start | bytes 24772612
  119.4 3.9 %copy-start.8 = (f32[24,896]{1,0:T(8,128)S(1)}, f32[24,896]{1,0:T(8,128)}, u32[]{:S(2)}) copy-start(f32[24,896]{1,0:T(8,128)} %copy-done.7) | copy-start | bytes 258052
  121.8 1.5 collective-permute-start.19
  152.6 2.9 %collective-permute-start.21 = (bf16[3,3584]{1,0:T(4,128)(2,1)S(1)}, bf16[3,3584]{1,0:T(4,128)(2,1)S(1)}, u32[]{:S(2)}, u32[]{:S(2)}) collective-permute-start(bf16[3,3584]{1,0:T(4,128)(2,1)S(1)} %get-tuple-element.66), channel_id=1, source_target_pairs={{0,1},{1,0},{2,3},{3,2},{4,5},{5,4},{6,7},{7,6},{8,9},{9,8},{10,11... | collective-permute-start | bytes 64520 | tf_op jit(solution)/shard_map/ppermute | solution.py:29

commit v8 on v7

--- a/solution.py
+++ b/solution.py
@@ -76,11 +76,17 @@
 
 
 def attend_kernel(
-    info_ref, lengths_ref, query_hbm, cache_hbm, out_proj_hbm, theirs_hbm, out_ref, *refs
+    info_ref,
+    lengths_ref,
+    query_hbm,
+    cache_hbm,
+    up_hbm,
+    stream_hbm,
+    out_ref,
+    *refs,
 ):
-    cuts, (query_ref, cache_ref, weight_ref, sems) = refs[:3], refs[3:]
-    half = theirs_hbm.shape[1]
-    mine = out_proj_hbm.at[:, pl.ds(pl.multiple_of(info_ref[3] * half, LANES), half)]
+    maps = refs[:4]
+    query_ref, cache_ref, up_ref, stream_ref, sems = refs[4:]
     rows, _, heads = query_ref.shape
     keys = cache_ref.shape[2]
     pairs = rows // 2
@@ -90,10 +96,10 @@
         )
         for pair in range(pairs)
     ]
-    for side, ref in enumerate((mine, theirs_hbm)):
-        copies.append(
-            pltpu.make_async_copy(ref, weight_ref.at[side], sems.at[pairs + 1 + side])
-        )
+    copies += [
+        pltpu.make_async_copy(up_hbm, up_ref, sems.at[pairs + 1]),
+        pltpu.make_async_copy(stream_hbm, stream_ref, sems.at[pairs + 2]),
+    ]
     for copy in copies:
         copy.start()
     copies[0].wait()
@@ -132,34 +138,43 @@
         table = jnp.where(lane == row + 2 * SUB, total_high, table)
         table = jnp.where(lane == row + 3 * SUB, total_low, table)
     out_ref[:, rows * len(tiles)] = table.reshape(heads // SUB, SUB, LANES).astype(BF16)
-    copies[-2].wait()
-    copies[-1].wait()
-    for step, cut_ref in enumerate(cuts):
-        columns = cut_ref.shape[0] // 2
-        first = lax.rem(info_ref[5] + step + 1, 4) * columns
-        for side in range(2):
-            for column in range(columns):
-                start = pl.multiple_of((first + column) * LANES, LANES)
-                cut_ref[side * columns + column] = weight_ref[side, :, pl.ds(start, LANES)]
-
-
-def attend(info, lengths, query, cache, out_proj, theirs):
+    for copy in copies[-2:]:
+        copy.wait()
+    eighth = stream_ref.shape[1] // 8
+    columns = eighth // LANES
+    ups = up_ref.shape[1] // LANES
+    lines_own = stream_ref.shape[0]
+    for step, map_ref in enumerate(maps):
+        map_ref[:ups] = up_ref[0].reshape(ups, LANES, LANES)
+        lines = []
+        for side in (3, 4):
+            chip = info_ref[side] * 4 + lax.rem(info_ref[5] + step, 4)
+            first = pl.multiple_of(chip * eighth, LANES)
+            data = stream_ref[:, pl.ds(first, eighth)].astype(F32)
+            for lane in range(0, eighth, LANES):
+                lines.append(data[:, lane : lane + LANES])
+                lines.append(jnp.zeros((SUB - lines_own, LANES), F32))
+            lines.append(jnp.zeros((LANES // 2 - columns * SUB, LANES), F32))
+        map_ref[ups] = jnp.concatenate(lines, axis=0).astype(BF16)
+
+
+def attend(info, lengths, query, cache, value_up, stream):
     rows, depth, heads = query.shape
     keys = cache.shape[2]
     shape = (heads // SUB, rows * (LAT // LANES) + 1, SUB, LANES)
-    columns = out_proj.shape[1] // 8 // LANES
     return call(
         attend_kernel,
         "attend",
         [info, lengths],
-        [query, cache, out_proj, theirs],
+        [query, cache, value_up, stream],
         [ANYWHERE] * 4,
         [jax.ShapeDtypeStruct(shape, BF16)]
-        + [jax.ShapeDtypeStruct((2 * columns, LANES, LANES), BF16)] * 3,
+        + [jax.ShapeDtypeStruct((value_up.shape[1] // LANES + 1, LANES, LANES), BF16)] * 4,
         [
             pltpu.VMEM(query.shape, BF16),
             pltpu.VMEM(cache.shape, BF16),
-            pltpu.VMEM((2,) + theirs.shape, BF16),
+            pltpu.VMEM(value_up.shape, BF16),
+            pltpu.VMEM(stream.shape, BF16),
             pltpu.SemaphoreType.DMA((rows // 2 + 3,)),
         ],
         2 * rows * heads * keys * (depth + LAT),
@@ -167,56 +182,56 @@
     )
 
 
-def early_kernel(info_ref, up_ref, stream_ref, half_ref, send_ref, *outs):
-    send_ref[...] = half_ref[...]
-    rows, width = stream_ref.shape
-    eighth = width // 8
-    ups = up_ref.shape[1] // LANES
-    for step, out_ref in enumerate(outs):
-        out_ref[:ups] = up_ref[0].reshape(ups, LANES, LANES)
-        chip = lax.rem(info_ref[5] + step, 4)
-        lines = []
-        for side in (3, 4):
-            start = pl.multiple_of((info_ref[side] * 4 + chip) * eighth, LANES)
-            data = stream_ref[:, pl.ds(start, eighth)].astype(F32)
-            for lane in range(0, eighth, LANES):
-                lines.append(data[:, lane : lane + LANES])
-                lines.append(jnp.zeros((SUB - rows, LANES), F32))
-            lines.append(jnp.zeros((LANES // 2 - eighth // LANES * SUB, LANES), F32))
-        out_ref[ups] = jnp.concatenate(lines, axis=0).astype(BF16)
-
-
-def early(info, value_up, stream, out_proj):
-    part = jax.ShapeDtypeStruct((value_up.shape[1] // LANES + 1, LANES, LANES), BF16)
-    half = (out_proj.shape[0], out_proj.shape[1] // 2)
-    return call(
-        early_kernel,
-        "early",
+def cut_kernel(info_ref, *refs):
+    del info_ref
+    steps = len(refs) // 3
+    for step in range(steps):
+        out_ref = refs[2 * steps + step]
+        columns = out_ref.shape[0] // 2
+        for side in range(2):
+            for column in range(columns):
+                span = slice(column * LANES, column * LANES + LANES)
+                out_ref[side * columns + column] = refs[side * steps + step][:, span]
+
+
+def cut(info, mine, theirs):
+    rows, half = theirs.shape
+    eighth = half // 4
+    part = jax.ShapeDtypeStruct((2 * eighth // LANES, rows, LANES), BF16)
+
+    def column(side, step):
+        return pl.BlockSpec(
+            (rows, eighth),
+            lambda i, info: (0, info[side] * 4 + lax.rem(info[5] + step, 4)),
+        )
+
+    return call(
+        cut_kernel,
+        "cut",
         [info],
-        [value_up, stream, out_proj],
-        [None, None, pl.BlockSpec(half, lambda i, info: (0, info[4]))],
-        [jax.ShapeDtypeStruct(half, BF16)] + [part] * 4,
+        [mine] * 3 + [theirs] * 3,
+        [column(3, step) for step in (1, 2, 3)] + [column(7, step) for step in (1, 2, 3)],
+        [part] * 3,
         limit=VMEM_MOST,
     )
 
 
-def stage_kernel(info_ref, gate_ref, up_ref, down_ref, out_ref, own_ref, send_ref, sems):
-    rows = gate_ref.shape[0]
-    half = own_ref.shape[1]
-    sides = [
-        down_ref.at[:, pl.ds(pl.multiple_of(info_ref[side] * half, LANES), half)]
-        for side in (4, 3)
-    ]
+def stage_kernel(info_ref, gate_ref, up_ref, down_ref, *refs):
+    outs, own_ref, send_ref, sems = refs[:2], refs[2], refs[3], refs[4]
+    rows, width = gate_ref.shape
+    half = width // 2
+
+    def part(ref, side):
+        return ref.at[:, pl.ds(pl.multiple_of(info_ref[side] * half, LANES), half)]
+
+    copies = [(part(down_ref, 4), send_ref)]
+    for side, out_ref in zip((3, 4), outs):
+        copies.append((part(gate_ref, side), out_ref.at[pl.ds(0, rows), :]))
+        copies.append((part(up_ref, side), out_ref.at[pl.ds(rows, rows), :]))
+    copies.append((part(down_ref, 3), own_ref))
     copies = [
         pltpu.make_async_copy(source, target, sems.at[index])
-        for index, (source, target) in enumerate(
-            [
-                (sides[0], send_ref),
-                (gate_ref, out_ref.at[pl.ds(0, rows), :]),
-                (up_ref, out_ref.at[pl.ds(rows, rows), :]),
-                (sides[1], own_ref),
-            ]
-        )
+        for index, (source, target) in enumerate(copies)
     ]
     for copy in copies:
         copy.start()
@@ -226,6 +241,7 @@
 
 def stage(info, gate, up, down_proj):
     rows, width = gate.shape
+    both = jax.ShapeDtypeStruct((2 * rows, width // 2), BF16)
     half = jax.ShapeDtypeStruct((down_proj.shape[0], down_proj.shape[1] // 2), BF16)
     return call(
         stage_kernel,
@@ -233,26 +249,32 @@
         [info],
         [gate, up, down_proj],
         [ANYWHERE] * 3,
-        [jax.ShapeDtypeStruct((2 * rows, width), BF16), half, half],
-        [pltpu.SemaphoreType.DMA((4,))],
+        [both, both, half, half],
+        [pltpu.SemaphoreType.DMA((6,))],
         limit=VMEM_STAGE,
-        out_specs=[WHOLE] * 3,
-    )
-
-
-def join_kernel(rows, info_ref, recv_ref, own_ref, place_ref, *refs):
+        out_specs=[WHOLE] * 4,
+    )
+
+
+def join_kernel(rows, info_ref, recv_ref, own_ref, *refs):
     blocks, sum_ref, out_ref, stream_ref = refs[:8], refs[8], refs[9], refs[10]
-    stream = []
+    lines_own = stream_ref.shape[0] // len(blocks)
+    shape = (stream_ref.shape[0], SUB)
+    target = lax.broadcasted_iota(jnp.int32, shape, 0)
+    line = lax.broadcasted_iota(jnp.int32, shape, 1)
+    stream = None
     for index, ref in enumerate(blocks):
         lines = ref[ref.shape[0] - 1].astype(F32)
         base = LANES // 2 * (index // 4)
         spans = range(base, base + stream_ref.shape[1] // LANES * SUB, SUB)
-        stream.append(jnp.concatenate([lines[span : span + SUB] for span in spans], axis=1))
-    stream = jnp.concatenate(stream, axis=0).astype(BF16)
-    shape = (stream_ref.shape[0], stream.shape[0])
-    order = lax.broadcasted_iota(jnp.int32, shape, 0) == place_ref[...]
-    order = jnp.where(order, F32(1.0), F32(0.0)).astype(BF16)
-    stream_ref[...] = jnp.dot(order, stream, preferred_element_type=F32)
+        lines = jnp.concatenate([lines[span : span + SUB] for span in spans], axis=1)
+        chip = lax.rem(info_ref[5] + 4 - index % 4, 4)
+        first = (chip * 2 + info_ref[3 + index // 4]) * lines_own
+        order = (target == line + first) & (line < lines_own)
+        order = jnp.where(order, F32(1.0), F32(0.0)).astype(BF16)
+        part = jnp.dot(order, lines.astype(BF16), preferred_element_type=F32)
+        stream = part if stream is None else stream + part
+    stream_ref[...] = stream
     sides = 2
     devs = recv_ref.shape[0] // sides
     tiles = LAT // LANES
@@ -296,11 +318,11 @@
     ).astype(BF16)
 
 
-def join(info, received, value_up, place, blocks, rows, eighth):
+def join(info, received, value_up, blocks, rows, eighth):
     devs = received.shape[0] // 2
     count = rows * devs
     sums = np.repeat(np.eye(count, dtype=np.float32), SUB, axis=1)
-    arrays = [received, value_up, place, *blocks, jnp.asarray(sums, BF16)]
+    arrays = [received, value_up, *blocks, jnp.asarray(sums, BF16)]
     return call(
         functools.partial(join_kernel, rows),
         "join",
@@ -316,10 +338,9 @@
     )
 
 
-def project_kernel(info_ref, place_ref, *refs):
+def project_kernel(info_ref, natural_ref, *refs):
     values, own_ref, theirs_ref = refs[:8], refs[8], refs[9]
     parts, out_ref = refs[10:13], refs[13]
-    del info_ref
     rows = []
     for source, ref in enumerate(values):
         data = ref[...]
@@ -332,7 +353,12 @@
         rows.append(jnp.concatenate(lanes, axis=1))
     left = jnp.concatenate(rows, axis=0)
     count = left.shape[0]
-    order = lax.broadcasted_iota(jnp.int32, (count, count), 0) == place_ref[...]
+    place = natural_ref[0:1]
+    for source in range(8):
+        chip = lax.rem(info_ref[5] + 4 - source % 4, 4)
+        first = (chip * 2 + info_ref[3 + source // 4]) * (count // 64)
+        place = place + jnp.where(natural_ref[1:2] == source, first, 0)
+    order = lax.broadcasted_iota(jnp.int32, (count, count), 0) == place
     order = jnp.where(order, F32(1.0), F32(0.0)).astype(BF16)
     left = jnp.dot(order, left, preferred_element_type=F32).astype(BF16)
     columns = own_ref.shape[1] // LANES
@@ -347,20 +373,24 @@
     out_ref[...] = total.reshape(out_ref.shape).astype(BF16)
 
 
-def project(info, place, values, out_proj, out_theirs, parts, chips):
+def project(info, values, out_proj, out_theirs, parts, chips):
     rows = sum(value.shape[0] for value in values)
     lanes = out_proj.shape[0]
     eighth = out_proj.shape[1] // 8
+    line = np.arange(rows) % (rows // 8)
+    natural = np.stack([line % 8 * (rows // 8) + line // 8, np.arange(rows) // (rows // 8)])
+    natural = jnp.asarray(natural, jnp.int32)
     own = pl.BlockSpec((lanes, eighth), lambda i, info: (0, info[0]))
     other = pl.BlockSpec((lanes, eighth), lambda i, info: (0, info[5]))
     return call(
         project_kernel,
         "project",
         [info],
-        [place, *values, out_proj, out_theirs, *parts],
+        [natural, *values, out_proj, out_theirs, *parts],
         [None] * 9 + [own, other] + [None] * 3,
         jax.ShapeDtypeStruct((chips, rows // chips, eighth), BF16),
         work=2 * rows * 8 * lanes * eighth,
+        limit=VMEM_MOST,
     )
 
 
@@ -406,12 +436,11 @@
     )
 
 
-def units_kernel(groups, last, info_ref, recv_ref, weight_ref, *refs):
+def units_kernel(groups, last, recv_ref, weight_ref, *refs):
     sides, quarters, tiles, _, _ = recv_ref.shape
     columns = (tiles - 1) // groups
     rows = sides * groups * SUB
     depth = columns * LANES
-    which = 4 if last else 3
     lane = lax.broadcasted_iota(jnp.int32, (SUB, LANES), 1)
     total = squares = None
     for quarter in range(quarters):
@@ -424,10 +453,9 @@
             ],
             axis=1,
         ).astype(BF16)
-        start = pl.multiple_of((info_ref[which] * quarters + quarter) * depth, LANES)
         part = lax.dot_general(
             left,
-            weight_ref[:, pl.ds(start, depth)],
+            weight_ref[:, quarter * depth : quarter * depth + depth],
             (((1,), (1,)), ((), ())),
             preferred_element_type=F32,
         )
@@ -450,14 +478,14 @@
     else:
         acc_ref, sq_ref, out_ref = refs
         hidden = out_ref.shape[1]
-        scale = lax.rsqrt((sq_ref[:, :1] + squares) / weight_ref.shape[1] + 1e-06)
+        scale = lax.rsqrt((sq_ref[:, :1] + squares) / (2 * weight_ref.shape[1]) + 1e-06)
         total = total + acc_ref[...]
         gate = total[:, :hidden] * scale
         upper = total[:, hidden:] * scale
         out_ref[...] = (gate / (1.0 + jnp.exp(-gate)) * upper).astype(BF16)
 
 
-def units(info, received, weight, groups, carry=()):
+def units(received, weight, groups, carry=()):
     sides, quarters, tiles = received.shape[:3]
     hidden = weight.shape[0] // 2
     rows = sides * groups * SUB
@@ -470,11 +498,11 @@
     return call(
         functools.partial(units_kernel, groups, last),
         "units_last" if last else "units_first",
-        [info],
+        [],
         [received, weight, *carry],
         [WHOLE] * (2 + len(carry)),
         single if last else double,
-        work=rows * weight.size,
+        work=2 * rows * weight.size,
         out_specs=WHOLE if last else [WHOLE] * 2,
     )
 
@@ -582,42 +610,33 @@
     info = [core * 4 + ring, core, group, core, 1 - core, ring, lax.axis_index("zh"), 0]
     info = jnp.stack(info).astype(jnp.int32)
 
-    out_send, own, *starts = early(info, value_up, stream, out_proj)
-    out_theirs = swap(out_send)
-    firsts = [shift(part, step) for step, part in zip((1, 2, 3), starts)]
     gain = block(norm_gain, core * 4 + ring, eighth, 0)[None]
 
-    payload, *cuts = attend(
+    out_theirs = swap(block(out_proj, 1 - core, half, 1))
+    payload, own, *firsts = attend(
         info,
         lengths,
         query_latent.transpose(0, 2, 1),
         latent_cache.transpose(0, 2, 1),
-        out_proj,
-        out_theirs,
-    )
-    payload, *firsts = lax.optimization_barrier((payload, *firsts))
+        value_up,
+        stream,
+    )
+    payload, out_theirs = lax.optimization_barrier((payload, out_theirs))
+    firsts = [shift(part, step) for step, part in zip((1, 2, 3), firsts)]
+    parts = list(cut(info, out_proj, out_theirs))
+    parts[0], parts[2], *firsts = lax.optimization_barrier((parts[0], parts[2], *firsts))
     firsts_theirs = [swap(part) for part in [own] + firsts]
-    parts = [shift(part, step) for step, part in zip((1, 2, 3), cuts)]
+    part_one, part_three = shift(parts[0], 1), shift(parts[2], 3)
     received = lax.all_to_all(payload, OUTER, split_axis=0, concat_axis=0, tiled=True)
-    chip = (ring - jnp.arange(8)) % 4
-    side = jnp.where(jnp.arange(8) < 4, core, 1 - core)
-    line = jnp.arange(SUB)[None]
-    place = ((chip * 2 + side) * rows_own)[:, None] + line
-    place = jnp.where(line < rows_own, place, -1).reshape(1, 8 * SUB).astype(jnp.int32)
     blocks = [own] + firsts + firsts_theirs
-    values, stream_rows = join(info, received, value_up, place, blocks, rows, eighth)
-
-    last, parts[0] = lax.optimization_barrier((values, parts[0]))
-    ring_values = [values, shift(values, 1), shift(values, 2), shift(last, 3)]
-    late, _ = lax.optimization_barrier((values, ring_values[1]))
-    both_values = ring_values + [swap(piece) for piece in [late] + ring_values[1:]]
-    row = jnp.arange(8 * rows)
-    natural = jnp.tile(row % 8 * (8 * rows) + row // 8, 8).reshape(8, 8 * rows)
-    place = natural[:, : 8 * rows] + ((chip * 2 + side) * rows)[:, None]
-    place = place.reshape(1, 64 * rows).astype(jnp.int32)
+    values, stream_rows = join(info, received, value_up, blocks, rows, eighth)
+    far, part_one, part_three = lax.optimization_barrier((parts[1], part_one, part_three))
+    parts = [part_one, shift(far, 2), part_three]
+
+    ring_values = [values] + [shift(values, step) for step in (1, 2, 3)]
+    both_values = ring_values + [swap(piece) for piece in ring_values]
     partial = project(
         info,
-        place,
         both_values,
         out_proj,
         out_theirs,
@@ -633,11 +652,11 @@
     piece = lax.all_to_all(payload, SIDE_CHIPS, split_axis=0, concat_axis=0, tiled=True)
     piece = piece.reshape((8, 4) + piece.shape[1:])
     other = swap(piece)
-    weight, down_own, down_send = stage(info, gate_proj.T, up_proj.T, down_proj)
+    first_weight, last_weight, down_own, down_send = stage(info, gate_proj.T, up_proj.T, down_proj)
     down_theirs = swap(down_send)
     groups = 8 * rows_own // SUB
-    carry = units(info, piece, weight, groups)
-    hidden = units(info, other, weight, groups, carry)
+    carry = units(piece, first_weight, groups)
+    hidden = units(other, last_weight, groups, carry)
     partial = down(info, hidden, swap(hidden), down_own, down_theirs, residual, 32)
     parts = lax.all_to_all(partial, SIDE_CHIPS, split_axis=0, concat_axis=0, tiled=True)
     mine, theirs = finish(info, parts)

time: 157 us -> 155 us (0.987)
  starting transfers between devices: 44 us -> 48 us
  local copies, waits for them, and re-layouts: 12.3 us -> 9.8 us
  waiting for transfers between devices: 37.2 us -> 35.4 us
    all_to_all x1, waiting for transfers between devices: 5.99 us -> 0.01 us  [local(): lax.all_to_all(payload, OUTER, split_axis=0, concat_axis=0, tiled=True)]
    ppermute x9, starting transfers between devices: 9.86 us -> 12.9 us  [shift(): return lax.ppermute(array, 'y', [(i, (i + step) % 4) for i in range(4)])]
    unnamed x34 -> x52, local copies, waits for them, and re-layouts: 10.1 us -> 7.1 us
    all_to_all x1, waiting for transfers between devices: 6.9 us -> 8.63 us  [local(): lax.all_to_all(payload, SIDE_CHIPS, split_axis=0, concat_axis=0, tiled=True)]
  transfers between devices with their start and end apart: 25 -> 25, of which waited for: 8 -> 13; matrix products, arithmetic and copies ran while one was open for 1% -> 1% of each run, Pallas kernels for 15% -> 16%
where the time goes in v8:
time: 155 us
  starting transfers between devices  48 us (31%)
  Pallas kernels  36.2 us (23%)
  waiting for transfers between devices  35.4 us (23%)
  blocking collectives  24.2 us (16%)
  local copies, waits for them, and re-layouts  9.8 us (6%)
    pallas_call x10, Pallas kernels, call(): pl.pallas_call(kernel, out_shape=outs, grid_spec=pltpu.PrefetchScalarGrid...  36.2 us
    all_to_all x1, blocking collectives, local(): lax.all_to_all(partial, SIDE_CHIPS, split_axis=0, concat_axis=0, tiled=True)  24.2 us
    ppermute x13, starting transfers between devices, swap(): return lax.ppermute(array, 'core', SWAP)  16.1 us
    ppermute x9, starting transfers between devices, shift(): return lax.ppermute(array, 'y', [(i, (i + step) % 4) for i in range(4)])  12.9 us
    all_to_all x1, waiting for transfers between devices, local(): lax.all_to_all(partial, OUTER, split_axis=0, concat_axis=0, tiled=True)  11.7 us
    ppermute x9, waiting for transfers between devices, shift(): return lax.ppermute(array, 'y', [(i, (i + step) % 4) for i in range(4)])  10.4 us
    all_to_all x1, waiting for transfers between devices, local(): lax.all_to_all(payload, SIDE_CHIPS, split_axis=0, concat_axis=0, tiled=True)  8.63 us
    all_to_all x1, starting transfers between devices, local(): lax.all_to_all(payload, OUTER, split_axis=0, concat_axis=0, tiled=True)  7.6 us
  transfers between devices with their start and end apart: 25, of which 13 were waited for; matrix products, arithmetic and copies ran while one was open for 1% of the time, Pallas kernels for 16%

profile of v8, /device:TPU:1, one launch (start us, length us, event | category | flops | bytes accessed | tf_op | source)
XLA Modules:
  0.0 154.5 jit_solution(11194634319910093929)
XLA Ops:
  0.0 1.2 constant_dynamic-slice_fusion
  1.2 1.5 collective-permute-start
  2.7 0.7 stack.28.info_ref
  3.4 6.5 %attend.1 = (bf16[16,25,8,128]{3,2,1,0:T(8,128)(2,1)}, bf16[5,128,128]{2,1,0:T(8,128)(2,1)}, bf16[5,128,128]{2,1,0:T(8,128)(2,1)}, bf16[5,128,128]{2,1,0:T(8,128)(2,1)}, bf16[5,128,128]{2,1,0:T(8,128)(2,1)}) custom-call(s32[8]{0:T(128)} %stack.28.info_ref, s32[6]{0:T(128)} %lengths_ref.1, bf16[6,576,128]{2,1,0:T(8,128)(2,1)} %bitcast.16, ...), custom_call_target="tpu_custom_call" | custom-call | flops 855638016 | bytes 6072320 | tf_op jit(solution)/shard_map/attend/pallas_call | solution.py:51
  9.9 1.5 collective-permute-start.1
  11.4 2.6 %collective-permute-start.2 = (bf16[5,128,128]{2,1,0:T(8,128)(2,1)}, bf16[5,128,128]{2,1,0:T(8,128)(2,1)S(1)}, u32[]{:S(2)}, u32[]{:S(2)}) collective-permute-start(bf16[5,128,128]{2,1,0:T(8,128)(2,1)} %get-tuple-element.46), channel_id=1, source_target_pairs={{0,4},{2,6},{4,0},{6,2},{1,5},{3,7},{5,1},{7,3},{8,12},{10,14},{12... | collective-permute-start | bytes 491528 | tf_op jit(solution)/shard_map/ppermute | solution.py:33
  14.0 1.1 collective-permute-start.3
  15.1 0.0 collective-permute-done.refs_3_.refs_4_.refs_5_.refs_9_
  15.1 7.6 %all-to-all-start = ((bf16[16,25,8,128]{3,2,1,0:T(8,128)(2,1)}), bf16[16,25,8,128]{3,2,1,0:T(8,128)(2,1)S(1)}, u32[]{:S(2)}, u32[]{:S(2)}) async-start(bf16[16,25,8,128]{3,2,1,0:T(8,128)(2,1)} %get-tuple-element.40), calls=%async_computation | async-start | bytes 1638400 | tf_op jit(solution)/shard_map/all_to_all | solution.py:630
  22.7 3.5 %cut.1 = (bf16[14,128,128]{2,1,0:T(8,128)(2,1)}, bf16[14,128,128]{2,1,0:T(8,128)(2,1)}, bf16[14,128,128]{2,1,0:T(8,128)(2,1)}) custom-call(s32[8]{0:T(128)} %stack.28.info_ref, bf16[128,7168]{1,0:T(8,128)(2,1)} %refs_8_.2, bf16[128,7168]{1,0:T(8,128)(2,1)} %refs_8_.2, bf16[128,7168]{1,0:T(8,128)(2,1)} %refs_8_.2, bf16[128,3584]{1,0:T(8,128)(2,1)} %copy-done.7, ...), custom_call_target="tpu_custom_call" | custom-call | bytes 9633792 | tf_op jit(solution)/shard_map/cut/pallas_call | solution.py:51
  26.3 0.0 collective-permute-done.2.refs_2_
  26.3 0.5 collective-permute-start.15
  26.8 2.3 %collective-permute-start.16 = (bf16[14,128,128]{2,1,0:T(8,128)(2,1)}, bf16[14,128,128]{2,1,0:T(8,128)(2,1)S(1)}, u32[]{:S(2)}, u32[]{:S(2)}) collective-permute-start(bf16[14,128,128]{2,1,0:T(8,128)(2,1)} %get-tuple-element.54), channel_id=1, source_target_pairs={{0,6},{2,0},{4,2},{6,4},{1,7},{3,1},{5,3},{7,5},{8,14},{10,8},{12,... | collective-permute-start | bytes 1376264 | tf_op jit(solution)/shard_map/ppermute | solution.py:33
  29.0 9.6 %collective-permute-done.15.refs_10_ = bf16[14,128,128]{2,1,0:T(8,128)(2,1)S(1)} collective-permute-done((bf16[14,128,128]{2,1,0:T(8,128)(2,1)}, bf16[14,128,128]{2,1,0:T(8,128)(2,1)S(1)}, u32[]{:S(2)}, u32[]{:S(2)}) %collective-permute-start.15) | collective-permute-done | bytes 458784 | tf_op jit(solution)/shard_map/ppermute | solution.py:33
  38.7 0.0 collective-permute-done.16.refs_12_
  38.7 1.2 collective-permute-start.17
  39.8 2.3 %collective-permute-start.4 = (bf16[5,128,128]{2,1,0:T(8,128)(2,1)S(1)}, bf16[5,128,128]{2,1,0:T(8,128)(2,1)S(1)}, u32[]{:S(2)}, u32[]{:S(2)}) collective-permute-start(bf16[5,128,128]{2,1,0:T(8,128)(2,1)S(1)} %copy-done.12), channel_id=1, source_target_pairs={{0,1},{1,0},{2,3},{3,2},{4,5},{5,4},{6,7},{7,6},{8,9},{9,8},{10,11... | collective-permute-start | bytes 491528 | tf_op jit(solution)/shard_map/ppermute | solution.py:29
  42.2 0.0 collective-permute-start.5
  42.2 0.5 collective-permute-start.6
  42.7 0.0 collective-permute-start.7
  42.7 0.5 collective-permute-done.4.refs_4_
  43.2 0.4 collective-permute-done.5.refs_5_
  43.6 0.3 collective-permute-done.6.refs_6_
  43.9 0.3 collective-permute-done.7.refs_7_
  44.3 0.3 copy-done.18
  44.6 0.9 copy-done.8
  45.5 3.9 %join.1 = (bf16[48,1024]{1,0:T(8,128)(2,1)}, f32[24,896]{1,0:T(8,128)}) custom-call(s32[8]{0:T(128)} %stack.28.info_ref, bf16[16,25,8,128]{3,2,1,0:T(8,128)(2,1)} %copy-done.8, bf16[1,512,128]{2,1,0:T(8,128)(2,1)} %own_ref.1, bf16[5,128,128]{2,1,0:T(8,128)(2,1)} %get-tuple-element.41.refs_0_, bf16[5,128,128]{2,1,0:T(8,128)(2,1)} %copy-done.13, ...), custom_call_target="tpu_custom_call" | custom-call | flops 480000000 | bytes 2439168 | tf_op jit(solution)/shard_map/join/pallas_call | solution.py:51
  49.3 1.2 collective-permute-start.10
  50.5 2.7 %collective-permute-start.9 = (bf16[48,1024]{1,0:T(8,128)(2,1)}, bf16[48,1024]{1,0:T(8,128)(2,1)S(1)}, u32[]{:S(2)}, u32[]{:S(2)}) collective-permute-start(bf16[48,1024]{1,0:T(8,128)(2,1)} %get-tuple-element.51.refs_0_), channel_id=1, source_target_pairs={{0,4},{2,6},{4,0},{6,2},{1,5},{3,7},{5,1},{7,3},{8,12},{10,14},{12... | collective-permute-start | bytes 294920 | tf_op jit(solution)/shard_map/ppermute | solution.py:33
  53.2 0.0 collective-permute-start.8
  53.2 0.9 collective-permute-start.11
  54.1 0.4 collective-permute-done.10.refs_3_
  54.6 1.3 collective-permute-start.14
  55.9 0.2 collective-permute-done.9.refs_2_
  56.0 2.0 %collective-permute-start.13 = (bf16[48,1024]{1,0:T(8,128)(2,1)S(1)}, bf16[48,1024]{1,0:T(8,128)(2,1)S(1)}, u32[]{:S(2)}, u32[]{:S(2)}) collective-permute-start(bf16[48,1024]{1,0:T(8,128)(2,1)S(1)} %collective-permute-done.9.refs_2_), channel_id=1, source_target_pairs={{0,1},{1,0},{2,3},{3,2},{4,5},{5,4},{6,7},{7,6},{8,9},{9,8},{10,11... | collective-permute-start | bytes 294920 | tf_op jit(solution)/shard_map/ppermute | solution.py:29
  58.1 0.2 collective-permute-done.8.refs_1_
  58.3 1.9 %collective-permute-start.12 = (bf16[48,1024]{1,0:T(8,128)(2,1)S(1)}, bf16[48,1024]{1,0:T(8,128)(2,1)S(1)}, u32[]{:S(2)}, u32[]{:S(2)}) collective-permute-start(bf16[48,1024]{1,0:T(8,128)(2,1)S(1)} %collective-permute-done.8.refs_1_), channel_id=1, source_target_pairs={{0,1},{1,0},{2,3},{3,2},{4,5},{5,4},{6,7},{7,6},{8,9},{9,8},{10,11... | collective-permute-start | bytes 294920 | tf_op jit(solution)/shard_map/ppermute | solution.py:29
  60.2 0.0 collective-permute-done.11.refs_4_
  60.2 0.9 collective-permute-done.12.refs_5_
  61.2 0.6 copy-done.25
  61.8 4.7 %project.1 = bf16[16,24,896]{2,1,0:T(8,128)(2,1)} custom-call(s32[8]{0:T(128)} %stack.28.info_ref, s32[2,384]{1,0:T(2,128)} %constant.38.clone.natural_ref, bf16[48,1024]{1,0:T(8,128)(2,1)} %get-tuple-element.51.refs_0_, bf16[48,1024]{1,0:T(8,128)(2,1)} %copy-done.21, bf16[48,1024]{1,0:T(8,128)(2,1)} %copy-done.20, bf16[48,1024]{1,0:T(8,128)(2,1)} %copy-done.19, ...), custom_call_target="tpu_custom_call" | custom-call | flops 704643072 | bytes 5604864 | tf_op jit(solution)/shard_map/project/pallas_call | solution.py:51
  66.5 6.7 %all-to-all-start.1 = ((bf16[16,24,896]{2,1,0:T(8,128)(2,1)}), bf16[16,24,896]{2,1,0:T(8,128)(2,1)S(1)}, u32[]{:S(2)}, u32[]{:S(2)}) async-start(bf16[16,24,896]{2,1,0:T(8,128)(2,1)} %project.1), calls=%async_computation.1 | async-start | bytes 1376256 | tf_op jit(solution)/shard_map/all_to_all | solution.py:646
  73.2 0.8 dynamic_slice.7
  74.0 11.7 %all-to-all-done.1.parts_ref = bf16[16,24,896]{2,1,0:T(8,128)(2,1)S(1)} async-done(((bf16[16,24,896]{2,1,0:T(8,128)(2,1)}), bf16[16,24,896]{2,1,0:T(8,128)(2,1)S(1)}, u32[]{:S(2)}, u32[]{:S(2)}) %all-to-all-start.1) | async-done | bytes 688160 | tf_op jit(solution)/shard_map/all_to_all | solution.py:646
  85.7 1.4 residual.1
  87.1 0.6 copy-done.4
  87.7 4.7 %all-to-all-start.2 = ((bf16[32,22,8,128]{3,2,1,0:T(8,128)(2,1)}), bf16[32,22,8,128]{3,2,1,0:T(8,128)(2,1)S(1)}, u32[]{:S(2)}, u32[]{:S(2)}) async-start(bf16[32,22,8,128]{3,2,1,0:T(8,128)(2,1)} %get-tuple-element.60), calls=%async_computation.2 | async-start | bytes 2883584 | tf_op jit(solution)/shard_map/all_to_all | solution.py:652
  92.4 7.9 %stage.1 = (bf16[576,3584]{1,0:T(8,128)(2,1)S(1)}, bf16[576,3584]{1,0:T(8,128)(2,1)}, bf16[288,3584]{1,0:T(8,128)(2,1)S(1)}, bf16[288,3584]{1,0:T(8,128)(2,1)}) custom-call(s32[8]{0:T(128)S(1)} %copy-done.6, bf16[288,7168]{1,0:T(8,128)(2,1)} %bitcast.13, bf16[288,7168]{1,0:T(8,128)(2,1)} %bitcast.14, bf16[288,7168]{1,0:T(8,128)(2,1)} %down_ref), custom_call_target="tpu_custom_call" | custom-call | bytes 24772608 | tf_op jit(solution)/shard_map/stage/pallas_call | solution.py:51
  100.3 2.0 %copy-done.1 = bf16[576,3584]{1,0:T(8,128)(2,1)} copy-done((bf16[576,3584]{1,0:T(8,128)(2,1)}, bf16[576,3584]{1,0:T(8,128)(2,1)S(1)}, u32[]{:S(2)}) %copy-start.1) | copy-done | bytes 4128792
  102.3 1.1 collective-permute-start.20
  103.4 8.6 %all-to-all-done.2 = bf16[32,22,8,128]{3,2,1,0:T(8,128)(2,1)S(1)} async-done(((bf16[32,22,8,128]{3,2,1,0:T(8,128)(2,1)}), bf16[32,22,8,128]{3,2,1,0:T(8,128)(2,1)S(1)}, u32[]{:S(2)}, u32[]{:S(2)}) %all-to-all-start.2) | async-done | bytes 1441824 | tf_op jit(solution)/shard_map/all_to_all | solution.py:652
  112.0 2.4 %collective-permute-start.18 = (bf16[8,4,22,8,128]{4,3,2,1,0:T(8,128)(2,1)S(1)}, bf16[8,4,22,8,128]{4,3,2,1,0:T(8,128)(2,1)S(1)}, u32[]{:S(2)}, u32[]{:S(2)}) collective-permute-start(bf16[8,4,22,8,128]{4,3,2,1,0:T(8,128)(2,1)S(1)} %bitcast.11), channel_id=1, source_target_pairs={{0,1},{1,0},{2,3},{3,2},{4,5},{5,4},{6,7},{7,6},{8,9},{9,8},{10,11... | collective-permute-start | bytes 4325384 | tf_op jit(solution)/shard_map/ppermute | solution.py:29
  114.4 2.2 %copy-done.2 = bf16[576,3584]{1,0:T(8,128)(2,1)S(1)} copy-done((bf16[576,3584]{1,0:T(8,128)(2,1)S(1)}, bf16[576,3584]{1,0:T(8,128)(2,1)}, u32[]{:S(2)}) %copy-start.2) | copy-done | bytes 4128792
  116.6 1.7 %units_first.1 = (f32[192,576]{1,0:T(8,128)S(1)}, f32[192,128]{1,0:T(8,128)S(1)}) custom-call(bf16[8,4,22,8,128]{4,3,2,1,0:T(8,128)(2,1)S(1)} %bitcast.12, bf16[576,3584]{1,0:T(8,128)(2,1)S(1)} %copy-done.2), custom_call_target="tpu_custom_call" | custom-call | flops 792723456 | bytes 5840896 | tf_op jit(solution)/shard_map/units_first/pallas_call | solution.py:51
  118.4 0.4 copy-done
  118.8 1.8 %units_last.1.mine_ref = bf16[192,288]{1,0:T(8,128)(2,1)S(1)} custom-call(bf16[8,4,22,8,128]{4,3,2,1,0:T(8,128)(2,1)S(1)} %collective-permute-done.18.recv_ref, bf16[576,3584]{1,0:T(8,128)(2,1)S(1)} %copy-done, f32[192,576]{1,0:T(8,128)S(1)} %get-tuple-element.66.refs_0_, f32[192,128]{1,0:T(8,128)S(1)} %get-tuple-element.67.refs_1_), custom_call_target="tpu_custom_call" | custom-call | flops 792723456 | bytes 5951488 | tf_op jit(solution)/shard_map/units_last/pallas_call | solution.py:51
  120.6 0.1 collective-permute-start.19
  120.7 1.3 collective-permute-done.19.theirs_ref
  122.1 3.9 %down.1 = bf16[32,7,24,128]{3,2,1,0:T(8,128)(2,1)S(1)} custom-call(s32[8]{0:T(128)S(1)} %copy-done.6, bf16[192,288]{1,0:T(8,128)(2,1)S(1)} %units_last.1.mine_ref, bf16[192,288]{1,0:T(8,128)(2,1)S(1)} %collective-permute-done.19.theirs_ref, bf16[288,3584]{1,0:T(8,128)(2,1)S(1)} %get-tuple-element.68.own_ref, ...), custom_call_target="tpu_custom_call" | custom-call | flops 792723456 | bytes 5769216 | tf_op jit(solution)/shard_map/down/pallas_call | solution.py:51
  126.0 24.2 %all_to_all.20.parts_ref = bf16[32,7,24,128]{3,2,1,0:T(8,128)(2,1)S(1)} all-to-all(bf16[32,7,24,128]{3,2,1,0:T(8,128)(2,1)S(1)} %down.1), channel_id=1, replica_groups=mesh['zh'=2,'zl'=2,'x'=4,'y'=4,'core'=2] {'zl','x','y'}, dimensions={0} | all-to-all | bytes 2752512 | tf_op jit(solution)/shard_map/all_to_all | solution.py:661
  150.2 0.8 finish.1
  151.0 2.0 %collective-permute-start.21 = (bf16[3,3584]{1,0:T(4,128)(2,1)S(1)}, bf16[3,3584]{1,0:T(4,128)(2,1)S(1)}, u32[]{:S(2)}, u32[]{:S(2)}) collective-permute-start(bf16[3,3584]{1,0:T(4,128)(2,1)S(1)} %get-tuple-element.72), channel_id=1, source_target_pairs={{0,1},{1,0},{2,3},{3,2},{4,5},{5,4},{6,7},{7,6},{8,9},{9,8},{10,11... | collective-permute-start | bytes 64520 | tf_op jit(solution)/shard_map/ppermute | solution.py:29
  153.0 0.9 collective-permute-done.21
  153.9 0.7 pad_maximum_fusion
  (55 shorter events, 0.1 us)
Async XLA Ops:
  1.2 13.8 %collective-permute-start = (bf16[128,3584]{1,0:T(8,128)(2,1)S(1)}, bf16[128,3584]{1,0:T(8,128)(2,1)S(1)}, u32[]{:S(2)}, u32[]{:S(2)}) collective-permute-start(bf16[128,3584]{1,0:T(8,128)(2,1)S(1)} %constant_dynamic-slice_fusion), channel_id=1, source_target_pairs={{0,1},{1,0},{2,3},{3,2},{4,5},{5,4},{6,7},{7,6},{8,9},{9,8},{10,11... | collective-permute-start | bytes 2752520 | tf_op jit(solution)/shard_map/ppermute | solution.py:29
  9.9 16.3 %collective-permute-start.1 = (bf16[5,128,128]{2,1,0:T(8,128)(2,1)}, bf16[5,128,128]{2,1,0:T(8,128)(2,1)S(1)}, u32[]{:S(2)}, u32[]{:S(2)}) collective-permute-start(bf16[5,128,128]{2,1,0:T(8,128)(2,1)} %get-tuple-element.45), channel_id=1, source_target_pairs={{0,2},{2,4},{4,6},{6,0},{1,3},{3,5},{5,7},{7,1},{8,10},{10,12},{12... | collective-permute-start | bytes 491528 | tf_op jit(solution)/shard_map/ppermute | solution.py:33
  11.4 14.9 %collective-permute-start.2 = (bf16[5,128,128]{2,1,0:T(8,128)(2,1)}, bf16[5,128,128]{2,1,0:T(8,128)(2,1)S(1)}, u32[]{:S(2)}, u32[]{:S(2)}) collective-permute-start(bf16[5,128,128]{2,1,0:T(8,128)(2,1)} %get-tuple-element.46), channel_id=1, source_target_pairs={{0,4},{2,6},{4,0},{6,2},{1,5},{3,7},{5,1},{7,3},{8,12},{10,14},{12... | collective-permute-start | bytes 491528 | tf_op jit(solution)/shard_map/ppermute | solution.py:33
  14.0 12.3 %collective-permute-start.3 = (bf16[5,128,128]{2,1,0:T(8,128)(2,1)}, bf16[5,128,128]{2,1,0:T(8,128)(2,1)S(1)}, u32[]{:S(2)}, u32[]{:S(2)}) collective-permute-start(bf16[5,128,128]{2,1,0:T(8,128)(2,1)} %get-tuple-element.47), channel_id=1, source_target_pairs={{0,6},{2,0},{4,2},{6,4},{1,7},{3,1},{5,3},{7,5},{8,14},{10,8},{12,... | collective-permute-start | bytes 491528 | tf_op jit(solution)/shard_map/ppermute | solution.py:33
  15.1 7.6 %copy-start.7 = (bf16[128,3584]{1,0:T(8,128)(2,1)}, bf16[128,3584]{1,0:T(8,128)(2,1)S(1)}, u32[]{:S(2)}) copy-start(bf16[128,3584]{1,0:T(8,128)(2,1)S(1)} %collective-permute-done.refs_3_.refs_4_.refs_5_.refs_9_) | copy-start | bytes 2752516
  15.1 29.1 %all-to-all-start = ((bf16[16,25,8,128]{3,2,1,0:T(8,128)(2,1)}), bf16[16,25,8,128]{3,2,1,0:T(8,128)(2,1)S(1)}, u32[]{:S(2)}, u32[]{:S(2)}) async-start(bf16[16,25,8,128]{3,2,1,0:T(8,128)(2,1)} %get-tuple-element.40), calls=%async_computation | async-start | bytes 1638400 | tf_op jit(solution)/shard_map/all_to_all | solution.py:630
  22.7 17.1 %copy-start.12 = (bf16[5,128,128]{2,1,0:T(8,128)(2,1)S(1)}, bf16[5,128,128]{2,1,0:T(8,128)(2,1)}, u32[]{:S(2)}) copy-start(bf16[5,128,128]{2,1,0:T(8,128)(2,1)} %get-tuple-element.41.refs_0_) | copy-start | bytes 491524
  26.3 18.0 %copy-start.13 = (bf16[5,128,128]{2,1,0:T(8,128)(2,1)}, bf16[5,128,128]{2,1,0:T(8,128)(2,1)S(1)}, u32[]{:S(2)}) copy-start(bf16[5,128,128]{2,1,0:T(8,128)(2,1)S(1)} %collective-permute-done.1.refs_1_) | copy-start | bytes 491524
  26.3 18.0 %copy-start.14 = (bf16[5,128,128]{2,1,0:T(8,128)(2,1)}, bf16[5,128,128]{2,1,0:T(8,128)(2,1)S(1)}, u32[]{:S(2)}) copy-start(bf16[5,128,128]{2,1,0:T(8,128)(2,1)S(1)} %collective-permute-done.2.refs_2_) | copy-start | bytes 491524
  26.3 18.0 %copy-start.15 = (bf16[5,128,128]{2,1,0:T(8,128)(2,1)}, bf16[5,128,128]{2,1,0:T(8,128)(2,1)S(1)}, u32[]{:S(2)}) copy-start(bf16[5,128,128]{2,1,0:T(8,128)(2,1)S(1)} %collective-permute-done.3.refs_3_) | copy-start | bytes 491524
  26.3 12.4 %collective-permute-start.15 = (bf16[14,128,128]{2,1,0:T(8,128)(2,1)}, bf16[14,128,128]{2,1,0:T(8,128)(2,1)S(1)}, u32[]{:S(2)}, u32[]{:S(2)}) collective-permute-start(bf16[14,128,128]{2,1,0:T(8,128)(2,1)} %get-tuple-element.53), channel_id=1, source_target_pairs={{0,2},{2,4},{4,6},{6,0},{1,3},{3,5},{5,7},{7,1},{8,10},{10,12},{12... | collective-permute-start | bytes 1376264 | tf_op jit(solution)/shard_map/ppermute | solution.py:33
  26.8 11.9 %collective-permute-start.16 = (bf16[14,128,128]{2,1,0:T(8,128)(2,1)}, bf16[14,128,128]{2,1,0:T(8,128)(2,1)S(1)}, u32[]{:S(2)}, u32[]{:S(2)}) collective-permute-start(bf16[14,128,128]{2,1,0:T(8,128)(2,1)} %get-tuple-element.54), channel_id=1, source_target_pairs={{0,6},{2,0},{4,2},{6,4},{1,7},{3,1},{5,3},{7,5},{8,14},{10,8},{12,... | collective-permute-start | bytes 1376264 | tf_op jit(solution)/shard_map/ppermute | solution.py:33
  38.6 22.5 %copy-start.9 = (bf16[14,128,128]{2,1,0:T(8,128)(2,1)}, bf16[14,128,128]{2,1,0:T(8,128)(2,1)S(1)}, u32[]{:S(2)}) copy-start(bf16[14,128,128]{2,1,0:T(8,128)(2,1)S(1)} %collective-permute-done.15.refs_10_) | copy-start | bytes 1376260
  38.7 22.5 %copy-start.10 = (bf16[14,128,128]{2,1,0:T(8,128)(2,1)}, bf16[14,128,128]{2,1,0:T(8,128)(2,1)S(1)}, u32[]{:S(2)}) copy-start(bf16[14,128,128]{2,1,0:T(8,128)(2,1)S(1)} %collective-permute-done.16.refs_12_) | copy-start | bytes 1376260
  38.7 21.5 %collective-permute-start.17 = (bf16[14,128,128]{2,1,0:T(8,128)(2,1)}, bf16[14,128,128]{2,1,0:T(8,128)(2,1)S(1)}, u32[]{:S(2)}, u32[]{:S(2)}) collective-permute-start(bf16[14,128,128]{2,1,0:T(8,128)(2,1)} %get-tuple-element.56), channel_id=1, source_target_pairs={{0,4},{2,6},{4,0},{6,2},{1,5},{3,7},{5,1},{7,3},{8,12},{10,14},{12... | collective-permute-start | bytes 1376264 | tf_op jit(solution)/shard_map/ppermute | solution.py:33
  39.8 3.4 %collective-permute-start.4 = (bf16[5,128,128]{2,1,0:T(8,128)(2,1)S(1)}, bf16[5,128,128]{2,1,0:T(8,128)(2,1)S(1)}, u32[]{:S(2)}, u32[]{:S(2)}) collective-permute-start(bf16[5,128,128]{2,1,0:T(8,128)(2,1)S(1)} %copy-done.12), channel_id=1, source_target_pairs={{0,1},{1,0},{2,3},{3,2},{4,5},{5,4},{6,7},{7,6},{8,9},{9,8},{10,11... | collective-permute-start | bytes 491528 | tf_op jit(solution)/shard_map/ppermute | solution.py:29
  42.2 1.4 collective-permute-start.5
  42.2 1.7 %collective-permute-start.6 = (bf16[5,128,128]{2,1,0:T(8,128)(2,1)S(1)}, bf16[5,128,128]{2,1,0:T(8,128)(2,1)S(1)}, u32[]{:S(2)}, u32[]{:S(2)}) collective-permute-start(bf16[5,128,128]{2,1,0:T(8,128)(2,1)S(1)} %collective-permute-done.2.refs_2_), channel_id=1, source_target_pairs={{0,1},{1,0},{2,3},{3,2},{4,5},{5,4},{6,7},{7,6},{8,9},{9,8},{10,11... | collective-permute-start | bytes 491528 | tf_op jit(solution)/shard_map/ppermute | solution.py:29
  42.7 1.5 collective-permute-start.7
  43.2 1.0 copy-start.16
  43.6 0.7 copy-start.17
  43.9 0.7 copy-start.18
  44.6 0.9 copy-start.8
  49.3 36.3 %copy-start.3 = (f32[24,896]{1,0:T(8,128)S(1)}, f32[24,896]{1,0:T(8,128)}, u32[]{:S(2)}) copy-start(f32[24,896]{1,0:T(8,128)} %get-tuple-element.58.stream_ref) | copy-start | bytes 258052
  49.3 5.2 %collective-permute-start.10 = (bf16[48,1024]{1,0:T(8,128)(2,1)}, bf16[48,1024]{1,0:T(8,128)(2,1)S(1)}, u32[]{:S(2)}, u32[]{:S(2)}) collective-permute-start(bf16[48,1024]{1,0:T(8,128)(2,1)} %get-tuple-element.51.refs_0_), channel_id=1, source_target_pairs={{0,6},{2,0},{4,2},{6,4},{1,7},{3,1},{5,3},{7,5},{8,14},{10,8},{12,... | collective-permute-start | bytes 294920 | tf_op jit(solution)/shard_map/ppermute | solution.py:33
  50.5 5.5 %collective-permute-start.9 = (bf16[48,1024]{1,0:T(8,128)(2,1)}, bf16[48,1024]{1,0:T(8,128)(2,1)S(1)}, u32[]{:S(2)}, u32[]{:S(2)}) collective-permute-start(bf16[48,1024]{1,0:T(8,128)(2,1)} %get-tuple-element.51.refs_0_), channel_id=1, source_target_pairs={{0,4},{2,6},{4,0},{6,2},{1,5},{3,7},{5,1},{7,3},{8,12},{10,14},{12... | collective-permute-start | bytes 294920 | tf_op jit(solution)/shard_map/ppermute | solution.py:33
  53.2 5.1 %collective-permute-start.8 = (bf16[48,1024]{1,0:T(8,128)(2,1)}, bf16[48,1024]{1,0:T(8,128)(2,1)S(1)}, u32[]{:S(2)}, u32[]{:S(2)}) collective-permute-start(bf16[48,1024]{1,0:T(8,128)(2,1)} %get-tuple-element.51.refs_0_), channel_id=1, source_target_pairs={{0,2},{2,4},{4,6},{6,0},{1,3},{3,5},{5,7},{7,1},{8,10},{10,12},{12... | collective-permute-start | bytes 294920 | tf_op jit(solution)/shard_map/ppermute | solution.py:33
  53.2 7.0 %collective-permute-start.11 = (bf16[48,1024]{1,0:T(8,128)(2,1)}, bf16[48,1024]{1,0:T(8,128)(2,1)S(1)}, u32[]{:S(2)}, u32[]{:S(2)}) collective-permute-start(bf16[48,1024]{1,0:T(8,128)(2,1)} %get-tuple-element.51.refs_0_), channel_id=1, source_target_pairs={{0,1},{1,0},{2,3},{3,2},{4,5},{5,4},{6,7},{7,6},{8,9},{9,8},{10,11... | collective-permute-start | bytes 294920 | tf_op jit(solution)/shard_map/ppermute | solution.py:29
  54.6 6.5 %copy-start.19 = (bf16[48,1024]{1,0:T(8,128)(2,1)}, bf16[48,1024]{1,0:T(8,128)(2,1)S(1)}, u32[]{:S(2)}) copy-start(bf16[48,1024]{1,0:T(8,128)(2,1)S(1)} %collective-permute-done.10.refs_3_) | copy-start | bytes 294916
  54.6 5.6 %collective-permute-start.14 = (bf16[48,1024]{1,0:T(8,128)(2,1)S(1)}, bf16[48,1024]{1,0:T(8,128)(2,1)S(1)}, u32[]{:S(2)}, u32[]{:S(2)}) collective-permute-start(bf16[48,1024]{1,0:T(8,128)(2,1)S(1)} %collective-permute-done.10.refs_3_), channel_id=1, source_target_pairs={{0,1},{1,0},{2,3},{3,2},{4,5},{5,4},{6,7},{7,6},{8,9},{9,8},{10,11... | collective-permute-start | bytes 294920 | tf_op jit(solution)/shard_map/ppermute | solution.py:29
  56.0 5.1 %copy-start.20 = (bf16[48,1024]{1,0:T(8,128)(2,1)}, bf16[48,1024]{1,0:T(8,128)(2,1)S(1)}, u32[]{:S(2)}) copy-start(bf16[48,1024]{1,0:T(8,128)(2,1)S(1)} %collective-permute-done.9.refs_2_) | copy-start | bytes 294916
  56.0 4.2 %collective-permute-start.13 = (bf16[48,1024]{1,0:T(8,128)(2,1)S(1)}, bf16[48,1024]{1,0:T(8,128)(2,1)S(1)}, u32[]{:S(2)}, u32[]{:S(2)}) collective-permute-start(bf16[48,1024]{1,0:T(8,128)(2,1)S(1)} %collective-permute-done.9.refs_2_), channel_id=1, source_target_pairs={{0,1},{1,0},{2,3},{3,2},{4,5},{5,4},{6,7},{7,6},{8,9},{9,8},{10,11... | collective-permute-start | bytes 294920 | tf_op jit(solution)/shard_map/ppermute | solution.py:29
  58.3 2.9 %copy-start.21 = (bf16[48,1024]{1,0:T(8,128)(2,1)}, bf16[48,1024]{1,0:T(8,128)(2,1)S(1)}, u32[]{:S(2)}) copy-start(bf16[48,1024]{1,0:T(8,128)(2,1)S(1)} %collective-permute-done.8.refs_1_) | copy-start | bytes 294916
  58.3 2.9 %collective-permute-start.12 = (bf16[48,1024]{1,0:T(8,128)(2,1)S(1)}, bf16[48,1024]{1,0:T(8,128)(2,1)S(1)}, u32[]{:S(2)}, u32[]{:S(2)}) collective-permute-start(bf16[48,1024]{1,0:T(8,128)(2,1)S(1)} %collective-permute-done.8.refs_1_), channel_id=1, source_target_pairs={{0,1},{1,0},{2,3},{3,2},{4,5},{5,4},{6,7},{7,6},{8,9},{9,8},{10,11... | collective-permute-start | bytes 294920 | tf_op jit(solution)/shard_map/ppermute | solution.py:29
  60.2 1.0 copy-start.22
  60.2 1.0 copy-start.11
  60.2 1.0 copy-start.23
  60.2 0.9 copy-start.24
  61.2 0.6 copy-start.25
  66.5 19.2 %all-to-all-start.1 = ((bf16[16,24,896]{2,1,0:T(8,128)(2,1)}), bf16[16,24,896]{2,1,0:T(8,128)(2,1)S(1)}, u32[]{:S(2)}, u32[]{:S(2)}) async-start(bf16[16,24,896]{2,1,0:T(8,128)(2,1)} %project.1), calls=%async_computation.1 | async-start | bytes 1376256 | tf_op jit(solution)/shard_map/all_to_all | solution.py:646
  73.2 19.2 %copy-start.6 = (s32[8]{0:T(128)S(1)}, s32[8]{0:T(128)}, u32[]{:S(2)}) copy-start(s32[8]{0:T(128)} %stack.28.info_ref) | copy-start | bytes 100
  87.1 0.6 copy-start.4
  87.7 24.3 %all-to-all-start.2 = ((bf16[32,22,8,128]{3,2,1,0:T(8,128)(2,1)}), bf16[32,22,8,128]{3,2,1,0:T(8,128)(2,1)S(1)}, u32[]{:S(2)}, u32[]{:S(2)}) async-start(bf16[32,22,8,128]{3,2,1,0:T(8,128)(2,1)} %get-tuple-element.60), calls=%async_computation.2 | async-start | bytes 2883584 | tf_op jit(solution)/shard_map/all_to_all | solution.py:652
  100.3 2.0 %copy-start.1 = (bf16[576,3584]{1,0:T(8,128)(2,1)}, bf16[576,3584]{1,0:T(8,128)(2,1)S(1)}, u32[]{:S(2)}) copy-start(bf16[576,3584]{1,0:T(8,128)(2,1)S(1)} %get-tuple-element.65.weight_ref) | copy-start | bytes 12386308
  102.3 18.4 %collective-permute-start.20 = (bf16[288,3584]{1,0:T(8,128)(2,1)}, bf16[288,3584]{1,0:T(8,128)(2,1)}, u32[]{:S(2)}, u32[]{:S(2)}) collective-permute-start(bf16[288,3584]{1,0:T(8,128)(2,1)} %get-tuple-element.69), channel_id=1, source_target_pairs={{0,1},{1,0},{2,3},{3,2},{4,5},{5,4},{6,7},{7,6},{8,9},{9,8},{10,11... | collective-permute-start | bytes 6193160 | tf_op jit(solution)/shard_map/ppermute | solution.py:29
  112.0 6.4 %collective-permute-start.18 = (bf16[8,4,22,8,128]{4,3,2,1,0:T(8,128)(2,1)S(1)}, bf16[8,4,22,8,128]{4,3,2,1,0:T(8,128)(2,1)S(1)}, u32[]{:S(2)}, u32[]{:S(2)}) collective-permute-start(bf16[8,4,22,8,128]{4,3,2,1,0:T(8,128)(2,1)S(1)} %bitcast.11), channel_id=1, source_target_pairs={{0,1},{1,0},{2,3},{3,2},{4,5},{5,4},{6,7},{7,6},{8,9},{9,8},{10,11... | collective-permute-start | bytes 4325384 | tf_op jit(solution)/shard_map/ppermute | solution.py:29
  114.4 2.2 %copy-start.2 = (bf16[576,3584]{1,0:T(8,128)(2,1)S(1)}, bf16[576,3584]{1,0:T(8,128)(2,1)}, u32[]{:S(2)}) copy-start(bf16[576,3584]{1,0:T(8,128)(2,1)} %copy-done.1) | copy-start | bytes 12386308
  116.6 2.2 %copy-start = (bf16[576,3584]{1,0:T(8,128)(2,1)S(1)}, bf16[576,3584]{1,0:T(8,128)(2,1)}, u32[]{:S(2)}) copy-start(bf16[576,3584]{1,0:T(8,128)(2,1)} %get-tuple-element.64.weight_ref) | copy-start | bytes 12386308
  118.8 3.3 %copy-start.5 = (f32[24,896]{1,0:T(8,128)S(1)}, f32[24,896]{1,0:T(8,128)}, u32[]{:S(2)}) copy-start(f32[24,896]{1,0:T(8,128)} %copy-done.4) | copy-start | bytes 258052
  120.6 1.5 collective-permute-start.19
  151.0 2.9 %collective-permute-start.21 = (bf16[3,3584]{1,0:T(4,128)(2,1)S(1)}, bf16[3,3584]{1,0:T(4,128)(2,1)S(1)}, u32[]{:S(2)}, u32[]{:S(2)}) collective-permute-start(bf16[3,3584]{1,0:T(4,128)(2,1)S(1)} %get-tuple-element.72), channel_id=1, source_target_pairs={{0,1},{1,0},{2,3},{3,2},{4,5},{5,4},{6,7},{7,6},{8,9},{9,8},{10,11... | collective-permute-start | bytes 64520 | tf_op jit(solution)/shard_map/ppermute | solution.py:29

commit v9 on v7

--- a/solution.py
+++ b/solution.py
@@ -200,23 +200,22 @@
     )
 
 
-def stage_kernel(info_ref, gate_ref, up_ref, down_ref, out_ref, own_ref, send_ref, sems):
-    rows = gate_ref.shape[0]
-    half = own_ref.shape[1]
-    sides = [
-        down_ref.at[:, pl.ds(pl.multiple_of(info_ref[side] * half, LANES), half)]
-        for side in (4, 3)
-    ]
+def stage_kernel(info_ref, gate_ref, up_ref, down_ref, *refs):
+    outs, own_ref, send_ref, sems = refs[:2], refs[2], refs[3], refs[4]
+    rows, width = gate_ref.shape
+    half = width // 2
+
+    def part(ref, side):
+        return ref.at[:, pl.ds(pl.multiple_of(info_ref[side] * half, LANES), half)]
+
+    copies = [(part(down_ref, 4), send_ref)]
+    for side, out_ref in zip((3, 4), outs):
+        copies.append((part(gate_ref, side), out_ref.at[pl.ds(0, rows), :]))
+        copies.append((part(up_ref, side), out_ref.at[pl.ds(rows, rows), :]))
+    copies.append((part(down_ref, 3), own_ref))
     copies = [
         pltpu.make_async_copy(source, target, sems.at[index])
-        for index, (source, target) in enumerate(
-            [
-                (sides[0], send_ref),
-                (gate_ref, out_ref.at[pl.ds(0, rows), :]),
-                (up_ref, out_ref.at[pl.ds(rows, rows), :]),
-                (sides[1], own_ref),
-            ]
-        )
+        for index, (source, target) in enumerate(copies)
     ]
     for copy in copies:
         copy.start()
@@ -226,6 +225,7 @@
 
 def stage(info, gate, up, down_proj):
     rows, width = gate.shape
+    both = jax.ShapeDtypeStruct((2 * rows, width // 2), BF16)
     half = jax.ShapeDtypeStruct((down_proj.shape[0], down_proj.shape[1] // 2), BF16)
     return call(
         stage_kernel,
@@ -233,26 +233,32 @@
         [info],
         [gate, up, down_proj],
         [ANYWHERE] * 3,
-        [jax.ShapeDtypeStruct((2 * rows, width), BF16), half, half],
-        [pltpu.SemaphoreType.DMA((4,))],
+        [both, both, half, half],
+        [pltpu.SemaphoreType.DMA((6,))],
         limit=VMEM_STAGE,
-        out_specs=[WHOLE] * 3,
-    )
-
-
-def join_kernel(rows, info_ref, recv_ref, own_ref, place_ref, *refs):
+        out_specs=[WHOLE] * 4,
+    )
+
+
+def join_kernel(rows, info_ref, recv_ref, own_ref, *refs):
     blocks, sum_ref, out_ref, stream_ref = refs[:8], refs[8], refs[9], refs[10]
-    stream = []
+    lines_own = stream_ref.shape[0] // len(blocks)
+    shape = (stream_ref.shape[0], SUB)
+    target = lax.broadcasted_iota(jnp.int32, shape, 0)
+    line = lax.broadcasted_iota(jnp.int32, shape, 1)
+    stream = None
     for index, ref in enumerate(blocks):
         lines = ref[ref.shape[0] - 1].astype(F32)
         base = LANES // 2 * (index // 4)
         spans = range(base, base + stream_ref.shape[1] // LANES * SUB, SUB)
-        stream.append(jnp.concatenate([lines[span : span + SUB] for span in spans], axis=1))
-    stream = jnp.concatenate(stream, axis=0).astype(BF16)
-    shape = (stream_ref.shape[0], stream.shape[0])
-    order = lax.broadcasted_iota(jnp.int32, shape, 0) == place_ref[...]
-    order = jnp.where(order, F32(1.0), F32(0.0)).astype(BF16)
-    stream_ref[...] = jnp.dot(order, stream, preferred_element_type=F32)
+        lines = jnp.concatenate([lines[span : span + SUB] for span in spans], axis=1)
+        chip = lax.rem(info_ref[5] + 4 - index % 4, 4)
+        first = (chip * 2 + info_ref[3 + index // 4]) * lines_own
+        order = (target == line + first) & (line < lines_own)
+        order = jnp.where(order, F32(1.0), F32(0.0)).astype(BF16)
+        part = jnp.dot(order, lines.astype(BF16), preferred_element_type=F32)
+        stream = part if stream is None else stream + part
+    stream_ref[...] = stream
     sides = 2
     devs = recv_ref.shape[0] // sides
     tiles = LAT // LANES
@@ -296,11 +302,11 @@
     ).astype(BF16)
 
 
-def join(info, received, value_up, place, blocks, rows, eighth):
+def join(info, received, value_up, blocks, rows, eighth):
     devs = received.shape[0] // 2
     count = rows * devs
     sums = np.repeat(np.eye(count, dtype=np.float32), SUB, axis=1)
-    arrays = [received, value_up, place, *blocks, jnp.asarray(sums, BF16)]
+    arrays = [received, value_up, *blocks, jnp.asarray(sums, BF16)]
     return call(
         functools.partial(join_kernel, rows),
         "join",
@@ -316,10 +322,9 @@
     )
 
 
-def project_kernel(info_ref, place_ref, *refs):
+def project_kernel(info_ref, natural_ref, *refs):
     values, own_ref, theirs_ref = refs[:8], refs[8], refs[9]
     parts, out_ref = refs[10:13], refs[13]
-    del info_ref
     rows = []
     for source, ref in enumerate(values):
         data = ref[...]
@@ -332,7 +337,12 @@
         rows.append(jnp.concatenate(lanes, axis=1))
     left = jnp.concatenate(rows, axis=0)
     count = left.shape[0]
-    order = lax.broadcasted_iota(jnp.int32, (count, count), 0) == place_ref[...]
+    place = natural_ref[0:1]
+    for source in range(8):
+        chip = lax.rem(info_ref[5] + 4 - source % 4, 4)
+        first = (chip * 2 + info_ref[3 + source // 4]) * (count // 64)
+        place = place + jnp.where(natural_ref[1:2] == source, first, 0)
+    order = lax.broadcasted_iota(jnp.int32, (count, count), 0) == place
     order = jnp.where(order, F32(1.0), F32(0.0)).astype(BF16)
     left = jnp.dot(order, left, preferred_element_type=F32).astype(BF16)
     columns = own_ref.shape[1] // LANES
@@ -347,17 +357,20 @@
     out_ref[...] = total.reshape(out_ref.shape).astype(BF16)
 
 
-def project(info, place, values, out_proj, out_theirs, parts, chips):
+def project(info, values, out_proj, out_theirs, parts, chips):
     rows = sum(value.shape[0] for value in values)
     lanes = out_proj.shape[0]
     eighth = out_proj.shape[1] // 8
+    line = np.arange(rows) % (rows // 8)
+    natural = np.stack([line % 8 * (rows // 8) + line // 8, np.arange(rows) // (rows // 8)])
+    natural = jnp.asarray(natural, jnp.int32)
     own = pl.BlockSpec((lanes, eighth), lambda i, info: (0, info[0]))
     other = pl.BlockSpec((lanes, eighth), lambda i, info: (0, info[5]))
     return call(
         project_kernel,
         "project",
         [info],
-        [place, *values, out_proj, out_theirs, *parts],
+        [natural, *values, out_proj, out_theirs, *parts],
         [None] * 9 + [own, other] + [None] * 3,
         jax.ShapeDtypeStruct((chips, rows // chips, eighth), BF16),
         work=2 * rows * 8 * lanes * eighth,
@@ -406,12 +419,11 @@
     )
 
 
-def units_kernel(groups, last, info_ref, recv_ref, weight_ref, *refs):
+def units_kernel(groups, last, recv_ref, weight_ref, *refs):
     sides, quarters, tiles, _, _ = recv_ref.shape
     columns = (tiles - 1) // groups
     rows = sides * groups * SUB
     depth = columns * LANES
-    which = 4 if last else 3
     lane = lax.broadcasted_iota(jnp.int32, (SUB, LANES), 1)
     total = squares = None
     for quarter in range(quarters):
@@ -424,10 +436,9 @@
             ],
             axis=1,
         ).astype(BF16)
-        start = pl.multiple_of((info_ref[which] * quarters + quarter) * depth, LANES)
         part = lax.dot_general(
             left,
-            weight_ref[:, pl.ds(start, depth)],
+            weight_ref[:, quarter * depth : quarter * depth + depth],
             (((1,), (1,)), ((), ())),
             preferred_element_type=F32,
         )
@@ -450,14 +461,14 @@
     else:
         acc_ref, sq_ref, out_ref = refs
         hidden = out_ref.shape[1]
-        scale = lax.rsqrt((sq_ref[:, :1] + squares) / weight_ref.shape[1] + 1e-06)
+        scale = lax.rsqrt((sq_ref[:, :1] + squares) / (2 * weight_ref.shape[1]) + 1e-06)
         total = total + acc_ref[...]
         gate = total[:, :hidden] * scale
         upper = total[:, hidden:] * scale
         out_ref[...] = (gate / (1.0 + jnp.exp(-gate)) * upper).astype(BF16)
 
 
-def units(info, received, weight, groups, carry=()):
+def units(received, weight, groups, carry=()):
     sides, quarters, tiles = received.shape[:3]
     hidden = weight.shape[0] // 2
     rows = sides * groups * SUB
@@ -470,11 +481,11 @@
     return call(
         functools.partial(units_kernel, groups, last),
         "units_last" if last else "units_first",
-        [info],
+        [],
         [received, weight, *carry],
         [WHOLE] * (2 + len(carry)),
         single if last else double,
-        work=rows * weight.size,
+        work=2 * rows * weight.size,
         out_specs=WHOLE if last else [WHOLE] * 2,
     )
 
@@ -599,25 +610,15 @@
     firsts_theirs = [swap(part) for part in [own] + firsts]
     parts = [shift(part, step) for step, part in zip((1, 2, 3), cuts)]
     received = lax.all_to_all(payload, OUTER, split_axis=0, concat_axis=0, tiled=True)
-    chip = (ring - jnp.arange(8)) % 4
-    side = jnp.where(jnp.arange(8) < 4, core, 1 - core)
-    line = jnp.arange(SUB)[None]
-    place = ((chip * 2 + side) * rows_own)[:, None] + line
-    place = jnp.where(line < rows_own, place, -1).reshape(1, 8 * SUB).astype(jnp.int32)
     blocks = [own] + firsts + firsts_theirs
-    values, stream_rows = join(info, received, value_up, place, blocks, rows, eighth)
+    values, stream_rows = join(info, received, value_up, blocks, rows, eighth)
 
     last, parts[0] = lax.optimization_barrier((values, parts[0]))
     ring_values = [values, shift(values, 1), shift(values, 2), shift(last, 3)]
     late, _ = lax.optimization_barrier((values, ring_values[1]))
     both_values = ring_values + [swap(piece) for piece in [late] + ring_values[1:]]
-    row = jnp.arange(8 * rows)
-    natural = jnp.tile(row % 8 * (8 * rows) + row // 8, 8).reshape(8, 8 * rows)
-    place = natural[:, : 8 * rows] + ((chip * 2 + side) * rows)[:, None]
-    place = place.reshape(1, 64 * rows).astype(jnp.int32)
     partial = project(
         info,
-        place,
         both_values,
         out_proj,
         out_theirs,
@@ -633,11 +634,11 @@
     piece = lax.all_to_all(payload, SIDE_CHIPS, split_axis=0, concat_axis=0, tiled=True)
     piece = piece.reshape((8, 4) + piece.shape[1:])
     other = swap(piece)
-    weight, down_own, down_send = stage(info, gate_proj.T, up_proj.T, down_proj)
+    first_weight, last_weight, down_own, down_send = stage(info, gate_proj.T, up_proj.T, down_proj)
     down_theirs = swap(down_send)
     groups = 8 * rows_own // SUB
-    carry = units(info, piece, weight, groups)
-    hidden = units(info, other, weight, groups, carry)
+    carry = units(piece, first_weight, groups)
+    hidden = units(other, last_weight, groups, carry)
     partial = down(info, hidden, swap(hidden), down_own, down_theirs, residual, 32)
     parts = lax.all_to_all(partial, SIDE_CHIPS, split_axis=0, concat_axis=0, tiled=True)
     mine, theirs = finish(info, parts)

time: 157 us -> 152 us (0.968)
  local copies, waits for them, and re-layouts: 12.3 us -> 8.52 us
    unnamed x34 -> x38, local copies, waits for them, and re-layouts: 10.1 us -> 7.11 us
    ppermute x13, starting transfers between devices: 15.3 us -> 13 us  [swap(): return lax.ppermute(array, 'core', SWAP)]
    ppermute x9, waiting for transfers between devices: 9.44 us -> 7.5 us  [shift(): return lax.ppermute(array, 'y', [(i, (i + step) % 4) for i in range(4)])]
    all_to_all x1, waiting for transfers between devices: 6.9 us -> 8.71 us  [local(): lax.all_to_all(payload, SIDE_CHIPS, split_axis=0, concat_axis=0, tiled=True)]
  transfers between devices with their start and end apart: 25 -> 25, of which waited for: 8 -> 10; matrix products, arithmetic and copies ran while one was open for 1% -> 1% of each run, Pallas kernels for 15% -> 15%
where the time goes in v9:
time: 152 us
  starting transfers between devices  44.2 us (29%)
  waiting for transfers between devices  38.2 us (25%)
  Pallas kernels  35.6 us (23%)
  blocking collectives  24.3 us (16%)
  local copies, waits for them, and re-layouts  8.52 us (6%)
    pallas_call x10, Pallas kernels, call(): pl.pallas_call(kernel, out_shape=outs, grid_spec=pltpu.PrefetchScalarGrid...  35.6 us
    all_to_all x1, blocking collectives, local(): lax.all_to_all(partial, SIDE_CHIPS, split_axis=0, concat_axis=0, tiled=True)  24.3 us
    ppermute x13, starting transfers between devices, swap(): return lax.ppermute(array, 'core', SWAP)  13 us
    all_to_all x1, waiting for transfers between devices, local(): lax.all_to_all(partial, OUTER, split_axis=0, concat_axis=0, tiled=True)  11.7 us
    ppermute x9, starting transfers between devices, shift(): return lax.ppermute(array, 'y', [(i, (i + step) % 4) for i in range(4)])  11 us
    all_to_all x1, waiting for transfers between devices, local(): lax.all_to_all(payload, SIDE_CHIPS, split_axis=0, concat_axis=0, tiled=True)  8.71 us
    all_to_all x1, starting transfers between devices, local(): lax.all_to_all(payload, OUTER, split_axis=0, concat_axis=0, tiled=True)  7.92 us
    ppermute x9, waiting for transfers between devices, shift(): return lax.ppermute(array, 'y', [(i, (i + step) % 4) for i in range(4)])  7.5 us
  transfers between devices with their start and end apart: 25, of which 10 were waited for; matrix products, arithmetic and copies ran while one was open for 1% of the time, Pallas kernels for 15%

profile of v9, /device:TPU:1, one launch (start us, length us, event | category | flops | bytes accessed | tf_op | source)
XLA Modules:
  0.0 151.8 jit_solution(13495394556811966401)
XLA Ops:
  0.0 0.6 stack.28.info_ref
  0.6 3.2 %early.1 = (bf16[128,3584]{1,0:T(8,128)(2,1)}, bf16[5,128,128]{2,1,0:T(8,128)(2,1)}, bf16[5,128,128]{2,1,0:T(8,128)(2,1)}, bf16[5,128,128]{2,1,0:T(8,128)(2,1)}, bf16[5,128,128]{2,1,0:T(8,128)(2,1)}) custom-call(s32[8]{0:T(128)} %stack.28.info_ref, bf16[1,512,128]{2,1,0:T(8,128)(2,1)} %own_ref.1, bf16[3,7168]{1,0:T(4,128)(2,1)} %stream_ref.1, ...), custom_call_target="tpu_custom_call" | custom-call | bytes 3581952 | tf_op jit(solution)/shard_map/early/pallas_call | solution.py:51
  3.8 1.4 collective-permute-start
  5.2 1.4 collective-permute-start.1
  6.6 2.6 %collective-permute-start.2 = (bf16[5,128,128]{2,1,0:T(8,128)(2,1)}, bf16[5,128,128]{2,1,0:T(8,128)(2,1)S(1)}, u32[]{:S(2)}, u32[]{:S(2)}) collective-permute-start(bf16[5,128,128]{2,1,0:T(8,128)(2,1)} %get-tuple-element.40), channel_id=1, source_target_pairs={{0,4},{2,6},{4,0},{6,2},{1,5},{3,7},{5,1},{7,3},{8,12},{10,14},{12... | collective-permute-start | bytes 491528 | tf_op jit(solution)/shard_map/ppermute | solution.py:33
  9.2 1.1 collective-permute-start.3
  10.3 1.0 copy-done.4
  11.3 7.0 %attend.1 = (bf16[16,25,8,128]{3,2,1,0:T(8,128)(2,1)}, bf16[14,128,128]{2,1,0:T(8,128)(2,1)}, bf16[14,128,128]{2,1,0:T(8,128)(2,1)}, bf16[14,128,128]{2,1,0:T(8,128)(2,1)}) custom-call(s32[8]{0:T(128)} %stack.28.info_ref, s32[6]{0:T(128)} %lengths_ref.1, bf16[6,576,128]{2,1,0:T(8,128)(2,1)} %bitcast.16, bf16[6,576,512]{2,1,0:T(8,128)(2,1)} %bitcast.15, ...), custom_call_target="tpu_custom_call" | custom-call | flops 855638016 | bytes 9371648 | tf_op jit(solution)/shard_map/attend/pallas_call | solution.py:51
  18.3 0.0 copy-start
  18.3 0.0 copy-start.11
  18.4 0.0 collective-permute-done.1.refs_1_
  18.4 0.0 collective-permute-done.2.refs_2_
  18.4 7.9 %all-to-all-start = ((bf16[16,25,8,128]{3,2,1,0:T(8,128)(2,1)}), bf16[16,25,8,128]{3,2,1,0:T(8,128)(2,1)}, u32[]{:S(2)}, u32[]{:S(2)}) async-start(bf16[16,25,8,128]{3,2,1,0:T(8,128)(2,1)} %get-tuple-element.42), calls=%async_computation | async-start | bytes 1638400 | tf_op jit(solution)/shard_map/all_to_all | solution.py:612
  26.4 0.5 collective-permute-start.10
  26.8 1.4 collective-permute-start.4
  28.2 0.0 collective-permute-start.5
  28.2 1.2 collective-permute-start.16
  29.4 1.4 collective-permute-start.17
  30.8 1.1 collective-permute-start.6
  31.9 0.0 collective-permute-done.5.refs_5_
  31.9 0.7 collective-permute-start.7
  32.5 0.6 collective-permute-done.6.refs_6_
  33.1 0.8 collective-permute-done.7.refs_7_
  33.9 5.8 %all-to-all-done.recv_ref = bf16[16,25,8,128]{3,2,1,0:T(8,128)(2,1)} async-done(((bf16[16,25,8,128]{3,2,1,0:T(8,128)(2,1)}), bf16[16,25,8,128]{3,2,1,0:T(8,128)(2,1)}, u32[]{:S(2)}, u32[]{:S(2)}) %all-to-all-start) | async-done | bytes 819232 | tf_op jit(solution)/shard_map/all_to_all | solution.py:612
  39.8 3.9 %join.1 = (bf16[48,1024]{1,0:T(8,128)(2,1)}, f32[24,896]{1,0:T(8,128)}) custom-call(s32[8]{0:T(128)} %stack.28.info_ref, bf16[16,25,8,128]{3,2,1,0:T(8,128)(2,1)} %all-to-all-done.recv_ref, bf16[1,512,128]{2,1,0:T(8,128)(2,1)} %own_ref.1, bf16[5,128,128]{2,1,0:T(8,128)(2,1)} %get-tuple-element.43.refs_0_, bf16[5,128,128]{2,1,0:T(8,128)(2,1)} %copy-done.13, ...), custom_call_target="tpu_custom_call" | custom-call | flops 480000000 | bytes 2439168 | tf_op jit(solution)/shard_map/join/pallas_call | solution.py:51
  43.6 0.4 collective-permute-start.8
  44.0 1.9 %collective-permute-start.9 = (bf16[48,1024]{1,0:T(8,128)(2,1)}, bf16[48,1024]{1,0:T(8,128)(2,1)S(1)}, u32[]{:S(2)}, u32[]{:S(2)}) collective-permute-start(bf16[48,1024]{1,0:T(8,128)(2,1)} %get-tuple-element.50.refs_0_), channel_id=1, source_target_pairs={{0,4},{2,6},{4,0},{6,2},{1,5},{3,7},{5,1},{7,3},{8,12},{10,14},{12... | collective-permute-start | bytes 294920 | tf_op jit(solution)/shard_map/ppermute | solution.py:33
  45.9 0.6 collective-permute-start.11
  46.5 7.3 %collective-permute-done.8.refs_1_ = bf16[48,1024]{1,0:T(8,128)(2,1)S(1)} collective-permute-done((bf16[48,1024]{1,0:T(8,128)(2,1)}, bf16[48,1024]{1,0:T(8,128)(2,1)S(1)}, u32[]{:S(2)}, u32[]{:S(2)}) %collective-permute-start.8) | collective-permute-done | bytes 98336 | tf_op jit(solution)/shard_map/ppermute | solution.py:33
  53.8 1.0 collective-permute-start.12
  54.8 0.0 collective-permute-done.9.refs_2_
  54.8 0.0 collective-permute-start.14
  54.8 0.5 collective-permute-start.13
  55.3 0.2 collective-permute-done.11.refs_3_
  55.5 1.4 collective-permute-start.15
  56.9 0.0 collective-permute-done.17.refs_12_
  56.9 0.0 collective-permute-done.14.refs_6_
  56.9 0.0 collective-permute-done.12.refs_4_
  56.9 0.9 collective-permute-done.15.refs_7_
  57.8 0.9 copy-done.6
  58.7 4.0 %project.1 = bf16[16,24,896]{2,1,0:T(8,128)(2,1)} custom-call(s32[8]{0:T(128)S(1)} %copy-done.10, s32[2,384]{1,0:T(2,128)S(1)} %copy-done.11, bf16[48,1024]{1,0:T(8,128)(2,1)S(1)} %copy-done.6, bf16[48,1024]{1,0:T(8,128)(2,1)S(1)} %collective-permute-done.8.refs_1_, bf16[48,1024]{1,0:T(8,128)(2,1)S(1)} %collective-permute-done.9.refs_2_, ...), custom_call_target="tpu_custom_call" | custom-call | flops 704643072 | bytes 5604864 | tf_op jit(solution)/shard_map/project/pallas_call | solution.py:51
  62.7 6.9 %all-to-all-start.1 = ((bf16[16,24,896]{2,1,0:T(8,128)(2,1)}), bf16[16,24,896]{2,1,0:T(8,128)(2,1)S(1)}, u32[]{:S(2)}, u32[]{:S(2)}) async-start(bf16[16,24,896]{2,1,0:T(8,128)(2,1)} %project.1), calls=%async_computation.1 | async-start | bytes 1376256 | tf_op jit(solution)/shard_map/all_to_all | solution.py:628
  69.6 0.8 dynamic_slice.3
  70.4 11.7 %all-to-all-done.1.parts_ref = bf16[16,24,896]{2,1,0:T(8,128)(2,1)S(1)} async-done(((bf16[16,24,896]{2,1,0:T(8,128)(2,1)}), bf16[16,24,896]{2,1,0:T(8,128)(2,1)S(1)}, u32[]{:S(2)}, u32[]{:S(2)}) %all-to-all-start.1) | async-done | bytes 688160 | tf_op jit(solution)/shard_map/all_to_all | solution.py:628
  82.1 1.4 residual.1
  83.5 0.6 copy-done.8
  84.1 5.4 %all-to-all-start.2 = ((bf16[32,22,8,128]{3,2,1,0:T(8,128)(2,1)}), bf16[32,22,8,128]{3,2,1,0:T(8,128)(2,1)S(1)}, u32[]{:S(2)}, u32[]{:S(2)}) async-start(bf16[32,22,8,128]{3,2,1,0:T(8,128)(2,1)} %get-tuple-element.56), calls=%async_computation.2 | async-start | bytes 2883584 | tf_op jit(solution)/shard_map/all_to_all | solution.py:634
  89.5 7.9 %stage.1 = (bf16[576,3584]{1,0:T(8,128)(2,1)S(1)}, bf16[576,3584]{1,0:T(8,128)(2,1)}, bf16[288,3584]{1,0:T(8,128)(2,1)S(1)}, bf16[288,3584]{1,0:T(8,128)(2,1)}) custom-call(s32[8]{0:T(128)S(1)} %copy-done.10, bf16[288,7168]{1,0:T(8,128)(2,1)} %bitcast.13, bf16[288,7168]{1,0:T(8,128)(2,1)} %bitcast.14, bf16[288,7168]{1,0:T(8,128)(2,1)} %down_ref), custom_call_target="tpu_custom_call" | custom-call | bytes 24772608 | tf_op jit(solution)/shard_map/stage/pallas_call | solution.py:51
  97.4 2.0 %copy-done.2 = bf16[576,3584]{1,0:T(8,128)(2,1)} copy-done((bf16[576,3584]{1,0:T(8,128)(2,1)}, bf16[576,3584]{1,0:T(8,128)(2,1)S(1)}, u32[]{:S(2)}) %copy-start.2) | copy-done | bytes 4128792
  99.4 1.0 collective-permute-start.20
  100.4 8.7 %all-to-all-done.2 = bf16[32,22,8,128]{3,2,1,0:T(8,128)(2,1)S(1)} async-done(((bf16[32,22,8,128]{3,2,1,0:T(8,128)(2,1)}), bf16[32,22,8,128]{3,2,1,0:T(8,128)(2,1)S(1)}, u32[]{:S(2)}, u32[]{:S(2)}) %all-to-all-start.2) | async-done | bytes 1441824 | tf_op jit(solution)/shard_map/all_to_all | solution.py:634
  109.1 2.4 %collective-permute-start.18 = (bf16[8,4,22,8,128]{4,3,2,1,0:T(8,128)(2,1)S(1)}, bf16[8,4,22,8,128]{4,3,2,1,0:T(8,128)(2,1)S(1)}, u32[]{:S(2)}, u32[]{:S(2)}) collective-permute-start(bf16[8,4,22,8,128]{4,3,2,1,0:T(8,128)(2,1)S(1)} %bitcast.11), channel_id=1, source_target_pairs={{0,1},{1,0},{2,3},{3,2},{4,5},{5,4},{6,7},{7,6},{8,9},{9,8},{10,11... | collective-permute-start | bytes 4325384 | tf_op jit(solution)/shard_map/ppermute | solution.py:29
  111.6 2.2 %copy-done.3 = bf16[576,3584]{1,0:T(8,128)(2,1)S(1)} copy-done((bf16[576,3584]{1,0:T(8,128)(2,1)S(1)}, bf16[576,3584]{1,0:T(8,128)(2,1)}, u32[]{:S(2)}) %copy-start.3) | copy-done | bytes 4128792
  113.7 1.7 %units_first.1 = (f32[192,576]{1,0:T(8,128)S(1)}, f32[192,128]{1,0:T(8,128)S(1)}) custom-call(bf16[8,4,22,8,128]{4,3,2,1,0:T(8,128)(2,1)S(1)} %bitcast.12, bf16[576,3584]{1,0:T(8,128)(2,1)S(1)} %copy-done.3), custom_call_target="tpu_custom_call" | custom-call | flops 792723456 | bytes 5840896 | tf_op jit(solution)/shard_map/units_first/pallas_call | solution.py:51
  115.5 0.4 copy-done.1
  115.9 1.8 %units_last.1.mine_ref = bf16[192,288]{1,0:T(8,128)(2,1)S(1)} custom-call(bf16[8,4,22,8,128]{4,3,2,1,0:T(8,128)(2,1)S(1)} %collective-permute-done.18.recv_ref, bf16[576,3584]{1,0:T(8,128)(2,1)S(1)} %copy-done.1, f32[192,576]{1,0:T(8,128)S(1)} %get-tuple-element.62.refs_0_, f32[192,128]{1,0:T(8,128)S(1)} %get-tuple-element.63.refs_1_), custom_call_target="tpu_custom_call" | custom-call | flops 792723456 | bytes 5951488 | tf_op jit(solution)/shard_map/units_last/pallas_call | solution.py:51
  117.7 0.1 collective-permute-start.19
  117.8 1.3 collective-permute-done.19.theirs_ref
  119.2 3.9 %down.1 = bf16[32,7,24,128]{3,2,1,0:T(8,128)(2,1)S(1)} custom-call(s32[8]{0:T(128)S(1)} %copy-done.10, bf16[192,288]{1,0:T(8,128)(2,1)S(1)} %units_last.1.mine_ref, bf16[192,288]{1,0:T(8,128)(2,1)S(1)} %collective-permute-done.19.theirs_ref, bf16[288,3584]{1,0:T(8,128)(2,1)S(1)} %get-tuple-element.64.own_ref, ...), custom_call_target="tpu_custom_call" | custom-call | flops 792723456 | bytes 5769216 | tf_op jit(solution)/shard_map/down/pallas_call | solution.py:51
  123.1 24.3 %all_to_all.20.parts_ref = bf16[32,7,24,128]{3,2,1,0:T(8,128)(2,1)S(1)} all-to-all(bf16[32,7,24,128]{3,2,1,0:T(8,128)(2,1)S(1)} %down.1), channel_id=1, replica_groups=mesh['zh'=2,'zl'=2,'x'=4,'y'=4,'core'=2] {'zl','x','y'}, dimensions={0} | all-to-all | bytes 2752512 | tf_op jit(solution)/shard_map/all_to_all | solution.py:643
  147.4 0.8 finish.1
  148.2 2.0 %collective-permute-start.21 = (bf16[3,3584]{1,0:T(4,128)(2,1)S(1)}, bf16[3,3584]{1,0:T(4,128)(2,1)S(1)}, u32[]{:S(2)}, u32[]{:S(2)}) collective-permute-start(bf16[3,3584]{1,0:T(4,128)(2,1)S(1)} %get-tuple-element.68), channel_id=1, source_target_pairs={{0,1},{1,0},{2,3},{3,2},{4,5},{5,4},{6,7},{7,6},{8,9},{9,8},{10,11... | collective-permute-start | bytes 64520 | tf_op jit(solution)/shard_map/ppermute | solution.py:29
  150.2 0.9 collective-permute-done.21
  151.1 0.7 pad_maximum_fusion
  (40 shorter events, 0.1 us)
Async XLA Ops:
  3.8 6.5 %collective-permute-start = (bf16[128,3584]{1,0:T(8,128)(2,1)}, bf16[128,3584]{1,0:T(8,128)(2,1)S(1)}, u32[]{:S(2)}, u32[]{:S(2)}) collective-permute-start(bf16[128,3584]{1,0:T(8,128)(2,1)} %get-tuple-element.37), channel_id=1, source_target_pairs={{0,1},{1,0},{2,3},{3,2},{4,5},{5,4},{6,7},{7,6},{8,9},{9,8},{10,11... | collective-permute-start | bytes 2752520 | tf_op jit(solution)/shard_map/ppermute | solution.py:29
  5.2 13.1 %collective-permute-start.1 = (bf16[5,128,128]{2,1,0:T(8,128)(2,1)}, bf16[5,128,128]{2,1,0:T(8,128)(2,1)S(1)}, u32[]{:S(2)}, u32[]{:S(2)}) collective-permute-start(bf16[5,128,128]{2,1,0:T(8,128)(2,1)} %get-tuple-element.39), channel_id=1, source_target_pairs={{0,2},{2,4},{4,6},{6,0},{1,3},{3,5},{5,7},{7,1},{8,10},{10,12},{12... | collective-permute-start | bytes 491528 | tf_op jit(solution)/shard_map/ppermute | solution.py:33
  6.6 11.8 %collective-permute-start.2 = (bf16[5,128,128]{2,1,0:T(8,128)(2,1)}, bf16[5,128,128]{2,1,0:T(8,128)(2,1)S(1)}, u32[]{:S(2)}, u32[]{:S(2)}) collective-permute-start(bf16[5,128,128]{2,1,0:T(8,128)(2,1)} %get-tuple-element.40), channel_id=1, source_target_pairs={{0,4},{2,6},{4,0},{6,2},{1,5},{3,7},{5,1},{7,3},{8,12},{10,14},{12... | collective-permute-start | bytes 491528 | tf_op jit(solution)/shard_map/ppermute | solution.py:33
  9.2 9.2 %collective-permute-start.3 = (bf16[5,128,128]{2,1,0:T(8,128)(2,1)}, bf16[5,128,128]{2,1,0:T(8,128)(2,1)S(1)}, u32[]{:S(2)}, u32[]{:S(2)}) collective-permute-start(bf16[5,128,128]{2,1,0:T(8,128)(2,1)} %get-tuple-element.41), channel_id=1, source_target_pairs={{0,6},{2,0},{4,2},{6,4},{1,7},{3,1},{5,3},{7,5},{8,14},{10,8},{12,... | collective-permute-start | bytes 491528 | tf_op jit(solution)/shard_map/ppermute | solution.py:33
  10.3 1.0 copy-start.4
  11.3 15.5 %copy-start.12 = (bf16[5,128,128]{2,1,0:T(8,128)(2,1)S(1)}, bf16[5,128,128]{2,1,0:T(8,128)(2,1)}, u32[]{:S(2)}) copy-start(bf16[5,128,128]{2,1,0:T(8,128)(2,1)} %get-tuple-element.43.refs_0_) | copy-start | bytes 491524
  18.3 39.5 %copy-start = (bf16[128,7168]{1,0:T(8,128)(2,1)S(1)}, bf16[128,7168]{1,0:T(8,128)(2,1)}, u32[]{:S(2)}) copy-start(bf16[128,7168]{1,0:T(8,128)(2,1)} %refs_8_.2) | copy-start | bytes 5505028
  18.3 39.5 %copy-start.5 = (bf16[128,3584]{1,0:T(8,128)(2,1)S(1)}, bf16[128,3584]{1,0:T(8,128)(2,1)}, u32[]{:S(2)}) copy-start(bf16[128,3584]{1,0:T(8,128)(2,1)} %copy-done.4) | copy-start | bytes 2752516
  18.3 39.5 %copy-start.10 = (s32[8]{0:T(128)S(1)}, s32[8]{0:T(128)}, u32[]{:S(2)}) copy-start(s32[8]{0:T(128)} %stack.28.info_ref) | copy-start | bytes 100
  18.3 39.5 %copy-start.11 = (s32[2,384]{1,0:T(2,128)S(1)}, s32[2,384]{1,0:T(2,128)}, u32[]{:S(2)}) copy-start(s32[2,384]{1,0:T(2,128)} %constant.36.clone.natural_ref) | copy-start | bytes 9220
  18.4 21.4 %copy-start.13 = (bf16[5,128,128]{2,1,0:T(8,128)(2,1)}, bf16[5,128,128]{2,1,0:T(8,128)(2,1)S(1)}, u32[]{:S(2)}) copy-start(bf16[5,128,128]{2,1,0:T(8,128)(2,1)S(1)} %collective-permute-done.1.refs_1_) | copy-start | bytes 491524
  18.4 8.0 %copy-start.14 = (bf16[5,128,128]{2,1,0:T(8,128)(2,1)}, bf16[5,128,128]{2,1,0:T(8,128)(2,1)S(1)}, u32[]{:S(2)}) copy-start(bf16[5,128,128]{2,1,0:T(8,128)(2,1)S(1)} %collective-permute-done.2.refs_2_) | copy-start | bytes 491524
  18.4 7.9 %copy-start.15 = (bf16[5,128,128]{2,1,0:T(8,128)(2,1)}, bf16[5,128,128]{2,1,0:T(8,128)(2,1)S(1)}, u32[]{:S(2)}) copy-start(bf16[5,128,128]{2,1,0:T(8,128)(2,1)S(1)} %collective-permute-done.3.refs_3_) | copy-start | bytes 491524
  18.4 21.3 %all-to-all-start = ((bf16[16,25,8,128]{3,2,1,0:T(8,128)(2,1)}), bf16[16,25,8,128]{3,2,1,0:T(8,128)(2,1)}, u32[]{:S(2)}, u32[]{:S(2)}) async-start(bf16[16,25,8,128]{3,2,1,0:T(8,128)(2,1)} %get-tuple-element.42), calls=%async_computation | async-start | bytes 1638400 | tf_op jit(solution)/shard_map/all_to_all | solution.py:612
  26.4 19.6 %collective-permute-start.10 = (bf16[14,128,128]{2,1,0:T(8,128)(2,1)}, bf16[14,128,128]{2,1,0:T(8,128)(2,1)S(1)}, u32[]{:S(2)}, u32[]{:S(2)}) collective-permute-start(bf16[14,128,128]{2,1,0:T(8,128)(2,1)} %get-tuple-element.48), channel_id=1, source_target_pairs={{0,2},{2,4},{4,6},{6,0},{1,3},{3,5},{5,7},{7,1},{8,10},{10,12},{12... | collective-permute-start | bytes 1376264 | tf_op jit(solution)/shard_map/ppermute | solution.py:33
  26.8 4.0 %collective-permute-start.4 = (bf16[5,128,128]{2,1,0:T(8,128)(2,1)S(1)}, bf16[5,128,128]{2,1,0:T(8,128)(2,1)S(1)}, u32[]{:S(2)}, u32[]{:S(2)}) collective-permute-start(bf16[5,128,128]{2,1,0:T(8,128)(2,1)S(1)} %copy-done.12), channel_id=1, source_target_pairs={{0,1},{1,0},{2,3},{3,2},{4,5},{5,4},{6,7},{7,6},{8,9},{9,8},{10,11... | collective-permute-start | bytes 491528 | tf_op jit(solution)/shard_map/ppermute | solution.py:29
  28.2 3.6 %collective-permute-start.5 = (bf16[5,128,128]{2,1,0:T(8,128)(2,1)S(1)}, bf16[5,128,128]{2,1,0:T(8,128)(2,1)S(1)}, u32[]{:S(2)}, u32[]{:S(2)}) collective-permute-start(bf16[5,128,128]{2,1,0:T(8,128)(2,1)S(1)} %collective-permute-done.1.refs_1_), channel_id=1, source_target_pairs={{0,1},{1,0},{2,3},{3,2},{4,5},{5,4},{6,7},{7,6},{8,9},{9,8},{10,11... | collective-permute-start | bytes 491528 | tf_op jit(solution)/shard_map/ppermute | solution.py:29
  28.2 26.6 %collective-permute-start.16 = (bf16[14,128,128]{2,1,0:T(8,128)(2,1)}, bf16[14,128,128]{2,1,0:T(8,128)(2,1)}, u32[]{:S(2)}, u32[]{:S(2)}) collective-permute-start(bf16[14,128,128]{2,1,0:T(8,128)(2,1)} %get-tuple-element.52), channel_id=1, source_target_pairs={{0,4},{2,6},{4,0},{6,2},{1,5},{3,7},{5,1},{7,3},{8,12},{10,14},{12... | collective-permute-start | bytes 1376264 | tf_op jit(solution)/shard_map/ppermute | solution.py:33
  29.4 27.5 %collective-permute-start.17 = (bf16[14,128,128]{2,1,0:T(8,128)(2,1)}, bf16[14,128,128]{2,1,0:T(8,128)(2,1)}, u32[]{:S(2)}, u32[]{:S(2)}) collective-permute-start(bf16[14,128,128]{2,1,0:T(8,128)(2,1)} %get-tuple-element.53), channel_id=1, source_target_pairs={{0,6},{2,0},{4,2},{6,4},{1,7},{3,1},{5,3},{7,5},{8,14},{10,8},{12,... | collective-permute-start | bytes 1376264 | tf_op jit(solution)/shard_map/ppermute | solution.py:33
  30.8 1.1 copy-start.16
  30.8 2.3 %collective-permute-start.6 = (bf16[5,128,128]{2,1,0:T(8,128)(2,1)}, bf16[5,128,128]{2,1,0:T(8,128)(2,1)S(1)}, u32[]{:S(2)}, u32[]{:S(2)}) collective-permute-start(bf16[5,128,128]{2,1,0:T(8,128)(2,1)} %copy-done.14), channel_id=1, source_target_pairs={{0,1},{1,0},{2,3},{3,2},{4,5},{5,4},{6,7},{7,6},{8,9},{9,8},{10,11... | collective-permute-start | bytes 491528 | tf_op jit(solution)/shard_map/ppermute | solution.py:29
  31.9 0.7 copy-start.17
  31.9 2.0 %collective-permute-start.7 = (bf16[5,128,128]{2,1,0:T(8,128)(2,1)}, bf16[5,128,128]{2,1,0:T(8,128)(2,1)}, u32[]{:S(2)}, u32[]{:S(2)}) collective-permute-start(bf16[5,128,128]{2,1,0:T(8,128)(2,1)} %copy-done.15), channel_id=1, source_target_pairs={{0,1},{1,0},{2,3},{3,2},{4,5},{5,4},{6,7},{7,6},{8,9},{9,8},{10,11... | collective-permute-start | bytes 491528 | tf_op jit(solution)/shard_map/ppermute | solution.py:29
  33.1 6.7 %copy-start.18 = (bf16[5,128,128]{2,1,0:T(8,128)(2,1)}, bf16[5,128,128]{2,1,0:T(8,128)(2,1)S(1)}, u32[]{:S(2)}) copy-start(bf16[5,128,128]{2,1,0:T(8,128)(2,1)S(1)} %collective-permute-done.6.refs_6_) | copy-start | bytes 491524
  43.6 10.2 %collective-permute-start.8 = (bf16[48,1024]{1,0:T(8,128)(2,1)}, bf16[48,1024]{1,0:T(8,128)(2,1)S(1)}, u32[]{:S(2)}, u32[]{:S(2)}) collective-permute-start(bf16[48,1024]{1,0:T(8,128)(2,1)} %get-tuple-element.50.refs_0_), channel_id=1, source_target_pairs={{0,2},{2,4},{4,6},{6,0},{1,3},{3,5},{5,7},{7,1},{8,10},{10,12},{12... | collective-permute-start | bytes 294920 | tf_op jit(solution)/shard_map/ppermute | solution.py:33
  44.0 10.8 %collective-permute-start.9 = (bf16[48,1024]{1,0:T(8,128)(2,1)}, bf16[48,1024]{1,0:T(8,128)(2,1)S(1)}, u32[]{:S(2)}, u32[]{:S(2)}) collective-permute-start(bf16[48,1024]{1,0:T(8,128)(2,1)} %get-tuple-element.50.refs_0_), channel_id=1, source_target_pairs={{0,4},{2,6},{4,0},{6,2},{1,5},{3,7},{5,1},{7,3},{8,12},{10,14},{12... | collective-permute-start | bytes 294920 | tf_op jit(solution)/shard_map/ppermute | solution.py:33
  45.9 9.6 %collective-permute-start.11 = (bf16[48,1024]{1,0:T(8,128)(2,1)}, bf16[48,1024]{1,0:T(8,128)(2,1)S(1)}, u32[]{:S(2)}, u32[]{:S(2)}) collective-permute-start(bf16[48,1024]{1,0:T(8,128)(2,1)} %get-tuple-element.50.refs_0_), channel_id=1, source_target_pairs={{0,6},{2,0},{4,2},{6,4},{1,7},{3,1},{5,3},{7,5},{8,14},{10,8},{12,... | collective-permute-start | bytes 294920 | tf_op jit(solution)/shard_map/ppermute | solution.py:33
  53.8 3.0 %collective-permute-start.12 = (bf16[48,1024]{1,0:T(8,128)(2,1)}, bf16[48,1024]{1,0:T(8,128)(2,1)S(1)}, u32[]{:S(2)}, u32[]{:S(2)}) collective-permute-start(bf16[48,1024]{1,0:T(8,128)(2,1)} %get-tuple-element.50.refs_0_), channel_id=1, source_target_pairs={{0,1},{1,0},{2,3},{3,2},{4,5},{5,4},{6,7},{7,6},{8,9},{9,8},{10,11... | collective-permute-start | bytes 294920 | tf_op jit(solution)/shard_map/ppermute | solution.py:29
  54.8 2.0 %collective-permute-start.14 = (bf16[48,1024]{1,0:T(8,128)(2,1)S(1)}, bf16[48,1024]{1,0:T(8,128)(2,1)S(1)}, u32[]{:S(2)}, u32[]{:S(2)}) collective-permute-start(bf16[48,1024]{1,0:T(8,128)(2,1)S(1)} %collective-permute-done.9.refs_2_), channel_id=1, source_target_pairs={{0,1},{1,0},{2,3},{3,2},{4,5},{5,4},{6,7},{7,6},{8,9},{9,8},{10,11... | collective-permute-start | bytes 294920 | tf_op jit(solution)/shard_map/ppermute | solution.py:29
  54.8 2.0 %collective-permute-start.13 = (bf16[48,1024]{1,0:T(8,128)(2,1)S(1)}, bf16[48,1024]{1,0:T(8,128)(2,1)S(1)}, u32[]{:S(2)}, u32[]{:S(2)}) collective-permute-start(bf16[48,1024]{1,0:T(8,128)(2,1)S(1)} %collective-permute-done.8.refs_1_), channel_id=1, source_target_pairs={{0,1},{1,0},{2,3},{3,2},{4,5},{5,4},{6,7},{7,6},{8,9},{9,8},{10,11... | collective-permute-start | bytes 294920 | tf_op jit(solution)/shard_map/ppermute | solution.py:29
  55.5 2.3 %collective-permute-start.15 = (bf16[48,1024]{1,0:T(8,128)(2,1)S(1)}, bf16[48,1024]{1,0:T(8,128)(2,1)S(1)}, u32[]{:S(2)}, u32[]{:S(2)}) collective-permute-start(bf16[48,1024]{1,0:T(8,128)(2,1)S(1)} %collective-permute-done.11.refs_3_), channel_id=1, source_target_pairs={{0,1},{1,0},{2,3},{3,2},{4,5},{5,4},{6,7},{7,6},{8,9},{9,8},{10,11... | collective-permute-start | bytes 294920 | tf_op jit(solution)/shard_map/ppermute | solution.py:29
  57.8 0.9 copy-start.6
  58.7 23.4 %copy-start.7 = (f32[24,896]{1,0:T(8,128)S(1)}, f32[24,896]{1,0:T(8,128)}, u32[]{:S(2)}) copy-start(f32[24,896]{1,0:T(8,128)} %get-tuple-element.54.stream_ref) | copy-start | bytes 258052
  62.7 19.4 %all-to-all-start.1 = ((bf16[16,24,896]{2,1,0:T(8,128)(2,1)}), bf16[16,24,896]{2,1,0:T(8,128)(2,1)S(1)}, u32[]{:S(2)}, u32[]{:S(2)}) async-start(bf16[16,24,896]{2,1,0:T(8,128)(2,1)} %project.1), calls=%async_computation.1 | async-start | bytes 1376256 | tf_op jit(solution)/shard_map/all_to_all | solution.py:628
  83.5 0.6 copy-start.8
  84.1 25.0 %all-to-all-start.2 = ((bf16[32,22,8,128]{3,2,1,0:T(8,128)(2,1)}), bf16[32,22,8,128]{3,2,1,0:T(8,128)(2,1)S(1)}, u32[]{:S(2)}, u32[]{:S(2)}) async-start(bf16[32,22,8,128]{3,2,1,0:T(8,128)(2,1)} %get-tuple-element.56), calls=%async_computation.2 | async-start | bytes 2883584 | tf_op jit(solution)/shard_map/all_to_all | solution.py:634
  97.4 2.0 %copy-start.2 = (bf16[576,3584]{1,0:T(8,128)(2,1)}, bf16[576,3584]{1,0:T(8,128)(2,1)S(1)}, u32[]{:S(2)}) copy-start(bf16[576,3584]{1,0:T(8,128)(2,1)S(1)} %get-tuple-element.61.weight_ref) | copy-start | bytes 12386308
  99.4 18.4 %collective-permute-start.20 = (bf16[288,3584]{1,0:T(8,128)(2,1)}, bf16[288,3584]{1,0:T(8,128)(2,1)}, u32[]{:S(2)}, u32[]{:S(2)}) collective-permute-start(bf16[288,3584]{1,0:T(8,128)(2,1)} %get-tuple-element.65), channel_id=1, source_target_pairs={{0,1},{1,0},{2,3},{3,2},{4,5},{5,4},{6,7},{7,6},{8,9},{9,8},{10,11... | collective-permute-start | bytes 6193160 | tf_op jit(solution)/shard_map/ppermute | solution.py:29
  109.1 6.3 %collective-permute-start.18 = (bf16[8,4,22,8,128]{4,3,2,1,0:T(8,128)(2,1)S(1)}, bf16[8,4,22,8,128]{4,3,2,1,0:T(8,128)(2,1)S(1)}, u32[]{:S(2)}, u32[]{:S(2)}) collective-permute-start(bf16[8,4,22,8,128]{4,3,2,1,0:T(8,128)(2,1)S(1)} %bitcast.11), channel_id=1, source_target_pairs={{0,1},{1,0},{2,3},{3,2},{4,5},{5,4},{6,7},{7,6},{8,9},{9,8},{10,11... | collective-permute-start | bytes 4325384 | tf_op jit(solution)/shard_map/ppermute | solution.py:29
  111.6 2.2 %copy-start.3 = (bf16[576,3584]{1,0:T(8,128)(2,1)S(1)}, bf16[576,3584]{1,0:T(8,128)(2,1)}, u32[]{:S(2)}) copy-start(bf16[576,3584]{1,0:T(8,128)(2,1)} %copy-done.2) | copy-start | bytes 12386308
  113.7 2.2 %copy-start.1 = (bf16[576,3584]{1,0:T(8,128)(2,1)S(1)}, bf16[576,3584]{1,0:T(8,128)(2,1)}, u32[]{:S(2)}) copy-start(bf16[576,3584]{1,0:T(8,128)(2,1)} %get-tuple-element.60.weight_ref) | copy-start | bytes 12386308
  115.9 3.3 %copy-start.9 = (f32[24,896]{1,0:T(8,128)S(1)}, f32[24,896]{1,0:T(8,128)}, u32[]{:S(2)}) copy-start(f32[24,896]{1,0:T(8,128)} %copy-done.8) | copy-start | bytes 258052
  117.7 1.5 collective-permute-start.19
  148.2 2.9 %collective-permute-start.21 = (bf16[3,3584]{1,0:T(4,128)(2,1)S(1)}, bf16[3,3584]{1,0:T(4,128)(2,1)S(1)}, u32[]{:S(2)}, u32[]{:S(2)}) collective-permute-start(bf16[3,3584]{1,0:T(4,128)(2,1)S(1)} %get-tuple-element.68), channel_id=1, source_target_pairs={{0,1},{1,0},{2,3},{3,2},{4,5},{5,4},{6,7},{7,6},{8,9},{9,8},{10,11... | collective-permute-start | bytes 64520 | tf_op jit(solution)/shard_map/ppermute | solution.py:29

commit v10 on v9

--- a/solution.py
+++ b/solution.py
@@ -490,7 +490,16 @@
     )
 
 
-def down_kernel(info_ref, mine_ref, theirs_ref, own_ref, other_ref, held_ref, out_ref, total):
+def down_kernel(
+    info_ref, mine_ref, theirs_ref, own_ref, other_hbm, held_ref, out_ref, total, other_ref, sems
+):
+    spans = [pl.ds(start, 4 * LANES) for start in range(0, own_ref.shape[1], 4 * LANES)]
+    copies = [
+        pltpu.make_async_copy(other_hbm.at[:, span], other_ref.at[:, span], sems.at[index])
+        for index, span in enumerate(spans)
+    ]
+    for copy in copies:
+        copy.start()
     chips, steps = out_ref.shape[:2]
     rows = mine_ref.shape[0]
     count = rows // chips
@@ -500,6 +509,7 @@
     width = 4 * LANES
     for step in range(steps):
         span = slice(step * width, step * width + width)
+        copies[step].wait()
         weight = jnp.concatenate([own_ref[:, span], other_ref[:, span]], axis=0)
         total[:rows, span] = jnp.dot(left, weight, preferred_element_type=F32)
     total[pl.ds(rows, SUB), :] = jnp.zeros((SUB, total.shape[1]), F32)
@@ -530,9 +540,13 @@
         "down",
         [info],
         [mine, theirs, own, other, held],
-        [WHOLE] * 5,
+        [WHOLE, WHOLE, WHOLE, ANYWHERE, WHOLE],
         jax.ShapeDtypeStruct((chips, half // (4 * LANES), 3 * SUB, LANES), BF16),
-        [pltpu.VMEM((rows + SUB, half), F32)],
+        [
+            pltpu.VMEM((rows + SUB, half), F32),
+            pltpu.VMEM(other.shape, BF16),
+            pltpu.SemaphoreType.DMA((half // (4 * LANES),)),
+        ],
         4 * rows * own.size,
         out_specs=WHOLE,
     )

time: 152 us -> 153 us (level)
  no operation moved by 1% of the time
where the time goes in v10:
time: 153 us; the launch traced here: 152 us
  starting transfers between devices  44.2 us (29%)
  waiting for transfers between devices  38.2 us (25%)
  Pallas kernels  36.1 us (24%)
  blocking collectives  24.3 us (16%)
  local copies, waits for them, and re-layouts  8.52 us (6%)
    pallas_call x10, Pallas kernels, call(): pl.pallas_call(kernel, out_shape=outs, grid_spec=pltpu.PrefetchScalarGrid...  36.1 us
    all_to_all x1, blocking collectives, local(): lax.all_to_all(partial, SIDE_CHIPS, split_axis=0, concat_axis=0, tiled=True)  24.3 us
    ppermute x13, starting transfers between devices, swap(): return lax.ppermute(array, 'core', SWAP)  13 us
    all_to_all x1, waiting for transfers between devices, local(): lax.all_to_all(partial, OUTER, split_axis=0, concat_axis=0, tiled=True)  11.7 us
    ppermute x9, starting transfers between devices, shift(): return lax.ppermute(array, 'y', [(i, (i + step) % 4) for i in range(4)])  11 us
    all_to_all x1, waiting for transfers between devices, local(): lax.all_to_all(payload, SIDE_CHIPS, split_axis=0, concat_axis=0, tiled=True)  8.71 us
    all_to_all x1, starting transfers between devices, local(): lax.all_to_all(payload, OUTER, split_axis=0, concat_axis=0, tiled=True)  7.92 us
    ppermute x9, waiting for transfers between devices, shift(): return lax.ppermute(array, 'y', [(i, (i + step) % 4) for i in range(4)])  7.5 us
  transfers between devices with their start and end apart: 25, of which 10 were waited for; matrix products, arithmetic and copies ran while one was open for 1% of the time, Pallas kernels for 15%

profile of v10, /device:TPU:1, one launch (start us, length us, event | category | flops | bytes accessed | tf_op | source)
XLA Modules:
  0.0 152.2 jit_solution(8140042545212825139)
XLA Ops:
  0.0 0.6 stack.28.info_ref
  0.6 3.2 %early.1 = (bf16[128,3584]{1,0:T(8,128)(2,1)}, bf16[5,128,128]{2,1,0:T(8,128)(2,1)}, bf16[5,128,128]{2,1,0:T(8,128)(2,1)}, bf16[5,128,128]{2,1,0:T(8,128)(2,1)}, bf16[5,128,128]{2,1,0:T(8,128)(2,1)}) custom-call(s32[8]{0:T(128)} %stack.28.info_ref, bf16[1,512,128]{2,1,0:T(8,128)(2,1)} %own_ref.1, bf16[3,7168]{1,0:T(4,128)(2,1)} %stream_ref.1, ...), custom_call_target="tpu_custom_call" | custom-call | bytes 3581952 | tf_op jit(solution)/shard_map/early/pallas_call | solution.py:51
  3.8 1.4 collective-permute-start
  5.2 1.4 collective-permute-start.1
  6.6 2.6 %collective-permute-start.2 = (bf16[5,128,128]{2,1,0:T(8,128)(2,1)}, bf16[5,128,128]{2,1,0:T(8,128)(2,1)S(1)}, u32[]{:S(2)}, u32[]{:S(2)}) collective-permute-start(bf16[5,128,128]{2,1,0:T(8,128)(2,1)} %get-tuple-element.40), channel_id=1, source_target_pairs={{0,4},{2,6},{4,0},{6,2},{1,5},{3,7},{5,1},{7,3},{8,12},{10,14},{12... | collective-permute-start | bytes 491528 | tf_op jit(solution)/shard_map/ppermute | solution.py:33
  9.2 1.1 collective-permute-start.3
  10.3 1.0 copy-done.4
  11.3 7.0 %attend.1 = (bf16[16,25,8,128]{3,2,1,0:T(8,128)(2,1)}, bf16[14,128,128]{2,1,0:T(8,128)(2,1)}, bf16[14,128,128]{2,1,0:T(8,128)(2,1)}, bf16[14,128,128]{2,1,0:T(8,128)(2,1)}) custom-call(s32[8]{0:T(128)} %stack.28.info_ref, s32[6]{0:T(128)} %lengths_ref.1, bf16[6,576,128]{2,1,0:T(8,128)(2,1)} %bitcast.16, bf16[6,576,512]{2,1,0:T(8,128)(2,1)} %bitcast.15, ...), custom_call_target="tpu_custom_call" | custom-call | flops 855638016 | bytes 9371648 | tf_op jit(solution)/shard_map/attend/pallas_call | solution.py:51
  18.3 0.0 copy-start
  18.3 0.0 copy-start.11
  18.4 0.0 collective-permute-done.1.refs_1_
  18.4 0.0 collective-permute-done.2.refs_2_
  18.4 7.9 %all-to-all-start = ((bf16[16,25,8,128]{3,2,1,0:T(8,128)(2,1)}), bf16[16,25,8,128]{3,2,1,0:T(8,128)(2,1)}, u32[]{:S(2)}, u32[]{:S(2)}) async-start(bf16[16,25,8,128]{3,2,1,0:T(8,128)(2,1)} %get-tuple-element.42), calls=%async_computation | async-start | bytes 1638400 | tf_op jit(solution)/shard_map/all_to_all | solution.py:626
  26.4 0.5 collective-permute-start.10
  26.8 1.4 collective-permute-start.4
  28.2 0.0 collective-permute-start.5
  28.2 1.2 collective-permute-start.16
  29.4 1.4 collective-permute-start.17
  30.8 1.1 collective-permute-start.6
  31.9 0.0 collective-permute-done.5.refs_5_
  31.9 0.7 collective-permute-start.7
  32.5 0.6 collective-permute-done.6.refs_6_
  33.1 0.8 collective-permute-done.7.refs_7_
  33.9 5.8 %all-to-all-done.recv_ref = bf16[16,25,8,128]{3,2,1,0:T(8,128)(2,1)} async-done(((bf16[16,25,8,128]{3,2,1,0:T(8,128)(2,1)}), bf16[16,25,8,128]{3,2,1,0:T(8,128)(2,1)}, u32[]{:S(2)}, u32[]{:S(2)}) %all-to-all-start) | async-done | bytes 819232 | tf_op jit(solution)/shard_map/all_to_all | solution.py:626
  39.8 3.9 %join.1 = (bf16[48,1024]{1,0:T(8,128)(2,1)}, f32[24,896]{1,0:T(8,128)}) custom-call(s32[8]{0:T(128)} %stack.28.info_ref, bf16[16,25,8,128]{3,2,1,0:T(8,128)(2,1)} %all-to-all-done.recv_ref, bf16[1,512,128]{2,1,0:T(8,128)(2,1)} %own_ref.1, bf16[5,128,128]{2,1,0:T(8,128)(2,1)} %get-tuple-element.43.refs_0_, bf16[5,128,128]{2,1,0:T(8,128)(2,1)} %copy-done.13, ...), custom_call_target="tpu_custom_call" | custom-call | flops 480000000 | bytes 2439168 | tf_op jit(solution)/shard_map/join/pallas_call | solution.py:51
  43.6 0.4 collective-permute-start.8
  44.0 1.9 %collective-permute-start.9 = (bf16[48,1024]{1,0:T(8,128)(2,1)}, bf16[48,1024]{1,0:T(8,128)(2,1)S(1)}, u32[]{:S(2)}, u32[]{:S(2)}) collective-permute-start(bf16[48,1024]{1,0:T(8,128)(2,1)} %get-tuple-element.50.refs_0_), channel_id=1, source_target_pairs={{0,4},{2,6},{4,0},{6,2},{1,5},{3,7},{5,1},{7,3},{8,12},{10,14},{12... | collective-permute-start | bytes 294920 | tf_op jit(solution)/shard_map/ppermute | solution.py:33
  45.9 0.6 collective-permute-start.11
  46.5 7.3 %collective-permute-done.8.refs_1_ = bf16[48,1024]{1,0:T(8,128)(2,1)S(1)} collective-permute-done((bf16[48,1024]{1,0:T(8,128)(2,1)}, bf16[48,1024]{1,0:T(8,128)(2,1)S(1)}, u32[]{:S(2)}, u32[]{:S(2)}) %collective-permute-start.8) | collective-permute-done | bytes 98336 | tf_op jit(solution)/shard_map/ppermute | solution.py:33
  53.8 1.0 collective-permute-start.12
  54.8 0.0 collective-permute-done.9.refs_2_
  54.8 0.0 collective-permute-start.14
  54.8 0.5 collective-permute-start.13
  55.3 0.2 collective-permute-done.11.refs_3_
  55.5 1.4 collective-permute-start.15
  56.9 0.0 collective-permute-done.17.refs_12_
  56.9 0.0 collective-permute-done.14.refs_6_
  56.9 0.0 collective-permute-done.12.refs_4_
  56.9 0.9 collective-permute-done.15.refs_7_
  57.8 0.9 copy-done.6
  58.7 4.0 %project.1 = bf16[16,24,896]{2,1,0:T(8,128)(2,1)} custom-call(s32[8]{0:T(128)S(1)} %copy-done.10, s32[2,384]{1,0:T(2,128)S(1)} %copy-done.11, bf16[48,1024]{1,0:T(8,128)(2,1)S(1)} %copy-done.6, bf16[48,1024]{1,0:T(8,128)(2,1)S(1)} %collective-permute-done.8.refs_1_, bf16[48,1024]{1,0:T(8,128)(2,1)S(1)} %collective-permute-done.9.refs_2_, ...), custom_call_target="tpu_custom_call" | custom-call | flops 704643072 | bytes 5604864 | tf_op jit(solution)/shard_map/project/pallas_call | solution.py:51
  62.7 6.9 %all-to-all-start.1 = ((bf16[16,24,896]{2,1,0:T(8,128)(2,1)}), bf16[16,24,896]{2,1,0:T(8,128)(2,1)S(1)}, u32[]{:S(2)}, u32[]{:S(2)}) async-start(bf16[16,24,896]{2,1,0:T(8,128)(2,1)} %project.1), calls=%async_computation.1 | async-start | bytes 1376256 | tf_op jit(solution)/shard_map/all_to_all | solution.py:642
  69.6 0.8 dynamic_slice.3
  70.4 11.7 %all-to-all-done.1.parts_ref = bf16[16,24,896]{2,1,0:T(8,128)(2,1)S(1)} async-done(((bf16[16,24,896]{2,1,0:T(8,128)(2,1)}), bf16[16,24,896]{2,1,0:T(8,128)(2,1)S(1)}, u32[]{:S(2)}, u32[]{:S(2)}) %all-to-all-start.1) | async-done | bytes 688160 | tf_op jit(solution)/shard_map/all_to_all | solution.py:642
  82.1 1.4 residual.1
  83.5 0.6 copy-done.8
  84.1 5.4 %all-to-all-start.2 = ((bf16[32,22,8,128]{3,2,1,0:T(8,128)(2,1)}), bf16[32,22,8,128]{3,2,1,0:T(8,128)(2,1)S(1)}, u32[]{:S(2)}, u32[]{:S(2)}) async-start(bf16[32,22,8,128]{3,2,1,0:T(8,128)(2,1)} %get-tuple-element.56), calls=%async_computation.2 | async-start | bytes 2883584 | tf_op jit(solution)/shard_map/all_to_all | solution.py:648
  89.5 7.9 %stage.1 = (bf16[576,3584]{1,0:T(8,128)(2,1)S(1)}, bf16[576,3584]{1,0:T(8,128)(2,1)}, bf16[288,3584]{1,0:T(8,128)(2,1)S(1)}, bf16[288,3584]{1,0:T(8,128)(2,1)}) custom-call(s32[8]{0:T(128)S(1)} %copy-done.10, bf16[288,7168]{1,0:T(8,128)(2,1)} %bitcast.13, bf16[288,7168]{1,0:T(8,128)(2,1)} %bitcast.14, bf16[288,7168]{1,0:T(8,128)(2,1)} %down_ref), custom_call_target="tpu_custom_call" | custom-call | bytes 24772608 | tf_op jit(solution)/shard_map/stage/pallas_call | solution.py:51
  97.4 2.0 %copy-done.2 = bf16[576,3584]{1,0:T(8,128)(2,1)} copy-done((bf16[576,3584]{1,0:T(8,128)(2,1)}, bf16[576,3584]{1,0:T(8,128)(2,1)S(1)}, u32[]{:S(2)}) %copy-start.2) | copy-done | bytes 4128792
  99.4 1.0 collective-permute-start.20
  100.4 8.7 %all-to-all-done.2 = bf16[32,22,8,128]{3,2,1,0:T(8,128)(2,1)S(1)} async-done(((bf16[32,22,8,128]{3,2,1,0:T(8,128)(2,1)}), bf16[32,22,8,128]{3,2,1,0:T(8,128)(2,1)S(1)}, u32[]{:S(2)}, u32[]{:S(2)}) %all-to-all-start.2) | async-done | bytes 1441824 | tf_op jit(solution)/shard_map/all_to_all | solution.py:648
  109.1 2.4 %collective-permute-start.18 = (bf16[8,4,22,8,128]{4,3,2,1,0:T(8,128)(2,1)S(1)}, bf16[8,4,22,8,128]{4,3,2,1,0:T(8,128)(2,1)S(1)}, u32[]{:S(2)}, u32[]{:S(2)}) collective-permute-start(bf16[8,4,22,8,128]{4,3,2,1,0:T(8,128)(2,1)S(1)} %bitcast.11), channel_id=1, source_target_pairs={{0,1},{1,0},{2,3},{3,2},{4,5},{5,4},{6,7},{7,6},{8,9},{9,8},{10,11... | collective-permute-start | bytes 4325384 | tf_op jit(solution)/shard_map/ppermute | solution.py:29
  111.6 2.2 %copy-done.3 = bf16[576,3584]{1,0:T(8,128)(2,1)S(1)} copy-done((bf16[576,3584]{1,0:T(8,128)(2,1)S(1)}, bf16[576,3584]{1,0:T(8,128)(2,1)}, u32[]{:S(2)}) %copy-start.3) | copy-done | bytes 4128792
  113.7 1.7 %units_first.1 = (f32[192,576]{1,0:T(8,128)S(1)}, f32[192,128]{1,0:T(8,128)S(1)}) custom-call(bf16[8,4,22,8,128]{4,3,2,1,0:T(8,128)(2,1)S(1)} %bitcast.12, bf16[576,3584]{1,0:T(8,128)(2,1)S(1)} %copy-done.3), custom_call_target="tpu_custom_call" | custom-call | flops 792723456 | bytes 5840896 | tf_op jit(solution)/shard_map/units_first/pallas_call | solution.py:51
  115.5 0.4 copy-done.1
  115.9 1.8 %units_last.1.mine_ref = bf16[192,288]{1,0:T(8,128)(2,1)S(1)} custom-call(bf16[8,4,22,8,128]{4,3,2,1,0:T(8,128)(2,1)S(1)} %collective-permute-done.18.recv_ref, bf16[576,3584]{1,0:T(8,128)(2,1)S(1)} %copy-done.1, f32[192,576]{1,0:T(8,128)S(1)} %get-tuple-element.62.refs_0_, f32[192,128]{1,0:T(8,128)S(1)} %get-tuple-element.63.refs_1_), custom_call_target="tpu_custom_call" | custom-call | flops 792723456 | bytes 5951488 | tf_op jit(solution)/shard_map/units_last/pallas_call | solution.py:51
  117.7 0.1 collective-permute-start.19
  117.8 1.3 collective-permute-done.19.theirs_ref
  119.2 4.4 %down.1 = bf16[32,7,24,128]{3,2,1,0:T(8,128)(2,1)S(1)} custom-call(s32[8]{0:T(128)S(1)} %copy-done.10, bf16[192,288]{1,0:T(8,128)(2,1)S(1)} %units_last.1.mine_ref, bf16[192,288]{1,0:T(8,128)(2,1)S(1)} %collective-permute-done.19.theirs_ref, bf16[288,3584]{1,0:T(8,128)(2,1)S(1)} %get-tuple-element.64.own_ref, ...), custom_call_target="tpu_custom_call" | custom-call | flops 792723456 | bytes 5769216 | tf_op jit(solution)/shard_map/down/pallas_call | solution.py:51
  123.6 24.3 %all_to_all.20.parts_ref = bf16[32,7,24,128]{3,2,1,0:T(8,128)(2,1)S(1)} all-to-all(bf16[32,7,24,128]{3,2,1,0:T(8,128)(2,1)S(1)} %down.1), channel_id=1, replica_groups=mesh['zh'=2,'zl'=2,'x'=4,'y'=4,'core'=2] {'zl','x','y'}, dimensions={0} | all-to-all | bytes 2752512 | tf_op jit(solution)/shard_map/all_to_all | solution.py:657
  147.8 0.8 finish.1
  148.6 2.0 %collective-permute-start.21 = (bf16[3,3584]{1,0:T(4,128)(2,1)S(1)}, bf16[3,3584]{1,0:T(4,128)(2,1)S(1)}, u32[]{:S(2)}, u32[]{:S(2)}) collective-permute-start(bf16[3,3584]{1,0:T(4,128)(2,1)S(1)} %get-tuple-element.68), channel_id=1, source_target_pairs={{0,1},{1,0},{2,3},{3,2},{4,5},{5,4},{6,7},{7,6},{8,9},{9,8},{10,11... | collective-permute-start | bytes 64520 | tf_op jit(solution)/shard_map/ppermute | solution.py:29
  150.7 0.9 collective-permute-done.21
  151.6 0.7 pad_maximum_fusion
  (40 shorter events, 0.1 us)
Async XLA Ops:
  3.8 6.5 %collective-permute-start = (bf16[128,3584]{1,0:T(8,128)(2,1)}, bf16[128,3584]{1,0:T(8,128)(2,1)S(1)}, u32[]{:S(2)}, u32[]{:S(2)}) collective-permute-start(bf16[128,3584]{1,0:T(8,128)(2,1)} %get-tuple-element.37), channel_id=1, source_target_pairs={{0,1},{1,0},{2,3},{3,2},{4,5},{5,4},{6,7},{7,6},{8,9},{9,8},{10,11... | collective-permute-start | bytes 2752520 | tf_op jit(solution)/shard_map/ppermute | solution.py:29
  5.2 13.1 %collective-permute-start.1 = (bf16[5,128,128]{2,1,0:T(8,128)(2,1)}, bf16[5,128,128]{2,1,0:T(8,128)(2,1)S(1)}, u32[]{:S(2)}, u32[]{:S(2)}) collective-permute-start(bf16[5,128,128]{2,1,0:T(8,128)(2,1)} %get-tuple-element.39), channel_id=1, source_target_pairs={{0,2},{2,4},{4,6},{6,0},{1,3},{3,5},{5,7},{7,1},{8,10},{10,12},{12... | collective-permute-start | bytes 491528 | tf_op jit(solution)/shard_map/ppermute | solution.py:33
  6.6 11.8 %collective-permute-start.2 = (bf16[5,128,128]{2,1,0:T(8,128)(2,1)}, bf16[5,128,128]{2,1,0:T(8,128)(2,1)S(1)}, u32[]{:S(2)}, u32[]{:S(2)}) collective-permute-start(bf16[5,128,128]{2,1,0:T(8,128)(2,1)} %get-tuple-element.40), channel_id=1, source_target_pairs={{0,4},{2,6},{4,0},{6,2},{1,5},{3,7},{5,1},{7,3},{8,12},{10,14},{12... | collective-permute-start | bytes 491528 | tf_op jit(solution)/shard_map/ppermute | solution.py:33
  9.2 9.2 %collective-permute-start.3 = (bf16[5,128,128]{2,1,0:T(8,128)(2,1)}, bf16[5,128,128]{2,1,0:T(8,128)(2,1)S(1)}, u32[]{:S(2)}, u32[]{:S(2)}) collective-permute-start(bf16[5,128,128]{2,1,0:T(8,128)(2,1)} %get-tuple-element.41), channel_id=1, source_target_pairs={{0,6},{2,0},{4,2},{6,4},{1,7},{3,1},{5,3},{7,5},{8,14},{10,8},{12,... | collective-permute-start | bytes 491528 | tf_op jit(solution)/shard_map/ppermute | solution.py:33
  10.3 1.0 copy-start.4
  11.3 15.5 %copy-start.12 = (bf16[5,128,128]{2,1,0:T(8,128)(2,1)S(1)}, bf16[5,128,128]{2,1,0:T(8,128)(2,1)}, u32[]{:S(2)}) copy-start(bf16[5,128,128]{2,1,0:T(8,128)(2,1)} %get-tuple-element.43.refs_0_) | copy-start | bytes 491524
  18.3 39.5 %copy-start = (bf16[128,7168]{1,0:T(8,128)(2,1)S(1)}, bf16[128,7168]{1,0:T(8,128)(2,1)}, u32[]{:S(2)}) copy-start(bf16[128,7168]{1,0:T(8,128)(2,1)} %refs_8_.2) | copy-start | bytes 5505028
  18.3 39.5 %copy-start.5 = (bf16[128,3584]{1,0:T(8,128)(2,1)S(1)}, bf16[128,3584]{1,0:T(8,128)(2,1)}, u32[]{:S(2)}) copy-start(bf16[128,3584]{1,0:T(8,128)(2,1)} %copy-done.4) | copy-start | bytes 2752516
  18.3 39.5 %copy-start.10 = (s32[8]{0:T(128)S(1)}, s32[8]{0:T(128)}, u32[]{:S(2)}) copy-start(s32[8]{0:T(128)} %stack.28.info_ref) | copy-start | bytes 100
  18.3 39.5 %copy-start.11 = (s32[2,384]{1,0:T(2,128)S(1)}, s32[2,384]{1,0:T(2,128)}, u32[]{:S(2)}) copy-start(s32[2,384]{1,0:T(2,128)} %constant.36.clone.natural_ref) | copy-start | bytes 9220
  18.4 21.4 %copy-start.13 = (bf16[5,128,128]{2,1,0:T(8,128)(2,1)}, bf16[5,128,128]{2,1,0:T(8,128)(2,1)S(1)}, u32[]{:S(2)}) copy-start(bf16[5,128,128]{2,1,0:T(8,128)(2,1)S(1)} %collective-permute-done.1.refs_1_) | copy-start | bytes 491524
  18.4 8.0 %copy-start.14 = (bf16[5,128,128]{2,1,0:T(8,128)(2,1)}, bf16[5,128,128]{2,1,0:T(8,128)(2,1)S(1)}, u32[]{:S(2)}) copy-start(bf16[5,128,128]{2,1,0:T(8,128)(2,1)S(1)} %collective-permute-done.2.refs_2_) | copy-start | bytes 491524
  18.4 7.9 %copy-start.15 = (bf16[5,128,128]{2,1,0:T(8,128)(2,1)}, bf16[5,128,128]{2,1,0:T(8,128)(2,1)S(1)}, u32[]{:S(2)}) copy-start(bf16[5,128,128]{2,1,0:T(8,128)(2,1)S(1)} %collective-permute-done.3.refs_3_) | copy-start | bytes 491524
  18.4 21.3 %all-to-all-start = ((bf16[16,25,8,128]{3,2,1,0:T(8,128)(2,1)}), bf16[16,25,8,128]{3,2,1,0:T(8,128)(2,1)}, u32[]{:S(2)}, u32[]{:S(2)}) async-start(bf16[16,25,8,128]{3,2,1,0:T(8,128)(2,1)} %get-tuple-element.42), calls=%async_computation | async-start | bytes 1638400 | tf_op jit(solution)/shard_map/all_to_all | solution.py:626
  26.4 19.6 %collective-permute-start.10 = (bf16[14,128,128]{2,1,0:T(8,128)(2,1)}, bf16[14,128,128]{2,1,0:T(8,128)(2,1)S(1)}, u32[]{:S(2)}, u32[]{:S(2)}) collective-permute-start(bf16[14,128,128]{2,1,0:T(8,128)(2,1)} %get-tuple-element.48), channel_id=1, source_target_pairs={{0,2},{2,4},{4,6},{6,0},{1,3},{3,5},{5,7},{7,1},{8,10},{10,12},{12... | collective-permute-start | bytes 1376264 | tf_op jit(solution)/shard_map/ppermute | solution.py:33
  26.8 4.0 %collective-permute-start.4 = (bf16[5,128,128]{2,1,0:T(8,128)(2,1)S(1)}, bf16[5,128,128]{2,1,0:T(8,128)(2,1)S(1)}, u32[]{:S(2)}, u32[]{:S(2)}) collective-permute-start(bf16[5,128,128]{2,1,0:T(8,128)(2,1)S(1)} %copy-done.12), channel_id=1, source_target_pairs={{0,1},{1,0},{2,3},{3,2},{4,5},{5,4},{6,7},{7,6},{8,9},{9,8},{10,11... | collective-permute-start | bytes 491528 | tf_op jit(solution)/shard_map/ppermute | solution.py:29
  28.2 3.6 %collective-permute-start.5 = (bf16[5,128,128]{2,1,0:T(8,128)(2,1)S(1)}, bf16[5,128,128]{2,1,0:T(8,128)(2,1)S(1)}, u32[]{:S(2)}, u32[]{:S(2)}) collective-permute-start(bf16[5,128,128]{2,1,0:T(8,128)(2,1)S(1)} %collective-permute-done.1.refs_1_), channel_id=1, source_target_pairs={{0,1},{1,0},{2,3},{3,2},{4,5},{5,4},{6,7},{7,6},{8,9},{9,8},{10,11... | collective-permute-start | bytes 491528 | tf_op jit(solution)/shard_map/ppermute | solution.py:29
  28.2 26.6 %collective-permute-start.16 = (bf16[14,128,128]{2,1,0:T(8,128)(2,1)}, bf16[14,128,128]{2,1,0:T(8,128)(2,1)}, u32[]{:S(2)}, u32[]{:S(2)}) collective-permute-start(bf16[14,128,128]{2,1,0:T(8,128)(2,1)} %get-tuple-element.52), channel_id=1, source_target_pairs={{0,4},{2,6},{4,0},{6,2},{1,5},{3,7},{5,1},{7,3},{8,12},{10,14},{12... | collective-permute-start | bytes 1376264 | tf_op jit(solution)/shard_map/ppermute | solution.py:33
  29.4 27.5 %collective-permute-start.17 = (bf16[14,128,128]{2,1,0:T(8,128)(2,1)}, bf16[14,128,128]{2,1,0:T(8,128)(2,1)}, u32[]{:S(2)}, u32[]{:S(2)}) collective-permute-start(bf16[14,128,128]{2,1,0:T(8,128)(2,1)} %get-tuple-element.53), channel_id=1, source_target_pairs={{0,6},{2,0},{4,2},{6,4},{1,7},{3,1},{5,3},{7,5},{8,14},{10,8},{12,... | collective-permute-start | bytes 1376264 | tf_op jit(solution)/shard_map/ppermute | solution.py:33
  30.8 1.1 copy-start.16
  30.8 2.3 %collective-permute-start.6 = (bf16[5,128,128]{2,1,0:T(8,128)(2,1)}, bf16[5,128,128]{2,1,0:T(8,128)(2,1)S(1)}, u32[]{:S(2)}, u32[]{:S(2)}) collective-permute-start(bf16[5,128,128]{2,1,0:T(8,128)(2,1)} %copy-done.14), channel_id=1, source_target_pairs={{0,1},{1,0},{2,3},{3,2},{4,5},{5,4},{6,7},{7,6},{8,9},{9,8},{10,11... | collective-permute-start | bytes 491528 | tf_op jit(solution)/shard_map/ppermute | solution.py:29
  31.9 0.7 copy-start.17
  31.9 2.0 %collective-permute-start.7 = (bf16[5,128,128]{2,1,0:T(8,128)(2,1)}, bf16[5,128,128]{2,1,0:T(8,128)(2,1)}, u32[]{:S(2)}, u32[]{:S(2)}) collective-permute-start(bf16[5,128,128]{2,1,0:T(8,128)(2,1)} %copy-done.15), channel_id=1, source_target_pairs={{0,1},{1,0},{2,3},{3,2},{4,5},{5,4},{6,7},{7,6},{8,9},{9,8},{10,11... | collective-permute-start | bytes 491528 | tf_op jit(solution)/shard_map/ppermute | solution.py:29
  33.1 6.7 %copy-start.18 = (bf16[5,128,128]{2,1,0:T(8,128)(2,1)}, bf16[5,128,128]{2,1,0:T(8,128)(2,1)S(1)}, u32[]{:S(2)}) copy-start(bf16[5,128,128]{2,1,0:T(8,128)(2,1)S(1)} %collective-permute-done.6.refs_6_) | copy-start | bytes 491524
  43.6 10.2 %collective-permute-start.8 = (bf16[48,1024]{1,0:T(8,128)(2,1)}, bf16[48,1024]{1,0:T(8,128)(2,1)S(1)}, u32[]{:S(2)}, u32[]{:S(2)}) collective-permute-start(bf16[48,1024]{1,0:T(8,128)(2,1)} %get-tuple-element.50.refs_0_), channel_id=1, source_target_pairs={{0,2},{2,4},{4,6},{6,0},{1,3},{3,5},{5,7},{7,1},{8,10},{10,12},{12... | collective-permute-start | bytes 294920 | tf_op jit(solution)/shard_map/ppermute | solution.py:33
  44.0 10.8 %collective-permute-start.9 = (bf16[48,1024]{1,0:T(8,128)(2,1)}, bf16[48,1024]{1,0:T(8,128)(2,1)S(1)}, u32[]{:S(2)}, u32[]{:S(2)}) collective-permute-start(bf16[48,1024]{1,0:T(8,128)(2,1)} %get-tuple-element.50.refs_0_), channel_id=1, source_target_pairs={{0,4},{2,6},{4,0},{6,2},{1,5},{3,7},{5,1},{7,3},{8,12},{10,14},{12... | collective-permute-start | bytes 294920 | tf_op jit(solution)/shard_map/ppermute | solution.py:33
  45.9 9.6 %collective-permute-start.11 = (bf16[48,1024]{1,0:T(8,128)(2,1)}, bf16[48,1024]{1,0:T(8,128)(2,1)S(1)}, u32[]{:S(2)}, u32[]{:S(2)}) collective-permute-start(bf16[48,1024]{1,0:T(8,128)(2,1)} %get-tuple-element.50.refs_0_), channel_id=1, source_target_pairs={{0,6},{2,0},{4,2},{6,4},{1,7},{3,1},{5,3},{7,5},{8,14},{10,8},{12,... | collective-permute-start | bytes 294920 | tf_op jit(solution)/shard_map/ppermute | solution.py:33
  53.8 3.0 %collective-permute-start.12 = (bf16[48,1024]{1,0:T(8,128)(2,1)}, bf16[48,1024]{1,0:T(8,128)(2,1)S(1)}, u32[]{:S(2)}, u32[]{:S(2)}) collective-permute-start(bf16[48,1024]{1,0:T(8,128)(2,1)} %get-tuple-element.50.refs_0_), channel_id=1, source_target_pairs={{0,1},{1,0},{2,3},{3,2},{4,5},{5,4},{6,7},{7,6},{8,9},{9,8},{10,11... | collective-permute-start | bytes 294920 | tf_op jit(solution)/shard_map/ppermute | solution.py:29
  54.8 2.0 %collective-permute-start.14 = (bf16[48,1024]{1,0:T(8,128)(2,1)S(1)}, bf16[48,1024]{1,0:T(8,128)(2,1)S(1)}, u32[]{:S(2)}, u32[]{:S(2)}) collective-permute-start(bf16[48,1024]{1,0:T(8,128)(2,1)S(1)} %collective-permute-done.9.refs_2_), channel_id=1, source_target_pairs={{0,1},{1,0},{2,3},{3,2},{4,5},{5,4},{6,7},{7,6},{8,9},{9,8},{10,11... | collective-permute-start | bytes 294920 | tf_op jit(solution)/shard_map/ppermute | solution.py:29
  54.8 2.0 %collective-permute-start.13 = (bf16[48,1024]{1,0:T(8,128)(2,1)S(1)}, bf16[48,1024]{1,0:T(8,128)(2,1)S(1)}, u32[]{:S(2)}, u32[]{:S(2)}) collective-permute-start(bf16[48,1024]{1,0:T(8,128)(2,1)S(1)} %collective-permute-done.8.refs_1_), channel_id=1, source_target_pairs={{0,1},{1,0},{2,3},{3,2},{4,5},{5,4},{6,7},{7,6},{8,9},{9,8},{10,11... | collective-permute-start | bytes 294920 | tf_op jit(solution)/shard_map/ppermute | solution.py:29
  55.5 2.3 %collective-permute-start.15 = (bf16[48,1024]{1,0:T(8,128)(2,1)S(1)}, bf16[48,1024]{1,0:T(8,128)(2,1)S(1)}, u32[]{:S(2)}, u32[]{:S(2)}) collective-permute-start(bf16[48,1024]{1,0:T(8,128)(2,1)S(1)} %collective-permute-done.11.refs_3_), channel_id=1, source_target_pairs={{0,1},{1,0},{2,3},{3,2},{4,5},{5,4},{6,7},{7,6},{8,9},{9,8},{10,11... | collective-permute-start | bytes 294920 | tf_op jit(solution)/shard_map/ppermute | solution.py:29
  57.8 0.9 copy-start.6
  58.7 23.4 %copy-start.7 = (f32[24,896]{1,0:T(8,128)S(1)}, f32[24,896]{1,0:T(8,128)}, u32[]{:S(2)}) copy-start(f32[24,896]{1,0:T(8,128)} %get-tuple-element.54.stream_ref) | copy-start | bytes 258052
  62.7 19.4 %all-to-all-start.1 = ((bf16[16,24,896]{2,1,0:T(8,128)(2,1)}), bf16[16,24,896]{2,1,0:T(8,128)(2,1)S(1)}, u32[]{:S(2)}, u32[]{:S(2)}) async-start(bf16[16,24,896]{2,1,0:T(8,128)(2,1)} %project.1), calls=%async_computation.1 | async-start | bytes 1376256 | tf_op jit(solution)/shard_map/all_to_all | solution.py:642
  83.5 0.6 copy-start.8
  84.1 25.0 %all-to-all-start.2 = ((bf16[32,22,8,128]{3,2,1,0:T(8,128)(2,1)}), bf16[32,22,8,128]{3,2,1,0:T(8,128)(2,1)S(1)}, u32[]{:S(2)}, u32[]{:S(2)}) async-start(bf16[32,22,8,128]{3,2,1,0:T(8,128)(2,1)} %get-tuple-element.56), calls=%async_computation.2 | async-start | bytes 2883584 | tf_op jit(solution)/shard_map/all_to_all | solution.py:648
  97.4 2.0 %copy-start.2 = (bf16[576,3584]{1,0:T(8,128)(2,1)}, bf16[576,3584]{1,0:T(8,128)(2,1)S(1)}, u32[]{:S(2)}) copy-start(bf16[576,3584]{1,0:T(8,128)(2,1)S(1)} %get-tuple-element.61.weight_ref) | copy-start | bytes 12386308
  99.4 18.4 %collective-permute-start.20 = (bf16[288,3584]{1,0:T(8,128)(2,1)}, bf16[288,3584]{1,0:T(8,128)(2,1)}, u32[]{:S(2)}, u32[]{:S(2)}) collective-permute-start(bf16[288,3584]{1,0:T(8,128)(2,1)} %get-tuple-element.65), channel_id=1, source_target_pairs={{0,1},{1,0},{2,3},{3,2},{4,5},{5,4},{6,7},{7,6},{8,9},{9,8},{10,11... | collective-permute-start | bytes 6193160 | tf_op jit(solution)/shard_map/ppermute | solution.py:29
  109.1 6.3 %collective-permute-start.18 = (bf16[8,4,22,8,128]{4,3,2,1,0:T(8,128)(2,1)S(1)}, bf16[8,4,22,8,128]{4,3,2,1,0:T(8,128)(2,1)S(1)}, u32[]{:S(2)}, u32[]{:S(2)}) collective-permute-start(bf16[8,4,22,8,128]{4,3,2,1,0:T(8,128)(2,1)S(1)} %bitcast.11), channel_id=1, source_target_pairs={{0,1},{1,0},{2,3},{3,2},{4,5},{5,4},{6,7},{7,6},{8,9},{9,8},{10,11... | collective-permute-start | bytes 4325384 | tf_op jit(solution)/shard_map/ppermute | solution.py:29
  111.6 2.2 %copy-start.3 = (bf16[576,3584]{1,0:T(8,128)(2,1)S(1)}, bf16[576,3584]{1,0:T(8,128)(2,1)}, u32[]{:S(2)}) copy-start(bf16[576,3584]{1,0:T(8,128)(2,1)} %copy-done.2) | copy-start | bytes 12386308
  113.7 2.2 %copy-start.1 = (bf16[576,3584]{1,0:T(8,128)(2,1)S(1)}, bf16[576,3584]{1,0:T(8,128)(2,1)}, u32[]{:S(2)}) copy-start(bf16[576,3584]{1,0:T(8,128)(2,1)} %get-tuple-element.60.weight_ref) | copy-start | bytes 12386308
  115.9 3.3 %copy-start.9 = (f32[24,896]{1,0:T(8,128)S(1)}, f32[24,896]{1,0:T(8,128)}, u32[]{:S(2)}) copy-start(f32[24,896]{1,0:T(8,128)} %copy-done.8) | copy-start | bytes 258052
  117.7 1.5 collective-permute-start.19
  148.6 2.9 %collective-permute-start.21 = (bf16[3,3584]{1,0:T(4,128)(2,1)S(1)}, bf16[3,3584]{1,0:T(4,128)(2,1)S(1)}, u32[]{:S(2)}, u32[]{:S(2)}) collective-permute-start(bf16[3,3584]{1,0:T(4,128)(2,1)S(1)} %get-tuple-element.68), channel_id=1, source_target_pairs={{0,1},{1,0},{2,3},{3,2},{4,5},{5,4},{6,7},{7,6},{8,9},{9,8},{10,11... | collective-permute-start | bytes 64520 | tf_op jit(solution)/shard_map/ppermute | solution.py:29
